TPU v7x, 256 devices: a whole 4x4x8 slice. The times are simulated.
256 devices in a mesh: ctx: 64 (over x, y, z_hi), grp: 4 (over z_lo, core).
Axes of the slice: x: 4, y: 4, z: 8 (z_hi: 4, z_lo: 2; z = z_hi * 2 + z_lo), core: 2. Of those that a mesh axis runs over, the one named last changes fastest.
Arguments:
- q_latent: bfloat16 [8, 128, 512], P('grp', 'ctx'), parts along dimension 0, may hold values from -48 to 48
- q_rope: bfloat16 [8, 128, 64], P('grp', 'ctx'), parts along dimension 0, may hold values from -48 to 48
- latent_cache: bfloat16 [2048, 64, 576], P(('grp', 'ctx')), parts along dimension 0, may hold values from -6 to 6
- page_table: int32 [8, 256], P('grp'), parts along dimension 0, may hold values from 0 to 511, as said below
- lengths: int32 [8], P('grp'), parts along dimension 0, may hold values from 1 to 16384, 20480 in all
- w_uv: bfloat16 [128, 512, 128], P('ctx'), may hold values from -6 to 6
- w_out: bfloat16 [16384, 7168], P('ctx'), may hold values from -0.046875 to 0.046875
Outputs:
- layer_out: bfloat16 [8, 7168], P('grp'), parts along dimension 0
There are 4 independent parts, one for each index of `grp`. A program takes and returns all parts, laid end to end along the dimension named above; an argument that names none is the same for every part. Nothing has to cross between parts.
Inputs may be any that keep to these rules, and one draw needn't show every extreme that they name: `page_table`: every page number stands exactly once in the table. The longest row is at most 16384; all lengths sum to 20480.
All inputs are finite; a program needn't handle non-finite values.
Results may differ from a plain program's by a relative error of at most 0.03.
Values may be sent and summed in bfloat16 or wider, within the bound.
No kernel may reach another device: no remote copies, remote signals or barrier semaphores. Data moves between devices by JAX's collectives and lax.ppermute only.
A program may use at most 128 MiB of HBM per device.

v0:
```python
import jax
import jax.numpy as jnp
from jax import lax
from jax.sharding import PartitionSpec as P

ROPE = 64
V = 128


NEG = -1e30


def finish(row_sums, row_outs, w_uv, w_out):
    latent = (row_outs / row_sums[..., None]).astype(jnp.bfloat16)
    head_out = jnp.einsum("rhc,hcv->rhv", latent, w_uv, preferred_element_type=jnp.float32).astype(
        jnp.bfloat16
    )
    flat = head_out.reshape(head_out.shape[0], -1)
    return jnp.dot(flat, w_out, preferred_element_type=jnp.float32)


def local(q_latent, q_rope, latent_cache, page_table, lengths, w_uv, w_out):
    score_scale = (V + ROPE) ** (-0.5)
    local_query = jnp.concatenate([q_latent, q_rope], axis=2)
    all_query = lax.all_gather(local_query, "ctx", axis=1, tiled=True)
    pages_here = latent_cache.shape[0]
    page_len = latent_cache.shape[1]
    row_count = page_table.shape[0]
    slot_width = page_table.shape[1]
    slot_count = row_count * slot_width
    latent_width = q_latent.shape[2]
    inverse = (
        jnp.zeros((slot_count,), jnp.int32)
        .at[page_table.reshape(-1)]
        .set(jnp.arange(slot_count, dtype=jnp.int32))
    )
    first_page = lax.axis_index("ctx") * pages_here
    slot_ids = lax.dynamic_slice_in_dim(inverse, first_page, pages_here)
    owner_row = slot_ids // slot_width
    logical = slot_ids % slot_width
    page_query = all_query[owner_row]
    scores = (
        jnp.einsum("phc,ptc->pht", page_query, latent_cache, preferred_element_type=jnp.float32)
        * score_scale
    )
    position = logical[:, None] * page_len + jnp.arange(page_len, dtype=jnp.int32)[None, :]
    live_mask = position < lengths[owner_row][:, None]
    scores = jnp.where(live_mask[:, None, :], scores, jnp.float32(NEG))
    page_top = jnp.max(scores, axis=2)
    member = owner_row[None, :] == jnp.arange(row_count, dtype=jnp.int32)[:, None]
    row_top = jnp.max(jnp.where(member[:, :, None], page_top[None, :, :], jnp.float32(NEG)), axis=1)
    row_shift = row_top[owner_row]
    weights = jnp.where(
        live_mask[:, None, :], jnp.exp(scores - row_shift[:, :, None]), jnp.float32(0.0)
    ).astype(jnp.bfloat16)
    page_sum = jnp.sum(weights.astype(jnp.float32), axis=2)
    page_out = jnp.einsum(
        "pht,ptc->phc",
        weights,
        latent_cache[:, :, :latent_width],
        preferred_element_type=jnp.float32,
    )
    onehot = member.astype(jnp.float32)
    row_sum = jnp.dot(onehot, page_sum, precision=lax.Precision.HIGHEST)
    row_out = jnp.dot(
        onehot, page_out.reshape(pages_here, -1), precision=lax.Precision.HIGHEST
    ).reshape(row_count, -1, latent_width)
    tops = lax.all_to_all(
        row_top[None].astype(jnp.bfloat16), "ctx", split_axis=2, concat_axis=0, tiled=True
    ).astype(jnp.float32)
    sums = lax.all_to_all(
        row_sum[None].astype(jnp.bfloat16), "ctx", split_axis=2, concat_axis=0, tiled=True
    ).astype(jnp.float32)
    outs = lax.all_to_all(
        row_out[None].astype(jnp.bfloat16), "ctx", split_axis=2, concat_axis=0, tiled=True
    ).astype(jnp.float32)
    best = jnp.max(tops, axis=0)
    factor = jnp.exp(tops - best[None])
    merged_sum = jnp.sum(factor * sums, axis=0)
    merged_out = jnp.sum(factor[..., None] * outs, axis=0)
    partial_out = finish(merged_sum, merged_out, w_uv, w_out)
    return lax.psum(partial_out, "ctx").astype(jnp.bfloat16)


def solution(mesh):
    in_specs = (
        P("grp", "ctx", None),
        P("grp", "ctx", None),
        P(("grp", "ctx"), None, None),
        P("grp", None),
        P("grp"),
        P("ctx", None, None),
        P("ctx", None),
    )
    out_specs = P("grp", None)
    return jax.shard_map(local, mesh=mesh, in_specs=in_specs, out_specs=out_specs, check_vma=False)
```

profile of v0, /device:TPU:0, one launch (start us, length us, event | category | flops | bytes accessed | tf_op | source)
XLA Modules:
  0.0 631.4 jit_solution(18011796447968477221)
XLA Ops:
  0.0 0.0 copy-start
  0.0 0.0 copy-start.1
  0.0 0.8 copy.43
  0.8 0.7 copy.52
  1.5 2.4 scatter_custom_fusion
  3.9 0.1 fusion.14
  4.0 0.1 compare_select_fusion.1
  4.1 0.7 copy.42
  4.8 194.5 %all_gather.3 = bf16[2,128,576]{2,0,1:T(2,128)(2,1)S(1)} all-gather(bf16[2,2,576]{2,0,1:T(2,128)(2,1)S(1)} %pad_maximum_fusion), channel_id=1, replica_groups=mesh['ctx'=64,'grp'=4] {'ctx'}, dimensions={1}, use_global_device_ids=true | all-gather | bytes 299520 | tf_op jit(solution)/shard_map/all_gather | solution.py:25
  199.3 0.7 copy.44
  200.0 1.3 gather_fusion
  201.3 0.8 gather_fusion.1
  202.1 0.1 add_compare_fusion
  202.2 0.0 copy-done.1
  202.2 0.4 fusion.16
  202.6 0.1 select_reduce_fusion
  202.7 0.6 gather_fusion.2
  203.2 0.1 convert_reduce_fusion
  203.4 0.1 fusion.3
  203.5 0.8 copy.49
  204.3 4.6 all-to-all-start.2
  208.9 0.7 convolution_bitcast_fusion
  209.6 0.8 copy.45
  210.4 10.7 %all-to-all-done.2 = bf16[1,2,128]{1,0,2:T(2,128)(2,1)S(1)} async-done(((bf16[1,2,128]{1,0,2:T(2,128)(2,1)}), bf16[1,2,128]{1,0,2:T(2,128)(2,1)S(1)}, u32[]{:S(2)}, u32[]{:S(2)}) %all-to-all-start.2) | async-done | bytes 544 | tf_op jit(solution)/shard_map/all_to_all | solution.py:71
  221.1 4.6 all-to-all-start
  225.7 2.9 fusion
  228.6 9.2 %all-to-all-done = bf16[1,2,128]{1,0,2:T(2,128)(2,1)S(1)} async-done(((bf16[1,2,128]{1,0,2:T(2,128)(2,1)}), bf16[1,2,128]{1,0,2:T(2,128)(2,1)S(1)}, u32[]{:S(2)}, u32[]{:S(2)}) %all-to-all-start) | async-done | bytes 544 | tf_op jit(solution)/shard_map/all_to_all | solution.py:68
  237.9 4.6 all-to-all-start.1
  242.5 0.1 copy.50
  242.6 0.2 reshape.128
  242.7 0.1 copy.46
  242.8 0.2 all_to_all.11
  243.1 0.1 copy.51
  243.2 0.5 copy.47
  243.7 12.7 %all-to-all-done.1 = bf16[1,2,128,512]{3,1,0,2:T(2,128)(2,1)S(1)} async-done(((bf16[1,2,128,512]{3,1,0,2:T(2,128)(2,1)}), bf16[1,2,128,512]{3,1,0,2:T(2,128)(2,1)S(1)}, u32[]{:S(2)}, u32[]{:S(2)}) %all-to-all-start.1) | async-done | bytes 262176 | tf_op jit(solution)/shard_map/all_to_all | solution.py:74
  256.4 0.3 fusion.5
  256.7 0.0 copy-done
  256.7 2.8 fusion.4
  259.5 371.9 %psum.7 = bf16[2,7168]{1,0:T(2,128)(2,1)} all-reduce(f32[2,7168]{1,0:T(2,128)S(1)} %fusion.4), channel_id=1, replica_groups=mesh['ctx'=64,'grp'=4] {'ctx'}, use_global_device_ids=true, to_apply=%region_7.8 | all-reduce | flops 14336 | bytes 86016 | tf_op jit(solution)/shard_map/psum | solution.py:82
  (9 shorter events, 0.1 us)
Async XLA Ops:
  0.0 256.7 %copy-start = (bf16[2,512,128]{2,1,0:T(8,128)(2,1)S(1)}, bf16[2,512,128]{2,1,0:T(8,128)(2,1)}, u32[]{:S(2)}) copy-start(bf16[2,512,128]{2,1,0:T(8,128)(2,1)} %param.12) | copy-start | bytes 786436
  0.0 202.2 %copy-start.1 = (bf16[8,64,576]{2,1,0:T(8,128)(2,1)S(1)}, bf16[8,64,576]{2,1,0:T(8,128)(2,1)}, u32[]{:S(2)}) copy-start(bf16[8,64,576]{2,1,0:T(8,128)(2,1)} %param.9) | copy-start | bytes 1769476
  204.3 16.9 %all-to-all-start.2 = ((bf16[1,2,128]{1,0,2:T(2,128)(2,1)}), bf16[1,2,128]{1,0,2:T(2,128)(2,1)S(1)}, u32[]{:S(2)}, u32[]{:S(2)}) async-start(bf16[1,2,128]{1,0,2:T(2,128)(2,1)} %copy.49), calls=%async_computation.2 | async-start | bytes 131072 | tf_op jit(solution)/shard_map/all_to_all | solution.py:71
  221.1 16.7 %all-to-all-start = ((bf16[1,2,128]{1,0,2:T(2,128)(2,1)}), bf16[1,2,128]{1,0,2:T(2,128)(2,1)S(1)}, u32[]{:S(2)}, u32[]{:S(2)}) async-start(bf16[1,2,128]{1,0,2:T(2,128)(2,1)} %copy.45), calls=%async_computation | async-start | bytes 131072 | tf_op jit(solution)/shard_map/all_to_all | solution.py:68
  237.9 18.5 %all-to-all-start.1 = ((bf16[1,2,128,512]{3,1,0,2:T(2,128)(2,1)}), bf16[1,2,128,512]{3,1,0,2:T(2,128)(2,1)S(1)}, u32[]{:S(2)}, u32[]{:S(2)}) async-start(bf16[1,2,128,512]{3,1,0,2:T(2,128)(2,1)} %fusion), calls=%async_computation.1 | async-start | bytes 524288 | tf_op jit(solution)/shard_map/all_to_all | solution.py:74
where the time goes:
time: 632 us; the launch traced here: 631 us
  blocking collectives  566 us (90%)
  waiting for transfers between devices  32.7 us (5%)
  starting transfers between devices  13.8 us (2%)
  local copies, waits for them, and re-layouts  10.6 us (2%)
  matrix products  6.91 us (1%)
    psum x1, blocking collectives, local(): return lax.psum(partial_out, 'ctx').astype(jnp.bfloat16)  372 us
    all_gather x1, blocking collectives, local(): all_query = lax.all_gather(local_query, 'ctx', axis=1, tiled=True)  194 us
    all_to_all x1, waiting for transfers between devices, local(): lax.all_to_all(row_out[None].astype(jnp.bfloat16), 'ctx', split_axis=2, c...  12.7 us
  transfers between devices with their start and end apart: 3, of which 3 were waited for; matrix products, arithmetic and copies ran while one was open for 1% of the time, Pallas kernels for 0%

commit v1 on v0

v1 whole, which is shorter than its diff:
```python
import jax
import jax.numpy as jnp
from jax import lax
from jax.sharding import PartitionSpec as P

ROPE = 64
V = 128
NEG = -1e30
CTX = "ctx"


def xor_pairs(count, mask):
    return [(i, i ^ mask) for i in range(count)]


def sum_of_four(x, count, low):
    a, b, c = (lax.ppermute(x, CTX, xor_pairs(count, k << low)) for k in (1, 2, 3))
    return (x + a) + (b + c)


def local(q_latent, q_rope, latent_cache, page_table, lengths, w_uv, w_out):
    score_scale = (V + ROPE) ** (-0.5)
    rows, heads, latent = q_latent.shape
    pages, page_len, width = latent_cache.shape
    count = lax.axis_size(CTX)
    mixed = rows * heads

    query = jnp.concatenate([q_latent, q_rope], axis=2).reshape(1, mixed, width)
    queries = lax.all_to_all(
        jnp.broadcast_to(query, (count, mixed, width)), CTX, split_axis=0, concat_axis=0, tiled=True
    ).reshape(count * mixed, width)

    slots = page_table.size
    page_ids = lax.axis_index(CTX) * pages + jnp.arange(pages, dtype=jnp.int32)
    table = page_table.reshape(1, slots)
    slot = jnp.sum(
        jnp.where(table == page_ids[:, None], jnp.arange(slots, dtype=jnp.int32)[None], 0), axis=1
    )
    owner = slot // page_table.shape[1]
    logical = slot % page_table.shape[1]
    position = logical[:, None] * page_len + jnp.arange(page_len, dtype=jnp.int32)[None]
    rank = jnp.arange(rows, dtype=jnp.int32)
    live = (owner[None, :, None] == rank[:, None, None]) & (
        position[None] < lengths[:, None, None]
    )
    live = live.reshape(rows, pages * page_len)
    live = jnp.broadcast_to(live[None, :, None], (count, rows, heads, pages * page_len))
    live = live.reshape(count * mixed, pages * page_len)

    keys = latent_cache.reshape(pages * page_len, width)
    scores = (
        lax.dot_general(queries, keys, (((1,), (1,)), ((), ())), preferred_element_type=jnp.float32)
        * score_scale
    )
    scores = jnp.where(live, scores, jnp.float32(NEG))
    shift = jnp.max(scores, axis=1, keepdims=True).astype(jnp.bfloat16)
    weights = jnp.where(live, jnp.exp(scores - shift.astype(jnp.float32)), 0.0).astype(jnp.bfloat16)
    sums = jnp.sum(weights.astype(jnp.float32), axis=1, keepdims=True)
    outs = jnp.dot(weights, keys[:, :latent], preferred_element_type=jnp.float32)
    sums_hi = sums.astype(jnp.bfloat16)
    sums_lo = (sums - sums_hi.astype(jnp.float32)).astype(jnp.bfloat16)
    state = jnp.concatenate([outs.astype(jnp.bfloat16), shift, sums_hi, sums_lo], axis=1)
    state = jnp.pad(state, ((0, 0), (0, 125))).reshape(count, mixed, latent + 128)

    state = lax.all_to_all(state, CTX, split_axis=0, concat_axis=0, tiled=True)
    shift = state[:, :, latent].astype(jnp.float32)
    sums = state[:, :, latent + 1].astype(jnp.float32) + state[:, :, latent + 2].astype(jnp.float32)
    factor = jnp.exp(shift - jnp.max(shift, axis=0, keepdims=True))
    total = jnp.sum(factor * sums, axis=0)
    merged = jnp.sum(factor[:, :, None] * state[:, :, :latent].astype(jnp.float32), axis=0)
    attended = (merged / total[:, None]).astype(jnp.bfloat16).reshape(rows, heads, latent)
    head_out = jnp.einsum("rhc,hcv->rhv", attended, w_uv, preferred_element_type=jnp.float32)
    flat = head_out.astype(jnp.bfloat16).reshape(rows, -1)
    term = jnp.dot(flat, w_out, preferred_element_type=jnp.float32)
    for low in (4, 2, 0):
        term = sum_of_four(term, count, low)
    return term.astype(jnp.bfloat16)


def solution(mesh):
    in_specs = (
        P("grp", "ctx", None),
        P("grp", "ctx", None),
        P(("grp", "ctx"), None, None),
        P("grp", None),
        P("grp"),
        P("ctx", None, None),
        P("ctx", None),
    )
    return jax.shard_map(local, mesh=mesh, in_specs=in_specs, out_specs=P("grp", None), check_vma=False)
```

time: 632 us -> 85.2 us (0.13)
  the two profiles are of different devices: /device:TPU:0 before, /device:TPU:2 now
where the time goes in v1:
time: 85.2 us; the launch traced here: 84.9 us
  starting transfers between devices  29.5 us (35%)
  waiting for transfers between devices  23.7 us (28%)
  blocking collectives  19.8 us (23%)
  matrix products  4.63 us (5%)
  other arithmetic  3.68 us (4%)
  local copies, waits for them, and re-layouts  3.55 us (4%)
    all_to_all x1, blocking collectives, local(): state = lax.all_to_all(state, CTX, split_axis=0, concat_axis=0, tiled=True)  19.8 us
    ppermute x9, starting transfers between devices, sum_of_four(): lax.ppermute(x, CTX, xor_pairs(count, k << low))  14.9 us
    all_to_all x1, starting transfers between devices, local(): lax.all_to_all(jnp.broadcast_to(query, (count, mixed, width)), CTX, split...  14.7 us
    all_to_all x1, waiting for transfers between devices, local(): lax.all_to_all(jnp.broadcast_to(query, (count, mixed, width)), CTX, split...  13.1 us
    ppermute x9, waiting for transfers between devices, sum_of_four(): lax.ppermute(x, CTX, xor_pairs(count, k << low))  10.6 us
    dot_general x1, matrix products, local(): term = jnp.dot(flat, w_out, preferred_element_type=jnp.float32)  2.74 us
  transfers between devices with their start and end apart: 10, of which 9 were waited for; matrix products, arithmetic and copies ran while one was open for 3% of the time, Pallas kernels for 0%

profile of v1, /device:TPU:2, one launch (start us, length us, event | category | flops | bytes accessed | tf_op | source)
XLA Modules:
  0.0 84.9 jit_solution(5847399593512223900)
XLA Ops:
  0.0 0.0 copy-start
  0.0 0.0 copy-start.1
  0.0 0.8 pad_maximum_fusion
  0.8 0.8 broadcast_in_dim.30
  1.6 14.7 %all-to-all-start = ((bf16[64,4,576]{2,1,0:T(4,128)(2,1)}), bf16[64,4,576]{2,1,0:T(4,128)(2,1)S(1)}, u32[]{:S(2)}, u32[]{:S(2)}) async-start(bf16[64,4,576]{2,1,0:T(4,128)(2,1)} %broadcast_in_dim.30), calls=%async_computation | async-start | bytes 655360 | tf_op jit(solution)/shard_map/all_to_all | solution.py:29
  16.3 0.7 copy.48
  17.0 0.2 select_reduce_fusion
  17.2 0.1 and.41
  17.3 0.1 and.42
  17.4 0.1 broadcast_reduce_fusion
  17.5 0.1 add.85
  17.5 0.1 add.87
  17.6 0.7 compare_and_fusion
  18.3 0.1 broadcast_in_dim.28
  18.5 0.3 reshape.179
  18.8 13.1 %all-to-all-done = bf16[64,4,576]{2,1,0:T(4,128)(2,1)S(1)} async-done(((bf16[64,4,576]{2,1,0:T(4,128)(2,1)}), bf16[64,4,576]{2,1,0:T(4,128)(2,1)S(1)}, u32[]{:S(2)}, u32[]{:S(2)}) %all-to-all-start) | async-done | bytes 294944 | tf_op jit(solution)/shard_map/all_to_all | solution.py:29
  31.9 0.2 reshape.180
  32.0 1.6 %fusion.21 = (bf16[256]{0:T(256)(128)(2,1)S(1)}, f32[256,512]{1,0:T(8,128)S(1)}) fusion(pred[256,512]{1,0:T(32,128)(4,1)S(1)} %reshape.179, bf16[256,576]{1,0:T(8,128)(2,1)S(1)} %reshape.180, bf16[512,576]{1,0:T(8,128)(2,1)} %bitcast.29), kind=kOutput, calls=%fused_computation.46 | convolution fusion | flops 151387904 | bytes 1540608 | tf_op jit(solution)/shard_map/dot_general | solution.py:52
  33.6 0.3 convert_reduce_fusion
  33.9 0.1 convert_element_type.126
  34.0 0.1 copy.34
  34.2 0.1 copy.35
  34.3 0.0 copy-done.1
  34.3 0.3 convolution_convert_fusion
  34.6 0.1 fusion.10
  34.8 0.1 reshape.182
  34.8 19.8 %all_to_all.10 = bf16[64,4,640]{2,1,0:T(4,128)(2,1)S(1)} all-to-all(bf16[64,4,640]{2,1,0:T(4,128)(2,1)S(1)} %reshape.182), channel_id=1, replica_groups=mesh['ctx'=64,'grp'=4] {'ctx'}, dimensions={0} | all-to-all | bytes 655360 | tf_op jit(solution)/shard_map/all_to_all | solution.py:65
  54.6 0.2 fusion.20
  54.8 0.1 copy.45
  54.9 0.1 copy.44
  55.1 0.1 copy.46
  55.2 0.1 fusion.14
  55.3 0.2 fusion.18
  55.5 0.1 div.27
  55.5 0.1 copy.37
  55.6 0.2 multiply_reduce_fusion
  55.9 0.1 divide_convert_fusion
  55.9 0.0 copy-done
  56.0 2.7 %fusion.6 = f32[2,7168]{1,0:T(2,128)S(1)} fusion(bf16[256,7168]{1,0:T(8,128)(2,1)} %param.13, bf16[2,512,128]{2,1,0:T(8,128)(2,1)S(1)} %copy-done, bf16[2,2,512]{2,1,0:T(2,128)(2,1)S(1)} %divide_convert_fusion), kind=kOutput, calls=%fused_computation.10 | convolution fusion | flops 7864832 | bytes 3993600 | tf_op jit(solution)/shard_map/dot_general | solution.py:74
  58.7 0.2 collective-permute-start.2
  58.9 3.5 %collective-permute-start.1 = (f32[2,7168]{1,0:T(2,128)S(1)}, f32[2,7168]{1,0:T(2,128)S(1)}, u32[]{:S(2)}, u32[]{:S(2)}) collective-permute-start(f32[2,7168]{1,0:T(2,128)S(1)} %fusion.6), channel_id=1, source_target_pairs={{0,128},{4,132},{8,136},{12,140},{16,144},{20,148},{24,152},{28,15... | collective-permute-start | bytes 172040 | tf_op jit(solution)/shard_map/ppermute | solution.py:17
  62.4 0.4 collective-permute-start
  62.8 0.1 collective-permute-done.2
  62.9 1.7 %collective-permute-done.1 = f32[2,7168]{1,0:T(2,128)S(1)} collective-permute-done((f32[2,7168]{1,0:T(2,128)S(1)}, f32[2,7168]{1,0:T(2,128)S(1)}, u32[]{:S(2)}, u32[]{:S(2)}) %collective-permute-start.1) | collective-permute-done | bytes 57376 | tf_op jit(solution)/shard_map/ppermute | solution.py:17
  64.6 2.0 %collective-permute-done = f32[2,7168]{1,0:T(2,128)S(1)} collective-permute-done((f32[2,7168]{1,0:T(2,128)S(1)}, f32[2,7168]{1,0:T(2,128)S(1)}, u32[]{:S(2)}, u32[]{:S(2)}) %collective-permute-start) | collective-permute-done | bytes 57376 | tf_op jit(solution)/shard_map/ppermute | solution.py:17
  66.6 0.1 add_add_fusion.1
  66.6 0.5 collective-permute-start.5
  67.1 2.3 %collective-permute-start.4 = (f32[2,7168]{1,0:T(2,128)S(1)}, f32[2,7168]{1,0:T(2,128)S(1)}, u32[]{:S(2)}, u32[]{:S(2)}) collective-permute-start(f32[2,7168]{1,0:T(2,128)S(1)} %add_add_fusion.1), channel_id=1, source_target_pairs={{0,32},{4,36},{8,40},{12,44},{16,48},{20,52},{24,56},{28,60},{32,0... | collective-permute-start | bytes 172040 | tf_op jit(solution)/shard_map/ppermute | solution.py:17
  69.4 1.4 %collective-permute-start.3 = (f32[2,7168]{1,0:T(2,128)S(1)}, f32[2,7168]{1,0:T(2,128)S(1)}, u32[]{:S(2)}, u32[]{:S(2)}) collective-permute-start(f32[2,7168]{1,0:T(2,128)S(1)} %add_add_fusion.1), channel_id=1, source_target_pairs={{0,16},{4,20},{8,24},{12,28},{16,0},{20,4},{24,8},{28,12},{32,48},... | collective-permute-start | bytes 172040 | tf_op jit(solution)/shard_map/ppermute | solution.py:17
  70.8 1.3 %collective-permute-done.5 = f32[2,7168]{1,0:T(2,128)S(1)} collective-permute-done((f32[2,7168]{1,0:T(2,128)S(1)}, f32[2,7168]{1,0:T(2,128)S(1)}, u32[]{:S(2)}, u32[]{:S(2)}) %collective-permute-start.5) | collective-permute-done | bytes 57376 | tf_op jit(solution)/shard_map/ppermute | solution.py:17
  72.1 0.7 collective-permute-done.4
  72.8 0.8 collective-permute-done.3
  73.6 0.1 add_add_fusion
  73.6 0.5 collective-permute-start.8
  74.1 4.4 %collective-permute-start.7 = (f32[2,7168]{1,0:T(2,128)S(1)}, f32[2,7168]{1,0:T(2,128)S(1)}, u32[]{:S(2)}, u32[]{:S(2)}) collective-permute-start(f32[2,7168]{1,0:T(2,128)S(1)} %add_add_fusion), channel_id=1, source_target_pairs={{0,8},{4,12},{8,0},{12,4},{16,24},{20,28},{24,16},{28,20},{32,40},... | collective-permute-start | bytes 172040 | tf_op jit(solution)/shard_map/ppermute | solution.py:17
  78.6 1.6 %collective-permute-start.6 = (f32[2,7168]{1,0:T(2,128)S(1)}, f32[2,7168]{1,0:T(2,128)S(1)}, u32[]{:S(2)}, u32[]{:S(2)}) collective-permute-start(f32[2,7168]{1,0:T(2,128)S(1)} %add_add_fusion), channel_id=1, source_target_pairs={{0,4},{4,0},{8,12},{12,8},{16,20},{20,16},{24,28},{28,24},{32,36},... | collective-permute-start | bytes 172040 | tf_op jit(solution)/shard_map/ppermute | solution.py:17
  80.2 0.0 collective-permute-done.8
  80.2 2.0 %collective-permute-done.7 = f32[2,7168]{1,0:T(2,128)S(1)} collective-permute-done((f32[2,7168]{1,0:T(2,128)S(1)}, f32[2,7168]{1,0:T(2,128)S(1)}, u32[]{:S(2)}, u32[]{:S(2)}) %collective-permute-start.7) | collective-permute-done | bytes 57376 | tf_op jit(solution)/shard_map/ppermute | solution.py:17
  82.2 2.0 %collective-permute-done.6 = f32[2,7168]{1,0:T(2,128)S(1)} collective-permute-done((f32[2,7168]{1,0:T(2,128)S(1)}, f32[2,7168]{1,0:T(2,128)S(1)}, u32[]{:S(2)}, u32[]{:S(2)}) %collective-permute-start.6) | collective-permute-done | bytes 57376 | tf_op jit(solution)/shard_map/ppermute | solution.py:17
  84.3 0.7 add_convert_fusion
  (11 shorter events, 0.1 us)
Async XLA Ops:
  0.0 56.0 %copy-start = (bf16[2,512,128]{2,1,0:T(8,128)(2,1)S(1)}, bf16[2,512,128]{2,1,0:T(8,128)(2,1)}, u32[]{:S(2)}) copy-start(bf16[2,512,128]{2,1,0:T(8,128)(2,1)} %param.12) | copy-start | bytes 786436
  0.0 34.3 %copy-start.1 = (bf16[8,64,576]{2,1,0:T(8,128)(2,1)S(1)}, bf16[8,64,576]{2,1,0:T(8,128)(2,1)}, u32[]{:S(2)}) copy-start(bf16[8,64,576]{2,1,0:T(8,128)(2,1)} %param.9) | copy-start | bytes 1769476
  1.6 30.3 %all-to-all-start = ((bf16[64,4,576]{2,1,0:T(4,128)(2,1)}), bf16[64,4,576]{2,1,0:T(4,128)(2,1)S(1)}, u32[]{:S(2)}, u32[]{:S(2)}) async-start(bf16[64,4,576]{2,1,0:T(4,128)(2,1)} %broadcast_in_dim.30), calls=%async_computation | async-start | bytes 655360 | tf_op jit(solution)/shard_map/all_to_all | solution.py:29
  58.7 4.2 %collective-permute-start.2 = (f32[2,7168]{1,0:T(2,128)S(1)}, f32[2,7168]{1,0:T(2,128)S(1)}, u32[]{:S(2)}, u32[]{:S(2)}) collective-permute-start(f32[2,7168]{1,0:T(2,128)S(1)} %fusion.6), channel_id=1, source_target_pairs={{0,192},{4,196},{8,200},{12,204},{16,208},{20,212},{24,216},{28,22... | collective-permute-start | bytes 172040 | tf_op jit(solution)/shard_map/ppermute | solution.py:17
  58.9 5.7 %collective-permute-start.1 = (f32[2,7168]{1,0:T(2,128)S(1)}, f32[2,7168]{1,0:T(2,128)S(1)}, u32[]{:S(2)}, u32[]{:S(2)}) collective-permute-start(f32[2,7168]{1,0:T(2,128)S(1)} %fusion.6), channel_id=1, source_target_pairs={{0,128},{4,132},{8,136},{12,140},{16,144},{20,148},{24,152},{28,15... | collective-permute-start | bytes 172040 | tf_op jit(solution)/shard_map/ppermute | solution.py:17
  62.4 4.2 %collective-permute-start = (f32[2,7168]{1,0:T(2,128)S(1)}, f32[2,7168]{1,0:T(2,128)S(1)}, u32[]{:S(2)}, u32[]{:S(2)}) collective-permute-start(f32[2,7168]{1,0:T(2,128)S(1)} %fusion.6), channel_id=1, source_target_pairs={{0,64},{4,68},{8,72},{12,76},{16,80},{20,84},{24,88},{28,92},{32,9... | collective-permute-start | bytes 172040 | tf_op jit(solution)/shard_map/ppermute | solution.py:17
  66.6 5.5 %collective-permute-start.5 = (f32[2,7168]{1,0:T(2,128)S(1)}, f32[2,7168]{1,0:T(2,128)S(1)}, u32[]{:S(2)}, u32[]{:S(2)}) collective-permute-start(f32[2,7168]{1,0:T(2,128)S(1)} %add_add_fusion.1), channel_id=1, source_target_pairs={{0,48},{4,52},{8,56},{12,60},{16,32},{20,36},{24,40},{28,44},{32,1... | collective-permute-start | bytes 172040 | tf_op jit(solution)/shard_map/ppermute | solution.py:17
  67.1 5.7 %collective-permute-start.4 = (f32[2,7168]{1,0:T(2,128)S(1)}, f32[2,7168]{1,0:T(2,128)S(1)}, u32[]{:S(2)}, u32[]{:S(2)}) collective-permute-start(f32[2,7168]{1,0:T(2,128)S(1)} %add_add_fusion.1), channel_id=1, source_target_pairs={{0,32},{4,36},{8,40},{12,44},{16,48},{20,52},{24,56},{28,60},{32,0... | collective-permute-start | bytes 172040 | tf_op jit(solution)/shard_map/ppermute | solution.py:17
  69.4 4.2 %collective-permute-start.3 = (f32[2,7168]{1,0:T(2,128)S(1)}, f32[2,7168]{1,0:T(2,128)S(1)}, u32[]{:S(2)}, u32[]{:S(2)}) collective-permute-start(f32[2,7168]{1,0:T(2,128)S(1)} %add_add_fusion.1), channel_id=1, source_target_pairs={{0,16},{4,20},{8,24},{12,28},{16,0},{20,4},{24,8},{28,12},{32,48},... | collective-permute-start | bytes 172040 | tf_op jit(solution)/shard_map/ppermute | solution.py:17
  73.6 6.6 %collective-permute-start.8 = (f32[2,7168]{1,0:T(2,128)S(1)}, f32[2,7168]{1,0:T(2,128)S(1)}, u32[]{:S(2)}, u32[]{:S(2)}) collective-permute-start(f32[2,7168]{1,0:T(2,128)S(1)} %add_add_fusion), channel_id=1, source_target_pairs={{0,12},{4,8},{8,4},{12,0},{16,28},{20,24},{24,20},{28,16},{32,44},... | collective-permute-start | bytes 172040 | tf_op jit(solution)/shard_map/ppermute | solution.py:17
  74.1 8.1 %collective-permute-start.7 = (f32[2,7168]{1,0:T(2,128)S(1)}, f32[2,7168]{1,0:T(2,128)S(1)}, u32[]{:S(2)}, u32[]{:S(2)}) collective-permute-start(f32[2,7168]{1,0:T(2,128)S(1)} %add_add_fusion), channel_id=1, source_target_pairs={{0,8},{4,12},{8,0},{12,4},{16,24},{20,28},{24,16},{28,20},{32,40},... | collective-permute-start | bytes 172040 | tf_op jit(solution)/shard_map/ppermute | solution.py:17
  78.6 5.7 %collective-permute-start.6 = (f32[2,7168]{1,0:T(2,128)S(1)}, f32[2,7168]{1,0:T(2,128)S(1)}, u32[]{:S(2)}, u32[]{:S(2)}) collective-permute-start(f32[2,7168]{1,0:T(2,128)S(1)} %add_add_fusion), channel_id=1, source_target_pairs={{0,4},{4,0},{8,12},{12,8},{16,20},{20,16},{24,28},{28,24},{32,36},... | collective-permute-start | bytes 172040 | tf_op jit(solution)/shard_map/ppermute | solution.py:17

commit v2 on v1

v2 whole, which is shorter than its diff:
```python
import functools
import jax
import jax.numpy as jnp
from jax import lax
from jax.experimental import pallas as pl
from jax.experimental.pallas import tpu as pltpu
from jax.sharding import PartitionSpec as P

ROPE = 64
V = 128
NEG = -1e30
CTX = "ctx"
LANES = 128


def xor_pairs(count, mask):
    return [(i, i ^ mask) for i in range(count)]


def sum_of_four(x, count, low):
    a, b, c = (lax.ppermute(x, CTX, xor_pairs(count, k << low)) for k in (1, 2, 3))
    f = jnp.float32
    return (x.astype(f) + a.astype(f)) + (b.astype(f) + c.astype(f))


def attend_kernel(rows, heads, page_len, latent, here_ref, lengths_ref, table_ref, q_ref, keys_ref, state_ref):
    tokens = keys_ref.shape[0]
    pages = tokens // page_len
    slots = table_ref.shape[1]
    page = here_ref[0] * pages + lax.broadcasted_iota(jnp.int32, (pages, slots), 0)
    place = lax.broadcasted_iota(jnp.int32, (pages, slots), 1)
    token = lax.broadcasted_iota(jnp.int32, (pages, tokens), 1)
    mine = token // page_len == lax.broadcasted_iota(jnp.int32, (pages, tokens), 0)
    lives = []
    for r in range(rows):
        hit = jnp.broadcast_to(table_ref[r : r + 1, :], (pages, slots)) == page
        room = jnp.where(hit, lengths_ref[r] - place * page_len, 0)
        room = jnp.max(room, axis=1, keepdims=True)
        alive = mine & (token % page_len < room)
        lives.append(jnp.max(jnp.where(alive, 1.0, 0.0), axis=0, keepdims=True))
    count = q_ref.shape[0]
    row = lax.broadcasted_iota(jnp.int32, (count, 1), 0) // heads % rows
    live = jnp.broadcast_to(lives[0], (count, tokens))
    for r in range(1, rows):
        live = jnp.where(row == r, lives[r], live)
    live = live > 0.5

    scores = lax.dot_general(
        q_ref[...], keys_ref[...], (((1,), (1,)), ((), ())), preferred_element_type=jnp.float32
    ) * ((V + ROPE) ** (-0.5))
    scores = jnp.where(live, scores, NEG)
    shift = jnp.max(scores, axis=1, keepdims=True).astype(jnp.bfloat16).astype(jnp.float32)
    weights = jnp.where(live, jnp.exp(scores - shift), 0.0).astype(jnp.bfloat16)
    total = jnp.sum(weights.astype(jnp.float32), axis=1, keepdims=True)
    outs = jnp.dot(weights, keys_ref[:, :latent], preferred_element_type=jnp.float32)
    state_ref[:, :latent] = outs.astype(jnp.bfloat16)
    high = total.astype(jnp.bfloat16).astype(jnp.float32)
    lane = lax.broadcasted_iota(jnp.int32, (count, LANES), 1)
    stats = jnp.where(lane == 0, shift, jnp.where(lane == 1, high, jnp.where(lane == 2, total - high, 0.0)))
    state_ref[:, latent:] = stats.astype(jnp.bfloat16)


def project_kernel(rows, heads, latent, state_ref, w_uv_ref, w_out_ref, term_ref):
    count = state_ref.shape[0]
    mixed = rows * heads
    lane = lax.broadcasted_iota(jnp.int32, (count, LANES), 1)
    kind = lax.broadcasted_iota(jnp.int32, (count, LANES), 0) % mixed
    own = (lane % mixed == kind) & (lane < 2 * mixed)
    shift = state_ref[:, latent : latent + 1].astype(jnp.float32)
    shift = jnp.where(own, shift, 2 * NEG)
    best = jnp.max(shift, axis=0, keepdims=True)
    factor = jnp.where(own, jnp.exp(shift - best), 0.0)
    high = factor.astype(jnp.bfloat16).astype(jnp.float32)
    factor = jnp.where(lane < mixed, high, factor - high).astype(jnp.bfloat16)
    merged = lax.dot_general(
        factor, state_ref[...], (((0,), (0,)), ((), ())), preferred_element_type=jnp.float32
    )
    merged = merged[:mixed] + merged[mixed : 2 * mixed]
    total = merged[:, latent + 1 : latent + 2] + merged[:, latent + 2 : latent + 3]
    attended = (merged[:, :latent] / total).astype(jnp.bfloat16)
    parts = [
        jnp.dot(attended, w_uv_ref[h], preferred_element_type=jnp.float32) for h in range(heads)
    ]
    flat = jnp.concatenate(
        [
            jnp.concatenate([parts[h][r * heads + h : r * heads + h + 1] for h in range(heads)], axis=1)
            for r in range(rows)
        ],
        axis=0,
    ).astype(jnp.bfloat16)
    term_ref[...] = jnp.dot(flat, w_out_ref[...], preferred_element_type=jnp.float32).astype(
        term_ref.dtype
    )


def local(q_latent, q_rope, latent_cache, page_table, lengths, w_uv, w_out):
    rows, heads, latent = q_latent.shape
    pages, page_len, width = latent_cache.shape
    count = lax.axis_size(CTX)
    mixed = rows * heads
    vmem = pl.BlockSpec(memory_space=pltpu.VMEM)
    smem = pl.BlockSpec(memory_space=pltpu.SMEM)

    query = jnp.concatenate([q_latent, q_rope], axis=2).reshape(1, mixed, width)
    queries = lax.all_to_all(
        jnp.broadcast_to(query, (count, mixed, width)), CTX, split_axis=0, concat_axis=0, tiled=True
    ).reshape(count * mixed, width)

    here = lax.axis_index(CTX).reshape(1).astype(jnp.int32)
    state = pl.pallas_call(
        functools.partial(attend_kernel, rows, heads, page_len, latent),
        out_shape=jax.ShapeDtypeStruct((count * mixed, latent + LANES), jnp.bfloat16),
        in_specs=[smem, smem, vmem, vmem, vmem],
        out_specs=vmem,
        compiler_params=pltpu.CompilerParams(vmem_limit_bytes=16 << 20),
        name="attend",
    )(here, lengths, page_table, queries, latent_cache.reshape(pages * page_len, width))

    state = lax.all_to_all(
        state.reshape(count, mixed, latent + LANES), CTX, split_axis=0, concat_axis=0, tiled=True
    ).reshape(count * mixed, latent + LANES)
    term = pl.pallas_call(
        functools.partial(project_kernel, rows, heads, latent),
        out_shape=jax.ShapeDtypeStruct((rows, w_out.shape[1]), jnp.bfloat16),
        in_specs=[vmem, vmem, vmem],
        out_specs=vmem,
        compiler_params=pltpu.CompilerParams(vmem_limit_bytes=16 << 20),
        name="project",
    )(state, w_uv, w_out)
    for low in (4, 2, 0):
        term = sum_of_four(term, count, low).astype(jnp.bfloat16)
    return term


def solution(mesh):
    in_specs = (
        P("grp", "ctx", None),
        P("grp", "ctx", None),
        P(("grp", "ctx"), None, None),
        P("grp", None),
        P("grp"),
        P("ctx", None, None),
        P("ctx", None),
    )
    return jax.shard_map(local, mesh=mesh, in_specs=in_specs, out_specs=P("grp", None), check_vma=False)
```

time: 85.2 us -> 85.1 us (level); the launches traced: 84.9 us -> 83.7 us
  matrix products: 4.63 us -> 0 us
  Pallas kernels: 0 us -> 2.52 us
  other arithmetic: 3.68 us -> 1.55 us
  local copies, waits for them, and re-layouts: 3.55 us -> 5.6 us
  waiting for transfers between devices: 23.7 us -> 24.6 us
    dot_general x3 -> x0, matrix products: 4.63 us -> none  [the longest x1 2.74 us: local(): term = jnp.dot(flat, w_out, preferred_element_type=jnp.float32)]
    unnamed x8 -> x10, local copies, waits for them, and re-layouts: 1.05 us -> 4.46 us
    all_to_all x1, waiting for transfers between devices: 13.1 us -> 15.6 us  [local(): lax.all_to_all(jnp.broadcast_to(query, (count, mixed, width)), CTX, split...]
    pallas_call x0 -> x2, Pallas kernels: none -> 2.52 us  [the longest x1 1.32 us: local(): pl.pallas_call(functools.partial(attend_kernel, rows, heads, page_len, la...]
    ppermute x9, waiting for transfers between devices: 10.6 us -> 9 us  [sum_of_four(): lax.ppermute(x, CTX, xor_pairs(count, k << low))]
    reduce_sum x4 -> x0, other arithmetic: 0.86 us -> none  [the longest x1 0.27 us: local(): sums = jnp.sum(weights.astype(jnp.float32), axis=1, keepdims=True)]
  transfers between devices with their start and end apart: 10 -> 10, of which waited for: 9 -> 6; matrix products, arithmetic and copies ran while one was open for 3% -> 0% of each run, Pallas kernels for 0% -> 0%
where the time goes in v2:
time: 85.1 us; the launch traced here: 83.7 us
  starting transfers between devices  29.6 us (35%)
  waiting for transfers between devices  24.6 us (29%)
  blocking collectives  19.8 us (23%)
  local copies, waits for them, and re-layouts  5.6 us (7%)
  Pallas kernels  2.52 us (3%)
  other arithmetic  1.55 us (2%)
    all_to_all x1, blocking collectives, local(): lax.all_to_all(state.reshape(count, mixed, latent + LANES), CTX, split_ax...  19.8 us
    all_to_all x1, waiting for transfers between devices, local(): lax.all_to_all(jnp.broadcast_to(query, (count, mixed, width)), CTX, split...  15.6 us
    ppermute x9, starting transfers between devices, sum_of_four(): lax.ppermute(x, CTX, xor_pairs(count, k << low))  14.9 us
    all_to_all x1, starting transfers between devices, local(): lax.all_to_all(jnp.broadcast_to(query, (count, mixed, width)), CTX, split...  14.7 us
    ppermute x9, waiting for transfers between devices, sum_of_four(): lax.ppermute(x, CTX, xor_pairs(count, k << low))  9 us
    unnamed x10, local copies, waits for them, and re-layouts  4.46 us
  transfers between devices with their start and end apart: 10, of which 6 were waited for; matrix products, arithmetic and copies ran while one was open for 0% of the time, Pallas kernels for 0%

profile of v2, /device:TPU:2, one launch (start us, length us, event | category | flops | bytes accessed | tf_op | source)
XLA Modules:
  0.0 83.7 jit_solution(7009351185097207487)
XLA Ops:
  0.0 0.0 copy-start.2
  0.0 0.8 pad_maximum_fusion
  0.8 0.8 broadcast_in_dim.8
  1.6 14.7 %all-to-all-start = ((bf16[64,4,576]{2,1,0:T(4,128)(2,1)}), bf16[64,4,576]{2,1,0:T(4,128)(2,1)S(1)}, u32[]{:S(2)}, u32[]{:S(2)}) async-start(bf16[64,4,576]{2,1,0:T(4,128)(2,1)} %broadcast_in_dim.8), calls=%async_computation | async-start | bytes 655360 | tf_op jit(solution)/shard_map/all_to_all | solution.py:105
  16.3 15.6 %all-to-all-done = bf16[64,4,576]{2,1,0:T(4,128)(2,1)S(1)} async-done(((bf16[64,4,576]{2,1,0:T(4,128)(2,1)}), bf16[64,4,576]{2,1,0:T(4,128)(2,1)S(1)}, u32[]{:S(2)}, u32[]{:S(2)}) %all-to-all-start) | async-done | bytes 294944 | tf_op jit(solution)/shard_map/all_to_all | solution.py:105
  31.9 0.2 reshape.18.q_ref
  32.0 0.0 copy-start.1
  32.0 1.1 %copy-done.1 = bf16[8,64,576]{2,1,0:T(8,128)(2,1)S(1)} copy-done((bf16[8,64,576]{2,1,0:T(8,128)(2,1)S(1)}, bf16[8,64,576]{2,1,0:T(8,128)(2,1)}, u32[]{:S(2)}) %copy-start.1) | copy-done | bytes 589848
  33.1 0.0 copy-start.3
  33.1 0.7 copy-done.3
  33.8 0.0 copy-start.4
  33.8 0.7 copy-done.4
  34.4 1.3 %attend.1 = bf16[256,640]{1,0:T(8,128)(2,1)S(1)} custom-call(s32[1]{0:T(128)} %bitcast.here_ref, s32[2]{0:T(128)S(1)} %copy-done.4, s32[2,256]{1,0:T(2,128)S(1)} %copy-done.3, bf16[256,576]{1,0:T(8,128)(2,1)S(1)} %reshape.18.q_ref, bf16[512,576]{1,0:T(8,128)(2,1)S(1)} %bitcast.2), custom_call_target="tpu_custom_call" | custom-call | tf_op jit(solution)/shard_map/attend/pallas_call | solution.py:110
  35.8 0.1 reshape.20
  35.9 19.8 %all_to_all.10 = bf16[64,4,640]{2,1,0:T(4,128)(2,1)S(1)} all-to-all(bf16[64,4,640]{2,1,0:T(4,128)(2,1)S(1)} %reshape.20), channel_id=1, replica_groups=mesh['ctx'=64,'grp'=4] {'ctx'}, dimensions={0} | all-to-all | bytes 655360 | tf_op jit(solution)/shard_map/all_to_all | solution.py:119
  55.6 0.1 reshape.21.state_ref
  55.7 0.0 copy-done.2
  55.7 0.0 copy-start
  55.7 2.0 %copy-done = bf16[256,7168]{1,0:T(8,128)(2,1)S(1)} copy-done((bf16[256,7168]{1,0:T(8,128)(2,1)S(1)}, bf16[256,7168]{1,0:T(8,128)(2,1)}, u32[]{:S(2)}) %copy-start) | copy-done | bytes 3670040
  57.8 1.2 %project.1 = bf16[2,7168]{1,0:T(2,128)(2,1)S(1)} custom-call(bf16[256,640]{1,0:T(8,128)(2,1)S(1)} %reshape.21.state_ref, bf16[2,512,128]{2,1,0:T(8,128)(2,1)S(1)} %copy-done.2, bf16[256,7168]{1,0:T(8,128)(2,1)S(1)} %copy-done), custom_call_target="tpu_custom_call" | custom-call | tf_op jit(solution)/shard_map/project/pallas_call | solution.py:122
  59.0 1.7 %collective-permute-start = (bf16[2,7168]{1,0:T(2,128)(2,1)S(1)}, bf16[2,7168]{1,0:T(2,128)(2,1)S(1)}, u32[]{:S(2)}, u32[]{:S(2)}) collective-permute-start(bf16[2,7168]{1,0:T(2,128)(2,1)S(1)} %project.1), channel_id=1, source_target_pairs={{0,64},{4,68},{8,72},{12,76},{16,80},{20,84},{24,88},{28,92},{32,9... | collective-permute-start | bytes 86024 | tf_op jit(solution)/shard_map/ppermute | solution.py:21
  60.6 0.0 collective-permute-start.1
  60.7 1.9 %collective-permute-start.2 = (bf16[2,7168]{1,0:T(2,128)(2,1)S(1)}, bf16[2,7168]{1,0:T(2,128)(2,1)S(1)}, u32[]{:S(2)}, u32[]{:S(2)}) collective-permute-start(bf16[2,7168]{1,0:T(2,128)(2,1)S(1)} %project.1), channel_id=1, source_target_pairs={{0,192},{4,196},{8,200},{12,204},{16,208},{20,212},{24,216},{28,22... | collective-permute-start | bytes 86024 | tf_op jit(solution)/shard_map/ppermute | solution.py:21
  62.5 0.4 collective-permute-done
  62.9 3.1 %collective-permute-done.1 = bf16[2,7168]{1,0:T(2,128)(2,1)S(1)} collective-permute-done((bf16[2,7168]{1,0:T(2,128)(2,1)S(1)}, bf16[2,7168]{1,0:T(2,128)(2,1)S(1)}, u32[]{:S(2)}, u32[]{:S(2)}) %collective-permute-start.1) | collective-permute-done | bytes 28704 | tf_op jit(solution)/shard_map/ppermute | solution.py:21
  66.0 0.0 collective-permute-done.2
  66.0 0.1 add_convert_fusion.2
  66.1 0.7 collective-permute-start.3
  66.7 1.3 %collective-permute-start.4 = (bf16[2,7168]{1,0:T(2,128)(2,1)S(1)}, bf16[2,7168]{1,0:T(2,128)(2,1)S(1)}, u32[]{:S(2)}, u32[]{:S(2)}) collective-permute-start(bf16[2,7168]{1,0:T(2,128)(2,1)S(1)} %add_convert_fusion.2), channel_id=1, source_target_pairs={{0,32},{4,36},{8,40},{12,44},{16,48},{20,52},{24,56},{28,60},{32,0... | collective-permute-start | bytes 86024 | tf_op jit(solution)/shard_map/ppermute | solution.py:21
  68.0 2.8 %collective-permute-start.5 = (bf16[2,7168]{1,0:T(2,128)(2,1)S(1)}, bf16[2,7168]{1,0:T(2,128)(2,1)S(1)}, u32[]{:S(2)}, u32[]{:S(2)}) collective-permute-start(bf16[2,7168]{1,0:T(2,128)(2,1)S(1)} %add_convert_fusion.2), channel_id=1, source_target_pairs={{0,48},{4,52},{8,56},{12,60},{16,32},{20,36},{24,40},{28,44},{32,1... | collective-permute-start | bytes 86024 | tf_op jit(solution)/shard_map/ppermute | solution.py:21
  70.9 0.0 collective-permute-done.3
  70.9 1.3 %collective-permute-done.4 = bf16[2,7168]{1,0:T(2,128)(2,1)S(1)} collective-permute-done((bf16[2,7168]{1,0:T(2,128)(2,1)S(1)}, bf16[2,7168]{1,0:T(2,128)(2,1)S(1)}, u32[]{:S(2)}, u32[]{:S(2)}) %collective-permute-start.4) | collective-permute-done | bytes 28704 | tf_op jit(solution)/shard_map/ppermute | solution.py:21
  72.1 1.0 %collective-permute-done.5 = bf16[2,7168]{1,0:T(2,128)(2,1)S(1)} collective-permute-done((bf16[2,7168]{1,0:T(2,128)(2,1)S(1)}, bf16[2,7168]{1,0:T(2,128)(2,1)S(1)}, u32[]{:S(2)}, u32[]{:S(2)}) %collective-permute-start.5) | collective-permute-done | bytes 28704 | tf_op jit(solution)/shard_map/ppermute | solution.py:21
  73.1 0.1 add_convert_fusion.1
  73.2 1.8 %collective-permute-start.6 = (bf16[2,7168]{1,0:T(2,128)(2,1)S(1)}, bf16[2,7168]{1,0:T(2,128)(2,1)S(1)}, u32[]{:S(2)}, u32[]{:S(2)}) collective-permute-start(bf16[2,7168]{1,0:T(2,128)(2,1)S(1)} %add_convert_fusion.1), channel_id=1, source_target_pairs={{0,4},{4,0},{8,12},{12,8},{16,20},{20,16},{24,28},{28,24},{32,36},... | collective-permute-start | bytes 86024 | tf_op jit(solution)/shard_map/ppermute | solution.py:21
  74.9 1.9 %collective-permute-start.7 = (bf16[2,7168]{1,0:T(2,128)(2,1)S(1)}, bf16[2,7168]{1,0:T(2,128)(2,1)S(1)}, u32[]{:S(2)}, u32[]{:S(2)}) collective-permute-start(bf16[2,7168]{1,0:T(2,128)(2,1)S(1)} %add_convert_fusion.1), channel_id=1, source_target_pairs={{0,8},{4,12},{8,0},{12,4},{16,24},{20,28},{24,16},{28,20},{32,40},... | collective-permute-start | bytes 86024 | tf_op jit(solution)/shard_map/ppermute | solution.py:21
  76.8 2.9 %collective-permute-start.8 = (bf16[2,7168]{1,0:T(2,128)(2,1)S(1)}, bf16[2,7168]{1,0:T(2,128)(2,1)S(1)}, u32[]{:S(2)}, u32[]{:S(2)}) collective-permute-start(bf16[2,7168]{1,0:T(2,128)(2,1)S(1)} %add_convert_fusion.1), channel_id=1, source_target_pairs={{0,12},{4,8},{8,4},{12,0},{16,28},{20,24},{24,20},{28,16},{32,44},... | collective-permute-start | bytes 86024 | tf_op jit(solution)/shard_map/ppermute | solution.py:21
  79.7 0.0 collective-permute-done.6
  79.8 3.3 %collective-permute-done.7 = bf16[2,7168]{1,0:T(2,128)(2,1)S(1)} collective-permute-done((bf16[2,7168]{1,0:T(2,128)(2,1)S(1)}, bf16[2,7168]{1,0:T(2,128)(2,1)S(1)}, u32[]{:S(2)}, u32[]{:S(2)}) %collective-permute-start.7) | collective-permute-done | bytes 28704 | tf_op jit(solution)/shard_map/ppermute | solution.py:21
  83.0 0.0 collective-permute-done.8
  83.0 0.7 add_convert_fusion
  (1 shorter events, 0.0 us)
Async XLA Ops:
  0.0 55.7 %copy-start.2 = (bf16[2,512,128]{2,1,0:T(8,128)(2,1)S(1)}, bf16[2,512,128]{2,1,0:T(8,128)(2,1)}, u32[]{:S(2)}) copy-start(bf16[2,512,128]{2,1,0:T(8,128)(2,1)} %w_uv_ref.1) | copy-start | bytes 786436
  1.6 30.3 %all-to-all-start = ((bf16[64,4,576]{2,1,0:T(4,128)(2,1)}), bf16[64,4,576]{2,1,0:T(4,128)(2,1)S(1)}, u32[]{:S(2)}, u32[]{:S(2)}) async-start(bf16[64,4,576]{2,1,0:T(4,128)(2,1)} %broadcast_in_dim.8), calls=%async_computation | async-start | bytes 655360 | tf_op jit(solution)/shard_map/all_to_all | solution.py:105
  32.0 1.1 %copy-start.1 = (bf16[8,64,576]{2,1,0:T(8,128)(2,1)S(1)}, bf16[8,64,576]{2,1,0:T(8,128)(2,1)}, u32[]{:S(2)}) copy-start(bf16[8,64,576]{2,1,0:T(8,128)(2,1)} %param.9) | copy-start | bytes 1769476
  33.1 0.7 copy-start.3
  33.8 0.7 copy-start.4
  55.7 2.0 %copy-start = (bf16[256,7168]{1,0:T(8,128)(2,1)S(1)}, bf16[256,7168]{1,0:T(8,128)(2,1)}, u32[]{:S(2)}) copy-start(bf16[256,7168]{1,0:T(8,128)(2,1)} %w_out_ref.1) | copy-start | bytes 11010052
  59.0 3.9 %collective-permute-start = (bf16[2,7168]{1,0:T(2,128)(2,1)S(1)}, bf16[2,7168]{1,0:T(2,128)(2,1)S(1)}, u32[]{:S(2)}, u32[]{:S(2)}) collective-permute-start(bf16[2,7168]{1,0:T(2,128)(2,1)S(1)} %project.1), channel_id=1, source_target_pairs={{0,64},{4,68},{8,72},{12,76},{16,80},{20,84},{24,88},{28,92},{32,9... | collective-permute-start | bytes 86024 | tf_op jit(solution)/shard_map/ppermute | solution.py:21
  60.6 5.4 %collective-permute-start.1 = (bf16[2,7168]{1,0:T(2,128)(2,1)S(1)}, bf16[2,7168]{1,0:T(2,128)(2,1)S(1)}, u32[]{:S(2)}, u32[]{:S(2)}) collective-permute-start(bf16[2,7168]{1,0:T(2,128)(2,1)S(1)} %project.1), channel_id=1, source_target_pairs={{0,128},{4,132},{8,136},{12,140},{16,144},{20,148},{24,152},{28,15... | collective-permute-start | bytes 86024 | tf_op jit(solution)/shard_map/ppermute | solution.py:21
  60.7 5.3 %collective-permute-start.2 = (bf16[2,7168]{1,0:T(2,128)(2,1)S(1)}, bf16[2,7168]{1,0:T(2,128)(2,1)S(1)}, u32[]{:S(2)}, u32[]{:S(2)}) collective-permute-start(bf16[2,7168]{1,0:T(2,128)(2,1)S(1)} %project.1), channel_id=1, source_target_pairs={{0,192},{4,196},{8,200},{12,204},{16,208},{20,212},{24,216},{28,22... | collective-permute-start | bytes 86024 | tf_op jit(solution)/shard_map/ppermute | solution.py:21
  66.1 4.8 %collective-permute-start.3 = (bf16[2,7168]{1,0:T(2,128)(2,1)S(1)}, bf16[2,7168]{1,0:T(2,128)(2,1)S(1)}, u32[]{:S(2)}, u32[]{:S(2)}) collective-permute-start(bf16[2,7168]{1,0:T(2,128)(2,1)S(1)} %add_convert_fusion.2), channel_id=1, source_target_pairs={{0,16},{4,20},{8,24},{12,28},{16,0},{20,4},{24,8},{28,12},{32,48},... | collective-permute-start | bytes 86024 | tf_op jit(solution)/shard_map/ppermute | solution.py:21
  66.7 5.4 %collective-permute-start.4 = (bf16[2,7168]{1,0:T(2,128)(2,1)S(1)}, bf16[2,7168]{1,0:T(2,128)(2,1)S(1)}, u32[]{:S(2)}, u32[]{:S(2)}) collective-permute-start(bf16[2,7168]{1,0:T(2,128)(2,1)S(1)} %add_convert_fusion.2), channel_id=1, source_target_pairs={{0,32},{4,36},{8,40},{12,44},{16,48},{20,52},{24,56},{28,60},{32,0... | collective-permute-start | bytes 86024 | tf_op jit(solution)/shard_map/ppermute | solution.py:21
  68.0 5.1 %collective-permute-start.5 = (bf16[2,7168]{1,0:T(2,128)(2,1)S(1)}, bf16[2,7168]{1,0:T(2,128)(2,1)S(1)}, u32[]{:S(2)}, u32[]{:S(2)}) collective-permute-start(bf16[2,7168]{1,0:T(2,128)(2,1)S(1)} %add_convert_fusion.2), channel_id=1, source_target_pairs={{0,48},{4,52},{8,56},{12,60},{16,32},{20,36},{24,40},{28,44},{32,1... | collective-permute-start | bytes 86024 | tf_op jit(solution)/shard_map/ppermute | solution.py:21
  73.2 6.6 %collective-permute-start.6 = (bf16[2,7168]{1,0:T(2,128)(2,1)S(1)}, bf16[2,7168]{1,0:T(2,128)(2,1)S(1)}, u32[]{:S(2)}, u32[]{:S(2)}) collective-permute-start(bf16[2,7168]{1,0:T(2,128)(2,1)S(1)} %add_convert_fusion.1), channel_id=1, source_target_pairs={{0,4},{4,0},{8,12},{12,8},{16,20},{20,16},{24,28},{28,24},{32,36},... | collective-permute-start | bytes 86024 | tf_op jit(solution)/shard_map/ppermute | solution.py:21
  74.9 8.1 %collective-permute-start.7 = (bf16[2,7168]{1,0:T(2,128)(2,1)S(1)}, bf16[2,7168]{1,0:T(2,128)(2,1)S(1)}, u32[]{:S(2)}, u32[]{:S(2)}) collective-permute-start(bf16[2,7168]{1,0:T(2,128)(2,1)S(1)} %add_convert_fusion.1), channel_id=1, source_target_pairs={{0,8},{4,12},{8,0},{12,4},{16,24},{20,28},{24,16},{28,20},{32,40},... | collective-permute-start | bytes 86024 | tf_op jit(solution)/shard_map/ppermute | solution.py:21
  76.8 6.2 %collective-permute-start.8 = (bf16[2,7168]{1,0:T(2,128)(2,1)S(1)}, bf16[2,7168]{1,0:T(2,128)(2,1)S(1)}, u32[]{:S(2)}, u32[]{:S(2)}) collective-permute-start(bf16[2,7168]{1,0:T(2,128)(2,1)S(1)} %add_convert_fusion.1), channel_id=1, source_target_pairs={{0,12},{4,8},{8,4},{12,0},{16,28},{20,24},{24,20},{28,16},{32,44},... | collective-permute-start | bytes 86024 | tf_op jit(solution)/shard_map/ppermute | solution.py:21

commit v3 on v2

v3 whole, which is shorter than its diff:
```python
import functools
import jax
import jax.numpy as jnp
from jax import lax
from jax.experimental import pallas as pl
from jax.experimental.pallas import tpu as pltpu
from jax.sharding import PartitionSpec as P

ROPE = 64
V = 128
NEG = -1e30
CTX = "ctx"
LANES = 128
F32 = jnp.float32
BF16 = jnp.bfloat16


def xor_pairs(count, mask):
    return [(i, i ^ mask) for i in range(count)]


def sum_of_four(x, count, low):
    a, b, c = (lax.ppermute(x, CTX, xor_pairs(count, k << low)) for k in (1, 2, 3))
    return (x.astype(F32) + a.astype(F32)) + (b.astype(F32) + c.astype(F32))


def prepare_kernel(
    page_len, here_ref, lengths_hbm, table_hbm, q_latent_hbm, q_rope_hbm, cache_hbm,
    query_ref, live_ref, keys_ref, lengths_ref, table_ref, q_latent_ref, q_rope_ref, sems,
):
    pairs = (
        (q_latent_hbm, q_latent_ref), (q_rope_hbm, q_rope_ref), (lengths_hbm, lengths_ref),
        (table_hbm, table_ref), (cache_hbm, keys_ref),
    )
    copies = [pltpu.make_async_copy(a, b, sems.at[k]) for k, (a, b) in enumerate(pairs)]
    for copy in copies:
        copy.start()
    rows, heads, latent = q_latent_ref.shape
    rope = q_rope_ref.shape[2]
    copies[0].wait()
    copies[1].wait()
    q_latent = q_latent_ref[...].astype(F32)
    q_rope = q_rope_ref[...].astype(F32)
    message = jnp.concatenate(
        [
            jnp.concatenate(
                [q_latent[r, h : h + 1] for h in range(heads)] + [q_rope[r, h : h + 1] for h in range(heads)],
                axis=1,
            )
            for r in range(rows)
        ],
        axis=0,
    )
    query_ref[...] = jnp.broadcast_to(message[None], query_ref.shape).astype(BF16)
    copies[2].wait()
    copies[3].wait()
    tokens = keys_ref.shape[0]
    pages = tokens // page_len
    slots = table_ref.shape[1]
    page = here_ref[0] * pages + lax.broadcasted_iota(jnp.int32, (pages, slots), 0)
    place = lax.broadcasted_iota(jnp.int32, (pages, slots), 1)
    token = lax.broadcasted_iota(jnp.int32, (pages, tokens), 1)
    mine = token // page_len == lax.broadcasted_iota(jnp.int32, (pages, tokens), 0)
    for r in range(rows):
        hit = jnp.broadcast_to(table_ref[r : r + 1, :], (pages, slots)) == page
        room = jnp.where(hit, lengths_ref[r] - place * page_len, 0)
        room = jnp.max(room, axis=1, keepdims=True)
        alive = mine & (token % page_len < room)
        live_ref[r : r + 1, :] = jnp.max(jnp.where(alive, 1.0, 0.0), axis=0, keepdims=True)
    copies[4].wait()


def attend_kernel(
    rows, heads, latent, rope, q_ref, keys_ref, live_ref, w_uv_hbm, w_out_hbm,
    state_ref, w_uv_ref, w_out_ref, sems,
):
    copies = [
        pltpu.make_async_copy(w_uv_hbm, w_uv_ref, sems.at[0]),
        pltpu.make_async_copy(w_out_hbm, w_out_ref, sems.at[1]),
    ]
    for copy in copies:
        copy.start()
    count = q_ref.shape[0]
    tokens = keys_ref.shape[0]
    row = lax.broadcasted_iota(jnp.int32, (count, 1), 0) % rows
    live = jnp.broadcast_to(live_ref[0:1, :], (count, tokens))
    for r in range(1, rows):
        live = jnp.where(row == r, live_ref[r : r + 1, :], live)
    live = live > 0.5
    side = heads * latent
    lane = lax.broadcasted_iota(jnp.int32, (count, state_ref.shape[1] - side), 1)
    stats = jnp.zeros(lane.shape, F32)
    for h in range(heads):
        query = jnp.concatenate(
            [q_ref[:, h * latent : (h + 1) * latent], q_ref[:, side + h * rope : side + (h + 1) * rope]], axis=1
        )
        scores = lax.dot_general(
            query, keys_ref[...], (((1,), (1,)), ((), ())), preferred_element_type=F32
        ) * ((V + ROPE) ** (-0.5))
        scores = jnp.where(live, scores, NEG)
        shift = jnp.max(scores, axis=1, keepdims=True).astype(BF16).astype(F32)
        weights = jnp.where(live, jnp.exp(scores - shift), 0.0).astype(BF16)
        total = jnp.sum(weights.astype(F32), axis=1, keepdims=True)
        outs = jnp.dot(weights, keys_ref[:, :latent], preferred_element_type=F32)
        state_ref[:, h * latent : (h + 1) * latent] = outs.astype(BF16)
        high = total.astype(BF16).astype(F32)
        for k, value in enumerate((shift, high, total - high)):
            stats = jnp.where(lane == 3 * h + k, value, stats)
    state_ref[:, side:] = stats.astype(BF16)
    for copy in copies:
        copy.wait()


def project_kernel(rows, heads, latent, state_ref, w_uv_ref, w_out_ref, term_ref):
    count = state_ref.shape[0]
    mixed = rows * heads
    side = heads * latent
    lane = lax.broadcasted_iota(jnp.int32, (count, LANES), 1)
    row = lax.broadcasted_iota(jnp.int32, (count, LANES), 0) % rows
    column = lane % mixed
    own = (column // heads == row) & (lane < 2 * mixed)
    stats = state_ref[:, side:].astype(F32)
    shift = jnp.full((count, LANES), 2 * NEG, F32)
    for h in range(heads):
        shift = jnp.where(own & (column % heads == h), stats[:, 3 * h : 3 * h + 1], shift)
    best = jnp.max(shift, axis=0, keepdims=True)
    factor = jnp.where(own, jnp.exp(shift - best), 0.0)
    high = factor.astype(BF16).astype(F32)
    factor = jnp.where(lane < mixed, high, factor - high).astype(BF16)
    merged = lax.dot_general(
        factor, state_ref[...], (((0,), (0,)), ((), ())), preferred_element_type=F32
    )
    merged = merged[:mixed] + merged[mixed : 2 * mixed]
    parts = []
    for h in range(heads):
        total = merged[:, side + 3 * h + 1 : side + 3 * h + 2] + merged[:, side + 3 * h + 2 : side + 3 * h + 3]
        attended = (merged[:, h * latent : (h + 1) * latent] / total).astype(BF16)
        parts.append(jnp.dot(attended, w_uv_ref[h], preferred_element_type=F32))
    flat = jnp.concatenate(
        [
            jnp.concatenate([parts[h][r * heads + h : r * heads + h + 1] for h in range(heads)], axis=1)
            for r in range(rows)
        ],
        axis=0,
    ).astype(BF16)
    term_ref[...] = jnp.dot(flat, w_out_ref[...], preferred_element_type=F32).astype(term_ref.dtype)


def local(q_latent, q_rope, latent_cache, page_table, lengths, w_uv, w_out):
    rows, heads, latent = q_latent.shape
    rope = q_rope.shape[2]
    pages, page_len, width = latent_cache.shape
    tokens = pages * page_len
    count = lax.axis_size(CTX)
    size = heads * (latent + rope)
    vmem = pl.BlockSpec(memory_space=pltpu.VMEM)
    smem = pl.BlockSpec(memory_space=pltpu.SMEM)
    hbm = pl.BlockSpec(memory_space=pltpu.HBM)
    params = pltpu.CompilerParams(vmem_limit_bytes=16 << 20)
    dma = pltpu.SemaphoreType.DMA

    here = lax.axis_index(CTX).reshape(1).astype(jnp.int32)
    query, live, keys = pl.pallas_call(
        functools.partial(prepare_kernel, page_len),
        out_shape=(
            jax.ShapeDtypeStruct((count, rows, size), BF16),
            jax.ShapeDtypeStruct((rows, tokens), F32),
            jax.ShapeDtypeStruct((tokens, width), BF16),
        ),
        in_specs=[smem, hbm, hbm, hbm, hbm, hbm],
        out_specs=(vmem, vmem, vmem),
        scratch_shapes=[
            pltpu.SMEM(lengths.shape, jnp.int32),
            pltpu.VMEM(page_table.shape, jnp.int32),
            pltpu.VMEM(q_latent.shape, BF16),
            pltpu.VMEM(q_rope.shape, BF16),
            dma((5,)),
        ],
        compiler_params=params,
        name="prepare",
    )(here, lengths, page_table, q_latent, q_rope, latent_cache.reshape(tokens, width))

    query = lax.all_to_all(query, CTX, split_axis=0, concat_axis=0, tiled=True)

    state_size = heads * latent + LANES
    state, w_uv, w_out = pl.pallas_call(
        functools.partial(attend_kernel, rows, heads, latent, rope),
        out_shape=(
            jax.ShapeDtypeStruct((count * rows, state_size), BF16),
            jax.ShapeDtypeStruct(w_uv.shape, BF16),
            jax.ShapeDtypeStruct(w_out.shape, BF16),
        ),
        in_specs=[vmem, vmem, vmem, hbm, hbm],
        out_specs=(vmem, vmem, vmem),
        scratch_shapes=[dma((2,))],
        compiler_params=params,
        name="attend",
    )(query.reshape(count * rows, size), keys, live, w_uv, w_out)

    state = lax.all_to_all(
        state.reshape(count, rows, state_size), CTX, split_axis=0, concat_axis=0, tiled=True
    )
    term = pl.pallas_call(
        functools.partial(project_kernel, rows, heads, latent),
        out_shape=jax.ShapeDtypeStruct((rows, w_out.shape[1]), BF16),
        in_specs=[vmem, vmem, vmem],
        out_specs=vmem,
        compiler_params=params,
        name="project",
    )(state.reshape(count * rows, state_size), w_uv, w_out)
    for low in (4, 2, 0):
        term = sum_of_four(term, count, low).astype(BF16)
    return term


def solution(mesh):
    in_specs = (
        P("grp", "ctx", None),
        P("grp", "ctx", None),
        P(("grp", "ctx"), None, None),
        P("grp", None),
        P("grp"),
        P("ctx", None, None),
        P("ctx", None),
    )
    return jax.shard_map(local, mesh=mesh, in_specs=in_specs, out_specs=P("grp", None), check_vma=False)
```

time: 85.1 us -> 88 us (1.034); the launches traced: 83.7 us -> 87.6 us
  blocking collectives: 19.8 us -> 48.6 us
  waiting for transfers between devices: 24.6 us -> 8.93 us
  starting transfers between devices: 29.6 us -> 14.9 us
  local copies, waits for them, and re-layouts: 5.6 us -> 10.9 us
    all_to_all x1 -> x2, blocking collectives: 19.8 us -> 48.6 us  [the longest x1 29.4 us: local(): query = lax.all_to_all(query, CTX, split_axis=0, concat_axis=0, tiled=True)]
    all_to_all x1 -> x0, waiting for transfers between devices: 15.6 us -> none  [local(): lax.all_to_all(jnp.broadcast_to(query, (count, mixed, width)), CTX, split...]
    all_to_all x1 -> x0, starting transfers between devices: 14.7 us -> none  [local(): lax.all_to_all(jnp.broadcast_to(query, (count, mixed, width)), CTX, split...]
    unnamed x10 -> x18, local copies, waits for them, and re-layouts: 4.46 us -> 10.6 us
    pallas_call x1 -> x2, Pallas kernels: 1.32 us -> 2.18 us  [the longest x1 1.41 us: local(): pl.pallas_call(functools.partial(attend_kernel, rows, heads, latent, rope...]
  transfers between devices with their start and end apart: 10 -> 9, of which waited for: 6 -> 7; matrix products, arithmetic and copies ran while one was open for 0% -> 0% of each run, Pallas kernels for 0% -> 0%
where the time goes in v3:
time: 88 us; the launch traced here: 87.6 us
  blocking collectives  48.6 us (55%)
  starting transfers between devices  14.9 us (17%)
  local copies, waits for them, and re-layouts  10.9 us (12%)
  waiting for transfers between devices  8.93 us (10%)
  Pallas kernels  3.39 us (4%)
    all_to_all x1, blocking collectives, local(): query = lax.all_to_all(query, CTX, split_axis=0, concat_axis=0, tiled=True)  29.4 us
    all_to_all x1, blocking collectives, local(): lax.all_to_all(state.reshape(count, rows, state_size), CTX, split_axis=0,...  19.2 us
    ppermute x9, starting transfers between devices, sum_of_four(): lax.ppermute(x, CTX, xor_pairs(count, k << low))  14.9 us
    unnamed x18, local copies, waits for them, and re-layouts  10.6 us
    ppermute x9, waiting for transfers between devices, sum_of_four(): lax.ppermute(x, CTX, xor_pairs(count, k << low))  8.93 us
  transfers between devices with their start and end apart: 9, of which 7 were waited for; matrix products, arithmetic and copies ran while one was open for 0% of the time, Pallas kernels for 0%

profile of v3, /device:TPU:2, one launch (start us, length us, event | category | flops | bytes accessed | tf_op | source)
XLA Modules:
  0.0 87.6 jit_solution(11702657803688680159)
XLA Ops:
  0.0 0.0 copy-start.3
  0.0 1.1 %copy-done.3 = bf16[8,64,576]{2,1,0:T(8,128)(2,1)S(1)} copy-done((bf16[8,64,576]{2,1,0:T(8,128)(2,1)S(1)}, bf16[8,64,576]{2,1,0:T(8,128)(2,1)}, u32[]{:S(2)}) %copy-start.3) | copy-done | bytes 589848
  1.1 0.0 copy-start.5
  1.1 0.7 copy-done.5
  1.8 0.0 copy-start.6
  1.8 0.7 copy-done.6
  2.5 0.0 copy-start.7
  2.5 0.7 copy-done.7
  3.1 0.0 copy-start.8
  3.1 0.7 copy-done.8
  3.8 0.8 prepare.1
  4.6 29.4 %all_to_all.10 = bf16[64,2,1152]{2,1,0:T(2,128)(2,1)S(1)} all-to-all(bf16[64,2,1152]{2,1,0:T(2,128)(2,1)S(1)} %get-tuple-element.11), channel_id=1, replica_groups=mesh['ctx'=64,'grp'=4] {'ctx'}, dimensions={0} | all-to-all | bytes 589824 | tf_op jit(solution)/shard_map/all_to_all | solution.py:183
  33.9 0.1 reshape.17.q_ref
  34.1 0.0 copy-start.2
  34.1 2.0 %copy-done.2 = bf16[256,7168]{1,0:T(8,128)(2,1)S(1)} copy-done((bf16[256,7168]{1,0:T(8,128)(2,1)S(1)}, bf16[256,7168]{1,0:T(8,128)(2,1)}, u32[]{:S(2)}) %copy-start.2) | copy-done | bytes 3670040
  36.1 0.0 copy-start.4
  36.1 0.9 %copy-done.4 = bf16[2,512,128]{2,1,0:T(8,128)(2,1)S(1)} copy-done((bf16[2,512,128]{2,1,0:T(8,128)(2,1)S(1)}, bf16[2,512,128]{2,1,0:T(8,128)(2,1)}, u32[]{:S(2)}) %copy-start.4) | copy-done | bytes 262168
  37.1 1.4 %attend.1 = (bf16[128,1152]{1,0:T(8,128)(2,1)S(1)}, bf16[2,512,128]{2,1,0:T(8,128)(2,1)S(1)}, bf16[256,7168]{1,0:T(8,128)(2,1)S(1)}) custom-call(bf16[128,1152]{1,0:T(8,128)(2,1)S(1)} %reshape.17.q_ref, bf16[512,576]{1,0:T(8,128)(2,1)S(1)} %get-tuple-element.12.keys_ref, f32[2,512]{1,0:T(2,128)S(1)} %get-tuple-element.13.live_ref, ...), custom_call_target="tpu_custom_call" | custom-call | tf_op jit(solution)/shard_map/attend/pallas_call | solution.py:186
  38.5 0.0 copy-start
  38.5 1.8 %copy-done = bf16[256,7168]{1,0:T(8,128)(2,1)} copy-done((bf16[256,7168]{1,0:T(8,128)(2,1)}, bf16[256,7168]{1,0:T(8,128)(2,1)S(1)}, u32[]{:S(2)}) %copy-start) | copy-done | bytes 3670040
  40.3 0.1 reshape.18
  40.4 19.2 %all_to_all.11 = bf16[64,2,1152]{2,1,0:T(2,128)(2,1)S(1)} all-to-all(bf16[64,2,1152]{2,1,0:T(2,128)(2,1)S(1)} %reshape.18), channel_id=1, replica_groups=mesh['ctx'=64,'grp'=4] {'ctx'}, dimensions={0} | all-to-all | bytes 589824 | tf_op jit(solution)/shard_map/all_to_all | solution.py:200
  59.6 0.1 reshape.19.state_ref
  59.7 0.0 copy-start.1
  59.7 2.0 %copy-done.1 = bf16[256,7168]{1,0:T(8,128)(2,1)S(1)} copy-done((bf16[256,7168]{1,0:T(8,128)(2,1)S(1)}, bf16[256,7168]{1,0:T(8,128)(2,1)}, u32[]{:S(2)}) %copy-start.1) | copy-done | bytes 3670040
  61.7 1.2 %project.1 = bf16[2,7168]{1,0:T(2,128)(2,1)S(1)} custom-call(bf16[128,1152]{1,0:T(8,128)(2,1)S(1)} %reshape.19.state_ref, bf16[2,512,128]{2,1,0:T(8,128)(2,1)S(1)} %get-tuple-element.15.w_uv_ref, bf16[256,7168]{1,0:T(8,128)(2,1)S(1)} %copy-done.1), custom_call_target="tpu_custom_call" | custom-call | tf_op jit(solution)/shard_map/project/pallas_call | solution.py:203
  62.9 0.2 collective-permute-start.2
  63.1 3.5 %collective-permute-start.1 = (bf16[2,7168]{1,0:T(2,128)(2,1)S(1)}, bf16[2,7168]{1,0:T(2,128)(2,1)S(1)}, u32[]{:S(2)}, u32[]{:S(2)}) collective-permute-start(bf16[2,7168]{1,0:T(2,128)(2,1)S(1)} %project.1), channel_id=1, source_target_pairs={{0,128},{4,132},{8,136},{12,140},{16,144},{20,148},{24,152},{28,15... | collective-permute-start | bytes 86024 | tf_op jit(solution)/shard_map/ppermute | solution.py:23
  66.6 0.4 collective-permute-start
  67.1 0.0 collective-permute-done.2
  67.1 1.4 %collective-permute-done.1 = bf16[2,7168]{1,0:T(2,128)(2,1)S(1)} collective-permute-done((bf16[2,7168]{1,0:T(2,128)(2,1)S(1)}, bf16[2,7168]{1,0:T(2,128)(2,1)S(1)}, u32[]{:S(2)}, u32[]{:S(2)}) %collective-permute-start.1) | collective-permute-done | bytes 28704 | tf_op jit(solution)/shard_map/ppermute | solution.py:23
  68.5 2.0 %collective-permute-done = bf16[2,7168]{1,0:T(2,128)(2,1)S(1)} collective-permute-done((bf16[2,7168]{1,0:T(2,128)(2,1)S(1)}, bf16[2,7168]{1,0:T(2,128)(2,1)S(1)}, u32[]{:S(2)}, u32[]{:S(2)}) %collective-permute-start) | collective-permute-done | bytes 28704 | tf_op jit(solution)/shard_map/ppermute | solution.py:23
  70.5 0.1 add_convert_fusion.2
  70.6 0.5 collective-permute-start.5
  71.1 2.2 %collective-permute-start.4 = (bf16[2,7168]{1,0:T(2,128)(2,1)S(1)}, bf16[2,7168]{1,0:T(2,128)(2,1)S(1)}, u32[]{:S(2)}, u32[]{:S(2)}) collective-permute-start(bf16[2,7168]{1,0:T(2,128)(2,1)S(1)} %add_convert_fusion.2), channel_id=1, source_target_pairs={{0,32},{4,36},{8,40},{12,44},{16,48},{20,52},{24,56},{28,60},{32,0... | collective-permute-start | bytes 86024 | tf_op jit(solution)/shard_map/ppermute | solution.py:23
  73.3 1.4 %collective-permute-start.3 = (bf16[2,7168]{1,0:T(2,128)(2,1)S(1)}, bf16[2,7168]{1,0:T(2,128)(2,1)S(1)}, u32[]{:S(2)}, u32[]{:S(2)}) collective-permute-start(bf16[2,7168]{1,0:T(2,128)(2,1)S(1)} %add_convert_fusion.2), channel_id=1, source_target_pairs={{0,16},{4,20},{8,24},{12,28},{16,0},{20,4},{24,8},{28,12},{32,48},... | collective-permute-start | bytes 86024 | tf_op jit(solution)/shard_map/ppermute | solution.py:23
  74.8 1.0 %collective-permute-done.5 = bf16[2,7168]{1,0:T(2,128)(2,1)S(1)} collective-permute-done((bf16[2,7168]{1,0:T(2,128)(2,1)S(1)}, bf16[2,7168]{1,0:T(2,128)(2,1)S(1)}, u32[]{:S(2)}, u32[]{:S(2)}) %collective-permute-start.5) | collective-permute-done | bytes 28704 | tf_op jit(solution)/shard_map/ppermute | solution.py:23
  75.7 0.7 collective-permute-done.4
  76.5 0.7 collective-permute-done.3
  77.2 0.1 add_convert_fusion.1
  77.3 0.6 collective-permute-start.8
  77.9 4.1 %collective-permute-start.7 = (bf16[2,7168]{1,0:T(2,128)(2,1)S(1)}, bf16[2,7168]{1,0:T(2,128)(2,1)S(1)}, u32[]{:S(2)}, u32[]{:S(2)}) collective-permute-start(bf16[2,7168]{1,0:T(2,128)(2,1)S(1)} %add_convert_fusion.1), channel_id=1, source_target_pairs={{0,8},{4,12},{8,0},{12,4},{16,24},{20,28},{24,16},{28,20},{32,40},... | collective-permute-start | bytes 86024 | tf_op jit(solution)/shard_map/ppermute | solution.py:23
  81.9 1.9 %collective-permute-start.6 = (bf16[2,7168]{1,0:T(2,128)(2,1)S(1)}, bf16[2,7168]{1,0:T(2,128)(2,1)S(1)}, u32[]{:S(2)}, u32[]{:S(2)}) collective-permute-start(bf16[2,7168]{1,0:T(2,128)(2,1)S(1)} %add_convert_fusion.1), channel_id=1, source_target_pairs={{0,4},{4,0},{8,12},{12,8},{16,20},{20,16},{24,28},{28,24},{32,36},... | collective-permute-start | bytes 86024 | tf_op jit(solution)/shard_map/ppermute | solution.py:23
  83.8 0.0 collective-permute-done.8
  83.9 1.8 %collective-permute-done.7 = bf16[2,7168]{1,0:T(2,128)(2,1)S(1)} collective-permute-done((bf16[2,7168]{1,0:T(2,128)(2,1)S(1)}, bf16[2,7168]{1,0:T(2,128)(2,1)S(1)}, u32[]{:S(2)}, u32[]{:S(2)}) %collective-permute-start.7) | collective-permute-done | bytes 28704 | tf_op jit(solution)/shard_map/ppermute | solution.py:23
  85.7 1.2 %collective-permute-done.6 = bf16[2,7168]{1,0:T(2,128)(2,1)S(1)} collective-permute-done((bf16[2,7168]{1,0:T(2,128)(2,1)S(1)}, bf16[2,7168]{1,0:T(2,128)(2,1)S(1)}, u32[]{:S(2)}, u32[]{:S(2)}) %collective-permute-start.6) | collective-permute-done | bytes 28704 | tf_op jit(solution)/shard_map/ppermute | solution.py:23
  86.9 0.7 add_convert_fusion
Async XLA Ops:
  0.0 1.1 %copy-start.3 = (bf16[8,64,576]{2,1,0:T(8,128)(2,1)S(1)}, bf16[8,64,576]{2,1,0:T(8,128)(2,1)}, u32[]{:S(2)}) copy-start(bf16[8,64,576]{2,1,0:T(8,128)(2,1)} %param.9) | copy-start | bytes 1769476
  1.1 0.7 copy-start.5
  1.8 0.7 copy-start.6
  2.5 0.7 copy-start.7
  3.1 0.7 copy-start.8
  34.1 2.0 %copy-start.2 = (bf16[256,7168]{1,0:T(8,128)(2,1)S(1)}, bf16[256,7168]{1,0:T(8,128)(2,1)}, u32[]{:S(2)}) copy-start(bf16[256,7168]{1,0:T(8,128)(2,1)} %w_out_hbm.1) | copy-start | bytes 11010052
  36.1 0.9 %copy-start.4 = (bf16[2,512,128]{2,1,0:T(8,128)(2,1)S(1)}, bf16[2,512,128]{2,1,0:T(8,128)(2,1)}, u32[]{:S(2)}) copy-start(bf16[2,512,128]{2,1,0:T(8,128)(2,1)} %w_uv_hbm.1) | copy-start | bytes 786436
  38.5 1.8 %copy-start = (bf16[256,7168]{1,0:T(8,128)(2,1)}, bf16[256,7168]{1,0:T(8,128)(2,1)S(1)}, u32[]{:S(2)}) copy-start(bf16[256,7168]{1,0:T(8,128)(2,1)S(1)} %get-tuple-element.16.w_out_ref) | copy-start | bytes 11010052
  59.7 2.0 %copy-start.1 = (bf16[256,7168]{1,0:T(8,128)(2,1)S(1)}, bf16[256,7168]{1,0:T(8,128)(2,1)}, u32[]{:S(2)}) copy-start(bf16[256,7168]{1,0:T(8,128)(2,1)} %copy-done) | copy-start | bytes 11010052
  62.9 4.2 %collective-permute-start.2 = (bf16[2,7168]{1,0:T(2,128)(2,1)S(1)}, bf16[2,7168]{1,0:T(2,128)(2,1)S(1)}, u32[]{:S(2)}, u32[]{:S(2)}) collective-permute-start(bf16[2,7168]{1,0:T(2,128)(2,1)S(1)} %project.1), channel_id=1, source_target_pairs={{0,192},{4,196},{8,200},{12,204},{16,208},{20,212},{24,216},{28,22... | collective-permute-start | bytes 86024 | tf_op jit(solution)/shard_map/ppermute | solution.py:23
  63.1 5.4 %collective-permute-start.1 = (bf16[2,7168]{1,0:T(2,128)(2,1)S(1)}, bf16[2,7168]{1,0:T(2,128)(2,1)S(1)}, u32[]{:S(2)}, u32[]{:S(2)}) collective-permute-start(bf16[2,7168]{1,0:T(2,128)(2,1)S(1)} %project.1), channel_id=1, source_target_pairs={{0,128},{4,132},{8,136},{12,140},{16,144},{20,148},{24,152},{28,15... | collective-permute-start | bytes 86024 | tf_op jit(solution)/shard_map/ppermute | solution.py:23
  66.6 3.9 %collective-permute-start = (bf16[2,7168]{1,0:T(2,128)(2,1)S(1)}, bf16[2,7168]{1,0:T(2,128)(2,1)S(1)}, u32[]{:S(2)}, u32[]{:S(2)}) collective-permute-start(bf16[2,7168]{1,0:T(2,128)(2,1)S(1)} %project.1), channel_id=1, source_target_pairs={{0,64},{4,68},{8,72},{12,76},{16,80},{20,84},{24,88},{28,92},{32,9... | collective-permute-start | bytes 86024 | tf_op jit(solution)/shard_map/ppermute | solution.py:23
  70.6 5.2 %collective-permute-start.5 = (bf16[2,7168]{1,0:T(2,128)(2,1)S(1)}, bf16[2,7168]{1,0:T(2,128)(2,1)S(1)}, u32[]{:S(2)}, u32[]{:S(2)}) collective-permute-start(bf16[2,7168]{1,0:T(2,128)(2,1)S(1)} %add_convert_fusion.2), channel_id=1, source_target_pairs={{0,48},{4,52},{8,56},{12,60},{16,32},{20,36},{24,40},{28,44},{32,1... | collective-permute-start | bytes 86024 | tf_op jit(solution)/shard_map/ppermute | solution.py:23
  71.1 5.4 %collective-permute-start.4 = (bf16[2,7168]{1,0:T(2,128)(2,1)S(1)}, bf16[2,7168]{1,0:T(2,128)(2,1)S(1)}, u32[]{:S(2)}, u32[]{:S(2)}) collective-permute-start(bf16[2,7168]{1,0:T(2,128)(2,1)S(1)} %add_convert_fusion.2), channel_id=1, source_target_pairs={{0,32},{4,36},{8,40},{12,44},{16,48},{20,52},{24,56},{28,60},{32,0... | collective-permute-start | bytes 86024 | tf_op jit(solution)/shard_map/ppermute | solution.py:23
  73.3 3.9 %collective-permute-start.3 = (bf16[2,7168]{1,0:T(2,128)(2,1)S(1)}, bf16[2,7168]{1,0:T(2,128)(2,1)S(1)}, u32[]{:S(2)}, u32[]{:S(2)}) collective-permute-start(bf16[2,7168]{1,0:T(2,128)(2,1)S(1)} %add_convert_fusion.2), channel_id=1, source_target_pairs={{0,16},{4,20},{8,24},{12,28},{16,0},{20,4},{24,8},{28,12},{32,48},... | collective-permute-start | bytes 86024 | tf_op jit(solution)/shard_map/ppermute | solution.py:23
  77.3 6.6 %collective-permute-start.8 = (bf16[2,7168]{1,0:T(2,128)(2,1)S(1)}, bf16[2,7168]{1,0:T(2,128)(2,1)S(1)}, u32[]{:S(2)}, u32[]{:S(2)}) collective-permute-start(bf16[2,7168]{1,0:T(2,128)(2,1)S(1)} %add_convert_fusion.1), channel_id=1, source_target_pairs={{0,12},{4,8},{8,4},{12,0},{16,28},{20,24},{24,20},{28,16},{32,44},... | collective-permute-start | bytes 86024 | tf_op jit(solution)/shard_map/ppermute | solution.py:23
  77.9 7.8 %collective-permute-start.7 = (bf16[2,7168]{1,0:T(2,128)(2,1)S(1)}, bf16[2,7168]{1,0:T(2,128)(2,1)S(1)}, u32[]{:S(2)}, u32[]{:S(2)}) collective-permute-start(bf16[2,7168]{1,0:T(2,128)(2,1)S(1)} %add_convert_fusion.1), channel_id=1, source_target_pairs={{0,8},{4,12},{8,0},{12,4},{16,24},{20,28},{24,16},{28,20},{32,40},... | collective-permute-start | bytes 86024 | tf_op jit(solution)/shard_map/ppermute | solution.py:23
  81.9 5.0 %collective-permute-start.6 = (bf16[2,7168]{1,0:T(2,128)(2,1)S(1)}, bf16[2,7168]{1,0:T(2,128)(2,1)S(1)}, u32[]{:S(2)}, u32[]{:S(2)}) collective-permute-start(bf16[2,7168]{1,0:T(2,128)(2,1)S(1)} %add_convert_fusion.1), channel_id=1, source_target_pairs={{0,4},{4,0},{8,12},{12,8},{16,20},{20,16},{24,28},{28,24},{32,36},... | collective-permute-start | bytes 86024 | tf_op jit(solution)/shard_map/ppermute | solution.py:23

commit v4 on v3

--- a/solution.py
+++ b/solution.py
@@ -155,7 +155,8 @@
     size = heads * (latent + rope)
     vmem = pl.BlockSpec(memory_space=pltpu.VMEM)
     smem = pl.BlockSpec(memory_space=pltpu.SMEM)
-    hbm = pl.BlockSpec(memory_space=pltpu.HBM)
+    hbm = pl.BlockSpec(memory_space=pl.ANY)
+    stay = functools.partial(pltpu.with_memory_space_constraint, memory_space=pltpu.HBM)
     params = pltpu.CompilerParams(vmem_limit_bytes=16 << 20)
     dma = pltpu.SemaphoreType.DMA
 
@@ -164,8 +165,8 @@
         functools.partial(prepare_kernel, page_len),
         out_shape=(
             jax.ShapeDtypeStruct((count, rows, size), BF16),
-            jax.ShapeDtypeStruct((rows, tokens), F32),
-            jax.ShapeDtypeStruct((tokens, width), BF16),
+            pltpu.VMEM((rows, tokens), F32),
+            pltpu.VMEM((tokens, width), BF16),
         ),
         in_specs=[smem, hbm, hbm, hbm, hbm, hbm],
         out_specs=(vmem, vmem, vmem),
@@ -178,7 +179,7 @@
         ],
         compiler_params=params,
         name="prepare",
-    )(here, lengths, page_table, q_latent, q_rope, latent_cache.reshape(tokens, width))
+    )(here, stay(lengths), stay(page_table), stay(q_latent), stay(q_rope), stay(latent_cache.reshape(tokens, width)))
 
     query = lax.all_to_all(query, CTX, split_axis=0, concat_axis=0, tiled=True)
 
@@ -187,15 +188,15 @@
         functools.partial(attend_kernel, rows, heads, latent, rope),
         out_shape=(
             jax.ShapeDtypeStruct((count * rows, state_size), BF16),
-            jax.ShapeDtypeStruct(w_uv.shape, BF16),
-            jax.ShapeDtypeStruct(w_out.shape, BF16),
+            pltpu.VMEM(w_uv.shape, BF16),
+            pltpu.VMEM(w_out.shape, BF16),
         ),
         in_specs=[vmem, vmem, vmem, hbm, hbm],
         out_specs=(vmem, vmem, vmem),
         scratch_shapes=[dma((2,))],
         compiler_params=params,
         name="attend",
-    )(query.reshape(count * rows, size), keys, live, w_uv, w_out)
+    )(query.reshape(count * rows, size), keys, live, stay(w_uv), stay(w_out))
 
     state = lax.all_to_all(
         state.reshape(count, rows, state_size), CTX, split_axis=0, concat_axis=0, tiled=True

time: 88 us -> 82.2 us (0.934)
  local copies, waits for them, and re-layouts: 10.9 us -> 4.15 us
  Pallas kernels: 3.39 us -> 4.55 us
    unnamed x18 -> x4, local copies, waits for them, and re-layouts: 10.6 us -> 3.82 us
where the time goes in v4:
time: 82.2 us; the launch traced here: 82 us
  blocking collectives  48.6 us (59%)
  starting transfers between devices  14.9 us (18%)
  waiting for transfers between devices  8.93 us (11%)
  Pallas kernels  4.55 us (6%)
  local copies, waits for them, and re-layouts  4.15 us (5%)
    all_to_all x1, blocking collectives, local(): query = lax.all_to_all(query, CTX, split_axis=0, concat_axis=0, tiled=True)  29.4 us
    all_to_all x1, blocking collectives, local(): lax.all_to_all(state.reshape(count, rows, state_size), CTX, split_axis=0,...  19.2 us
    ppermute x9, starting transfers between devices, sum_of_four(): lax.ppermute(x, CTX, xor_pairs(count, k << low))  14.9 us
    ppermute x9, waiting for transfers between devices, sum_of_four(): lax.ppermute(x, CTX, xor_pairs(count, k << low))  8.93 us
    unnamed x4, local copies, waits for them, and re-layouts  3.82 us
    pallas_call x1, Pallas kernels, local(): pl.pallas_call(functools.partial(attend_kernel, rows, heads, latent, rope...  2.17 us
  transfers between devices with their start and end apart: 9, of which 7 were waited for; matrix products, arithmetic and copies ran while one was open for 0% of the time, Pallas kernels for 0%

profile of v4, /device:TPU:2, one launch (start us, length us, event | category | flops | bytes accessed | tf_op | source)
XLA Modules:
  0.0 82.0 jit_solution(15927329246588779940)
XLA Ops:
  0.0 1.2 %prepare.1 = (bf16[64,2,1152]{2,1,0:T(2,128)(2,1)S(1)}, f32[2,512]{1,0:T(2,128)S(1)}, bf16[512,576]{1,0:T(8,128)(2,1)S(1)}) custom-call(s32[1]{0:T(128)} %bitcast.here_ref, s32[2]{0:T(128)} %lengths_hbm.1, s32[2,256]{1,0:T(2,128)} %table_hbm.1, bf16[2,2,512]{2,1,0:T(2,128)(2,1)} %q_latent_hbm.1, bf16[2,2,64]{2,1,0:T(2,128)(2,1)} %q_rope_hbm.1, ...), custom_call_target="tpu_custom_call" | custom-call | tf_op jit(solution)/shard_map/prepare/pallas_call | solution.py:164
  1.2 29.4 %all_to_all.10 = bf16[64,2,1152]{2,1,0:T(2,128)(2,1)S(1)} all-to-all(bf16[64,2,1152]{2,1,0:T(2,128)(2,1)S(1)} %get-tuple-element.11), channel_id=1, replica_groups=mesh['ctx'=64,'grp'=4] {'ctx'}, dimensions={0} | all-to-all | bytes 589824 | tf_op jit(solution)/shard_map/all_to_all | solution.py:184
  30.6 0.1 reshape.17.q_ref
  30.7 2.2 %attend.1 = (bf16[128,1152]{1,0:T(8,128)(2,1)S(1)}, bf16[2,512,128]{2,1,0:T(8,128)(2,1)S(1)}, bf16[256,7168]{1,0:T(8,128)(2,1)S(1)}) custom-call(bf16[128,1152]{1,0:T(8,128)(2,1)S(1)} %reshape.17.q_ref, bf16[512,576]{1,0:T(8,128)(2,1)S(1)} %get-tuple-element.12.keys_ref, f32[2,512]{1,0:T(2,128)S(1)} %get-tuple-element.13.live_ref, ...), custom_call_target="tpu_custom_call" | custom-call | tf_op jit(solution)/shard_map/attend/pallas_call | solution.py:187
  32.9 0.0 copy-start
  32.9 1.8 %copy-done = bf16[256,7168]{1,0:T(8,128)(2,1)} copy-done((bf16[256,7168]{1,0:T(8,128)(2,1)}, bf16[256,7168]{1,0:T(8,128)(2,1)S(1)}, u32[]{:S(2)}) %copy-start) | copy-done | bytes 3670040
  34.6 0.1 reshape.18
  34.8 19.2 %all_to_all.11 = bf16[64,2,1152]{2,1,0:T(2,128)(2,1)S(1)} all-to-all(bf16[64,2,1152]{2,1,0:T(2,128)(2,1)S(1)} %reshape.18), channel_id=1, replica_groups=mesh['ctx'=64,'grp'=4] {'ctx'}, dimensions={0} | all-to-all | bytes 589824 | tf_op jit(solution)/shard_map/all_to_all | solution.py:201
  54.0 0.1 reshape.19.state_ref
  54.1 0.0 copy-start.1
  54.1 2.0 %copy-done.1 = bf16[256,7168]{1,0:T(8,128)(2,1)S(1)} copy-done((bf16[256,7168]{1,0:T(8,128)(2,1)S(1)}, bf16[256,7168]{1,0:T(8,128)(2,1)}, u32[]{:S(2)}) %copy-start.1) | copy-done | bytes 3670040
  56.1 1.2 %project.1 = bf16[2,7168]{1,0:T(2,128)(2,1)S(1)} custom-call(bf16[128,1152]{1,0:T(8,128)(2,1)S(1)} %reshape.19.state_ref, bf16[2,512,128]{2,1,0:T(8,128)(2,1)S(1)} %get-tuple-element.15.w_uv_ref, bf16[256,7168]{1,0:T(8,128)(2,1)S(1)} %copy-done.1), custom_call_target="tpu_custom_call" | custom-call | tf_op jit(solution)/shard_map/project/pallas_call | solution.py:204
  57.3 0.2 collective-permute-start.2
  57.5 3.5 %collective-permute-start.1 = (bf16[2,7168]{1,0:T(2,128)(2,1)S(1)}, bf16[2,7168]{1,0:T(2,128)(2,1)S(1)}, u32[]{:S(2)}, u32[]{:S(2)}) collective-permute-start(bf16[2,7168]{1,0:T(2,128)(2,1)S(1)} %project.1), channel_id=1, source_target_pairs={{0,128},{4,132},{8,136},{12,140},{16,144},{20,148},{24,152},{28,15... | collective-permute-start | bytes 86024 | tf_op jit(solution)/shard_map/ppermute | solution.py:23
  61.0 0.4 collective-permute-start
  61.5 0.0 collective-permute-done.2
  61.5 1.4 %collective-permute-done.1 = bf16[2,7168]{1,0:T(2,128)(2,1)S(1)} collective-permute-done((bf16[2,7168]{1,0:T(2,128)(2,1)S(1)}, bf16[2,7168]{1,0:T(2,128)(2,1)S(1)}, u32[]{:S(2)}, u32[]{:S(2)}) %collective-permute-start.1) | collective-permute-done | bytes 28704 | tf_op jit(solution)/shard_map/ppermute | solution.py:23
  62.9 2.0 %collective-permute-done = bf16[2,7168]{1,0:T(2,128)(2,1)S(1)} collective-permute-done((bf16[2,7168]{1,0:T(2,128)(2,1)S(1)}, bf16[2,7168]{1,0:T(2,128)(2,1)S(1)}, u32[]{:S(2)}, u32[]{:S(2)}) %collective-permute-start) | collective-permute-done | bytes 28704 | tf_op jit(solution)/shard_map/ppermute | solution.py:23
  64.9 0.1 add_convert_fusion.2
  65.0 0.5 collective-permute-start.5
  65.5 2.2 %collective-permute-start.4 = (bf16[2,7168]{1,0:T(2,128)(2,1)S(1)}, bf16[2,7168]{1,0:T(2,128)(2,1)S(1)}, u32[]{:S(2)}, u32[]{:S(2)}) collective-permute-start(bf16[2,7168]{1,0:T(2,128)(2,1)S(1)} %add_convert_fusion.2), channel_id=1, source_target_pairs={{0,32},{4,36},{8,40},{12,44},{16,48},{20,52},{24,56},{28,60},{32,0... | collective-permute-start | bytes 86024 | tf_op jit(solution)/shard_map/ppermute | solution.py:23
  67.7 1.4 %collective-permute-start.3 = (bf16[2,7168]{1,0:T(2,128)(2,1)S(1)}, bf16[2,7168]{1,0:T(2,128)(2,1)S(1)}, u32[]{:S(2)}, u32[]{:S(2)}) collective-permute-start(bf16[2,7168]{1,0:T(2,128)(2,1)S(1)} %add_convert_fusion.2), channel_id=1, source_target_pairs={{0,16},{4,20},{8,24},{12,28},{16,0},{20,4},{24,8},{28,12},{32,48},... | collective-permute-start | bytes 86024 | tf_op jit(solution)/shard_map/ppermute | solution.py:23
  69.1 1.0 %collective-permute-done.5 = bf16[2,7168]{1,0:T(2,128)(2,1)S(1)} collective-permute-done((bf16[2,7168]{1,0:T(2,128)(2,1)S(1)}, bf16[2,7168]{1,0:T(2,128)(2,1)S(1)}, u32[]{:S(2)}, u32[]{:S(2)}) %collective-permute-start.5) | collective-permute-done | bytes 28704 | tf_op jit(solution)/shard_map/ppermute | solution.py:23
  70.1 0.7 collective-permute-done.4
  70.8 0.7 collective-permute-done.3
  71.6 0.1 add_convert_fusion.1
  71.6 0.6 collective-permute-start.8
  72.3 4.1 %collective-permute-start.7 = (bf16[2,7168]{1,0:T(2,128)(2,1)S(1)}, bf16[2,7168]{1,0:T(2,128)(2,1)S(1)}, u32[]{:S(2)}, u32[]{:S(2)}) collective-permute-start(bf16[2,7168]{1,0:T(2,128)(2,1)S(1)} %add_convert_fusion.1), channel_id=1, source_target_pairs={{0,8},{4,12},{8,0},{12,4},{16,24},{20,28},{24,16},{28,20},{32,40},... | collective-permute-start | bytes 86024 | tf_op jit(solution)/shard_map/ppermute | solution.py:23
  76.3 1.9 %collective-permute-start.6 = (bf16[2,7168]{1,0:T(2,128)(2,1)S(1)}, bf16[2,7168]{1,0:T(2,128)(2,1)S(1)}, u32[]{:S(2)}, u32[]{:S(2)}) collective-permute-start(bf16[2,7168]{1,0:T(2,128)(2,1)S(1)} %add_convert_fusion.1), channel_id=1, source_target_pairs={{0,4},{4,0},{8,12},{12,8},{16,20},{20,16},{24,28},{28,24},{32,36},... | collective-permute-start | bytes 86024 | tf_op jit(solution)/shard_map/ppermute | solution.py:23
  78.2 0.0 collective-permute-done.8
  78.2 1.8 %collective-permute-done.7 = bf16[2,7168]{1,0:T(2,128)(2,1)S(1)} collective-permute-done((bf16[2,7168]{1,0:T(2,128)(2,1)S(1)}, bf16[2,7168]{1,0:T(2,128)(2,1)S(1)}, u32[]{:S(2)}, u32[]{:S(2)}) %collective-permute-start.7) | collective-permute-done | bytes 28704 | tf_op jit(solution)/shard_map/ppermute | solution.py:23
  80.1 1.2 %collective-permute-done.6 = bf16[2,7168]{1,0:T(2,128)(2,1)S(1)} collective-permute-done((bf16[2,7168]{1,0:T(2,128)(2,1)S(1)}, bf16[2,7168]{1,0:T(2,128)(2,1)S(1)}, u32[]{:S(2)}, u32[]{:S(2)}) %collective-permute-start.6) | collective-permute-done | bytes 28704 | tf_op jit(solution)/shard_map/ppermute | solution.py:23
  81.3 0.7 add_convert_fusion
Async XLA Ops:
  32.9 1.8 %copy-start = (bf16[256,7168]{1,0:T(8,128)(2,1)}, bf16[256,7168]{1,0:T(8,128)(2,1)S(1)}, u32[]{:S(2)}) copy-start(bf16[256,7168]{1,0:T(8,128)(2,1)S(1)} %get-tuple-element.16.w_out_ref) | copy-start | bytes 11010052
  54.1 2.0 %copy-start.1 = (bf16[256,7168]{1,0:T(8,128)(2,1)S(1)}, bf16[256,7168]{1,0:T(8,128)(2,1)}, u32[]{:S(2)}) copy-start(bf16[256,7168]{1,0:T(8,128)(2,1)} %copy-done) | copy-start | bytes 11010052
  57.3 4.2 %collective-permute-start.2 = (bf16[2,7168]{1,0:T(2,128)(2,1)S(1)}, bf16[2,7168]{1,0:T(2,128)(2,1)S(1)}, u32[]{:S(2)}, u32[]{:S(2)}) collective-permute-start(bf16[2,7168]{1,0:T(2,128)(2,1)S(1)} %project.1), channel_id=1, source_target_pairs={{0,192},{4,196},{8,200},{12,204},{16,208},{20,212},{24,216},{28,22... | collective-permute-start | bytes 86024 | tf_op jit(solution)/shard_map/ppermute | solution.py:23
  57.5 5.4 %collective-permute-start.1 = (bf16[2,7168]{1,0:T(2,128)(2,1)S(1)}, bf16[2,7168]{1,0:T(2,128)(2,1)S(1)}, u32[]{:S(2)}, u32[]{:S(2)}) collective-permute-start(bf16[2,7168]{1,0:T(2,128)(2,1)S(1)} %project.1), channel_id=1, source_target_pairs={{0,128},{4,132},{8,136},{12,140},{16,144},{20,148},{24,152},{28,15... | collective-permute-start | bytes 86024 | tf_op jit(solution)/shard_map/ppermute | solution.py:23
  61.0 3.9 %collective-permute-start = (bf16[2,7168]{1,0:T(2,128)(2,1)S(1)}, bf16[2,7168]{1,0:T(2,128)(2,1)S(1)}, u32[]{:S(2)}, u32[]{:S(2)}) collective-permute-start(bf16[2,7168]{1,0:T(2,128)(2,1)S(1)} %project.1), channel_id=1, source_target_pairs={{0,64},{4,68},{8,72},{12,76},{16,80},{20,84},{24,88},{28,92},{32,9... | collective-permute-start | bytes 86024 | tf_op jit(solution)/shard_map/ppermute | solution.py:23
  65.0 5.2 %collective-permute-start.5 = (bf16[2,7168]{1,0:T(2,128)(2,1)S(1)}, bf16[2,7168]{1,0:T(2,128)(2,1)S(1)}, u32[]{:S(2)}, u32[]{:S(2)}) collective-permute-start(bf16[2,7168]{1,0:T(2,128)(2,1)S(1)} %add_convert_fusion.2), channel_id=1, source_target_pairs={{0,48},{4,52},{8,56},{12,60},{16,32},{20,36},{24,40},{28,44},{32,1... | collective-permute-start | bytes 86024 | tf_op jit(solution)/shard_map/ppermute | solution.py:23
  65.5 5.4 %collective-permute-start.4 = (bf16[2,7168]{1,0:T(2,128)(2,1)S(1)}, bf16[2,7168]{1,0:T(2,128)(2,1)S(1)}, u32[]{:S(2)}, u32[]{:S(2)}) collective-permute-start(bf16[2,7168]{1,0:T(2,128)(2,1)S(1)} %add_convert_fusion.2), channel_id=1, source_target_pairs={{0,32},{4,36},{8,40},{12,44},{16,48},{20,52},{24,56},{28,60},{32,0... | collective-permute-start | bytes 86024 | tf_op jit(solution)/shard_map/ppermute | solution.py:23
  67.7 3.9 %collective-permute-start.3 = (bf16[2,7168]{1,0:T(2,128)(2,1)S(1)}, bf16[2,7168]{1,0:T(2,128)(2,1)S(1)}, u32[]{:S(2)}, u32[]{:S(2)}) collective-permute-start(bf16[2,7168]{1,0:T(2,128)(2,1)S(1)} %add_convert_fusion.2), channel_id=1, source_target_pairs={{0,16},{4,20},{8,24},{12,28},{16,0},{20,4},{24,8},{28,12},{32,48},... | collective-permute-start | bytes 86024 | tf_op jit(solution)/shard_map/ppermute | solution.py:23
  71.6 6.6 %collective-permute-start.8 = (bf16[2,7168]{1,0:T(2,128)(2,1)S(1)}, bf16[2,7168]{1,0:T(2,128)(2,1)S(1)}, u32[]{:S(2)}, u32[]{:S(2)}) collective-permute-start(bf16[2,7168]{1,0:T(2,128)(2,1)S(1)} %add_convert_fusion.1), channel_id=1, source_target_pairs={{0,12},{4,8},{8,4},{12,0},{16,28},{20,24},{24,20},{28,16},{32,44},... | collective-permute-start | bytes 86024 | tf_op jit(solution)/shard_map/ppermute | solution.py:23
  72.3 7.8 %collective-permute-start.7 = (bf16[2,7168]{1,0:T(2,128)(2,1)S(1)}, bf16[2,7168]{1,0:T(2,128)(2,1)S(1)}, u32[]{:S(2)}, u32[]{:S(2)}) collective-permute-start(bf16[2,7168]{1,0:T(2,128)(2,1)S(1)} %add_convert_fusion.1), channel_id=1, source_target_pairs={{0,8},{4,12},{8,0},{12,4},{16,24},{20,28},{24,16},{28,20},{32,40},... | collective-permute-start | bytes 86024 | tf_op jit(solution)/shard_map/ppermute | solution.py:23
  76.3 5.0 %collective-permute-start.6 = (bf16[2,7168]{1,0:T(2,128)(2,1)S(1)}, bf16[2,7168]{1,0:T(2,128)(2,1)S(1)}, u32[]{:S(2)}, u32[]{:S(2)}) collective-permute-start(bf16[2,7168]{1,0:T(2,128)(2,1)S(1)} %add_convert_fusion.1), channel_id=1, source_target_pairs={{0,4},{4,0},{8,12},{12,8},{16,20},{20,16},{24,28},{28,24},{32,36},... | collective-permute-start | bytes 86024 | tf_op jit(solution)/shard_map/ppermute | solution.py:23

commit v5 on v4

--- a/solution.py
+++ b/solution.py
@@ -24,36 +24,45 @@
     return (x.astype(F32) + a.astype(F32)) + (b.astype(F32) + c.astype(F32))
 
 
-def prepare_kernel(
-    page_len, here_ref, lengths_hbm, table_hbm, q_latent_hbm, q_rope_hbm, cache_hbm,
-    query_ref, live_ref, keys_ref, lengths_ref, table_ref, q_latent_ref, q_rope_ref, sems,
+def message_kernel(q_latent_hbm, q_rope_hbm, message_ref, q_latent_ref, q_rope_ref, sems):
+    copies = [
+        pltpu.make_async_copy(q_latent_hbm, q_latent_ref, sems.at[0]),
+        pltpu.make_async_copy(q_rope_hbm, q_rope_ref, sems.at[1]),
+    ]
+    for copy in copies:
+        copy.start()
+    for copy in copies:
+        copy.wait()
+    rows, heads, _ = q_latent_ref.shape
+    q_latent = q_latent_ref[...].astype(F32)
+    q_rope = q_rope_ref[...].astype(F32)
+    message = [
+        jnp.concatenate(
+            [q_latent[r, h : h + 1] for h in range(heads)] + [q_rope[r, h : h + 1] for h in range(heads)],
+            axis=1,
+        )
+        for r in range(rows)
+    ]
+    message_ref[...] = jnp.concatenate(message, axis=0).astype(BF16)
+
+
+def fetch_kernel(
+    page_len, here_ref, lengths_hbm, table_hbm, cache_hbm, w_uv_hbm, w_out_hbm,
+    live_ref, keys_ref, w_uv_ref, *rest,
 ):
-    pairs = (
-        (q_latent_hbm, q_latent_ref), (q_rope_hbm, q_rope_ref), (lengths_hbm, lengths_ref),
-        (table_hbm, table_ref), (cache_hbm, keys_ref),
-    )
+    *w_out_refs, lengths_ref, table_ref, sems = rest
+    columns = w_out_refs[0].shape[1]
+    pairs = [
+        (lengths_hbm, lengths_ref), (table_hbm, table_ref), (cache_hbm, keys_ref), (w_uv_hbm, w_uv_ref),
+    ]
+    for k, ref in enumerate(w_out_refs):
+        pairs.append((w_out_hbm.at[:, k * columns : (k + 1) * columns], ref))
     copies = [pltpu.make_async_copy(a, b, sems.at[k]) for k, (a, b) in enumerate(pairs)]
     for copy in copies:
         copy.start()
-    rows, heads, latent = q_latent_ref.shape
-    rope = q_rope_ref.shape[2]
     copies[0].wait()
     copies[1].wait()
-    q_latent = q_latent_ref[...].astype(F32)
-    q_rope = q_rope_ref[...].astype(F32)
-    message = jnp.concatenate(
-        [
-            jnp.concatenate(
-                [q_latent[r, h : h + 1] for h in range(heads)] + [q_rope[r, h : h + 1] for h in range(heads)],
-                axis=1,
-            )
-            for r in range(rows)
-        ],
-        axis=0,
-    )
-    query_ref[...] = jnp.broadcast_to(message[None], query_ref.shape).astype(BF16)
-    copies[2].wait()
-    copies[3].wait()
+    rows = live_ref.shape[0]
     tokens = keys_ref.shape[0]
     pages = tokens // page_len
     slots = table_ref.shape[1]
@@ -67,19 +76,11 @@
         room = jnp.max(room, axis=1, keepdims=True)
         alive = mine & (token % page_len < room)
         live_ref[r : r + 1, :] = jnp.max(jnp.where(alive, 1.0, 0.0), axis=0, keepdims=True)
-    copies[4].wait()
-
-
-def attend_kernel(
-    rows, heads, latent, rope, q_ref, keys_ref, live_ref, w_uv_hbm, w_out_hbm,
-    state_ref, w_uv_ref, w_out_ref, sems,
-):
-    copies = [
-        pltpu.make_async_copy(w_uv_hbm, w_uv_ref, sems.at[0]),
-        pltpu.make_async_copy(w_out_hbm, w_out_ref, sems.at[1]),
-    ]
-    for copy in copies:
-        copy.start()
+    for copy in copies[2:]:
+        copy.wait()
+
+
+def attend_kernel(rows, heads, latent, rope, q_ref, keys_ref, live_ref, state_ref):
     count = q_ref.shape[0]
     tokens = keys_ref.shape[0]
     row = lax.broadcasted_iota(jnp.int32, (count, 1), 0) % rows
@@ -107,11 +108,10 @@
         for k, value in enumerate((shift, high, total - high)):
             stats = jnp.where(lane == 3 * h + k, value, stats)
     state_ref[:, side:] = stats.astype(BF16)
-    for copy in copies:
-        copy.wait()
-
-
-def project_kernel(rows, heads, latent, state_ref, w_uv_ref, w_out_ref, term_ref):
+
+
+def project_kernel(rows, heads, latent, state_ref, w_uv_ref, *rest):
+    *w_out_refs, term_ref = rest
     count = state_ref.shape[0]
     mixed = rows * heads
     side = heads * latent
@@ -143,7 +143,11 @@
         ],
         axis=0,
     ).astype(BF16)
-    term_ref[...] = jnp.dot(flat, w_out_ref[...], preferred_element_type=F32).astype(term_ref.dtype)
+    columns = w_out_refs[0].shape[1]
+    for k, ref in enumerate(w_out_refs):
+        term_ref[:, k * columns : (k + 1) * columns] = jnp.dot(
+            flat, ref[...], preferred_element_type=F32
+        ).astype(term_ref.dtype)
 
 
 def local(q_latent, q_rope, latent_cache, page_table, lengths, w_uv, w_out):
@@ -159,44 +163,60 @@
     stay = functools.partial(pltpu.with_memory_space_constraint, memory_space=pltpu.HBM)
     params = pltpu.CompilerParams(vmem_limit_bytes=16 << 20)
     dma = pltpu.SemaphoreType.DMA
-
-    here = lax.axis_index(CTX).reshape(1).astype(jnp.int32)
-    query, live, keys = pl.pallas_call(
-        functools.partial(prepare_kernel, page_len),
+    here = lax.axis_index(CTX).astype(jnp.int32)
+
+    message = pl.pallas_call(
+        message_kernel,
+        out_shape=jax.ShapeDtypeStruct((rows, size), BF16),
+        in_specs=[hbm, hbm],
+        out_specs=vmem,
+        scratch_shapes=[pltpu.VMEM(q_latent.shape, BF16), pltpu.VMEM(q_rope.shape, BF16), dma((2,))],
+        compiler_params=params,
+        name="message",
+    )(stay(q_latent), stay(q_rope))
+
+    near = 4
+    others = [lax.ppermute(message, CTX, xor_pairs(count, k)) for k in range(1, near)]
+    parts = w_out.shape[1] // 1024
+    live, keys, w_uv, *w_outs = pl.pallas_call(
+        functools.partial(fetch_kernel, page_len),
         out_shape=(
-            jax.ShapeDtypeStruct((count, rows, size), BF16),
             pltpu.VMEM((rows, tokens), F32),
             pltpu.VMEM((tokens, width), BF16),
+            pltpu.VMEM(w_uv.shape, BF16),
+            *[pltpu.VMEM((w_out.shape[0], w_out.shape[1] // parts), BF16) for _ in range(parts)],
         ),
         in_specs=[smem, hbm, hbm, hbm, hbm, hbm],
-        out_specs=(vmem, vmem, vmem),
+        out_specs=(vmem,) * (3 + parts),
         scratch_shapes=[
-            pltpu.SMEM(lengths.shape, jnp.int32),
-            pltpu.VMEM(page_table.shape, jnp.int32),
-            pltpu.VMEM(q_latent.shape, BF16),
-            pltpu.VMEM(q_rope.shape, BF16),
-            dma((5,)),
+            pltpu.SMEM(lengths.shape, jnp.int32), pltpu.VMEM(page_table.shape, jnp.int32), dma((4 + parts,)),
         ],
         compiler_params=params,
-        name="prepare",
-    )(here, stay(lengths), stay(page_table), stay(q_latent), stay(q_rope), stay(latent_cache.reshape(tokens, width)))
-
-    query = lax.all_to_all(query, CTX, split_axis=0, concat_axis=0, tiled=True)
+        cost_estimate=pl.CostEstimate(flops=0, bytes_accessed=9 << 20, transcendentals=0),
+        name="fetch",
+    )(
+        here.reshape(1), stay(lengths), stay(page_table), stay(latent_cache.reshape(tokens, width)),
+        stay(w_uv), stay(w_out),
+    )
+    away = lax.broadcasted_iota(jnp.int32, (near, 1, 1), 0) ^ (here % near)
+    column = jnp.broadcast_to(message[None], (near, rows, size))
+    for k in range(1, near):
+        column = jnp.where(away == k, others[k - 1][None], column)
+    planes = [[i * near + k for i in range(count // near)] for k in range(near)]
+    query = lax.all_to_all(
+        jnp.broadcast_to(column[None], (count // near, near, rows, size)),
+        CTX, split_axis=0, concat_axis=0, axis_index_groups=planes, tiled=True,
+    )
 
     state_size = heads * latent + LANES
-    state, w_uv, w_out = pl.pallas_call(
+    state = pl.pallas_call(
         functools.partial(attend_kernel, rows, heads, latent, rope),
-        out_shape=(
-            jax.ShapeDtypeStruct((count * rows, state_size), BF16),
-            pltpu.VMEM(w_uv.shape, BF16),
-            pltpu.VMEM(w_out.shape, BF16),
-        ),
-        in_specs=[vmem, vmem, vmem, hbm, hbm],
-        out_specs=(vmem, vmem, vmem),
-        scratch_shapes=[dma((2,))],
+        out_shape=jax.ShapeDtypeStruct((count * rows, state_size), BF16),
+        in_specs=[vmem, vmem, vmem],
+        out_specs=vmem,
         compiler_params=params,
         name="attend",
-    )(query.reshape(count * rows, size), keys, live, stay(w_uv), stay(w_out))
+    )(query.reshape(count * rows, size), keys, live)
 
     state = lax.all_to_all(
         state.reshape(count, rows, state_size), CTX, split_axis=0, concat_axis=0, tiled=True
@@ -204,11 +224,11 @@
     term = pl.pallas_call(
         functools.partial(project_kernel, rows, heads, latent),
         out_shape=jax.ShapeDtypeStruct((rows, w_out.shape[1]), BF16),
-        in_specs=[vmem, vmem, vmem],
+        in_specs=[vmem] * (2 + parts),
         out_specs=vmem,
         compiler_params=params,
         name="project",
-    )(state.reshape(count * rows, state_size), w_uv, w_out)
+    )(state.reshape(count * rows, state_size), w_uv, *w_outs)
     for low in (4, 2, 0):
         term = sum_of_four(term, count, low).astype(BF16)
     return term

time: 82.2 us -> 82.7 us (level)
  blocking collectives: 48.6 us -> 20.5 us
  starting transfers between devices: 14.9 us -> 31.1 us
  waiting for transfers between devices: 8.93 us -> 15.7 us
  local copies, waits for them, and re-layouts: 4.15 us -> 8.36 us
  Pallas kernels: 4.55 us -> 5.51 us
    all_to_all x1 -> x0, blocking collectives: 29.4 us -> none  [local(): query = lax.all_to_all(query, CTX, split_axis=0, concat_axis=0, tiled=True)]
    ppermute x0 -> x3, starting transfers between devices: none -> 8.75 us  [local(): lax.ppermute(message, CTX, xor_pairs(count, k))]
    all_to_all x0 -> x1, starting transfers between devices: none -> 7.48 us  [local(): lax.all_to_all(jnp.broadcast_to(column[None], (count // near, near, rows,...]
    ppermute x0 -> x3, waiting for transfers between devices: none -> 5.69 us  [local(): lax.ppermute(message, CTX, xor_pairs(count, k))]
    unnamed x4 -> x16, local copies, waits for them, and re-layouts: 3.82 us -> 7.15 us
    pallas_call x1 -> x2, Pallas kernels: 1.18 us -> 3.18 us  [the longest x1 2.39 us: local(): pl.pallas_call(functools.partial(fetch_kernel, page_len), out_shape=(pltp...]
    all_to_all x0 -> x1, waiting for transfers between devices: none -> 1.42 us  [local(): lax.all_to_all(jnp.broadcast_to(column[None], (count // near, near, rows,...]
    all_to_all x1, blocking collectives: 19.2 us -> 20.5 us  [local(): lax.all_to_all(state.reshape(count, rows, state_size), CTX, split_axis=0,...]
  transfers between devices with their start and end apart: 9 -> 13, of which waited for: 7 -> 10; matrix products, arithmetic and copies ran while one was open for 0% -> 0% of each run, Pallas kernels for 0% -> 3%
where the time goes in v5:
time: 82.7 us; the launch traced here: 82.2 us
  starting transfers between devices  31.1 us (38%)
  blocking collectives  20.5 us (25%)
  waiting for transfers between devices  15.7 us (19%)
  local copies, waits for them, and re-layouts  8.36 us (10%)
  Pallas kernels  5.51 us (7%)
  other arithmetic  0.91 us (1%)
    all_to_all x1, blocking collectives, local(): lax.all_to_all(state.reshape(count, rows, state_size), CTX, split_axis=0,...  20.5 us
    ppermute x9, starting transfers between devices, sum_of_four(): lax.ppermute(x, CTX, xor_pairs(count, k << low))  14.9 us
    ppermute x3, starting transfers between devices, local(): lax.ppermute(message, CTX, xor_pairs(count, k))  8.75 us
    ppermute x9, waiting for transfers between devices, sum_of_four(): lax.ppermute(x, CTX, xor_pairs(count, k << low))  8.63 us
    all_to_all x1, starting transfers between devices, local(): lax.all_to_all(jnp.broadcast_to(column[None], (count // near, near, rows,...  7.48 us
    unnamed x16, local copies, waits for them, and re-layouts  7.15 us
    ppermute x3, waiting for transfers between devices, local(): lax.ppermute(message, CTX, xor_pairs(count, k))  5.69 us
    pallas_call x1, Pallas kernels, local(): pl.pallas_call(functools.partial(fetch_kernel, page_len), out_shape=(pltp...  2.39 us
  transfers between devices with their start and end apart: 13, of which 10 were waited for; matrix products, arithmetic and copies ran while one was open for 0% of the time, Pallas kernels for 3%

profile of v5, /device:TPU:2, one launch (start us, length us, event | category | flops | bytes accessed | tf_op | source)
XLA Modules:
  0.0 82.2 jit_solution(12463802166840819625)
XLA Ops:
  0.0 0.8 message.1
  0.8 3.4 %collective-permute-start.2 = (bf16[2,1152]{1,0:T(2,128)(2,1)S(1)}, bf16[2,1152]{1,0:T(2,128)(2,1)S(1)}, u32[]{:S(2)}, u32[]{:S(2)}) collective-permute-start(bf16[2,1152]{1,0:T(2,128)(2,1)S(1)} %message.1), channel_id=1, source_target_pairs={{0,4},{4,0},{8,12},{12,8},{16,20},{20,16},{24,28},{28,24},{32,36},... | collective-permute-start | bytes 13832 | tf_op jit(solution)/shard_map/ppermute | solution.py:179
  4.2 5.4 %collective-permute-start.1 = (bf16[2,1152]{1,0:T(2,128)(2,1)S(1)}, bf16[2,1152]{1,0:T(2,128)(2,1)S(1)}, u32[]{:S(2)}, u32[]{:S(2)}) collective-permute-start(bf16[2,1152]{1,0:T(2,128)(2,1)S(1)} %message.1), channel_id=1, source_target_pairs={{0,8},{4,12},{8,0},{12,4},{16,24},{20,28},{24,16},{28,20},{32,40},... | collective-permute-start | bytes 13832 | tf_op jit(solution)/shard_map/ppermute | solution.py:179
  9.6 0.0 collective-permute-start
  9.6 0.0 collective-permute-done.2
  9.6 2.1 %collective-permute-done.1 = bf16[2,1152]{1,0:T(2,128)(2,1)S(1)} collective-permute-done((bf16[2,1152]{1,0:T(2,128)(2,1)S(1)}, bf16[2,1152]{1,0:T(2,128)(2,1)S(1)}, u32[]{:S(2)}, u32[]{:S(2)}) %collective-permute-start.1) | collective-permute-done | bytes 4640 | tf_op jit(solution)/shard_map/ppermute | solution.py:179
  11.7 3.6 %collective-permute-done = bf16[2,1152]{1,0:T(2,128)(2,1)S(1)} collective-permute-done((bf16[2,1152]{1,0:T(2,128)(2,1)S(1)}, bf16[2,1152]{1,0:T(2,128)(2,1)S(1)}, u32[]{:S(2)}, u32[]{:S(2)}) %collective-permute-start) | collective-permute-done | bytes 4640 | tf_op jit(solution)/shard_map/ppermute | solution.py:179
  15.3 0.1 broadcast_select_fusion.1
  15.4 0.9 %broadcast_in_dim.58 = bf16[16,4,2,1152]{3,2,1,0:T(2,128)(2,1)} broadcast(bf16[4,2,1152]{2,1,0:T(2,128)(2,1)S(1)} %broadcast_select_fusion.1), dimensions={1,2,3} | broadcast | bytes 313344 | tf_op jit(solution)/shard_map/broadcast_in_dim | solution.py:207
  16.2 7.5 %all-to-all-start = ((bf16[16,4,2,1152]{3,2,1,0:T(2,128)(2,1)}), bf16[16,4,2,1152]{3,2,1,0:T(2,128)(2,1)S(1)}, u32[]{:S(2)}, u32[]{:S(2)}) async-start(bf16[16,4,2,1152]{3,2,1,0:T(2,128)(2,1)} %broadcast_in_dim.58), calls=%async_computation | async-start | bytes 589824 | tf_op jit(solution)/shard_map/all_to_all | solution.py:206
  23.7 2.4 %fetch.1 = (f32[2,512]{1,0:T(2,128)S(1)}, bf16[512,576]{1,0:T(8,128)(2,1)S(1)}, bf16[2,512,128]{2,1,0:T(8,128)(2,1)S(1)}, bf16[256,1024]{1,0:T(8,128)(2,1)S(1)},...) custom-call(s32[1]{0:T(128)} %bitcast.here_ref, ...), custom_call_target="tpu_custom_call" | custom-call | bytes 9437184 | tf_op jit(solution)/shard_map/fetch/pallas_call | solution.py:181
  26.1 0.0 copy-start
  26.1 0.8 copy-done
  26.9 0.0 copy-start.2
  26.9 0.8 copy-done.2
  27.7 0.0 copy-start.4
  27.7 0.8 copy-done.4
  28.5 0.0 copy-start.6
  28.5 0.7 copy-done.6
  29.2 1.4 %all-to-all-done = bf16[16,4,2,1152]{3,2,1,0:T(2,128)(2,1)S(1)} async-done(((bf16[16,4,2,1152]{3,2,1,0:T(2,128)(2,1)}), bf16[16,4,2,1152]{3,2,1,0:T(2,128)(2,1)S(1)}, u32[]{:S(2)}, u32[]{:S(2)}) %all-to-all-start) | async-done | bytes 294944 | tf_op jit(solution)/shard_map/all_to_all | solution.py:206
  30.6 0.1 reshape.35.q_ref
  30.8 1.1 %attend.1 = bf16[128,1152]{1,0:T(8,128)(2,1)S(1)} custom-call(bf16[128,1152]{1,0:T(8,128)(2,1)S(1)} %reshape.35.q_ref, bf16[512,576]{1,0:T(8,128)(2,1)S(1)} %get-tuple-element.15.keys_ref, f32[2,512]{1,0:T(2,128)S(1)} %get-tuple-element.16.live_ref), custom_call_target="tpu_custom_call" | custom-call | tf_op jit(solution)/shard_map/attend/pallas_call | solution.py:212
  31.9 0.1 reshape.38
  32.0 20.5 %all_to_all.10 = bf16[64,2,1152]{2,1,0:T(2,128)(2,1)S(1)} all-to-all(bf16[64,2,1152]{2,1,0:T(2,128)(2,1)S(1)} %reshape.38), channel_id=1, replica_groups=mesh['ctx'=64,'grp'=4] {'ctx'}, dimensions={0} | all-to-all | bytes 589824 | tf_op jit(solution)/shard_map/all_to_all | solution.py:221
  52.5 0.1 reshape.39.state_ref
  52.6 0.0 copy-start.1
  52.6 1.0 %copy-done.1 = bf16[256,1024]{1,0:T(8,128)(2,1)S(1)} copy-done((bf16[256,1024]{1,0:T(8,128)(2,1)S(1)}, bf16[256,1024]{1,0:T(8,128)(2,1)}, u32[]{:S(2)}) %copy-start.1) | copy-done | bytes 524312
  53.6 0.0 copy-start.3
  53.6 1.0 %copy-done.3 = bf16[256,1024]{1,0:T(8,128)(2,1)S(1)} copy-done((bf16[256,1024]{1,0:T(8,128)(2,1)S(1)}, bf16[256,1024]{1,0:T(8,128)(2,1)}, u32[]{:S(2)}) %copy-start.3) | copy-done | bytes 524312
  54.7 0.0 copy-start.5
  54.7 1.0 %copy-done.5 = bf16[256,1024]{1,0:T(8,128)(2,1)S(1)} copy-done((bf16[256,1024]{1,0:T(8,128)(2,1)S(1)}, bf16[256,1024]{1,0:T(8,128)(2,1)}, u32[]{:S(2)}) %copy-start.5) | copy-done | bytes 524312
  55.7 0.0 copy-start.7
  55.7 0.9 %copy-done.7 = bf16[2,512,128]{2,1,0:T(8,128)(2,1)S(1)} copy-done((bf16[2,512,128]{2,1,0:T(8,128)(2,1)S(1)}, bf16[2,512,128]{2,1,0:T(8,128)(2,1)}, u32[]{:S(2)}) %copy-start.7) | copy-done | bytes 262168
  56.7 1.2 %project.1 = bf16[2,7168]{1,0:T(2,128)(2,1)S(1)} custom-call(bf16[128,1152]{1,0:T(8,128)(2,1)S(1)} %reshape.39.state_ref, bf16[2,512,128]{2,1,0:T(8,128)(2,1)S(1)} %copy-done.7, bf16[256,1024]{1,0:T(8,128)(2,1)S(1)} %get-tuple-element.18.rest_0_, bf16[256,1024]{1,0:T(8,128)(2,1)S(1)} %get-tuple-element.19.rest_1_, ...), custom_call_target="tpu_custom_call" | custom-call | tf_op jit(solution)/shard_map/project/pallas_call | solution.py:224
  57.9 0.2 collective-permute-start.5
  58.1 3.5 %collective-permute-start.4 = (bf16[2,7168]{1,0:T(2,128)(2,1)S(1)}, bf16[2,7168]{1,0:T(2,128)(2,1)S(1)}, u32[]{:S(2)}, u32[]{:S(2)}) collective-permute-start(bf16[2,7168]{1,0:T(2,128)(2,1)S(1)} %project.1), channel_id=1, source_target_pairs={{0,128},{4,132},{8,136},{12,140},{16,144},{20,148},{24,152},{28,15... | collective-permute-start | bytes 86024 | tf_op jit(solution)/shard_map/ppermute | solution.py:23
  61.6 0.4 collective-permute-start.3
  62.0 0.0 collective-permute-done.5
  62.0 1.5 %collective-permute-done.4 = bf16[2,7168]{1,0:T(2,128)(2,1)S(1)} collective-permute-done((bf16[2,7168]{1,0:T(2,128)(2,1)S(1)}, bf16[2,7168]{1,0:T(2,128)(2,1)S(1)}, u32[]{:S(2)}, u32[]{:S(2)}) %collective-permute-start.4) | collective-permute-done | bytes 28704 | tf_op jit(solution)/shard_map/ppermute | solution.py:23
  63.5 2.0 %collective-permute-done.3 = bf16[2,7168]{1,0:T(2,128)(2,1)S(1)} collective-permute-done((bf16[2,7168]{1,0:T(2,128)(2,1)S(1)}, bf16[2,7168]{1,0:T(2,128)(2,1)S(1)}, u32[]{:S(2)}, u32[]{:S(2)}) %collective-permute-start.3) | collective-permute-done | bytes 28704 | tf_op jit(solution)/shard_map/ppermute | solution.py:23
  65.5 0.1 add_convert_fusion.2
  65.5 0.5 collective-permute-start.8
  66.0 2.3 %collective-permute-start.7 = (bf16[2,7168]{1,0:T(2,128)(2,1)S(1)}, bf16[2,7168]{1,0:T(2,128)(2,1)S(1)}, u32[]{:S(2)}, u32[]{:S(2)}) collective-permute-start(bf16[2,7168]{1,0:T(2,128)(2,1)S(1)} %add_convert_fusion.2), channel_id=1, source_target_pairs={{0,32},{4,36},{8,40},{12,44},{16,48},{20,52},{24,56},{28,60},{32,0... | collective-permute-start | bytes 86024 | tf_op jit(solution)/shard_map/ppermute | solution.py:23
  68.3 1.4 %collective-permute-start.6 = (bf16[2,7168]{1,0:T(2,128)(2,1)S(1)}, bf16[2,7168]{1,0:T(2,128)(2,1)S(1)}, u32[]{:S(2)}, u32[]{:S(2)}) collective-permute-start(bf16[2,7168]{1,0:T(2,128)(2,1)S(1)} %add_convert_fusion.2), channel_id=1, source_target_pairs={{0,16},{4,20},{8,24},{12,28},{16,0},{20,4},{24,8},{28,12},{32,48},... | collective-permute-start | bytes 86024 | tf_op jit(solution)/shard_map/ppermute | solution.py:23
  69.7 1.0 %collective-permute-done.8 = bf16[2,7168]{1,0:T(2,128)(2,1)S(1)} collective-permute-done((bf16[2,7168]{1,0:T(2,128)(2,1)S(1)}, bf16[2,7168]{1,0:T(2,128)(2,1)S(1)}, u32[]{:S(2)}, u32[]{:S(2)}) %collective-permute-start.8) | collective-permute-done | bytes 28704 | tf_op jit(solution)/shard_map/ppermute | solution.py:23
  70.7 0.7 collective-permute-done.7
  71.4 0.8 collective-permute-done.6
  72.2 0.1 add_convert_fusion.1
  72.2 0.4 collective-permute-start.11
  72.6 4.1 %collective-permute-start.10 = (bf16[2,7168]{1,0:T(2,128)(2,1)S(1)}, bf16[2,7168]{1,0:T(2,128)(2,1)S(1)}, u32[]{:S(2)}, u32[]{:S(2)}) collective-permute-start(bf16[2,7168]{1,0:T(2,128)(2,1)S(1)} %add_convert_fusion.1), channel_id=1, source_target_pairs={{0,8},{4,12},{8,0},{12,4},{16,24},{20,28},{24,16},{28,20},{32,40},... | collective-permute-start | bytes 86024 | tf_op jit(solution)/shard_map/ppermute | solution.py:23
  76.7 2.1 %collective-permute-start.9 = (bf16[2,7168]{1,0:T(2,128)(2,1)S(1)}, bf16[2,7168]{1,0:T(2,128)(2,1)S(1)}, u32[]{:S(2)}, u32[]{:S(2)}) collective-permute-start(bf16[2,7168]{1,0:T(2,128)(2,1)S(1)} %add_convert_fusion.1), channel_id=1, source_target_pairs={{0,4},{4,0},{8,12},{12,8},{16,20},{20,16},{24,28},{28,24},{32,36},... | collective-permute-start | bytes 86024 | tf_op jit(solution)/shard_map/ppermute | solution.py:23
  78.8 0.0 collective-permute-done.11
  78.8 1.5 %collective-permute-done.10 = bf16[2,7168]{1,0:T(2,128)(2,1)S(1)} collective-permute-done((bf16[2,7168]{1,0:T(2,128)(2,1)S(1)}, bf16[2,7168]{1,0:T(2,128)(2,1)S(1)}, u32[]{:S(2)}, u32[]{:S(2)}) %collective-permute-start.10) | collective-permute-done | bytes 28704 | tf_op jit(solution)/shard_map/ppermute | solution.py:23
  80.4 1.2 %collective-permute-done.9 = bf16[2,7168]{1,0:T(2,128)(2,1)S(1)} collective-permute-done((bf16[2,7168]{1,0:T(2,128)(2,1)S(1)}, bf16[2,7168]{1,0:T(2,128)(2,1)S(1)}, u32[]{:S(2)}, u32[]{:S(2)}) %collective-permute-start.9) | collective-permute-done | bytes 28704 | tf_op jit(solution)/shard_map/ppermute | solution.py:23
  81.6 0.7 add_convert_fusion
  (2 shorter events, 0.0 us)
Async XLA Ops:
  0.8 8.8 %collective-permute-start.2 = (bf16[2,1152]{1,0:T(2,128)(2,1)S(1)}, bf16[2,1152]{1,0:T(2,128)(2,1)S(1)}, u32[]{:S(2)}, u32[]{:S(2)}) collective-permute-start(bf16[2,1152]{1,0:T(2,128)(2,1)S(1)} %message.1), channel_id=1, source_target_pairs={{0,4},{4,0},{8,12},{12,8},{16,20},{20,16},{24,28},{28,24},{32,36},... | collective-permute-start | bytes 13832 | tf_op jit(solution)/shard_map/ppermute | solution.py:179
  4.2 7.5 %collective-permute-start.1 = (bf16[2,1152]{1,0:T(2,128)(2,1)S(1)}, bf16[2,1152]{1,0:T(2,128)(2,1)S(1)}, u32[]{:S(2)}, u32[]{:S(2)}) collective-permute-start(bf16[2,1152]{1,0:T(2,128)(2,1)S(1)} %message.1), channel_id=1, source_target_pairs={{0,8},{4,12},{8,0},{12,4},{16,24},{20,28},{24,16},{28,20},{32,40},... | collective-permute-start | bytes 13832 | tf_op jit(solution)/shard_map/ppermute | solution.py:179
  9.6 5.7 %collective-permute-start = (bf16[2,1152]{1,0:T(2,128)(2,1)S(1)}, bf16[2,1152]{1,0:T(2,128)(2,1)S(1)}, u32[]{:S(2)}, u32[]{:S(2)}) collective-permute-start(bf16[2,1152]{1,0:T(2,128)(2,1)S(1)} %message.1), channel_id=1, source_target_pairs={{0,12},{4,8},{8,4},{12,0},{16,28},{20,24},{24,20},{28,16},{32,44},... | collective-permute-start | bytes 13832 | tf_op jit(solution)/shard_map/ppermute | solution.py:179
  16.2 14.4 %all-to-all-start = ((bf16[16,4,2,1152]{3,2,1,0:T(2,128)(2,1)}), bf16[16,4,2,1152]{3,2,1,0:T(2,128)(2,1)S(1)}, u32[]{:S(2)}, u32[]{:S(2)}) async-start(bf16[16,4,2,1152]{3,2,1,0:T(2,128)(2,1)} %broadcast_in_dim.58), calls=%async_computation | async-start | bytes 589824 | tf_op jit(solution)/shard_map/all_to_all | solution.py:206
  26.1 0.8 copy-start
  26.9 0.8 copy-start.2
  27.7 0.8 copy-start.4
  28.5 0.7 copy-start.6
  52.6 1.0 %copy-start.1 = (bf16[256,1024]{1,0:T(8,128)(2,1)S(1)}, bf16[256,1024]{1,0:T(8,128)(2,1)}, u32[]{:S(2)}) copy-start(bf16[256,1024]{1,0:T(8,128)(2,1)} %copy-done) | copy-start | bytes 1572868
  53.6 1.0 %copy-start.3 = (bf16[256,1024]{1,0:T(8,128)(2,1)S(1)}, bf16[256,1024]{1,0:T(8,128)(2,1)}, u32[]{:S(2)}) copy-start(bf16[256,1024]{1,0:T(8,128)(2,1)} %copy-done.2) | copy-start | bytes 1572868
  54.7 1.0 %copy-start.5 = (bf16[256,1024]{1,0:T(8,128)(2,1)S(1)}, bf16[256,1024]{1,0:T(8,128)(2,1)}, u32[]{:S(2)}) copy-start(bf16[256,1024]{1,0:T(8,128)(2,1)} %copy-done.4) | copy-start | bytes 1572868
  55.7 0.9 %copy-start.7 = (bf16[2,512,128]{2,1,0:T(8,128)(2,1)S(1)}, bf16[2,512,128]{2,1,0:T(8,128)(2,1)}, u32[]{:S(2)}) copy-start(bf16[2,512,128]{2,1,0:T(8,128)(2,1)} %copy-done.6) | copy-start | bytes 786436
  57.9 4.2 %collective-permute-start.5 = (bf16[2,7168]{1,0:T(2,128)(2,1)S(1)}, bf16[2,7168]{1,0:T(2,128)(2,1)S(1)}, u32[]{:S(2)}, u32[]{:S(2)}) collective-permute-start(bf16[2,7168]{1,0:T(2,128)(2,1)S(1)} %project.1), channel_id=1, source_target_pairs={{0,192},{4,196},{8,200},{12,204},{16,208},{20,212},{24,216},{28,22... | collective-permute-start | bytes 86024 | tf_op jit(solution)/shard_map/ppermute | solution.py:23
  58.1 5.4 %collective-permute-start.4 = (bf16[2,7168]{1,0:T(2,128)(2,1)S(1)}, bf16[2,7168]{1,0:T(2,128)(2,1)S(1)}, u32[]{:S(2)}, u32[]{:S(2)}) collective-permute-start(bf16[2,7168]{1,0:T(2,128)(2,1)S(1)} %project.1), channel_id=1, source_target_pairs={{0,128},{4,132},{8,136},{12,140},{16,144},{20,148},{24,152},{28,15... | collective-permute-start | bytes 86024 | tf_op jit(solution)/shard_map/ppermute | solution.py:23
  61.6 3.9 %collective-permute-start.3 = (bf16[2,7168]{1,0:T(2,128)(2,1)S(1)}, bf16[2,7168]{1,0:T(2,128)(2,1)S(1)}, u32[]{:S(2)}, u32[]{:S(2)}) collective-permute-start(bf16[2,7168]{1,0:T(2,128)(2,1)S(1)} %project.1), channel_id=1, source_target_pairs={{0,64},{4,68},{8,72},{12,76},{16,80},{20,84},{24,88},{28,92},{32,9... | collective-permute-start | bytes 86024 | tf_op jit(solution)/shard_map/ppermute | solution.py:23
  65.5 5.2 %collective-permute-start.8 = (bf16[2,7168]{1,0:T(2,128)(2,1)S(1)}, bf16[2,7168]{1,0:T(2,128)(2,1)S(1)}, u32[]{:S(2)}, u32[]{:S(2)}) collective-permute-start(bf16[2,7168]{1,0:T(2,128)(2,1)S(1)} %add_convert_fusion.2), channel_id=1, source_target_pairs={{0,48},{4,52},{8,56},{12,60},{16,32},{20,36},{24,40},{28,44},{32,1... | collective-permute-start | bytes 86024 | tf_op jit(solution)/shard_map/ppermute | solution.py:23
  66.0 5.4 %collective-permute-start.7 = (bf16[2,7168]{1,0:T(2,128)(2,1)S(1)}, bf16[2,7168]{1,0:T(2,128)(2,1)S(1)}, u32[]{:S(2)}, u32[]{:S(2)}) collective-permute-start(bf16[2,7168]{1,0:T(2,128)(2,1)S(1)} %add_convert_fusion.2), channel_id=1, source_target_pairs={{0,32},{4,36},{8,40},{12,44},{16,48},{20,52},{24,56},{28,60},{32,0... | collective-permute-start | bytes 86024 | tf_op jit(solution)/shard_map/ppermute | solution.py:23
  68.3 3.9 %collective-permute-start.6 = (bf16[2,7168]{1,0:T(2,128)(2,1)S(1)}, bf16[2,7168]{1,0:T(2,128)(2,1)S(1)}, u32[]{:S(2)}, u32[]{:S(2)}) collective-permute-start(bf16[2,7168]{1,0:T(2,128)(2,1)S(1)} %add_convert_fusion.2), channel_id=1, source_target_pairs={{0,16},{4,20},{8,24},{12,28},{16,0},{20,4},{24,8},{28,12},{32,48},... | collective-permute-start | bytes 86024 | tf_op jit(solution)/shard_map/ppermute | solution.py:23
  72.2 6.6 %collective-permute-start.11 = (bf16[2,7168]{1,0:T(2,128)(2,1)S(1)}, bf16[2,7168]{1,0:T(2,128)(2,1)S(1)}, u32[]{:S(2)}, u32[]{:S(2)}) collective-permute-start(bf16[2,7168]{1,0:T(2,128)(2,1)S(1)} %add_convert_fusion.1), channel_id=1, source_target_pairs={{0,12},{4,8},{8,4},{12,0},{16,28},{20,24},{24,20},{28,16},{32,44},... | collective-permute-start | bytes 86024 | tf_op jit(solution)/shard_map/ppermute | solution.py:23
  72.6 7.8 %collective-permute-start.10 = (bf16[2,7168]{1,0:T(2,128)(2,1)S(1)}, bf16[2,7168]{1,0:T(2,128)(2,1)S(1)}, u32[]{:S(2)}, u32[]{:S(2)}) collective-permute-start(bf16[2,7168]{1,0:T(2,128)(2,1)S(1)} %add_convert_fusion.1), channel_id=1, source_target_pairs={{0,8},{4,12},{8,0},{12,4},{16,24},{20,28},{24,16},{28,20},{32,40},... | collective-permute-start | bytes 86024 | tf_op jit(solution)/shard_map/ppermute | solution.py:23
  76.7 4.8 %collective-permute-start.9 = (bf16[2,7168]{1,0:T(2,128)(2,1)S(1)}, bf16[2,7168]{1,0:T(2,128)(2,1)S(1)}, u32[]{:S(2)}, u32[]{:S(2)}) collective-permute-start(bf16[2,7168]{1,0:T(2,128)(2,1)S(1)} %add_convert_fusion.1), channel_id=1, source_target_pairs={{0,4},{4,0},{8,12},{12,8},{16,20},{20,16},{24,28},{28,24},{32,36},... | collective-permute-start | bytes 86024 | tf_op jit(solution)/shard_map/ppermute | solution.py:23

commit v6 on v5

--- a/solution.py
+++ b/solution.py
@@ -47,16 +47,9 @@
 
 
 def fetch_kernel(
-    page_len, here_ref, lengths_hbm, table_hbm, cache_hbm, w_uv_hbm, w_out_hbm,
-    live_ref, keys_ref, w_uv_ref, *rest,
+    page_len, here_ref, lengths_hbm, table_hbm, cache_hbm, live_ref, keys_ref, lengths_ref, table_ref, sems
 ):
-    *w_out_refs, lengths_ref, table_ref, sems = rest
-    columns = w_out_refs[0].shape[1]
-    pairs = [
-        (lengths_hbm, lengths_ref), (table_hbm, table_ref), (cache_hbm, keys_ref), (w_uv_hbm, w_uv_ref),
-    ]
-    for k, ref in enumerate(w_out_refs):
-        pairs.append((w_out_hbm.at[:, k * columns : (k + 1) * columns], ref))
+    pairs = [(lengths_hbm, lengths_ref), (table_hbm, table_ref), (cache_hbm, keys_ref)]
     copies = [pltpu.make_async_copy(a, b, sems.at[k]) for k, (a, b) in enumerate(pairs)]
     for copy in copies:
         copy.start()
@@ -76,11 +69,19 @@
         room = jnp.max(room, axis=1, keepdims=True)
         alive = mine & (token % page_len < room)
         live_ref[r : r + 1, :] = jnp.max(jnp.where(alive, 1.0, 0.0), axis=0, keepdims=True)
-    for copy in copies[2:]:
-        copy.wait()
-
-
-def attend_kernel(rows, heads, latent, rope, q_ref, keys_ref, live_ref, state_ref):
+    copies[2].wait()
+
+
+def attend_kernel(
+    rows, heads, latent, rope, q_ref, keys_ref, live_ref, w_uv_hbm, w_out_hbm,
+    state_ref, w_uv_ref, w_out_ref, sems,
+):
+    copies = [
+        pltpu.make_async_copy(w_uv_hbm, w_uv_ref, sems.at[0]),
+        pltpu.make_async_copy(w_out_hbm.at[:, : w_out_ref.shape[1]], w_out_ref, sems.at[1]),
+    ]
+    for copy in copies:
+        copy.start()
     count = q_ref.shape[0]
     tokens = keys_ref.shape[0]
     row = lax.broadcasted_iota(jnp.int32, (count, 1), 0) % rows
@@ -108,10 +109,14 @@
         for k, value in enumerate((shift, high, total - high)):
             stats = jnp.where(lane == 3 * h + k, value, stats)
     state_ref[:, side:] = stats.astype(BF16)
-
-
-def project_kernel(rows, heads, latent, state_ref, w_uv_ref, *rest):
-    *w_out_refs, term_ref = rest
+    for copy in copies:
+        copy.wait()
+
+
+def project_kernel(rows, heads, latent, state_ref, w_uv_ref, first_ref, w_out_hbm, term_ref, second_ref, sem):
+    split = first_ref.shape[1]
+    copy = pltpu.make_async_copy(w_out_hbm.at[:, split:], second_ref, sem)
+    copy.start()
     count = state_ref.shape[0]
     mixed = rows * heads
     side = heads * latent
@@ -143,11 +148,9 @@
         ],
         axis=0,
     ).astype(BF16)
-    columns = w_out_refs[0].shape[1]
-    for k, ref in enumerate(w_out_refs):
-        term_ref[:, k * columns : (k + 1) * columns] = jnp.dot(
-            flat, ref[...], preferred_element_type=F32
-        ).astype(term_ref.dtype)
+    term_ref[:, :split] = jnp.dot(flat, first_ref[...], preferred_element_type=F32).astype(term_ref.dtype)
+    copy.wait()
+    term_ref[:, split:] = jnp.dot(flat, second_ref[...], preferred_element_type=F32).astype(term_ref.dtype)
 
 
 def local(q_latent, q_rope, latent_cache, page_table, lengths, w_uv, w_out):
@@ -177,31 +180,28 @@
 
     near = 4
     others = [lax.ppermute(message, CTX, xor_pairs(count, k)) for k in range(1, near)]
-    parts = w_out.shape[1] // 1024
-    live, keys, w_uv, *w_outs = pl.pallas_call(
+    live, keys = pl.pallas_call(
         functools.partial(fetch_kernel, page_len),
         out_shape=(
             pltpu.VMEM((rows, tokens), F32),
             pltpu.VMEM((tokens, width), BF16),
-            pltpu.VMEM(w_uv.shape, BF16),
-            *[pltpu.VMEM((w_out.shape[0], w_out.shape[1] // parts), BF16) for _ in range(parts)],
         ),
-        in_specs=[smem, hbm, hbm, hbm, hbm, hbm],
-        out_specs=(vmem,) * (3 + parts),
+        in_specs=[smem, hbm, hbm, hbm],
+        out_specs=(vmem, vmem),
         scratch_shapes=[
-            pltpu.SMEM(lengths.shape, jnp.int32), pltpu.VMEM(page_table.shape, jnp.int32), dma((4 + parts,)),
+            pltpu.SMEM(lengths.shape, jnp.int32), pltpu.VMEM(page_table.shape, jnp.int32), dma((3,)),
         ],
         compiler_params=params,
-        cost_estimate=pl.CostEstimate(flops=0, bytes_accessed=9 << 20, transcendentals=0),
+        cost_estimate=pl.CostEstimate(flops=0, bytes_accessed=2 << 20, transcendentals=0),
         name="fetch",
     )(
         here.reshape(1), stay(lengths), stay(page_table), stay(latent_cache.reshape(tokens, width)),
-        stay(w_uv), stay(w_out),
     )
     away = lax.broadcasted_iota(jnp.int32, (near, 1, 1), 0) ^ (here % near)
     column = jnp.broadcast_to(message[None], (near, rows, size))
     for k in range(1, near):
         column = jnp.where(away == k, others[k - 1][None], column)
+    column, live, keys = lax.optimization_barrier((column, live, keys))
     planes = [[i * near + k for i in range(count // near)] for k in range(near)]
     query = lax.all_to_all(
         jnp.broadcast_to(column[None], (count // near, near, rows, size)),
@@ -209,14 +209,20 @@
     )
 
     state_size = heads * latent + LANES
-    state = pl.pallas_call(
+    split = w_out.shape[1] * 4 // 7 // LANES * LANES
+    state, w_uv, w_first = pl.pallas_call(
         functools.partial(attend_kernel, rows, heads, latent, rope),
-        out_shape=jax.ShapeDtypeStruct((count * rows, state_size), BF16),
-        in_specs=[vmem, vmem, vmem],
-        out_specs=vmem,
+        out_shape=(
+            jax.ShapeDtypeStruct((count * rows, state_size), BF16),
+            pltpu.VMEM(w_uv.shape, BF16),
+            pltpu.VMEM((w_out.shape[0], split), BF16),
+        ),
+        in_specs=[vmem, vmem, vmem, hbm, hbm],
+        out_specs=(vmem, vmem, vmem),
+        scratch_shapes=[dma((2,))],
         compiler_params=params,
         name="attend",
-    )(query.reshape(count * rows, size), keys, live)
+    )(query.reshape(count * rows, size), keys, live, stay(w_uv), stay(w_out))
 
     state = lax.all_to_all(
         state.reshape(count, rows, state_size), CTX, split_axis=0, concat_axis=0, tiled=True
@@ -224,11 +230,12 @@
     term = pl.pallas_call(
         functools.partial(project_kernel, rows, heads, latent),
         out_shape=jax.ShapeDtypeStruct((rows, w_out.shape[1]), BF16),
-        in_specs=[vmem] * (2 + parts),
+        in_specs=[vmem, vmem, vmem, hbm],
         out_specs=vmem,
+        scratch_shapes=[pltpu.VMEM((w_out.shape[0], w_out.shape[1] - split), BF16), dma],
         compiler_params=params,
         name="project",
-    )(state.reshape(count * rows, state_size), w_uv, *w_outs)
+    )(state.reshape(count * rows, state_size), w_uv, w_first, stay(w_out))
     for low in (4, 2, 0):
         term = sum_of_four(term, count, low).astype(BF16)
     return term

time: 82.7 us -> 79.8 us (0.965)
  blocking collectives: 20.5 us -> 34.3 us
  starting transfers between devices: 31.1 us -> 23.7 us
  local copies, waits for them, and re-layouts: 8.36 us -> 2.12 us
  waiting for transfers between devices: 15.7 us -> 13 us
    all_to_all x0 -> x1, blocking collectives: none -> 14.2 us  [local(): lax.all_to_all(jnp.broadcast_to(column[None], (count // near, near, rows,...]
    all_to_all x1 -> x0, starting transfers between devices: 7.48 us -> none  [local(): lax.all_to_all(jnp.broadcast_to(column[None], (count // near, near, rows,...]
    unnamed x16 -> x4, local copies, waits for them, and re-layouts: 7.15 us -> 1.63 us
    all_to_all x1 -> x0, waiting for transfers between devices: 1.42 us -> none  [local(): lax.all_to_all(jnp.broadcast_to(column[None], (count // near, near, rows,...]
    pallas_call x1, Pallas kernels: 2.39 us -> 1.14 us  [local(): pl.pallas_call(functools.partial(fetch_kernel, page_len), out_shape=(pltp...]
    ppermute x3, waiting for transfers between devices: 5.69 us -> 4.55 us  [local(): lax.ppermute(message, CTX, xor_pairs(count, k))]
  transfers between devices with their start and end apart: 13 -> 12, of which waited for: 10 -> 9; matrix products, arithmetic and copies ran while one was open for 0% -> 0% of each run, Pallas kernels for 3% -> 1%
where the time goes in v6:
time: 79.8 us; the launch traced here: 79.5 us
  blocking collectives  34.3 us (43%)
  starting transfers between devices  23.7 us (30%)
  waiting for transfers between devices  13 us (16%)
  Pallas kernels  5.4 us (7%)
  local copies, waits for them, and re-layouts  2.12 us (3%)
  other arithmetic  0.91 us (1%)
    all_to_all x1, blocking collectives, local(): lax.all_to_all(state.reshape(count, rows, state_size), CTX, split_axis=0,...  20.1 us
    ppermute x9, starting transfers between devices, sum_of_four(): lax.ppermute(x, CTX, xor_pairs(count, k << low))  14.9 us
    all_to_all x1, blocking collectives, local(): lax.all_to_all(jnp.broadcast_to(column[None], (count // near, near, rows,...  14.2 us
    ppermute x3, starting transfers between devices, local(): lax.ppermute(message, CTX, xor_pairs(count, k))  8.75 us
    ppermute x9, waiting for transfers between devices, sum_of_four(): lax.ppermute(x, CTX, xor_pairs(count, k << low))  8.45 us
    ppermute x3, waiting for transfers between devices, local(): lax.ppermute(message, CTX, xor_pairs(count, k))  4.55 us
    pallas_call x1, Pallas kernels, local(): pl.pallas_call(functools.partial(project_kernel, rows, heads, latent), ou...  1.75 us
    pallas_call x1, Pallas kernels, local(): pl.pallas_call(functools.partial(attend_kernel, rows, heads, latent, rope...  1.72 us
  transfers between devices with their start and end apart: 12, of which 9 were waited for; matrix products, arithmetic and copies ran while one was open for 0% of the time, Pallas kernels for 1%

profile of v6, /device:TPU:2, one launch (start us, length us, event | category | flops | bytes accessed | tf_op | source)
XLA Modules:
  0.0 79.5 jit_solution(2514639155826305530)
XLA Ops:
  0.0 0.8 message.1
  0.8 3.4 %collective-permute-start.2 = (bf16[2,1152]{1,0:T(2,128)(2,1)S(1)}, bf16[2,1152]{1,0:T(2,128)(2,1)S(1)}, u32[]{:S(2)}, u32[]{:S(2)}) collective-permute-start(bf16[2,1152]{1,0:T(2,128)(2,1)S(1)} %message.1), channel_id=1, source_target_pairs={{0,4},{4,0},{8,12},{12,8},{16,20},{20,16},{24,28},{28,24},{32,36},... | collective-permute-start | bytes 13832 | tf_op jit(solution)/shard_map/ppermute | solution.py:182
  4.2 5.4 %collective-permute-start.1 = (bf16[2,1152]{1,0:T(2,128)(2,1)S(1)}, bf16[2,1152]{1,0:T(2,128)(2,1)S(1)}, u32[]{:S(2)}, u32[]{:S(2)}) collective-permute-start(bf16[2,1152]{1,0:T(2,128)(2,1)S(1)} %message.1), channel_id=1, source_target_pairs={{0,8},{4,12},{8,0},{12,4},{16,24},{20,28},{24,16},{28,20},{32,40},... | collective-permute-start | bytes 13832 | tf_op jit(solution)/shard_map/ppermute | solution.py:182
  9.6 0.0 collective-permute-start
  9.6 1.1 %fetch.1 = (f32[2,512]{1,0:T(2,128)S(1)}, bf16[512,576]{1,0:T(8,128)(2,1)S(1)}) custom-call(s32[1]{0:T(128)} %bitcast.here_ref, s32[2]{0:T(128)} %lengths_hbm.1, s32[2,256]{1,0:T(2,128)} %table_hbm.1, bf16[512,576]{1,0:T(8,128)(2,1)} %bitcast.2), custom_call_target="tpu_custom_call" | custom-call | bytes 2097152 | tf_op jit(solution)/shard_map/fetch/pallas_call | solution.py:183
  10.7 0.0 collective-permute-done.2
  10.7 0.9 %collective-permute-done.1 = bf16[2,1152]{1,0:T(2,128)(2,1)S(1)} collective-permute-done((bf16[2,1152]{1,0:T(2,128)(2,1)S(1)}, bf16[2,1152]{1,0:T(2,128)(2,1)S(1)}, u32[]{:S(2)}, u32[]{:S(2)}) %collective-permute-start.1) | collective-permute-done | bytes 4640 | tf_op jit(solution)/shard_map/ppermute | solution.py:182
  11.7 3.6 %collective-permute-done = bf16[2,1152]{1,0:T(2,128)(2,1)S(1)} collective-permute-done((bf16[2,1152]{1,0:T(2,128)(2,1)S(1)}, bf16[2,1152]{1,0:T(2,128)(2,1)S(1)}, u32[]{:S(2)}, u32[]{:S(2)}) %collective-permute-start) | collective-permute-done | bytes 4640 | tf_op jit(solution)/shard_map/ppermute | solution.py:182
  15.3 0.1 broadcast_select_fusion.1
  15.4 0.2 broadcast_in_dim.58
  15.5 14.2 %all_to_all.10 = bf16[16,4,2,1152]{3,2,1,0:T(2,128)(2,1)S(1)} all-to-all(bf16[16,4,2,1152]{3,2,1,0:T(2,128)(2,1)S(1)} %broadcast_in_dim.58), channel_id=1, replica_groups={{0,16,32,48,64,80,96,112,128,144,160,176,192,208,224,240},{4,20,36,52,6..., dimensions={0} | all-to-all | bytes 589824 | tf_op jit(solution)/shard_map/all_to_all | solution.py:206
  29.7 0.1 reshape.35.q_ref
  29.8 1.7 %attend.1 = (bf16[128,1152]{1,0:T(8,128)(2,1)S(1)}, bf16[2,512,128]{2,1,0:T(8,128)(2,1)S(1)}, bf16[256,4096]{1,0:T(8,128)(2,1)S(1)}) custom-call(bf16[128,1152]{1,0:T(8,128)(2,1)S(1)} %reshape.35.q_ref, bf16[512,576]{1,0:T(8,128)(2,1)S(1)} %get-tuple-element.16.keys_ref, f32[2,512]{1,0:T(2,128)S(1)} %get-tuple-element.17.live_ref, ...), custom_call_target="tpu_custom_call" | custom-call | tf_op jit(solution)/shard_map/attend/pallas_call | solution.py:213
  31.6 0.0 copy-start
  31.6 0.7 copy-done
  32.3 0.1 reshape.36
  32.4 20.1 %all_to_all.11 = bf16[64,2,1152]{2,1,0:T(2,128)(2,1)S(1)} all-to-all(bf16[64,2,1152]{2,1,0:T(2,128)(2,1)S(1)} %reshape.36), channel_id=1, replica_groups=mesh['ctx'=64,'grp'=4] {'ctx'}, dimensions={0} | all-to-all | bytes 589824 | tf_op jit(solution)/shard_map/all_to_all | solution.py:227
  52.5 0.1 reshape.37.state_ref
  52.6 0.0 copy-start.1
  52.6 0.9 %copy-done.1 = bf16[2,512,128]{2,1,0:T(8,128)(2,1)S(1)} copy-done((bf16[2,512,128]{2,1,0:T(8,128)(2,1)S(1)}, bf16[2,512,128]{2,1,0:T(8,128)(2,1)}, u32[]{:S(2)}) %copy-start.1) | copy-done | bytes 262168
  53.5 1.8 %project.1 = bf16[2,7168]{1,0:T(2,128)(2,1)S(1)} custom-call(bf16[128,1152]{1,0:T(8,128)(2,1)S(1)} %reshape.37.state_ref, bf16[2,512,128]{2,1,0:T(8,128)(2,1)S(1)} %copy-done.1, bf16[256,4096]{1,0:T(8,128)(2,1)S(1)} %get-tuple-element.20.first_ref, bf16[256,7168]{1,0:T(8,128)(2,1)} %w_out_hbm.3), custom_call_target="tpu_custom_call" | custom-call | tf_op jit(solution)/shard_map/project/pallas_call | solution.py:230
  55.3 0.1 collective-permute-start.5
  55.4 3.5 %collective-permute-start.4 = (bf16[2,7168]{1,0:T(2,128)(2,1)S(1)}, bf16[2,7168]{1,0:T(2,128)(2,1)S(1)}, u32[]{:S(2)}, u32[]{:S(2)}) collective-permute-start(bf16[2,7168]{1,0:T(2,128)(2,1)S(1)} %project.1), channel_id=1, source_target_pairs={{0,128},{4,132},{8,136},{12,140},{16,144},{20,148},{24,152},{28,15... | collective-permute-start | bytes 86024 | tf_op jit(solution)/shard_map/ppermute | solution.py:23
  58.9 0.5 collective-permute-start.3
  59.5 0.0 collective-permute-done.5
  59.5 1.4 %collective-permute-done.4 = bf16[2,7168]{1,0:T(2,128)(2,1)S(1)} collective-permute-done((bf16[2,7168]{1,0:T(2,128)(2,1)S(1)}, bf16[2,7168]{1,0:T(2,128)(2,1)S(1)}, u32[]{:S(2)}, u32[]{:S(2)}) %collective-permute-start.4) | collective-permute-done | bytes 28704 | tf_op jit(solution)/shard_map/ppermute | solution.py:23
  60.8 1.9 %collective-permute-done.3 = bf16[2,7168]{1,0:T(2,128)(2,1)S(1)} collective-permute-done((bf16[2,7168]{1,0:T(2,128)(2,1)S(1)}, bf16[2,7168]{1,0:T(2,128)(2,1)S(1)}, u32[]{:S(2)}, u32[]{:S(2)}) %collective-permute-start.3) | collective-permute-done | bytes 28704 | tf_op jit(solution)/shard_map/ppermute | solution.py:23
  62.8 0.1 add_convert_fusion.2
  62.9 0.6 collective-permute-start.8
  63.5 2.1 %collective-permute-start.7 = (bf16[2,7168]{1,0:T(2,128)(2,1)S(1)}, bf16[2,7168]{1,0:T(2,128)(2,1)S(1)}, u32[]{:S(2)}, u32[]{:S(2)}) collective-permute-start(bf16[2,7168]{1,0:T(2,128)(2,1)S(1)} %add_convert_fusion.2), channel_id=1, source_target_pairs={{0,32},{4,36},{8,40},{12,44},{16,48},{20,52},{24,56},{28,60},{32,0... | collective-permute-start | bytes 86024 | tf_op jit(solution)/shard_map/ppermute | solution.py:23
  65.6 1.4 %collective-permute-start.6 = (bf16[2,7168]{1,0:T(2,128)(2,1)S(1)}, bf16[2,7168]{1,0:T(2,128)(2,1)S(1)}, u32[]{:S(2)}, u32[]{:S(2)}) collective-permute-start(bf16[2,7168]{1,0:T(2,128)(2,1)S(1)} %add_convert_fusion.2), channel_id=1, source_target_pairs={{0,16},{4,20},{8,24},{12,28},{16,0},{20,4},{24,8},{28,12},{32,48},... | collective-permute-start | bytes 86024 | tf_op jit(solution)/shard_map/ppermute | solution.py:23
  67.0 1.0 %collective-permute-done.8 = bf16[2,7168]{1,0:T(2,128)(2,1)S(1)} collective-permute-done((bf16[2,7168]{1,0:T(2,128)(2,1)S(1)}, bf16[2,7168]{1,0:T(2,128)(2,1)S(1)}, u32[]{:S(2)}, u32[]{:S(2)}) %collective-permute-start.8) | collective-permute-done | bytes 28704 | tf_op jit(solution)/shard_map/ppermute | solution.py:23
  68.0 0.8 %collective-permute-done.7 = bf16[2,7168]{1,0:T(2,128)(2,1)S(1)} collective-permute-done((bf16[2,7168]{1,0:T(2,128)(2,1)S(1)}, bf16[2,7168]{1,0:T(2,128)(2,1)S(1)}, u32[]{:S(2)}, u32[]{:S(2)}) %collective-permute-start.7) | collective-permute-done | bytes 28704 | tf_op jit(solution)/shard_map/ppermute | solution.py:23
  68.8 0.6 collective-permute-done.6
  69.5 0.1 add_convert_fusion.1
  69.5 1.0 %collective-permute-start.11 = (bf16[2,7168]{1,0:T(2,128)(2,1)S(1)}, bf16[2,7168]{1,0:T(2,128)(2,1)S(1)}, u32[]{:S(2)}, u32[]{:S(2)}) collective-permute-start(bf16[2,7168]{1,0:T(2,128)(2,1)S(1)} %add_convert_fusion.1), channel_id=1, source_target_pairs={{0,12},{4,8},{8,4},{12,0},{16,28},{20,24},{24,20},{28,16},{32,44},... | collective-permute-start | bytes 86024 | tf_op jit(solution)/shard_map/ppermute | solution.py:23
  70.5 3.2 %collective-permute-start.10 = (bf16[2,7168]{1,0:T(2,128)(2,1)S(1)}, bf16[2,7168]{1,0:T(2,128)(2,1)S(1)}, u32[]{:S(2)}, u32[]{:S(2)}) collective-permute-start(bf16[2,7168]{1,0:T(2,128)(2,1)S(1)} %add_convert_fusion.1), channel_id=1, source_target_pairs={{0,8},{4,12},{8,0},{12,4},{16,24},{20,28},{24,16},{28,20},{32,40},... | collective-permute-start | bytes 86024 | tf_op jit(solution)/shard_map/ppermute | solution.py:23
  73.7 2.4 %collective-permute-start.9 = (bf16[2,7168]{1,0:T(2,128)(2,1)S(1)}, bf16[2,7168]{1,0:T(2,128)(2,1)S(1)}, u32[]{:S(2)}, u32[]{:S(2)}) collective-permute-start(bf16[2,7168]{1,0:T(2,128)(2,1)S(1)} %add_convert_fusion.1), channel_id=1, source_target_pairs={{0,4},{4,0},{8,12},{12,8},{16,20},{20,16},{24,28},{28,24},{32,36},... | collective-permute-start | bytes 86024 | tf_op jit(solution)/shard_map/ppermute | solution.py:23
  76.1 0.0 collective-permute-done.11
  76.1 2.2 %collective-permute-done.10 = bf16[2,7168]{1,0:T(2,128)(2,1)S(1)} collective-permute-done((bf16[2,7168]{1,0:T(2,128)(2,1)S(1)}, bf16[2,7168]{1,0:T(2,128)(2,1)S(1)}, u32[]{:S(2)}, u32[]{:S(2)}) %collective-permute-start.10) | collective-permute-done | bytes 28704 | tf_op jit(solution)/shard_map/ppermute | solution.py:23
  78.3 0.5 collective-permute-done.9
  78.8 0.7 add_convert_fusion
  (2 shorter events, 0.0 us)
Async XLA Ops:
  0.8 9.9 %collective-permute-start.2 = (bf16[2,1152]{1,0:T(2,128)(2,1)S(1)}, bf16[2,1152]{1,0:T(2,128)(2,1)S(1)}, u32[]{:S(2)}, u32[]{:S(2)}) collective-permute-start(bf16[2,1152]{1,0:T(2,128)(2,1)S(1)} %message.1), channel_id=1, source_target_pairs={{0,4},{4,0},{8,12},{12,8},{16,20},{20,16},{24,28},{28,24},{32,36},... | collective-permute-start | bytes 13832 | tf_op jit(solution)/shard_map/ppermute | solution.py:182
  4.2 7.5 %collective-permute-start.1 = (bf16[2,1152]{1,0:T(2,128)(2,1)S(1)}, bf16[2,1152]{1,0:T(2,128)(2,1)S(1)}, u32[]{:S(2)}, u32[]{:S(2)}) collective-permute-start(bf16[2,1152]{1,0:T(2,128)(2,1)S(1)} %message.1), channel_id=1, source_target_pairs={{0,8},{4,12},{8,0},{12,4},{16,24},{20,28},{24,16},{28,20},{32,40},... | collective-permute-start | bytes 13832 | tf_op jit(solution)/shard_map/ppermute | solution.py:182
  9.6 5.7 %collective-permute-start = (bf16[2,1152]{1,0:T(2,128)(2,1)S(1)}, bf16[2,1152]{1,0:T(2,128)(2,1)S(1)}, u32[]{:S(2)}, u32[]{:S(2)}) collective-permute-start(bf16[2,1152]{1,0:T(2,128)(2,1)S(1)} %message.1), channel_id=1, source_target_pairs={{0,12},{4,8},{8,4},{12,0},{16,28},{20,24},{24,20},{28,16},{32,44},... | collective-permute-start | bytes 13832 | tf_op jit(solution)/shard_map/ppermute | solution.py:182
  31.6 0.7 copy-start
  52.6 1.0 %copy-start.1 = (bf16[2,512,128]{2,1,0:T(8,128)(2,1)S(1)}, bf16[2,512,128]{2,1,0:T(8,128)(2,1)}, u32[]{:S(2)}) copy-start(bf16[2,512,128]{2,1,0:T(8,128)(2,1)} %copy-done) | copy-start | bytes 786436
  55.3 4.2 %collective-permute-start.5 = (bf16[2,7168]{1,0:T(2,128)(2,1)S(1)}, bf16[2,7168]{1,0:T(2,128)(2,1)S(1)}, u32[]{:S(2)}, u32[]{:S(2)}) collective-permute-start(bf16[2,7168]{1,0:T(2,128)(2,1)S(1)} %project.1), channel_id=1, source_target_pairs={{0,192},{4,196},{8,200},{12,204},{16,208},{20,212},{24,216},{28,22... | collective-permute-start | bytes 86024 | tf_op jit(solution)/shard_map/ppermute | solution.py:23
  55.4 5.4 %collective-permute-start.4 = (bf16[2,7168]{1,0:T(2,128)(2,1)S(1)}, bf16[2,7168]{1,0:T(2,128)(2,1)S(1)}, u32[]{:S(2)}, u32[]{:S(2)}) collective-permute-start(bf16[2,7168]{1,0:T(2,128)(2,1)S(1)} %project.1), channel_id=1, source_target_pairs={{0,128},{4,132},{8,136},{12,140},{16,144},{20,148},{24,152},{28,15... | collective-permute-start | bytes 86024 | tf_op jit(solution)/shard_map/ppermute | solution.py:23
  58.9 3.9 %collective-permute-start.3 = (bf16[2,7168]{1,0:T(2,128)(2,1)S(1)}, bf16[2,7168]{1,0:T(2,128)(2,1)S(1)}, u32[]{:S(2)}, u32[]{:S(2)}) collective-permute-start(bf16[2,7168]{1,0:T(2,128)(2,1)S(1)} %project.1), channel_id=1, source_target_pairs={{0,64},{4,68},{8,72},{12,76},{16,80},{20,84},{24,88},{28,92},{32,9... | collective-permute-start | bytes 86024 | tf_op jit(solution)/shard_map/ppermute | solution.py:23
  62.9 5.2 %collective-permute-start.8 = (bf16[2,7168]{1,0:T(2,128)(2,1)S(1)}, bf16[2,7168]{1,0:T(2,128)(2,1)S(1)}, u32[]{:S(2)}, u32[]{:S(2)}) collective-permute-start(bf16[2,7168]{1,0:T(2,128)(2,1)S(1)} %add_convert_fusion.2), channel_id=1, source_target_pairs={{0,48},{4,52},{8,56},{12,60},{16,32},{20,36},{24,40},{28,44},{32,1... | collective-permute-start | bytes 86024 | tf_op jit(solution)/shard_map/ppermute | solution.py:23
  63.5 5.4 %collective-permute-start.7 = (bf16[2,7168]{1,0:T(2,128)(2,1)S(1)}, bf16[2,7168]{1,0:T(2,128)(2,1)S(1)}, u32[]{:S(2)}, u32[]{:S(2)}) collective-permute-start(bf16[2,7168]{1,0:T(2,128)(2,1)S(1)} %add_convert_fusion.2), channel_id=1, source_target_pairs={{0,32},{4,36},{8,40},{12,44},{16,48},{20,52},{24,56},{28,60},{32,0... | collective-permute-start | bytes 86024 | tf_op jit(solution)/shard_map/ppermute | solution.py:23
  65.6 3.9 %collective-permute-start.6 = (bf16[2,7168]{1,0:T(2,128)(2,1)S(1)}, bf16[2,7168]{1,0:T(2,128)(2,1)S(1)}, u32[]{:S(2)}, u32[]{:S(2)}) collective-permute-start(bf16[2,7168]{1,0:T(2,128)(2,1)S(1)} %add_convert_fusion.2), channel_id=1, source_target_pairs={{0,16},{4,20},{8,24},{12,28},{16,0},{20,4},{24,8},{28,12},{32,48},... | collective-permute-start | bytes 86024 | tf_op jit(solution)/shard_map/ppermute | solution.py:23
  69.5 6.6 %collective-permute-start.11 = (bf16[2,7168]{1,0:T(2,128)(2,1)S(1)}, bf16[2,7168]{1,0:T(2,128)(2,1)S(1)}, u32[]{:S(2)}, u32[]{:S(2)}) collective-permute-start(bf16[2,7168]{1,0:T(2,128)(2,1)S(1)} %add_convert_fusion.1), channel_id=1, source_target_pairs={{0,12},{4,8},{8,4},{12,0},{16,28},{20,24},{24,20},{28,16},{32,44},... | collective-permute-start | bytes 86024 | tf_op jit(solution)/shard_map/ppermute | solution.py:23
  70.5 7.8 %collective-permute-start.10 = (bf16[2,7168]{1,0:T(2,128)(2,1)S(1)}, bf16[2,7168]{1,0:T(2,128)(2,1)S(1)}, u32[]{:S(2)}, u32[]{:S(2)}) collective-permute-start(bf16[2,7168]{1,0:T(2,128)(2,1)S(1)} %add_convert_fusion.1), channel_id=1, source_target_pairs={{0,8},{4,12},{8,0},{12,4},{16,24},{20,28},{24,16},{28,20},{32,40},... | collective-permute-start | bytes 86024 | tf_op jit(solution)/shard_map/ppermute | solution.py:23
  73.7 5.1 %collective-permute-start.9 = (bf16[2,7168]{1,0:T(2,128)(2,1)S(1)}, bf16[2,7168]{1,0:T(2,128)(2,1)S(1)}, u32[]{:S(2)}, u32[]{:S(2)}) collective-permute-start(bf16[2,7168]{1,0:T(2,128)(2,1)S(1)} %add_convert_fusion.1), channel_id=1, source_target_pairs={{0,4},{4,0},{8,12},{12,8},{16,20},{20,16},{24,28},{28,24},{32,36},... | collective-permute-start | bytes 86024 | tf_op jit(solution)/shard_map/ppermute | solution.py:23

commit v7 on v6

--- a/solution.py
+++ b/solution.py
@@ -73,15 +73,10 @@
 
 
 def attend_kernel(
-    rows, heads, latent, rope, q_ref, keys_ref, live_ref, w_uv_hbm, w_out_hbm,
-    state_ref, w_uv_ref, w_out_ref, sems,
+    rows, heads, latent, rope, q_ref, keys_ref, live_ref, w_out_hbm, state_ref, w_out_ref, sem
 ):
-    copies = [
-        pltpu.make_async_copy(w_uv_hbm, w_uv_ref, sems.at[0]),
-        pltpu.make_async_copy(w_out_hbm.at[:, : w_out_ref.shape[1]], w_out_ref, sems.at[1]),
-    ]
-    for copy in copies:
-        copy.start()
+    copy = pltpu.make_async_copy(w_out_hbm.at[:, : w_out_ref.shape[1]], w_out_ref, sem)
+    copy.start()
     count = q_ref.shape[0]
     tokens = keys_ref.shape[0]
     row = lax.broadcasted_iota(jnp.int32, (count, 1), 0) % rows
@@ -109,14 +104,19 @@
         for k, value in enumerate((shift, high, total - high)):
             stats = jnp.where(lane == 3 * h + k, value, stats)
     state_ref[:, side:] = stats.astype(BF16)
-    for copy in copies:
-        copy.wait()
-
-
-def project_kernel(rows, heads, latent, state_ref, w_uv_ref, first_ref, w_out_hbm, term_ref, second_ref, sem):
+    copy.wait()
+
+
+def project_kernel(
+    rows, heads, latent, state_ref, first_ref, w_uv_hbm, w_out_hbm, term_ref, w_uv_ref, second_ref, sems
+):
     split = first_ref.shape[1]
-    copy = pltpu.make_async_copy(w_out_hbm.at[:, split:], second_ref, sem)
-    copy.start()
+    copies = [
+        pltpu.make_async_copy(w_uv_hbm, w_uv_ref, sems.at[0]),
+        pltpu.make_async_copy(w_out_hbm.at[:, split:], second_ref, sems.at[1]),
+    ]
+    for copy in copies:
+        copy.start()
     count = state_ref.shape[0]
     mixed = rows * heads
     side = heads * latent
@@ -136,6 +136,7 @@
         factor, state_ref[...], (((0,), (0,)), ((), ())), preferred_element_type=F32
     )
     merged = merged[:mixed] + merged[mixed : 2 * mixed]
+    copies[0].wait()
     parts = []
     for h in range(heads):
         total = merged[:, side + 3 * h + 1 : side + 3 * h + 2] + merged[:, side + 3 * h + 2 : side + 3 * h + 3]
@@ -149,7 +150,7 @@
         axis=0,
     ).astype(BF16)
     term_ref[:, :split] = jnp.dot(flat, first_ref[...], preferred_element_type=F32).astype(term_ref.dtype)
-    copy.wait()
+    copies[1].wait()
     term_ref[:, split:] = jnp.dot(flat, second_ref[...], preferred_element_type=F32).astype(term_ref.dtype)
 
 
@@ -209,20 +210,19 @@
     )
 
     state_size = heads * latent + LANES
-    split = w_out.shape[1] * 4 // 7 // LANES * LANES
-    state, w_uv, w_first = pl.pallas_call(
+    split = w_out.shape[1] * 5 // 7 // LANES * LANES
+    state, w_first = pl.pallas_call(
         functools.partial(attend_kernel, rows, heads, latent, rope),
         out_shape=(
             jax.ShapeDtypeStruct((count * rows, state_size), BF16),
-            pltpu.VMEM(w_uv.shape, BF16),
             pltpu.VMEM((w_out.shape[0], split), BF16),
         ),
-        in_specs=[vmem, vmem, vmem, hbm, hbm],
-        out_specs=(vmem, vmem, vmem),
-        scratch_shapes=[dma((2,))],
+        in_specs=[vmem, vmem, vmem, hbm],
+        out_specs=(vmem, vmem),
+        scratch_shapes=[dma],
         compiler_params=params,
         name="attend",
-    )(query.reshape(count * rows, size), keys, live, stay(w_uv), stay(w_out))
+    )(query.reshape(count * rows, size), keys, live, stay(w_out))
 
     state = lax.all_to_all(
         state.reshape(count, rows, state_size), CTX, split_axis=0, concat_axis=0, tiled=True
@@ -230,12 +230,14 @@
     term = pl.pallas_call(
         functools.partial(project_kernel, rows, heads, latent),
         out_shape=jax.ShapeDtypeStruct((rows, w_out.shape[1]), BF16),
-        in_specs=[vmem, vmem, vmem, hbm],
+        in_specs=[vmem, vmem, hbm, hbm],
         out_specs=vmem,
-        scratch_shapes=[pltpu.VMEM((w_out.shape[0], w_out.shape[1] - split), BF16), dma],
+        scratch_shapes=[
+            pltpu.VMEM(w_uv.shape, BF16), pltpu.VMEM((w_out.shape[0], w_out.shape[1] - split), BF16), dma((2,)),
+        ],
         compiler_params=params,
         name="project",
-    )(state.reshape(count * rows, state_size), w_uv, w_first, stay(w_out))
+    )(state.reshape(count * rows, state_size), w_first, stay(w_uv), stay(w_out))
     for low in (4, 2, 0):
         term = sum_of_four(term, count, low).astype(BF16)
     return term

time: 79.8 us -> 80 us (level)
  waiting for transfers between devices: 13 us -> 12.2 us
    ppermute x3, waiting for transfers between devices: 4.55 us -> 3.7 us  [local(): lax.ppermute(message, CTX, xor_pairs(count, k))]
where the time goes in v7:
time: 80 us; the launch traced here: 79.3 us
  blocking collectives  34.3 us (43%)
  starting transfers between devices  23.7 us (30%)
  waiting for transfers between devices  12.2 us (15%)
  Pallas kernels  5.76 us (7%)
  local copies, waits for them, and re-layouts  2.41 us (3%)
  other arithmetic  0.91 us (1%)
    all_to_all x1, blocking collectives, local(): lax.all_to_all(state.reshape(count, rows, state_size), CTX, split_axis=0,...  20.1 us
    ppermute x9, starting transfers between devices, sum_of_four(): lax.ppermute(x, CTX, xor_pairs(count, k << low))  14.9 us
    all_to_all x1, blocking collectives, local(): lax.all_to_all(jnp.broadcast_to(column[None], (count // near, near, rows,...  14.2 us
    ppermute x3, starting transfers between devices, local(): lax.ppermute(message, CTX, xor_pairs(count, k))  8.75 us
    ppermute x9, waiting for transfers between devices, sum_of_four(): lax.ppermute(x, CTX, xor_pairs(count, k << low))  8.45 us
    ppermute x3, waiting for transfers between devices, local(): lax.ppermute(message, CTX, xor_pairs(count, k))  3.7 us
    pallas_call x1, Pallas kernels, local(): pl.pallas_call(functools.partial(project_kernel, rows, heads, latent), ou...  2.06 us
    unnamed x4, local copies, waits for them, and re-layouts  1.92 us
  transfers between devices with their start and end apart: 12, of which 9 were waited for; matrix products, arithmetic and copies ran while one was open for 0% of the time, Pallas kernels for 1%

profile of v7, /device:TPU:2, one launch (start us, length us, event | category | flops | bytes accessed | tf_op | source)
XLA Modules:
  0.0 79.3 jit_solution(10991199670923607687)
XLA Ops:
  0.0 0.8 message.1
  0.8 3.4 %collective-permute-start.2 = (bf16[2,1152]{1,0:T(2,128)(2,1)S(1)}, bf16[2,1152]{1,0:T(2,128)(2,1)S(1)}, u32[]{:S(2)}, u32[]{:S(2)}) collective-permute-start(bf16[2,1152]{1,0:T(2,128)(2,1)S(1)} %message.1), channel_id=1, source_target_pairs={{0,4},{4,0},{8,12},{12,8},{16,20},{20,16},{24,28},{28,24},{32,36},... | collective-permute-start | bytes 13832 | tf_op jit(solution)/shard_map/ppermute | solution.py:183
  4.2 5.4 %collective-permute-start.1 = (bf16[2,1152]{1,0:T(2,128)(2,1)S(1)}, bf16[2,1152]{1,0:T(2,128)(2,1)S(1)}, u32[]{:S(2)}, u32[]{:S(2)}) collective-permute-start(bf16[2,1152]{1,0:T(2,128)(2,1)S(1)} %message.1), channel_id=1, source_target_pairs={{0,8},{4,12},{8,0},{12,4},{16,24},{20,28},{24,16},{28,20},{32,40},... | collective-permute-start | bytes 13832 | tf_op jit(solution)/shard_map/ppermute | solution.py:183
  9.6 0.0 collective-permute-start
  9.6 1.1 %fetch.1 = (f32[2,512]{1,0:T(2,128)S(1)}, bf16[512,576]{1,0:T(8,128)(2,1)S(1)}) custom-call(s32[1]{0:T(128)} %bitcast.here_ref, s32[2]{0:T(128)} %lengths_hbm.1, s32[2,256]{1,0:T(2,128)} %table_hbm.1, bf16[512,576]{1,0:T(8,128)(2,1)} %bitcast.2), custom_call_target="tpu_custom_call" | custom-call | bytes 2097152 | tf_op jit(solution)/shard_map/fetch/pallas_call | solution.py:184
  10.7 0.0 copy-start
  10.7 0.8 %copy-done = bf16[512,576]{1,0:T(8,128)(2,1)} copy-done((bf16[512,576]{1,0:T(8,128)(2,1)}, bf16[512,576]{1,0:T(8,128)(2,1)S(1)}, u32[]{:S(2)}) %copy-start) | copy-done | bytes 589848
  11.6 0.0 collective-permute-done.2
  11.6 0.1 collective-permute-done.1
  11.7 3.6 %collective-permute-done = bf16[2,1152]{1,0:T(2,128)(2,1)S(1)} collective-permute-done((bf16[2,1152]{1,0:T(2,128)(2,1)S(1)}, bf16[2,1152]{1,0:T(2,128)(2,1)S(1)}, u32[]{:S(2)}, u32[]{:S(2)}) %collective-permute-start) | collective-permute-done | bytes 4640 | tf_op jit(solution)/shard_map/ppermute | solution.py:183
  15.3 0.1 broadcast_select_fusion.1
  15.4 0.2 broadcast_in_dim.58
  15.5 14.2 %all_to_all.10 = bf16[16,4,2,1152]{3,2,1,0:T(2,128)(2,1)S(1)} all-to-all(bf16[16,4,2,1152]{3,2,1,0:T(2,128)(2,1)S(1)} %broadcast_in_dim.58), channel_id=1, replica_groups={{0,16,32,48,64,80,96,112,128,144,160,176,192,208,224,240},{4,20,36,52,6..., dimensions={0} | all-to-all | bytes 589824 | tf_op jit(solution)/shard_map/all_to_all | solution.py:207
  29.7 0.1 reshape.35.q_ref
  29.8 0.0 copy-start.1
  29.8 1.1 %copy-done.1 = bf16[512,576]{1,0:T(8,128)(2,1)S(1)} copy-done((bf16[512,576]{1,0:T(8,128)(2,1)S(1)}, bf16[512,576]{1,0:T(8,128)(2,1)}, u32[]{:S(2)}) %copy-start.1) | copy-done | bytes 589848
  30.9 1.8 %attend.1 = (bf16[128,1152]{1,0:T(8,128)(2,1)S(1)}, bf16[256,5120]{1,0:T(8,128)(2,1)S(1)}) custom-call(bf16[128,1152]{1,0:T(8,128)(2,1)S(1)} %reshape.35.q_ref, bf16[512,576]{1,0:T(8,128)(2,1)S(1)} %copy-done.1, f32[2,512]{1,0:T(2,128)S(1)} %get-tuple-element.16.live_ref, bf16[256,7168]{1,0:T(8,128)(2,1)} %w_out_hbm.3), custom_call_target="tpu_custom_call" | custom-call | tf_op jit(solution)/shard_map/attend/pallas_call | solution.py:214
  32.7 0.1 reshape.36
  32.8 20.1 %all_to_all.11 = bf16[64,2,1152]{2,1,0:T(2,128)(2,1)S(1)} all-to-all(bf16[64,2,1152]{2,1,0:T(2,128)(2,1)S(1)} %reshape.36), channel_id=1, replica_groups=mesh['ctx'=64,'grp'=4] {'ctx'}, dimensions={0} | all-to-all | bytes 589824 | tf_op jit(solution)/shard_map/all_to_all | solution.py:227
  52.9 0.1 reshape.37.state_ref
  53.0 2.1 %project.1 = bf16[2,7168]{1,0:T(2,128)(2,1)S(1)} custom-call(bf16[128,1152]{1,0:T(8,128)(2,1)S(1)} %reshape.37.state_ref, bf16[256,5120]{1,0:T(8,128)(2,1)S(1)} %get-tuple-element.18.first_ref, bf16[2,512,128]{2,1,0:T(8,128)(2,1)} %w_uv_hbm.1, bf16[256,7168]{1,0:T(8,128)(2,1)} %w_out_hbm.3), custom_call_target="tpu_custom_call" | custom-call | tf_op jit(solution)/shard_map/project/pallas_call | solution.py:230
  55.1 0.1 collective-permute-start.5
  55.2 3.5 %collective-permute-start.4 = (bf16[2,7168]{1,0:T(2,128)(2,1)S(1)}, bf16[2,7168]{1,0:T(2,128)(2,1)S(1)}, u32[]{:S(2)}, u32[]{:S(2)}) collective-permute-start(bf16[2,7168]{1,0:T(2,128)(2,1)S(1)} %project.1), channel_id=1, source_target_pairs={{0,128},{4,132},{8,136},{12,140},{16,144},{20,148},{24,152},{28,15... | collective-permute-start | bytes 86024 | tf_op jit(solution)/shard_map/ppermute | solution.py:23
  58.8 0.5 collective-permute-start.3
  59.3 0.0 collective-permute-done.5
  59.3 1.4 %collective-permute-done.4 = bf16[2,7168]{1,0:T(2,128)(2,1)S(1)} collective-permute-done((bf16[2,7168]{1,0:T(2,128)(2,1)S(1)}, bf16[2,7168]{1,0:T(2,128)(2,1)S(1)}, u32[]{:S(2)}, u32[]{:S(2)}) %collective-permute-start.4) | collective-permute-done | bytes 28704 | tf_op jit(solution)/shard_map/ppermute | solution.py:23
  60.7 2.0 %collective-permute-done.3 = bf16[2,7168]{1,0:T(2,128)(2,1)S(1)} collective-permute-done((bf16[2,7168]{1,0:T(2,128)(2,1)S(1)}, bf16[2,7168]{1,0:T(2,128)(2,1)S(1)}, u32[]{:S(2)}, u32[]{:S(2)}) %collective-permute-start.3) | collective-permute-done | bytes 28704 | tf_op jit(solution)/shard_map/ppermute | solution.py:23
  62.6 0.1 add_convert_fusion.2
  62.7 0.6 collective-permute-start.8
  63.3 2.1 %collective-permute-start.7 = (bf16[2,7168]{1,0:T(2,128)(2,1)S(1)}, bf16[2,7168]{1,0:T(2,128)(2,1)S(1)}, u32[]{:S(2)}, u32[]{:S(2)}) collective-permute-start(bf16[2,7168]{1,0:T(2,128)(2,1)S(1)} %add_convert_fusion.2), channel_id=1, source_target_pairs={{0,32},{4,36},{8,40},{12,44},{16,48},{20,52},{24,56},{28,60},{32,0... | collective-permute-start | bytes 86024 | tf_op jit(solution)/shard_map/ppermute | solution.py:23
  65.4 1.5 %collective-permute-start.6 = (bf16[2,7168]{1,0:T(2,128)(2,1)S(1)}, bf16[2,7168]{1,0:T(2,128)(2,1)S(1)}, u32[]{:S(2)}, u32[]{:S(2)}) collective-permute-start(bf16[2,7168]{1,0:T(2,128)(2,1)S(1)} %add_convert_fusion.2), channel_id=1, source_target_pairs={{0,16},{4,20},{8,24},{12,28},{16,0},{20,4},{24,8},{28,12},{32,48},... | collective-permute-start | bytes 86024 | tf_op jit(solution)/shard_map/ppermute | solution.py:23
  66.9 1.0 %collective-permute-done.8 = bf16[2,7168]{1,0:T(2,128)(2,1)S(1)} collective-permute-done((bf16[2,7168]{1,0:T(2,128)(2,1)S(1)}, bf16[2,7168]{1,0:T(2,128)(2,1)S(1)}, u32[]{:S(2)}, u32[]{:S(2)}) %collective-permute-start.8) | collective-permute-done | bytes 28704 | tf_op jit(solution)/shard_map/ppermute | solution.py:23
  67.9 0.8 %collective-permute-done.7 = bf16[2,7168]{1,0:T(2,128)(2,1)S(1)} collective-permute-done((bf16[2,7168]{1,0:T(2,128)(2,1)S(1)}, bf16[2,7168]{1,0:T(2,128)(2,1)S(1)}, u32[]{:S(2)}, u32[]{:S(2)}) %collective-permute-start.7) | collective-permute-done | bytes 28704 | tf_op jit(solution)/shard_map/ppermute | solution.py:23
  68.7 0.6 collective-permute-done.6
  69.3 0.1 add_convert_fusion.1
  69.3 1.0 %collective-permute-start.11 = (bf16[2,7168]{1,0:T(2,128)(2,1)S(1)}, bf16[2,7168]{1,0:T(2,128)(2,1)S(1)}, u32[]{:S(2)}, u32[]{:S(2)}) collective-permute-start(bf16[2,7168]{1,0:T(2,128)(2,1)S(1)} %add_convert_fusion.1), channel_id=1, source_target_pairs={{0,12},{4,8},{8,4},{12,0},{16,28},{20,24},{24,20},{28,16},{32,44},... | collective-permute-start | bytes 86024 | tf_op jit(solution)/shard_map/ppermute | solution.py:23
  70.3 3.2 %collective-permute-start.10 = (bf16[2,7168]{1,0:T(2,128)(2,1)S(1)}, bf16[2,7168]{1,0:T(2,128)(2,1)S(1)}, u32[]{:S(2)}, u32[]{:S(2)}) collective-permute-start(bf16[2,7168]{1,0:T(2,128)(2,1)S(1)} %add_convert_fusion.1), channel_id=1, source_target_pairs={{0,8},{4,12},{8,0},{12,4},{16,24},{20,28},{24,16},{28,20},{32,40},... | collective-permute-start | bytes 86024 | tf_op jit(solution)/shard_map/ppermute | solution.py:23
  73.5 2.4 %collective-permute-start.9 = (bf16[2,7168]{1,0:T(2,128)(2,1)S(1)}, bf16[2,7168]{1,0:T(2,128)(2,1)S(1)}, u32[]{:S(2)}, u32[]{:S(2)}) collective-permute-start(bf16[2,7168]{1,0:T(2,128)(2,1)S(1)} %add_convert_fusion.1), channel_id=1, source_target_pairs={{0,4},{4,0},{8,12},{12,8},{16,20},{20,16},{24,28},{28,24},{32,36},... | collective-permute-start | bytes 86024 | tf_op jit(solution)/shard_map/ppermute | solution.py:23
  75.9 0.0 collective-permute-done.11
  75.9 2.2 %collective-permute-done.10 = bf16[2,7168]{1,0:T(2,128)(2,1)S(1)} collective-permute-done((bf16[2,7168]{1,0:T(2,128)(2,1)S(1)}, bf16[2,7168]{1,0:T(2,128)(2,1)S(1)}, u32[]{:S(2)}, u32[]{:S(2)}) %collective-permute-start.10) | collective-permute-done | bytes 28704 | tf_op jit(solution)/shard_map/ppermute | solution.py:23
  78.2 0.4 collective-permute-done.9
  78.6 0.7 add_convert_fusion
  (2 shorter events, 0.0 us)
Async XLA Ops:
  0.8 10.8 %collective-permute-start.2 = (bf16[2,1152]{1,0:T(2,128)(2,1)S(1)}, bf16[2,1152]{1,0:T(2,128)(2,1)S(1)}, u32[]{:S(2)}, u32[]{:S(2)}) collective-permute-start(bf16[2,1152]{1,0:T(2,128)(2,1)S(1)} %message.1), channel_id=1, source_target_pairs={{0,4},{4,0},{8,12},{12,8},{16,20},{20,16},{24,28},{28,24},{32,36},... | collective-permute-start | bytes 13832 | tf_op jit(solution)/shard_map/ppermute | solution.py:183
  4.2 7.5 %collective-permute-start.1 = (bf16[2,1152]{1,0:T(2,128)(2,1)S(1)}, bf16[2,1152]{1,0:T(2,128)(2,1)S(1)}, u32[]{:S(2)}, u32[]{:S(2)}) collective-permute-start(bf16[2,1152]{1,0:T(2,128)(2,1)S(1)} %message.1), channel_id=1, source_target_pairs={{0,8},{4,12},{8,0},{12,4},{16,24},{20,28},{24,16},{28,20},{32,40},... | collective-permute-start | bytes 13832 | tf_op jit(solution)/shard_map/ppermute | solution.py:183
  9.6 5.7 %collective-permute-start = (bf16[2,1152]{1,0:T(2,128)(2,1)S(1)}, bf16[2,1152]{1,0:T(2,128)(2,1)S(1)}, u32[]{:S(2)}, u32[]{:S(2)}) collective-permute-start(bf16[2,1152]{1,0:T(2,128)(2,1)S(1)} %message.1), channel_id=1, source_target_pairs={{0,12},{4,8},{8,4},{12,0},{16,28},{20,24},{24,20},{28,16},{32,44},... | collective-permute-start | bytes 13832 | tf_op jit(solution)/shard_map/ppermute | solution.py:183
  10.7 0.8 %copy-start = (bf16[512,576]{1,0:T(8,128)(2,1)}, bf16[512,576]{1,0:T(8,128)(2,1)S(1)}, u32[]{:S(2)}) copy-start(bf16[512,576]{1,0:T(8,128)(2,1)S(1)} %get-tuple-element.15.keys_ref) | copy-start | bytes 1769476
  29.8 1.1 %copy-start.1 = (bf16[512,576]{1,0:T(8,128)(2,1)S(1)}, bf16[512,576]{1,0:T(8,128)(2,1)}, u32[]{:S(2)}) copy-start(bf16[512,576]{1,0:T(8,128)(2,1)} %copy-done) | copy-start | bytes 1769476
  55.1 4.2 %collective-permute-start.5 = (bf16[2,7168]{1,0:T(2,128)(2,1)S(1)}, bf16[2,7168]{1,0:T(2,128)(2,1)S(1)}, u32[]{:S(2)}, u32[]{:S(2)}) collective-permute-start(bf16[2,7168]{1,0:T(2,128)(2,1)S(1)} %project.1), channel_id=1, source_target_pairs={{0,192},{4,196},{8,200},{12,204},{16,208},{20,212},{24,216},{28,22... | collective-permute-start | bytes 86024 | tf_op jit(solution)/shard_map/ppermute | solution.py:23
  55.2 5.4 %collective-permute-start.4 = (bf16[2,7168]{1,0:T(2,128)(2,1)S(1)}, bf16[2,7168]{1,0:T(2,128)(2,1)S(1)}, u32[]{:S(2)}, u32[]{:S(2)}) collective-permute-start(bf16[2,7168]{1,0:T(2,128)(2,1)S(1)} %project.1), channel_id=1, source_target_pairs={{0,128},{4,132},{8,136},{12,140},{16,144},{20,148},{24,152},{28,15... | collective-permute-start | bytes 86024 | tf_op jit(solution)/shard_map/ppermute | solution.py:23
  58.8 3.9 %collective-permute-start.3 = (bf16[2,7168]{1,0:T(2,128)(2,1)S(1)}, bf16[2,7168]{1,0:T(2,128)(2,1)S(1)}, u32[]{:S(2)}, u32[]{:S(2)}) collective-permute-start(bf16[2,7168]{1,0:T(2,128)(2,1)S(1)} %project.1), channel_id=1, source_target_pairs={{0,64},{4,68},{8,72},{12,76},{16,80},{20,84},{24,88},{28,92},{32,9... | collective-permute-start | bytes 86024 | tf_op jit(solution)/shard_map/ppermute | solution.py:23
  62.7 5.2 %collective-permute-start.8 = (bf16[2,7168]{1,0:T(2,128)(2,1)S(1)}, bf16[2,7168]{1,0:T(2,128)(2,1)S(1)}, u32[]{:S(2)}, u32[]{:S(2)}) collective-permute-start(bf16[2,7168]{1,0:T(2,128)(2,1)S(1)} %add_convert_fusion.2), channel_id=1, source_target_pairs={{0,48},{4,52},{8,56},{12,60},{16,32},{20,36},{24,40},{28,44},{32,1... | collective-permute-start | bytes 86024 | tf_op jit(solution)/shard_map/ppermute | solution.py:23
  63.3 5.4 %collective-permute-start.7 = (bf16[2,7168]{1,0:T(2,128)(2,1)S(1)}, bf16[2,7168]{1,0:T(2,128)(2,1)S(1)}, u32[]{:S(2)}, u32[]{:S(2)}) collective-permute-start(bf16[2,7168]{1,0:T(2,128)(2,1)S(1)} %add_convert_fusion.2), channel_id=1, source_target_pairs={{0,32},{4,36},{8,40},{12,44},{16,48},{20,52},{24,56},{28,60},{32,0... | collective-permute-start | bytes 86024 | tf_op jit(solution)/shard_map/ppermute | solution.py:23
  65.4 3.9 %collective-permute-start.6 = (bf16[2,7168]{1,0:T(2,128)(2,1)S(1)}, bf16[2,7168]{1,0:T(2,128)(2,1)S(1)}, u32[]{:S(2)}, u32[]{:S(2)}) collective-permute-start(bf16[2,7168]{1,0:T(2,128)(2,1)S(1)} %add_convert_fusion.2), channel_id=1, source_target_pairs={{0,16},{4,20},{8,24},{12,28},{16,0},{20,4},{24,8},{28,12},{32,48},... | collective-permute-start | bytes 86024 | tf_op jit(solution)/shard_map/ppermute | solution.py:23
  69.3 6.6 %collective-permute-start.11 = (bf16[2,7168]{1,0:T(2,128)(2,1)S(1)}, bf16[2,7168]{1,0:T(2,128)(2,1)S(1)}, u32[]{:S(2)}, u32[]{:S(2)}) collective-permute-start(bf16[2,7168]{1,0:T(2,128)(2,1)S(1)} %add_convert_fusion.1), channel_id=1, source_target_pairs={{0,12},{4,8},{8,4},{12,0},{16,28},{20,24},{24,20},{28,16},{32,44},... | collective-permute-start | bytes 86024 | tf_op jit(solution)/shard_map/ppermute | solution.py:23
  70.3 7.8 %collective-permute-start.10 = (bf16[2,7168]{1,0:T(2,128)(2,1)S(1)}, bf16[2,7168]{1,0:T(2,128)(2,1)S(1)}, u32[]{:S(2)}, u32[]{:S(2)}) collective-permute-start(bf16[2,7168]{1,0:T(2,128)(2,1)S(1)} %add_convert_fusion.1), channel_id=1, source_target_pairs={{0,8},{4,12},{8,0},{12,4},{16,24},{20,28},{24,16},{28,20},{32,40},... | collective-permute-start | bytes 86024 | tf_op jit(solution)/shard_map/ppermute | solution.py:23
  73.5 5.1 %collective-permute-start.9 = (bf16[2,7168]{1,0:T(2,128)(2,1)S(1)}, bf16[2,7168]{1,0:T(2,128)(2,1)S(1)}, u32[]{:S(2)}, u32[]{:S(2)}) collective-permute-start(bf16[2,7168]{1,0:T(2,128)(2,1)S(1)} %add_convert_fusion.1), channel_id=1, source_target_pairs={{0,4},{4,0},{8,12},{12,8},{16,20},{20,16},{24,28},{28,24},{32,36},... | collective-permute-start | bytes 86024 | tf_op jit(solution)/shard_map/ppermute | solution.py:23

commit v8 on v5

--- a/solution.py
+++ b/solution.py
@@ -48,15 +48,12 @@
 
 def fetch_kernel(
     page_len, here_ref, lengths_hbm, table_hbm, cache_hbm, w_uv_hbm, w_out_hbm,
-    live_ref, keys_ref, w_uv_ref, *rest,
+    live_ref, keys_ref, w_uv_ref, w_out_ref, lengths_ref, table_ref, sems,
 ):
-    *w_out_refs, lengths_ref, table_ref, sems = rest
-    columns = w_out_refs[0].shape[1]
     pairs = [
         (lengths_hbm, lengths_ref), (table_hbm, table_ref), (cache_hbm, keys_ref), (w_uv_hbm, w_uv_ref),
+        (w_out_hbm.at[:, : w_out_ref.shape[1]], w_out_ref),
     ]
-    for k, ref in enumerate(w_out_refs):
-        pairs.append((w_out_hbm.at[:, k * columns : (k + 1) * columns], ref))
     copies = [pltpu.make_async_copy(a, b, sems.at[k]) for k, (a, b) in enumerate(pairs)]
     for copy in copies:
         copy.start()
@@ -110,8 +107,10 @@
     state_ref[:, side:] = stats.astype(BF16)
 
 
-def project_kernel(rows, heads, latent, state_ref, w_uv_ref, *rest):
-    *w_out_refs, term_ref = rest
+def project_kernel(rows, heads, latent, state_ref, w_uv_ref, first_ref, w_out_hbm, term_ref, second_ref, sem):
+    split = first_ref.shape[1]
+    copy = pltpu.make_async_copy(w_out_hbm.at[:, split:], second_ref, sem)
+    copy.start()
     count = state_ref.shape[0]
     mixed = rows * heads
     side = heads * latent
@@ -143,11 +142,9 @@
         ],
         axis=0,
     ).astype(BF16)
-    columns = w_out_refs[0].shape[1]
-    for k, ref in enumerate(w_out_refs):
-        term_ref[:, k * columns : (k + 1) * columns] = jnp.dot(
-            flat, ref[...], preferred_element_type=F32
-        ).astype(term_ref.dtype)
+    term_ref[:, :split] = jnp.dot(flat, first_ref[...], preferred_element_type=F32).astype(term_ref.dtype)
+    copy.wait()
+    term_ref[:, split:] = jnp.dot(flat, second_ref[...], preferred_element_type=F32).astype(term_ref.dtype)
 
 
 def local(q_latent, q_rope, latent_cache, page_table, lengths, w_uv, w_out):
@@ -177,22 +174,22 @@
 
     near = 4
     others = [lax.ppermute(message, CTX, xor_pairs(count, k)) for k in range(1, near)]
-    parts = w_out.shape[1] // 1024
-    live, keys, w_uv, *w_outs = pl.pallas_call(
+    split = w_out.shape[1] // 2 // LANES * LANES
+    live, keys, w_uv, w_first = pl.pallas_call(
         functools.partial(fetch_kernel, page_len),
         out_shape=(
             pltpu.VMEM((rows, tokens), F32),
             pltpu.VMEM((tokens, width), BF16),
             pltpu.VMEM(w_uv.shape, BF16),
-            *[pltpu.VMEM((w_out.shape[0], w_out.shape[1] // parts), BF16) for _ in range(parts)],
+            pltpu.VMEM((w_out.shape[0], split), BF16),
         ),
         in_specs=[smem, hbm, hbm, hbm, hbm, hbm],
-        out_specs=(vmem,) * (3 + parts),
+        out_specs=(vmem, vmem, vmem, vmem),
         scratch_shapes=[
-            pltpu.SMEM(lengths.shape, jnp.int32), pltpu.VMEM(page_table.shape, jnp.int32), dma((4 + parts,)),
+            pltpu.SMEM(lengths.shape, jnp.int32), pltpu.VMEM(page_table.shape, jnp.int32), dma((5,)),
         ],
         compiler_params=params,
-        cost_estimate=pl.CostEstimate(flops=0, bytes_accessed=9 << 20, transcendentals=0),
+        cost_estimate=pl.CostEstimate(flops=0, bytes_accessed=5 << 20, transcendentals=0),
         name="fetch",
     )(
         here.reshape(1), stay(lengths), stay(page_table), stay(latent_cache.reshape(tokens, width)),
@@ -202,6 +199,7 @@
     column = jnp.broadcast_to(message[None], (near, rows, size))
     for k in range(1, near):
         column = jnp.where(away == k, others[k - 1][None], column)
+    column, live, keys, w_uv, w_first = lax.optimization_barrier((column, live, keys, w_uv, w_first))
     planes = [[i * near + k for i in range(count // near)] for k in range(near)]
     query = lax.all_to_all(
         jnp.broadcast_to(column[None], (count // near, near, rows, size)),
@@ -224,11 +222,12 @@
     term = pl.pallas_call(
         functools.partial(project_kernel, rows, heads, latent),
         out_shape=jax.ShapeDtypeStruct((rows, w_out.shape[1]), BF16),
-        in_specs=[vmem] * (2 + parts),
+        in_specs=[vmem, vmem, vmem, hbm],
         out_specs=vmem,
+        scratch_shapes=[pltpu.VMEM((w_out.shape[0], w_out.shape[1] - split), BF16), dma],
         compiler_params=params,
         name="project",
-    )(state.reshape(count * rows, state_size), w_uv, *w_outs)
+    )(state.reshape(count * rows, state_size), w_uv, w_first, stay(w_out))
     for low in (4, 2, 0):
         term = sum_of_four(term, count, low).astype(BF16)
     return term

time: 82.7 us -> 78.2 us (0.946)
  blocking collectives: 20.5 us -> 34.2 us
  local copies, waits for them, and re-layouts: 8.36 us -> 0.49 us
  starting transfers between devices: 31.1 us -> 23.7 us
  waiting for transfers between devices: 15.7 us -> 12.3 us
    all_to_all x0 -> x1, blocking collectives: none -> 14.2 us  [local(): lax.all_to_all(jnp.broadcast_to(column[None], (count // near, near, rows,...]
    all_to_all x1 -> x0, starting transfers between devices: 7.48 us -> none  [local(): lax.all_to_all(jnp.broadcast_to(column[None], (count // near, near, rows,...]
    unnamed x16 -> x0, local copies, waits for them, and re-layouts: 7.15 us -> none
    ppermute x3, waiting for transfers between devices: 5.69 us -> 3.83 us  [local(): lax.ppermute(message, CTX, xor_pairs(count, k))]
    all_to_all x1 -> x0, waiting for transfers between devices: 1.42 us -> none  [local(): lax.all_to_all(jnp.broadcast_to(column[None], (count // near, near, rows,...]
    pallas_call x1, Pallas kernels: 1.2 us -> 2.37 us  [local(): pl.pallas_call(functools.partial(project_kernel, rows, heads, latent), ou...]
  transfers between devices with their start and end apart: 13 -> 12, of which waited for: 10 -> 9; matrix products, arithmetic and copies ran while one was open for 0% -> 0% of each run, Pallas kernels for 3% -> 2%
where the time goes in v8:
time: 78.2 us; the launch traced here: 77.9 us
  blocking collectives  34.2 us (44%)
  starting transfers between devices  23.7 us (30%)
  waiting for transfers between devices  12.3 us (16%)
  Pallas kernels  6.15 us (8%)
  other arithmetic  0.91 us (1%)
    all_to_all x1, blocking collectives, local(): lax.all_to_all(state.reshape(count, rows, state_size), CTX, split_axis=0,...  20.1 us
    ppermute x9, starting transfers between devices, sum_of_four(): lax.ppermute(x, CTX, xor_pairs(count, k << low))  14.9 us
    all_to_all x1, blocking collectives, local(): lax.all_to_all(jnp.broadcast_to(column[None], (count // near, near, rows,...  14.2 us
    ppermute x3, starting transfers between devices, local(): lax.ppermute(message, CTX, xor_pairs(count, k))  8.75 us
    ppermute x9, waiting for transfers between devices, sum_of_four(): lax.ppermute(x, CTX, xor_pairs(count, k << low))  8.46 us
    ppermute x3, waiting for transfers between devices, local(): lax.ppermute(message, CTX, xor_pairs(count, k))  3.83 us
    pallas_call x1, Pallas kernels, local(): pl.pallas_call(functools.partial(project_kernel, rows, heads, latent), ou...  2.37 us
    pallas_call x1, Pallas kernels, local(): pl.pallas_call(functools.partial(fetch_kernel, page_len), out_shape=(pltp...  1.85 us
  transfers between devices with their start and end apart: 12, of which 9 were waited for; matrix products, arithmetic and copies ran while one was open for 0% of the time, Pallas kernels for 2%

profile of v8, /device:TPU:2, one launch (start us, length us, event | category | flops | bytes accessed | tf_op | source)
XLA Modules:
  0.0 77.9 jit_solution(11934278753781524550)
XLA Ops:
  0.0 0.8 %message.1 = bf16[2,1152]{1,0:T(2,128)(2,1)S(1)} custom-call(bf16[2,2,512]{2,1,0:T(2,128)(2,1)} %q_latent_hbm.1, bf16[2,2,64]{2,1,0:T(2,128)(2,1)} %q_rope_hbm.1), custom_call_target="tpu_custom_call" | custom-call | tf_op jit(solution)/shard_map/message/pallas_call | solution.py:165
  0.8 3.4 %collective-permute-start.2 = (bf16[2,1152]{1,0:T(2,128)(2,1)S(1)}, bf16[2,1152]{1,0:T(2,128)(2,1)S(1)}, u32[]{:S(2)}, u32[]{:S(2)}) collective-permute-start(bf16[2,1152]{1,0:T(2,128)(2,1)S(1)} %message.1), channel_id=1, source_target_pairs={{0,4},{4,0},{8,12},{12,8},{16,20},{20,16},{24,28},{28,24},{32,36},... | collective-permute-start | bytes 13832 | tf_op jit(solution)/shard_map/ppermute | solution.py:176
  4.2 5.4 %collective-permute-start.1 = (bf16[2,1152]{1,0:T(2,128)(2,1)S(1)}, bf16[2,1152]{1,0:T(2,128)(2,1)S(1)}, u32[]{:S(2)}, u32[]{:S(2)}) collective-permute-start(bf16[2,1152]{1,0:T(2,128)(2,1)S(1)} %message.1), channel_id=1, source_target_pairs={{0,8},{4,12},{8,0},{12,4},{16,24},{20,28},{24,16},{28,20},{32,40},... | collective-permute-start | bytes 13832 | tf_op jit(solution)/shard_map/ppermute | solution.py:176
  9.6 0.0 collective-permute-start
  9.6 1.9 %fetch.1 = (f32[2,512]{1,0:T(2,128)S(1)}, bf16[512,576]{1,0:T(8,128)(2,1)S(1)}, bf16[2,512,128]{2,1,0:T(8,128)(2,1)S(1)}, bf16[256,3584]{1,0:T(8,128)(2,1)S(1)}) custom-call(s32[1]{0:T(128)} %bitcast.here_ref, s32[2]{0:T(128)} %lengths_hbm.1, s32[2,256]{1,0:T(2,128)} %table_hbm.1, bf16[512,576]{1,0:T(8,128)(2,1)} %bitcast.2, bf16[2,512,128]{2,1,0:T(8,128)(2,1)} %w_uv_hbm.1, ...), custom_call_target="tpu_custom_call" | custom-call | bytes 5242880 | tf_op jit(solution)/shard_map/fetch/pallas_call | solution.py:178
  11.4 0.0 collective-permute-done.2
  11.4 0.2 collective-permute-done.1
  11.7 3.6 %collective-permute-done = bf16[2,1152]{1,0:T(2,128)(2,1)S(1)} collective-permute-done((bf16[2,1152]{1,0:T(2,128)(2,1)S(1)}, bf16[2,1152]{1,0:T(2,128)(2,1)S(1)}, u32[]{:S(2)}, u32[]{:S(2)}) %collective-permute-start) | collective-permute-done | bytes 4640 | tf_op jit(solution)/shard_map/ppermute | solution.py:176
  15.3 0.1 broadcast_select_fusion.1
  15.4 0.2 broadcast_in_dim.58
  15.5 14.2 %all_to_all.10 = bf16[16,4,2,1152]{3,2,1,0:T(2,128)(2,1)S(1)} all-to-all(bf16[16,4,2,1152]{3,2,1,0:T(2,128)(2,1)S(1)} %broadcast_in_dim.58), channel_id=1, replica_groups={{0,16,32,48,64,80,96,112,128,144,160,176,192,208,224,240},{4,20,36,52,6..., dimensions={0} | all-to-all | bytes 589824 | tf_op jit(solution)/shard_map/all_to_all | solution.py:204
  29.7 0.1 reshape.35.q_ref
  29.8 1.1 %attend.1 = bf16[128,1152]{1,0:T(8,128)(2,1)S(1)} custom-call(bf16[128,1152]{1,0:T(8,128)(2,1)S(1)} %reshape.35.q_ref, bf16[512,576]{1,0:T(8,128)(2,1)S(1)} %get-tuple-element.19.keys_ref, f32[2,512]{1,0:T(2,128)S(1)} %get-tuple-element.20.live_ref), custom_call_target="tpu_custom_call" | custom-call | tf_op jit(solution)/shard_map/attend/pallas_call | solution.py:210
  31.0 0.1 reshape.36
  31.1 20.1 %all_to_all.11 = bf16[64,2,1152]{2,1,0:T(2,128)(2,1)S(1)} all-to-all(bf16[64,2,1152]{2,1,0:T(2,128)(2,1)S(1)} %reshape.36), channel_id=1, replica_groups=mesh['ctx'=64,'grp'=4] {'ctx'}, dimensions={0} | all-to-all | bytes 589824 | tf_op jit(solution)/shard_map/all_to_all | solution.py:219
  51.2 0.1 reshape.37.state_ref
  51.3 2.4 %project.1 = bf16[2,7168]{1,0:T(2,128)(2,1)S(1)} custom-call(bf16[128,1152]{1,0:T(8,128)(2,1)S(1)} %reshape.37.state_ref, bf16[2,512,128]{2,1,0:T(8,128)(2,1)S(1)} %get-tuple-element.21.w_uv_ref, bf16[256,3584]{1,0:T(8,128)(2,1)S(1)} %get-tuple-element.22.first_ref, bf16[256,7168]{1,0:T(8,128)(2,1)} %w_out_hbm.3), custom_call_target="tpu_custom_call" | custom-call | tf_op jit(solution)/shard_map/project/pallas_call | solution.py:222
  53.6 0.1 collective-permute-start.5
  53.8 3.5 %collective-permute-start.4 = (bf16[2,7168]{1,0:T(2,128)(2,1)S(1)}, bf16[2,7168]{1,0:T(2,128)(2,1)S(1)}, u32[]{:S(2)}, u32[]{:S(2)}) collective-permute-start(bf16[2,7168]{1,0:T(2,128)(2,1)S(1)} %project.1), channel_id=1, source_target_pairs={{0,128},{4,132},{8,136},{12,140},{16,144},{20,148},{24,152},{28,15... | collective-permute-start | bytes 86024 | tf_op jit(solution)/shard_map/ppermute | solution.py:23
  57.3 0.5 collective-permute-start.3
  57.8 0.0 collective-permute-done.5
  57.8 1.4 %collective-permute-done.4 = bf16[2,7168]{1,0:T(2,128)(2,1)S(1)} collective-permute-done((bf16[2,7168]{1,0:T(2,128)(2,1)S(1)}, bf16[2,7168]{1,0:T(2,128)(2,1)S(1)}, u32[]{:S(2)}, u32[]{:S(2)}) %collective-permute-start.4) | collective-permute-done | bytes 28704 | tf_op jit(solution)/shard_map/ppermute | solution.py:23
  59.2 2.0 %collective-permute-done.3 = bf16[2,7168]{1,0:T(2,128)(2,1)S(1)} collective-permute-done((bf16[2,7168]{1,0:T(2,128)(2,1)S(1)}, bf16[2,7168]{1,0:T(2,128)(2,1)S(1)}, u32[]{:S(2)}, u32[]{:S(2)}) %collective-permute-start.3) | collective-permute-done | bytes 28704 | tf_op jit(solution)/shard_map/ppermute | solution.py:23
  61.2 0.1 add_convert_fusion.2
  61.2 0.6 collective-permute-start.8
  61.8 2.1 %collective-permute-start.7 = (bf16[2,7168]{1,0:T(2,128)(2,1)S(1)}, bf16[2,7168]{1,0:T(2,128)(2,1)S(1)}, u32[]{:S(2)}, u32[]{:S(2)}) collective-permute-start(bf16[2,7168]{1,0:T(2,128)(2,1)S(1)} %add_convert_fusion.2), channel_id=1, source_target_pairs={{0,32},{4,36},{8,40},{12,44},{16,48},{20,52},{24,56},{28,60},{32,0... | collective-permute-start | bytes 86024 | tf_op jit(solution)/shard_map/ppermute | solution.py:23
  64.0 1.4 %collective-permute-start.6 = (bf16[2,7168]{1,0:T(2,128)(2,1)S(1)}, bf16[2,7168]{1,0:T(2,128)(2,1)S(1)}, u32[]{:S(2)}, u32[]{:S(2)}) collective-permute-start(bf16[2,7168]{1,0:T(2,128)(2,1)S(1)} %add_convert_fusion.2), channel_id=1, source_target_pairs={{0,16},{4,20},{8,24},{12,28},{16,0},{20,4},{24,8},{28,12},{32,48},... | collective-permute-start | bytes 86024 | tf_op jit(solution)/shard_map/ppermute | solution.py:23
  65.4 1.0 %collective-permute-done.8 = bf16[2,7168]{1,0:T(2,128)(2,1)S(1)} collective-permute-done((bf16[2,7168]{1,0:T(2,128)(2,1)S(1)}, bf16[2,7168]{1,0:T(2,128)(2,1)S(1)}, u32[]{:S(2)}, u32[]{:S(2)}) %collective-permute-start.8) | collective-permute-done | bytes 28704 | tf_op jit(solution)/shard_map/ppermute | solution.py:23
  66.4 0.8 %collective-permute-done.7 = bf16[2,7168]{1,0:T(2,128)(2,1)S(1)} collective-permute-done((bf16[2,7168]{1,0:T(2,128)(2,1)S(1)}, bf16[2,7168]{1,0:T(2,128)(2,1)S(1)}, u32[]{:S(2)}, u32[]{:S(2)}) %collective-permute-start.7) | collective-permute-done | bytes 28704 | tf_op jit(solution)/shard_map/ppermute | solution.py:23
  67.2 0.6 collective-permute-done.6
  67.8 0.1 add_convert_fusion.1
  67.9 1.0 %collective-permute-start.11 = (bf16[2,7168]{1,0:T(2,128)(2,1)S(1)}, bf16[2,7168]{1,0:T(2,128)(2,1)S(1)}, u32[]{:S(2)}, u32[]{:S(2)}) collective-permute-start(bf16[2,7168]{1,0:T(2,128)(2,1)S(1)} %add_convert_fusion.1), channel_id=1, source_target_pairs={{0,12},{4,8},{8,4},{12,0},{16,28},{20,24},{24,20},{28,16},{32,44},... | collective-permute-start | bytes 86024 | tf_op jit(solution)/shard_map/ppermute | solution.py:23
  68.9 3.2 %collective-permute-start.10 = (bf16[2,7168]{1,0:T(2,128)(2,1)S(1)}, bf16[2,7168]{1,0:T(2,128)(2,1)S(1)}, u32[]{:S(2)}, u32[]{:S(2)}) collective-permute-start(bf16[2,7168]{1,0:T(2,128)(2,1)S(1)} %add_convert_fusion.1), channel_id=1, source_target_pairs={{0,8},{4,12},{8,0},{12,4},{16,24},{20,28},{24,16},{28,20},{32,40},... | collective-permute-start | bytes 86024 | tf_op jit(solution)/shard_map/ppermute | solution.py:23
  72.1 2.4 %collective-permute-start.9 = (bf16[2,7168]{1,0:T(2,128)(2,1)S(1)}, bf16[2,7168]{1,0:T(2,128)(2,1)S(1)}, u32[]{:S(2)}, u32[]{:S(2)}) collective-permute-start(bf16[2,7168]{1,0:T(2,128)(2,1)S(1)} %add_convert_fusion.1), channel_id=1, source_target_pairs={{0,4},{4,0},{8,12},{12,8},{16,20},{20,16},{24,28},{28,24},{32,36},... | collective-permute-start | bytes 86024 | tf_op jit(solution)/shard_map/ppermute | solution.py:23
  74.5 0.0 collective-permute-done.11
  74.5 2.2 %collective-permute-done.10 = bf16[2,7168]{1,0:T(2,128)(2,1)S(1)} collective-permute-done((bf16[2,7168]{1,0:T(2,128)(2,1)S(1)}, bf16[2,7168]{1,0:T(2,128)(2,1)S(1)}, u32[]{:S(2)}, u32[]{:S(2)}) %collective-permute-start.10) | collective-permute-done | bytes 28704 | tf_op jit(solution)/shard_map/ppermute | solution.py:23
  76.7 0.5 collective-permute-done.9
  77.2 0.7 add_convert_fusion
  (2 shorter events, 0.0 us)
Async XLA Ops:
  0.8 10.6 %collective-permute-start.2 = (bf16[2,1152]{1,0:T(2,128)(2,1)S(1)}, bf16[2,1152]{1,0:T(2,128)(2,1)S(1)}, u32[]{:S(2)}, u32[]{:S(2)}) collective-permute-start(bf16[2,1152]{1,0:T(2,128)(2,1)S(1)} %message.1), channel_id=1, source_target_pairs={{0,4},{4,0},{8,12},{12,8},{16,20},{20,16},{24,28},{28,24},{32,36},... | collective-permute-start | bytes 13832 | tf_op jit(solution)/shard_map/ppermute | solution.py:176
  4.2 7.5 %collective-permute-start.1 = (bf16[2,1152]{1,0:T(2,128)(2,1)S(1)}, bf16[2,1152]{1,0:T(2,128)(2,1)S(1)}, u32[]{:S(2)}, u32[]{:S(2)}) collective-permute-start(bf16[2,1152]{1,0:T(2,128)(2,1)S(1)} %message.1), channel_id=1, source_target_pairs={{0,8},{4,12},{8,0},{12,4},{16,24},{20,28},{24,16},{28,20},{32,40},... | collective-permute-start | bytes 13832 | tf_op jit(solution)/shard_map/ppermute | solution.py:176
  9.6 5.7 %collective-permute-start = (bf16[2,1152]{1,0:T(2,128)(2,1)S(1)}, bf16[2,1152]{1,0:T(2,128)(2,1)S(1)}, u32[]{:S(2)}, u32[]{:S(2)}) collective-permute-start(bf16[2,1152]{1,0:T(2,128)(2,1)S(1)} %message.1), channel_id=1, source_target_pairs={{0,12},{4,8},{8,4},{12,0},{16,28},{20,24},{24,20},{28,16},{32,44},... | collective-permute-start | bytes 13832 | tf_op jit(solution)/shard_map/ppermute | solution.py:176
  53.6 4.2 %collective-permute-start.5 = (bf16[2,7168]{1,0:T(2,128)(2,1)S(1)}, bf16[2,7168]{1,0:T(2,128)(2,1)S(1)}, u32[]{:S(2)}, u32[]{:S(2)}) collective-permute-start(bf16[2,7168]{1,0:T(2,128)(2,1)S(1)} %project.1), channel_id=1, source_target_pairs={{0,192},{4,196},{8,200},{12,204},{16,208},{20,212},{24,216},{28,22... | collective-permute-start | bytes 86024 | tf_op jit(solution)/shard_map/ppermute | solution.py:23
  53.8 5.4 %collective-permute-start.4 = (bf16[2,7168]{1,0:T(2,128)(2,1)S(1)}, bf16[2,7168]{1,0:T(2,128)(2,1)S(1)}, u32[]{:S(2)}, u32[]{:S(2)}) collective-permute-start(bf16[2,7168]{1,0:T(2,128)(2,1)S(1)} %project.1), channel_id=1, source_target_pairs={{0,128},{4,132},{8,136},{12,140},{16,144},{20,148},{24,152},{28,15... | collective-permute-start | bytes 86024 | tf_op jit(solution)/shard_map/ppermute | solution.py:23
  57.3 3.9 %collective-permute-start.3 = (bf16[2,7168]{1,0:T(2,128)(2,1)S(1)}, bf16[2,7168]{1,0:T(2,128)(2,1)S(1)}, u32[]{:S(2)}, u32[]{:S(2)}) collective-permute-start(bf16[2,7168]{1,0:T(2,128)(2,1)S(1)} %project.1), channel_id=1, source_target_pairs={{0,64},{4,68},{8,72},{12,76},{16,80},{20,84},{24,88},{28,92},{32,9... | collective-permute-start | bytes 86024 | tf_op jit(solution)/shard_map/ppermute | solution.py:23
  61.2 5.2 %collective-permute-start.8 = (bf16[2,7168]{1,0:T(2,128)(2,1)S(1)}, bf16[2,7168]{1,0:T(2,128)(2,1)S(1)}, u32[]{:S(2)}, u32[]{:S(2)}) collective-permute-start(bf16[2,7168]{1,0:T(2,128)(2,1)S(1)} %add_convert_fusion.2), channel_id=1, source_target_pairs={{0,48},{4,52},{8,56},{12,60},{16,32},{20,36},{24,40},{28,44},{32,1... | collective-permute-start | bytes 86024 | tf_op jit(solution)/shard_map/ppermute | solution.py:23
  61.8 5.4 %collective-permute-start.7 = (bf16[2,7168]{1,0:T(2,128)(2,1)S(1)}, bf16[2,7168]{1,0:T(2,128)(2,1)S(1)}, u32[]{:S(2)}, u32[]{:S(2)}) collective-permute-start(bf16[2,7168]{1,0:T(2,128)(2,1)S(1)} %add_convert_fusion.2), channel_id=1, source_target_pairs={{0,32},{4,36},{8,40},{12,44},{16,48},{20,52},{24,56},{28,60},{32,0... | collective-permute-start | bytes 86024 | tf_op jit(solution)/shard_map/ppermute | solution.py:23
  64.0 3.9 %collective-permute-start.6 = (bf16[2,7168]{1,0:T(2,128)(2,1)S(1)}, bf16[2,7168]{1,0:T(2,128)(2,1)S(1)}, u32[]{:S(2)}, u32[]{:S(2)}) collective-permute-start(bf16[2,7168]{1,0:T(2,128)(2,1)S(1)} %add_convert_fusion.2), channel_id=1, source_target_pairs={{0,16},{4,20},{8,24},{12,28},{16,0},{20,4},{24,8},{28,12},{32,48},... | collective-permute-start | bytes 86024 | tf_op jit(solution)/shard_map/ppermute | solution.py:23
  67.9 6.6 %collective-permute-start.11 = (bf16[2,7168]{1,0:T(2,128)(2,1)S(1)}, bf16[2,7168]{1,0:T(2,128)(2,1)S(1)}, u32[]{:S(2)}, u32[]{:S(2)}) collective-permute-start(bf16[2,7168]{1,0:T(2,128)(2,1)S(1)} %add_convert_fusion.1), channel_id=1, source_target_pairs={{0,12},{4,8},{8,4},{12,0},{16,28},{20,24},{24,20},{28,16},{32,44},... | collective-permute-start | bytes 86024 | tf_op jit(solution)/shard_map/ppermute | solution.py:23
  68.9 7.8 %collective-permute-start.10 = (bf16[2,7168]{1,0:T(2,128)(2,1)S(1)}, bf16[2,7168]{1,0:T(2,128)(2,1)S(1)}, u32[]{:S(2)}, u32[]{:S(2)}) collective-permute-start(bf16[2,7168]{1,0:T(2,128)(2,1)S(1)} %add_convert_fusion.1), channel_id=1, source_target_pairs={{0,8},{4,12},{8,0},{12,4},{16,24},{20,28},{24,16},{28,20},{32,40},... | collective-permute-start | bytes 86024 | tf_op jit(solution)/shard_map/ppermute | solution.py:23
  72.1 5.1 %collective-permute-start.9 = (bf16[2,7168]{1,0:T(2,128)(2,1)S(1)}, bf16[2,7168]{1,0:T(2,128)(2,1)S(1)}, u32[]{:S(2)}, u32[]{:S(2)}) collective-permute-start(bf16[2,7168]{1,0:T(2,128)(2,1)S(1)} %add_convert_fusion.1), channel_id=1, source_target_pairs={{0,4},{4,0},{8,12},{12,8},{16,20},{20,16},{24,28},{28,24},{32,36},... | collective-permute-start | bytes 86024 | tf_op jit(solution)/shard_map/ppermute | solution.py:23

commit v9 on v8

--- a/solution.py
+++ b/solution.py
@@ -107,10 +107,17 @@
     state_ref[:, side:] = stats.astype(BF16)
 
 
-def project_kernel(rows, heads, latent, state_ref, w_uv_ref, first_ref, w_out_hbm, term_ref, second_ref, sem):
+def project_kernel(rows, heads, latent, state_ref, w_uv_ref, first_ref, w_out_hbm, term_ref, second_ref, sems):
     split = first_ref.shape[1]
-    copy = pltpu.make_async_copy(w_out_hbm.at[:, split:], second_ref, sem)
-    copy.start()
+    parts, _, step = second_ref.shape
+    copies = [
+        pltpu.make_async_copy(
+            w_out_hbm.at[:, split + k * step : split + (k + 1) * step], second_ref.at[k], sems.at[k]
+        )
+        for k in range(parts)
+    ]
+    for copy in copies:
+        copy.start()
     count = state_ref.shape[0]
     mixed = rows * heads
     side = heads * latent
@@ -143,8 +150,11 @@
         axis=0,
     ).astype(BF16)
     term_ref[:, :split] = jnp.dot(flat, first_ref[...], preferred_element_type=F32).astype(term_ref.dtype)
-    copy.wait()
-    term_ref[:, split:] = jnp.dot(flat, second_ref[...], preferred_element_type=F32).astype(term_ref.dtype)
+    for k, copy in enumerate(copies):
+        copy.wait()
+        term_ref[:, split + k * step : split + (k + 1) * step] = jnp.dot(
+            flat, second_ref[k], preferred_element_type=F32
+        ).astype(term_ref.dtype)
 
 
 def local(q_latent, q_rope, latent_cache, page_table, lengths, w_uv, w_out):
@@ -219,12 +229,13 @@
     state = lax.all_to_all(
         state.reshape(count, rows, state_size), CTX, split_axis=0, concat_axis=0, tiled=True
     )
+    parts = 4
     term = pl.pallas_call(
         functools.partial(project_kernel, rows, heads, latent),
         out_shape=jax.ShapeDtypeStruct((rows, w_out.shape[1]), BF16),
         in_specs=[vmem, vmem, vmem, hbm],
         out_specs=vmem,
-        scratch_shapes=[pltpu.VMEM((w_out.shape[0], w_out.shape[1] - split), BF16), dma],
+        scratch_shapes=[pltpu.VMEM((parts, w_out.shape[0], (w_out.shape[1] - split) // parts), BF16), dma((parts,))],
         compiler_params=params,
         name="project",
     )(state.reshape(count * rows, state_size), w_uv, w_first, stay(w_out))

time: 78.2 us -> 78.1 us (level)
  no operation moved by 1% of the time
where the time goes in v9:
time: 78.1 us; the launch traced here: 77.8 us
  blocking collectives  34.2 us (44%)
  starting transfers between devices  23.7 us (30%)
  waiting for transfers between devices  12.3 us (16%)
  Pallas kernels  6.09 us (8%)
  other arithmetic  0.91 us (1%)
    all_to_all x1, blocking collectives, local(): lax.all_to_all(state.reshape(count, rows, state_size), CTX, split_axis=0,...  20.1 us
    ppermute x9, starting transfers between devices, sum_of_four(): lax.ppermute(x, CTX, xor_pairs(count, k << low))  14.9 us
    all_to_all x1, blocking collectives, local(): lax.all_to_all(jnp.broadcast_to(column[None], (count // near, near, rows,...  14.2 us
    ppermute x3, starting transfers between devices, local(): lax.ppermute(message, CTX, xor_pairs(count, k))  8.75 us
    ppermute x9, waiting for transfers between devices, sum_of_four(): lax.ppermute(x, CTX, xor_pairs(count, k << low))  8.46 us
    ppermute x3, waiting for transfers between devices, local(): lax.ppermute(message, CTX, xor_pairs(count, k))  3.83 us
    pallas_call x1, Pallas kernels, local(): pl.pallas_call(functools.partial(project_kernel, rows, heads, latent), ou...  2.31 us
    pallas_call x1, Pallas kernels, local(): pl.pallas_call(functools.partial(fetch_kernel, page_len), out_shape=(pltp...  1.85 us
  transfers between devices with their start and end apart: 12, of which 9 were waited for; matrix products, arithmetic and copies ran while one was open for 0% of the time, Pallas kernels for 2%

profile of v9, /device:TPU:2, one launch (start us, length us, event | category | flops | bytes accessed | tf_op | source)
XLA Modules:
  0.0 77.8 jit_solution(14597647579863938878)
XLA Ops:
  0.0 0.8 %message.1 = bf16[2,1152]{1,0:T(2,128)(2,1)S(1)} custom-call(bf16[2,2,512]{2,1,0:T(2,128)(2,1)} %q_latent_hbm.1, bf16[2,2,64]{2,1,0:T(2,128)(2,1)} %q_rope_hbm.1), custom_call_target="tpu_custom_call" | custom-call | tf_op jit(solution)/shard_map/message/pallas_call | solution.py:175
  0.8 3.4 %collective-permute-start.2 = (bf16[2,1152]{1,0:T(2,128)(2,1)S(1)}, bf16[2,1152]{1,0:T(2,128)(2,1)S(1)}, u32[]{:S(2)}, u32[]{:S(2)}) collective-permute-start(bf16[2,1152]{1,0:T(2,128)(2,1)S(1)} %message.1), channel_id=1, source_target_pairs={{0,4},{4,0},{8,12},{12,8},{16,20},{20,16},{24,28},{28,24},{32,36},... | collective-permute-start | bytes 13832 | tf_op jit(solution)/shard_map/ppermute | solution.py:186
  4.2 5.4 %collective-permute-start.1 = (bf16[2,1152]{1,0:T(2,128)(2,1)S(1)}, bf16[2,1152]{1,0:T(2,128)(2,1)S(1)}, u32[]{:S(2)}, u32[]{:S(2)}) collective-permute-start(bf16[2,1152]{1,0:T(2,128)(2,1)S(1)} %message.1), channel_id=1, source_target_pairs={{0,8},{4,12},{8,0},{12,4},{16,24},{20,28},{24,16},{28,20},{32,40},... | collective-permute-start | bytes 13832 | tf_op jit(solution)/shard_map/ppermute | solution.py:186
  9.6 0.0 collective-permute-start
  9.6 1.9 %fetch.1 = (f32[2,512]{1,0:T(2,128)S(1)}, bf16[512,576]{1,0:T(8,128)(2,1)S(1)}, bf16[2,512,128]{2,1,0:T(8,128)(2,1)S(1)}, bf16[256,3584]{1,0:T(8,128)(2,1)S(1)}) custom-call(s32[1]{0:T(128)} %bitcast.here_ref, s32[2]{0:T(128)} %lengths_hbm.1, s32[2,256]{1,0:T(2,128)} %table_hbm.1, bf16[512,576]{1,0:T(8,128)(2,1)} %bitcast.2, bf16[2,512,128]{2,1,0:T(8,128)(2,1)} %w_uv_hbm.1, ...), custom_call_target="tpu_custom_call" | custom-call | bytes 5242880 | tf_op jit(solution)/shard_map/fetch/pallas_call | solution.py:188
  11.4 0.0 collective-permute-done.2
  11.4 0.2 collective-permute-done.1
  11.7 3.6 %collective-permute-done = bf16[2,1152]{1,0:T(2,128)(2,1)S(1)} collective-permute-done((bf16[2,1152]{1,0:T(2,128)(2,1)S(1)}, bf16[2,1152]{1,0:T(2,128)(2,1)S(1)}, u32[]{:S(2)}, u32[]{:S(2)}) %collective-permute-start) | collective-permute-done | bytes 4640 | tf_op jit(solution)/shard_map/ppermute | solution.py:186
  15.3 0.1 broadcast_select_fusion.1
  15.4 0.2 broadcast_in_dim.58
  15.5 14.2 %all_to_all.10 = bf16[16,4,2,1152]{3,2,1,0:T(2,128)(2,1)S(1)} all-to-all(bf16[16,4,2,1152]{3,2,1,0:T(2,128)(2,1)S(1)} %broadcast_in_dim.58), channel_id=1, replica_groups={{0,16,32,48,64,80,96,112,128,144,160,176,192,208,224,240},{4,20,36,52,6..., dimensions={0} | all-to-all | bytes 589824 | tf_op jit(solution)/shard_map/all_to_all | solution.py:214
  29.7 0.1 reshape.35.q_ref
  29.8 1.1 %attend.1 = bf16[128,1152]{1,0:T(8,128)(2,1)S(1)} custom-call(bf16[128,1152]{1,0:T(8,128)(2,1)S(1)} %reshape.35.q_ref, bf16[512,576]{1,0:T(8,128)(2,1)S(1)} %get-tuple-element.19.keys_ref, f32[2,512]{1,0:T(2,128)S(1)} %get-tuple-element.20.live_ref), custom_call_target="tpu_custom_call" | custom-call | tf_op jit(solution)/shard_map/attend/pallas_call | solution.py:220
  31.0 0.1 reshape.36
  31.1 20.1 %all_to_all.11 = bf16[64,2,1152]{2,1,0:T(2,128)(2,1)S(1)} all-to-all(bf16[64,2,1152]{2,1,0:T(2,128)(2,1)S(1)} %reshape.36), channel_id=1, replica_groups=mesh['ctx'=64,'grp'=4] {'ctx'}, dimensions={0} | all-to-all | bytes 589824 | tf_op jit(solution)/shard_map/all_to_all | solution.py:229
  51.2 0.1 reshape.37.state_ref
  51.3 2.3 %project.1 = bf16[2,7168]{1,0:T(2,128)(2,1)S(1)} custom-call(bf16[128,1152]{1,0:T(8,128)(2,1)S(1)} %reshape.37.state_ref, bf16[2,512,128]{2,1,0:T(8,128)(2,1)S(1)} %get-tuple-element.21.w_uv_ref, bf16[256,3584]{1,0:T(8,128)(2,1)S(1)} %get-tuple-element.22.first_ref, bf16[256,7168]{1,0:T(8,128)(2,1)} %w_out_hbm.3), custom_call_target="tpu_custom_call" | custom-call | tf_op jit(solution)/shard_map/project/pallas_call | solution.py:233
  53.6 0.1 collective-permute-start.5
  53.7 3.5 %collective-permute-start.4 = (bf16[2,7168]{1,0:T(2,128)(2,1)S(1)}, bf16[2,7168]{1,0:T(2,128)(2,1)S(1)}, u32[]{:S(2)}, u32[]{:S(2)}) collective-permute-start(bf16[2,7168]{1,0:T(2,128)(2,1)S(1)} %project.1), channel_id=1, source_target_pairs={{0,128},{4,132},{8,136},{12,140},{16,144},{20,148},{24,152},{28,15... | collective-permute-start | bytes 86024 | tf_op jit(solution)/shard_map/ppermute | solution.py:23
  57.2 0.5 collective-permute-start.3
  57.8 0.0 collective-permute-done.5
  57.8 1.4 %collective-permute-done.4 = bf16[2,7168]{1,0:T(2,128)(2,1)S(1)} collective-permute-done((bf16[2,7168]{1,0:T(2,128)(2,1)S(1)}, bf16[2,7168]{1,0:T(2,128)(2,1)S(1)}, u32[]{:S(2)}, u32[]{:S(2)}) %collective-permute-start.4) | collective-permute-done | bytes 28704 | tf_op jit(solution)/shard_map/ppermute | solution.py:23
  59.2 2.0 %collective-permute-done.3 = bf16[2,7168]{1,0:T(2,128)(2,1)S(1)} collective-permute-done((bf16[2,7168]{1,0:T(2,128)(2,1)S(1)}, bf16[2,7168]{1,0:T(2,128)(2,1)S(1)}, u32[]{:S(2)}, u32[]{:S(2)}) %collective-permute-start.3) | collective-permute-done | bytes 28704 | tf_op jit(solution)/shard_map/ppermute | solution.py:23
  61.1 0.1 add_convert_fusion.2
  61.2 0.6 collective-permute-start.8
  61.8 2.1 %collective-permute-start.7 = (bf16[2,7168]{1,0:T(2,128)(2,1)S(1)}, bf16[2,7168]{1,0:T(2,128)(2,1)S(1)}, u32[]{:S(2)}, u32[]{:S(2)}) collective-permute-start(bf16[2,7168]{1,0:T(2,128)(2,1)S(1)} %add_convert_fusion.2), channel_id=1, source_target_pairs={{0,32},{4,36},{8,40},{12,44},{16,48},{20,52},{24,56},{28,60},{32,0... | collective-permute-start | bytes 86024 | tf_op jit(solution)/shard_map/ppermute | solution.py:23
  63.9 1.4 %collective-permute-start.6 = (bf16[2,7168]{1,0:T(2,128)(2,1)S(1)}, bf16[2,7168]{1,0:T(2,128)(2,1)S(1)}, u32[]{:S(2)}, u32[]{:S(2)}) collective-permute-start(bf16[2,7168]{1,0:T(2,128)(2,1)S(1)} %add_convert_fusion.2), channel_id=1, source_target_pairs={{0,16},{4,20},{8,24},{12,28},{16,0},{20,4},{24,8},{28,12},{32,48},... | collective-permute-start | bytes 86024 | tf_op jit(solution)/shard_map/ppermute | solution.py:23
  65.4 1.0 %collective-permute-done.8 = bf16[2,7168]{1,0:T(2,128)(2,1)S(1)} collective-permute-done((bf16[2,7168]{1,0:T(2,128)(2,1)S(1)}, bf16[2,7168]{1,0:T(2,128)(2,1)S(1)}, u32[]{:S(2)}, u32[]{:S(2)}) %collective-permute-start.8) | collective-permute-done | bytes 28704 | tf_op jit(solution)/shard_map/ppermute | solution.py:23
  66.3 0.8 %collective-permute-done.7 = bf16[2,7168]{1,0:T(2,128)(2,1)S(1)} collective-permute-done((bf16[2,7168]{1,0:T(2,128)(2,1)S(1)}, bf16[2,7168]{1,0:T(2,128)(2,1)S(1)}, u32[]{:S(2)}, u32[]{:S(2)}) %collective-permute-start.7) | collective-permute-done | bytes 28704 | tf_op jit(solution)/shard_map/ppermute | solution.py:23
  67.2 0.6 collective-permute-done.6
  67.8 0.1 add_convert_fusion.1
  67.9 1.0 %collective-permute-start.11 = (bf16[2,7168]{1,0:T(2,128)(2,1)S(1)}, bf16[2,7168]{1,0:T(2,128)(2,1)S(1)}, u32[]{:S(2)}, u32[]{:S(2)}) collective-permute-start(bf16[2,7168]{1,0:T(2,128)(2,1)S(1)} %add_convert_fusion.1), channel_id=1, source_target_pairs={{0,12},{4,8},{8,4},{12,0},{16,28},{20,24},{24,20},{28,16},{32,44},... | collective-permute-start | bytes 86024 | tf_op jit(solution)/shard_map/ppermute | solution.py:23
  68.9 3.2 %collective-permute-start.10 = (bf16[2,7168]{1,0:T(2,128)(2,1)S(1)}, bf16[2,7168]{1,0:T(2,128)(2,1)S(1)}, u32[]{:S(2)}, u32[]{:S(2)}) collective-permute-start(bf16[2,7168]{1,0:T(2,128)(2,1)S(1)} %add_convert_fusion.1), channel_id=1, source_target_pairs={{0,8},{4,12},{8,0},{12,4},{16,24},{20,28},{24,16},{28,20},{32,40},... | collective-permute-start | bytes 86024 | tf_op jit(solution)/shard_map/ppermute | solution.py:23
  72.1 2.4 %collective-permute-start.9 = (bf16[2,7168]{1,0:T(2,128)(2,1)S(1)}, bf16[2,7168]{1,0:T(2,128)(2,1)S(1)}, u32[]{:S(2)}, u32[]{:S(2)}) collective-permute-start(bf16[2,7168]{1,0:T(2,128)(2,1)S(1)} %add_convert_fusion.1), channel_id=1, source_target_pairs={{0,4},{4,0},{8,12},{12,8},{16,20},{20,16},{24,28},{28,24},{32,36},... | collective-permute-start | bytes 86024 | tf_op jit(solution)/shard_map/ppermute | solution.py:23
  74.4 0.0 collective-permute-done.11
  74.4 2.2 %collective-permute-done.10 = bf16[2,7168]{1,0:T(2,128)(2,1)S(1)} collective-permute-done((bf16[2,7168]{1,0:T(2,128)(2,1)S(1)}, bf16[2,7168]{1,0:T(2,128)(2,1)S(1)}, u32[]{:S(2)}, u32[]{:S(2)}) %collective-permute-start.10) | collective-permute-done | bytes 28704 | tf_op jit(solution)/shard_map/ppermute | solution.py:23
  76.7 0.5 collective-permute-done.9
  77.1 0.7 add_convert_fusion
  (2 shorter events, 0.0 us)
Async XLA Ops:
  0.8 10.6 %collective-permute-start.2 = (bf16[2,1152]{1,0:T(2,128)(2,1)S(1)}, bf16[2,1152]{1,0:T(2,128)(2,1)S(1)}, u32[]{:S(2)}, u32[]{:S(2)}) collective-permute-start(bf16[2,1152]{1,0:T(2,128)(2,1)S(1)} %message.1), channel_id=1, source_target_pairs={{0,4},{4,0},{8,12},{12,8},{16,20},{20,16},{24,28},{28,24},{32,36},... | collective-permute-start | bytes 13832 | tf_op jit(solution)/shard_map/ppermute | solution.py:186
  4.2 7.5 %collective-permute-start.1 = (bf16[2,1152]{1,0:T(2,128)(2,1)S(1)}, bf16[2,1152]{1,0:T(2,128)(2,1)S(1)}, u32[]{:S(2)}, u32[]{:S(2)}) collective-permute-start(bf16[2,1152]{1,0:T(2,128)(2,1)S(1)} %message.1), channel_id=1, source_target_pairs={{0,8},{4,12},{8,0},{12,4},{16,24},{20,28},{24,16},{28,20},{32,40},... | collective-permute-start | bytes 13832 | tf_op jit(solution)/shard_map/ppermute | solution.py:186
  9.6 5.7 %collective-permute-start = (bf16[2,1152]{1,0:T(2,128)(2,1)S(1)}, bf16[2,1152]{1,0:T(2,128)(2,1)S(1)}, u32[]{:S(2)}, u32[]{:S(2)}) collective-permute-start(bf16[2,1152]{1,0:T(2,128)(2,1)S(1)} %message.1), channel_id=1, source_target_pairs={{0,12},{4,8},{8,4},{12,0},{16,28},{20,24},{24,20},{28,16},{32,44},... | collective-permute-start | bytes 13832 | tf_op jit(solution)/shard_map/ppermute | solution.py:186
  53.6 4.2 %collective-permute-start.5 = (bf16[2,7168]{1,0:T(2,128)(2,1)S(1)}, bf16[2,7168]{1,0:T(2,128)(2,1)S(1)}, u32[]{:S(2)}, u32[]{:S(2)}) collective-permute-start(bf16[2,7168]{1,0:T(2,128)(2,1)S(1)} %project.1), channel_id=1, source_target_pairs={{0,192},{4,196},{8,200},{12,204},{16,208},{20,212},{24,216},{28,22... | collective-permute-start | bytes 86024 | tf_op jit(solution)/shard_map/ppermute | solution.py:23
  53.7 5.4 %collective-permute-start.4 = (bf16[2,7168]{1,0:T(2,128)(2,1)S(1)}, bf16[2,7168]{1,0:T(2,128)(2,1)S(1)}, u32[]{:S(2)}, u32[]{:S(2)}) collective-permute-start(bf16[2,7168]{1,0:T(2,128)(2,1)S(1)} %project.1), channel_id=1, source_target_pairs={{0,128},{4,132},{8,136},{12,140},{16,144},{20,148},{24,152},{28,15... | collective-permute-start | bytes 86024 | tf_op jit(solution)/shard_map/ppermute | solution.py:23
  57.2 3.9 %collective-permute-start.3 = (bf16[2,7168]{1,0:T(2,128)(2,1)S(1)}, bf16[2,7168]{1,0:T(2,128)(2,1)S(1)}, u32[]{:S(2)}, u32[]{:S(2)}) collective-permute-start(bf16[2,7168]{1,0:T(2,128)(2,1)S(1)} %project.1), channel_id=1, source_target_pairs={{0,64},{4,68},{8,72},{12,76},{16,80},{20,84},{24,88},{28,92},{32,9... | collective-permute-start | bytes 86024 | tf_op jit(solution)/shard_map/ppermute | solution.py:23
  61.2 5.2 %collective-permute-start.8 = (bf16[2,7168]{1,0:T(2,128)(2,1)S(1)}, bf16[2,7168]{1,0:T(2,128)(2,1)S(1)}, u32[]{:S(2)}, u32[]{:S(2)}) collective-permute-start(bf16[2,7168]{1,0:T(2,128)(2,1)S(1)} %add_convert_fusion.2), channel_id=1, source_target_pairs={{0,48},{4,52},{8,56},{12,60},{16,32},{20,36},{24,40},{28,44},{32,1... | collective-permute-start | bytes 86024 | tf_op jit(solution)/shard_map/ppermute | solution.py:23
  61.8 5.4 %collective-permute-start.7 = (bf16[2,7168]{1,0:T(2,128)(2,1)S(1)}, bf16[2,7168]{1,0:T(2,128)(2,1)S(1)}, u32[]{:S(2)}, u32[]{:S(2)}) collective-permute-start(bf16[2,7168]{1,0:T(2,128)(2,1)S(1)} %add_convert_fusion.2), channel_id=1, source_target_pairs={{0,32},{4,36},{8,40},{12,44},{16,48},{20,52},{24,56},{28,60},{32,0... | collective-permute-start | bytes 86024 | tf_op jit(solution)/shard_map/ppermute | solution.py:23
  63.9 3.9 %collective-permute-start.6 = (bf16[2,7168]{1,0:T(2,128)(2,1)S(1)}, bf16[2,7168]{1,0:T(2,128)(2,1)S(1)}, u32[]{:S(2)}, u32[]{:S(2)}) collective-permute-start(bf16[2,7168]{1,0:T(2,128)(2,1)S(1)} %add_convert_fusion.2), channel_id=1, source_target_pairs={{0,16},{4,20},{8,24},{12,28},{16,0},{20,4},{24,8},{28,12},{32,48},... | collective-permute-start | bytes 86024 | tf_op jit(solution)/shard_map/ppermute | solution.py:23
  67.9 6.6 %collective-permute-start.11 = (bf16[2,7168]{1,0:T(2,128)(2,1)S(1)}, bf16[2,7168]{1,0:T(2,128)(2,1)S(1)}, u32[]{:S(2)}, u32[]{:S(2)}) collective-permute-start(bf16[2,7168]{1,0:T(2,128)(2,1)S(1)} %add_convert_fusion.1), channel_id=1, source_target_pairs={{0,12},{4,8},{8,4},{12,0},{16,28},{20,24},{24,20},{28,16},{32,44},... | collective-permute-start | bytes 86024 | tf_op jit(solution)/shard_map/ppermute | solution.py:23
  68.9 7.8 %collective-permute-start.10 = (bf16[2,7168]{1,0:T(2,128)(2,1)S(1)}, bf16[2,7168]{1,0:T(2,128)(2,1)S(1)}, u32[]{:S(2)}, u32[]{:S(2)}) collective-permute-start(bf16[2,7168]{1,0:T(2,128)(2,1)S(1)} %add_convert_fusion.1), channel_id=1, source_target_pairs={{0,8},{4,12},{8,0},{12,4},{16,24},{20,28},{24,16},{28,20},{32,40},... | collective-permute-start | bytes 86024 | tf_op jit(solution)/shard_map/ppermute | solution.py:23
  72.1 5.1 %collective-permute-start.9 = (bf16[2,7168]{1,0:T(2,128)(2,1)S(1)}, bf16[2,7168]{1,0:T(2,128)(2,1)S(1)}, u32[]{:S(2)}, u32[]{:S(2)}) collective-permute-start(bf16[2,7168]{1,0:T(2,128)(2,1)S(1)} %add_convert_fusion.1), channel_id=1, source_target_pairs={{0,4},{4,0},{8,12},{12,8},{16,20},{20,16},{24,28},{28,24},{32,36},... | collective-permute-start | bytes 86024 | tf_op jit(solution)/shard_map/ppermute | solution.py:23

commit v10 on v9

--- a/solution.py
+++ b/solution.py
@@ -52,7 +52,7 @@
 ):
     pairs = [
         (lengths_hbm, lengths_ref), (table_hbm, table_ref), (cache_hbm, keys_ref), (w_uv_hbm, w_uv_ref),
-        (w_out_hbm.at[:, : w_out_ref.shape[1]], w_out_ref),
+        (w_out_hbm.at[: w_out_ref.shape[0]], w_out_ref),
     ]
     copies = [pltpu.make_async_copy(a, b, sems.at[k]) for k, (a, b) in enumerate(pairs)]
     for copy in copies:
@@ -108,11 +108,12 @@
 
 
 def project_kernel(rows, heads, latent, state_ref, w_uv_ref, first_ref, w_out_hbm, term_ref, second_ref, sems):
-    split = first_ref.shape[1]
-    parts, _, step = second_ref.shape
+    split = first_ref.shape[0]
+    parts = sems.shape[0]
+    step = second_ref.shape[0] // parts
     copies = [
         pltpu.make_async_copy(
-            w_out_hbm.at[:, split + k * step : split + (k + 1) * step], second_ref.at[k], sems.at[k]
+            w_out_hbm.at[split + k * step : split + (k + 1) * step], second_ref.at[k * step : (k + 1) * step], sems.at[k]
         )
         for k in range(parts)
     ]
@@ -149,12 +150,11 @@
         ],
         axis=0,
     ).astype(BF16)
-    term_ref[:, :split] = jnp.dot(flat, first_ref[...], preferred_element_type=F32).astype(term_ref.dtype)
-    for k, copy in enumerate(copies):
+    term = jnp.dot(flat[:, :split], first_ref[...], preferred_element_type=F32)
+    for copy in copies:
         copy.wait()
-        term_ref[:, split + k * step : split + (k + 1) * step] = jnp.dot(
-            flat, second_ref[k], preferred_element_type=F32
-        ).astype(term_ref.dtype)
+    term += jnp.dot(flat[:, split:], second_ref[...], preferred_element_type=F32)
+    term_ref[...] = term.astype(term_ref.dtype)
 
 
 def local(q_latent, q_rope, latent_cache, page_table, lengths, w_uv, w_out):
@@ -184,14 +184,14 @@
 
     near = 4
     others = [lax.ppermute(message, CTX, xor_pairs(count, k)) for k in range(1, near)]
-    split = w_out.shape[1] // 2 // LANES * LANES
+    split = w_out.shape[0] // 2
     live, keys, w_uv, w_first = pl.pallas_call(
         functools.partial(fetch_kernel, page_len),
         out_shape=(
             pltpu.VMEM((rows, tokens), F32),
             pltpu.VMEM((tokens, width), BF16),
             pltpu.VMEM(w_uv.shape, BF16),
-            pltpu.VMEM((w_out.shape[0], split), BF16),
+            pltpu.VMEM((split, w_out.shape[1]), BF16),
         ),
         in_specs=[smem, hbm, hbm, hbm, hbm, hbm],
         out_specs=(vmem, vmem, vmem, vmem),
@@ -235,7 +235,7 @@
         out_shape=jax.ShapeDtypeStruct((rows, w_out.shape[1]), BF16),
         in_specs=[vmem, vmem, vmem, hbm],
         out_specs=vmem,
-        scratch_shapes=[pltpu.VMEM((parts, w_out.shape[0], (w_out.shape[1] - split) // parts), BF16), dma((parts,))],
+        scratch_shapes=[pltpu.VMEM((w_out.shape[0] - split, w_out.shape[1]), BF16), dma((parts,))],
         compiler_params=params,
         name="project",
     )(state.reshape(count * rows, state_size), w_uv, w_first, stay(w_out))

time: 78.1 us -> 77.9 us (level)
  no operation moved by 1% of the time
where the time goes in v10:
time: 77.9 us; the launch traced here: 77.6 us
  blocking collectives  34.2 us (44%)
  starting transfers between devices  23.7 us (30%)
  waiting for transfers between devices  12.3 us (16%)
  Pallas kernels  5.85 us (8%)
  other arithmetic  0.91 us (1%)
    all_to_all x1, blocking collectives, local(): lax.all_to_all(state.reshape(count, rows, state_size), CTX, split_axis=0,...  20.1 us
    ppermute x9, starting transfers between devices, sum_of_four(): lax.ppermute(x, CTX, xor_pairs(count, k << low))  14.9 us
    all_to_all x1, blocking collectives, local(): lax.all_to_all(jnp.broadcast_to(column[None], (count // near, near, rows,...  14.2 us
    ppermute x3, starting transfers between devices, local(): lax.ppermute(message, CTX, xor_pairs(count, k))  8.75 us
    ppermute x9, waiting for transfers between devices, sum_of_four(): lax.ppermute(x, CTX, xor_pairs(count, k << low))  8.46 us
    ppermute x3, waiting for transfers between devices, local(): lax.ppermute(message, CTX, xor_pairs(count, k))  3.83 us
    pallas_call x1, Pallas kernels, local(): pl.pallas_call(functools.partial(project_kernel, rows, heads, latent), ou...  2.07 us
    pallas_call x1, Pallas kernels, local(): pl.pallas_call(functools.partial(fetch_kernel, page_len), out_shape=(pltp...  1.85 us
  transfers between devices with their start and end apart: 12, of which 9 were waited for; matrix products, arithmetic and copies ran while one was open for 0% of the time, Pallas kernels for 2%

profile of v10, /device:TPU:2, one launch (start us, length us, event | category | flops | bytes accessed | tf_op | source)
XLA Modules:
  0.0 77.6 jit_solution(16209297149909705660)
XLA Ops:
  0.0 0.8 %message.1 = bf16[2,1152]{1,0:T(2,128)(2,1)S(1)} custom-call(bf16[2,2,512]{2,1,0:T(2,128)(2,1)} %q_latent_hbm.1, bf16[2,2,64]{2,1,0:T(2,128)(2,1)} %q_rope_hbm.1), custom_call_target="tpu_custom_call" | custom-call | tf_op jit(solution)/shard_map/message/pallas_call | solution.py:175
  0.8 3.4 %collective-permute-start.2 = (bf16[2,1152]{1,0:T(2,128)(2,1)S(1)}, bf16[2,1152]{1,0:T(2,128)(2,1)S(1)}, u32[]{:S(2)}, u32[]{:S(2)}) collective-permute-start(bf16[2,1152]{1,0:T(2,128)(2,1)S(1)} %message.1), channel_id=1, source_target_pairs={{0,4},{4,0},{8,12},{12,8},{16,20},{20,16},{24,28},{28,24},{32,36},... | collective-permute-start | bytes 13832 | tf_op jit(solution)/shard_map/ppermute | solution.py:186
  4.2 5.4 %collective-permute-start.1 = (bf16[2,1152]{1,0:T(2,128)(2,1)S(1)}, bf16[2,1152]{1,0:T(2,128)(2,1)S(1)}, u32[]{:S(2)}, u32[]{:S(2)}) collective-permute-start(bf16[2,1152]{1,0:T(2,128)(2,1)S(1)} %message.1), channel_id=1, source_target_pairs={{0,8},{4,12},{8,0},{12,4},{16,24},{20,28},{24,16},{28,20},{32,40},... | collective-permute-start | bytes 13832 | tf_op jit(solution)/shard_map/ppermute | solution.py:186
  9.6 0.0 collective-permute-start
  9.6 1.9 %fetch.1 = (f32[2,512]{1,0:T(2,128)S(1)}, bf16[512,576]{1,0:T(8,128)(2,1)S(1)}, bf16[2,512,128]{2,1,0:T(8,128)(2,1)S(1)}, bf16[128,7168]{1,0:T(8,128)(2,1)S(1)}) custom-call(s32[1]{0:T(128)} %bitcast.here_ref, s32[2]{0:T(128)} %lengths_hbm.1, s32[2,256]{1,0:T(2,128)} %table_hbm.1, bf16[512,576]{1,0:T(8,128)(2,1)} %bitcast.2, bf16[2,512,128]{2,1,0:T(8,128)(2,1)} %w_uv_hbm.1, ...), custom_call_target="tpu_custom_call" | custom-call | bytes 5242880 | tf_op jit(solution)/shard_map/fetch/pallas_call | solution.py:188
  11.4 0.0 collective-permute-done.2
  11.4 0.2 collective-permute-done.1
  11.7 3.6 %collective-permute-done = bf16[2,1152]{1,0:T(2,128)(2,1)S(1)} collective-permute-done((bf16[2,1152]{1,0:T(2,128)(2,1)S(1)}, bf16[2,1152]{1,0:T(2,128)(2,1)S(1)}, u32[]{:S(2)}, u32[]{:S(2)}) %collective-permute-start) | collective-permute-done | bytes 4640 | tf_op jit(solution)/shard_map/ppermute | solution.py:186
  15.3 0.1 broadcast_select_fusion.1
  15.4 0.2 broadcast_in_dim.58
  15.5 14.2 %all_to_all.10 = bf16[16,4,2,1152]{3,2,1,0:T(2,128)(2,1)S(1)} all-to-all(bf16[16,4,2,1152]{3,2,1,0:T(2,128)(2,1)S(1)} %broadcast_in_dim.58), channel_id=1, replica_groups={{0,16,32,48,64,80,96,112,128,144,160,176,192,208,224,240},{4,20,36,52,6..., dimensions={0} | all-to-all | bytes 589824 | tf_op jit(solution)/shard_map/all_to_all | solution.py:214
  29.7 0.1 reshape.35.q_ref
  29.8 1.1 %attend.1 = bf16[128,1152]{1,0:T(8,128)(2,1)S(1)} custom-call(bf16[128,1152]{1,0:T(8,128)(2,1)S(1)} %reshape.35.q_ref, bf16[512,576]{1,0:T(8,128)(2,1)S(1)} %get-tuple-element.19.keys_ref, f32[2,512]{1,0:T(2,128)S(1)} %get-tuple-element.20.live_ref), custom_call_target="tpu_custom_call" | custom-call | tf_op jit(solution)/shard_map/attend/pallas_call | solution.py:220
  31.0 0.1 reshape.36
  31.1 20.1 %all_to_all.11 = bf16[64,2,1152]{2,1,0:T(2,128)(2,1)S(1)} all-to-all(bf16[64,2,1152]{2,1,0:T(2,128)(2,1)S(1)} %reshape.36), channel_id=1, replica_groups=mesh['ctx'=64,'grp'=4] {'ctx'}, dimensions={0} | all-to-all | bytes 589824 | tf_op jit(solution)/shard_map/all_to_all | solution.py:229
  51.2 0.1 reshape.37.state_ref
  51.3 2.1 %project.1 = bf16[2,7168]{1,0:T(2,128)(2,1)S(1)} custom-call(bf16[128,1152]{1,0:T(8,128)(2,1)S(1)} %reshape.37.state_ref, bf16[2,512,128]{2,1,0:T(8,128)(2,1)S(1)} %get-tuple-element.21.w_uv_ref, bf16[128,7168]{1,0:T(8,128)(2,1)S(1)} %get-tuple-element.22.first_ref, bf16[256,7168]{1,0:T(8,128)(2,1)} %w_out_hbm.3), custom_call_target="tpu_custom_call" | custom-call | tf_op jit(solution)/shard_map/project/pallas_call | solution.py:233
  53.4 0.1 collective-permute-start.5
  53.5 3.5 %collective-permute-start.4 = (bf16[2,7168]{1,0:T(2,128)(2,1)S(1)}, bf16[2,7168]{1,0:T(2,128)(2,1)S(1)}, u32[]{:S(2)}, u32[]{:S(2)}) collective-permute-start(bf16[2,7168]{1,0:T(2,128)(2,1)S(1)} %project.1), channel_id=1, source_target_pairs={{0,128},{4,132},{8,136},{12,140},{16,144},{20,148},{24,152},{28,15... | collective-permute-start | bytes 86024 | tf_op jit(solution)/shard_map/ppermute | solution.py:23
  57.0 0.5 collective-permute-start.3
  57.5 0.0 collective-permute-done.5
  57.5 1.4 %collective-permute-done.4 = bf16[2,7168]{1,0:T(2,128)(2,1)S(1)} collective-permute-done((bf16[2,7168]{1,0:T(2,128)(2,1)S(1)}, bf16[2,7168]{1,0:T(2,128)(2,1)S(1)}, u32[]{:S(2)}, u32[]{:S(2)}) %collective-permute-start.4) | collective-permute-done | bytes 28704 | tf_op jit(solution)/shard_map/ppermute | solution.py:23
  58.9 1.9 %collective-permute-done.3 = bf16[2,7168]{1,0:T(2,128)(2,1)S(1)} collective-permute-done((bf16[2,7168]{1,0:T(2,128)(2,1)S(1)}, bf16[2,7168]{1,0:T(2,128)(2,1)S(1)}, u32[]{:S(2)}, u32[]{:S(2)}) %collective-permute-start.3) | collective-permute-done | bytes 28704 | tf_op jit(solution)/shard_map/ppermute | solution.py:23
  60.9 0.1 add_convert_fusion.2
  60.9 0.6 collective-permute-start.8
  61.5 2.1 %collective-permute-start.7 = (bf16[2,7168]{1,0:T(2,128)(2,1)S(1)}, bf16[2,7168]{1,0:T(2,128)(2,1)S(1)}, u32[]{:S(2)}, u32[]{:S(2)}) collective-permute-start(bf16[2,7168]{1,0:T(2,128)(2,1)S(1)} %add_convert_fusion.2), channel_id=1, source_target_pairs={{0,32},{4,36},{8,40},{12,44},{16,48},{20,52},{24,56},{28,60},{32,0... | collective-permute-start | bytes 86024 | tf_op jit(solution)/shard_map/ppermute | solution.py:23
  63.7 1.4 %collective-permute-start.6 = (bf16[2,7168]{1,0:T(2,128)(2,1)S(1)}, bf16[2,7168]{1,0:T(2,128)(2,1)S(1)}, u32[]{:S(2)}, u32[]{:S(2)}) collective-permute-start(bf16[2,7168]{1,0:T(2,128)(2,1)S(1)} %add_convert_fusion.2), channel_id=1, source_target_pairs={{0,16},{4,20},{8,24},{12,28},{16,0},{20,4},{24,8},{28,12},{32,48},... | collective-permute-start | bytes 86024 | tf_op jit(solution)/shard_map/ppermute | solution.py:23
  65.1 1.0 %collective-permute-done.8 = bf16[2,7168]{1,0:T(2,128)(2,1)S(1)} collective-permute-done((bf16[2,7168]{1,0:T(2,128)(2,1)S(1)}, bf16[2,7168]{1,0:T(2,128)(2,1)S(1)}, u32[]{:S(2)}, u32[]{:S(2)}) %collective-permute-start.8) | collective-permute-done | bytes 28704 | tf_op jit(solution)/shard_map/ppermute | solution.py:23
  66.1 0.8 %collective-permute-done.7 = bf16[2,7168]{1,0:T(2,128)(2,1)S(1)} collective-permute-done((bf16[2,7168]{1,0:T(2,128)(2,1)S(1)}, bf16[2,7168]{1,0:T(2,128)(2,1)S(1)}, u32[]{:S(2)}, u32[]{:S(2)}) %collective-permute-start.7) | collective-permute-done | bytes 28704 | tf_op jit(solution)/shard_map/ppermute | solution.py:23
  66.9 0.6 collective-permute-done.6
  67.5 0.1 add_convert_fusion.1
  67.6 1.0 %collective-permute-start.11 = (bf16[2,7168]{1,0:T(2,128)(2,1)S(1)}, bf16[2,7168]{1,0:T(2,128)(2,1)S(1)}, u32[]{:S(2)}, u32[]{:S(2)}) collective-permute-start(bf16[2,7168]{1,0:T(2,128)(2,1)S(1)} %add_convert_fusion.1), channel_id=1, source_target_pairs={{0,12},{4,8},{8,4},{12,0},{16,28},{20,24},{24,20},{28,16},{32,44},... | collective-permute-start | bytes 86024 | tf_op jit(solution)/shard_map/ppermute | solution.py:23
  68.6 3.2 %collective-permute-start.10 = (bf16[2,7168]{1,0:T(2,128)(2,1)S(1)}, bf16[2,7168]{1,0:T(2,128)(2,1)S(1)}, u32[]{:S(2)}, u32[]{:S(2)}) collective-permute-start(bf16[2,7168]{1,0:T(2,128)(2,1)S(1)} %add_convert_fusion.1), channel_id=1, source_target_pairs={{0,8},{4,12},{8,0},{12,4},{16,24},{20,28},{24,16},{28,20},{32,40},... | collective-permute-start | bytes 86024 | tf_op jit(solution)/shard_map/ppermute | solution.py:23
  71.8 2.4 %collective-permute-start.9 = (bf16[2,7168]{1,0:T(2,128)(2,1)S(1)}, bf16[2,7168]{1,0:T(2,128)(2,1)S(1)}, u32[]{:S(2)}, u32[]{:S(2)}) collective-permute-start(bf16[2,7168]{1,0:T(2,128)(2,1)S(1)} %add_convert_fusion.1), channel_id=1, source_target_pairs={{0,4},{4,0},{8,12},{12,8},{16,20},{20,16},{24,28},{28,24},{32,36},... | collective-permute-start | bytes 86024 | tf_op jit(solution)/shard_map/ppermute | solution.py:23
  74.2 0.0 collective-permute-done.11
  74.2 2.2 %collective-permute-done.10 = bf16[2,7168]{1,0:T(2,128)(2,1)S(1)} collective-permute-done((bf16[2,7168]{1,0:T(2,128)(2,1)S(1)}, bf16[2,7168]{1,0:T(2,128)(2,1)S(1)}, u32[]{:S(2)}, u32[]{:S(2)}) %collective-permute-start.10) | collective-permute-done | bytes 28704 | tf_op jit(solution)/shard_map/ppermute | solution.py:23
  76.4 0.5 collective-permute-done.9
  76.9 0.7 add_convert_fusion
  (2 shorter events, 0.0 us)
Async XLA Ops:
  0.8 10.6 %collective-permute-start.2 = (bf16[2,1152]{1,0:T(2,128)(2,1)S(1)}, bf16[2,1152]{1,0:T(2,128)(2,1)S(1)}, u32[]{:S(2)}, u32[]{:S(2)}) collective-permute-start(bf16[2,1152]{1,0:T(2,128)(2,1)S(1)} %message.1), channel_id=1, source_target_pairs={{0,4},{4,0},{8,12},{12,8},{16,20},{20,16},{24,28},{28,24},{32,36},... | collective-permute-start | bytes 13832 | tf_op jit(solution)/shard_map/ppermute | solution.py:186
  4.2 7.5 %collective-permute-start.1 = (bf16[2,1152]{1,0:T(2,128)(2,1)S(1)}, bf16[2,1152]{1,0:T(2,128)(2,1)S(1)}, u32[]{:S(2)}, u32[]{:S(2)}) collective-permute-start(bf16[2,1152]{1,0:T(2,128)(2,1)S(1)} %message.1), channel_id=1, source_target_pairs={{0,8},{4,12},{8,0},{12,4},{16,24},{20,28},{24,16},{28,20},{32,40},... | collective-permute-start | bytes 13832 | tf_op jit(solution)/shard_map/ppermute | solution.py:186
  9.6 5.7 %collective-permute-start = (bf16[2,1152]{1,0:T(2,128)(2,1)S(1)}, bf16[2,1152]{1,0:T(2,128)(2,1)S(1)}, u32[]{:S(2)}, u32[]{:S(2)}) collective-permute-start(bf16[2,1152]{1,0:T(2,128)(2,1)S(1)} %message.1), channel_id=1, source_target_pairs={{0,12},{4,8},{8,4},{12,0},{16,28},{20,24},{24,20},{28,16},{32,44},... | collective-permute-start | bytes 13832 | tf_op jit(solution)/shard_map/ppermute | solution.py:186
  53.4 4.2 %collective-permute-start.5 = (bf16[2,7168]{1,0:T(2,128)(2,1)S(1)}, bf16[2,7168]{1,0:T(2,128)(2,1)S(1)}, u32[]{:S(2)}, u32[]{:S(2)}) collective-permute-start(bf16[2,7168]{1,0:T(2,128)(2,1)S(1)} %project.1), channel_id=1, source_target_pairs={{0,192},{4,196},{8,200},{12,204},{16,208},{20,212},{24,216},{28,22... | collective-permute-start | bytes 86024 | tf_op jit(solution)/shard_map/ppermute | solution.py:23
  53.5 5.4 %collective-permute-start.4 = (bf16[2,7168]{1,0:T(2,128)(2,1)S(1)}, bf16[2,7168]{1,0:T(2,128)(2,1)S(1)}, u32[]{:S(2)}, u32[]{:S(2)}) collective-permute-start(bf16[2,7168]{1,0:T(2,128)(2,1)S(1)} %project.1), channel_id=1, source_target_pairs={{0,128},{4,132},{8,136},{12,140},{16,144},{20,148},{24,152},{28,15... | collective-permute-start | bytes 86024 | tf_op jit(solution)/shard_map/ppermute | solution.py:23
  57.0 3.9 %collective-permute-start.3 = (bf16[2,7168]{1,0:T(2,128)(2,1)S(1)}, bf16[2,7168]{1,0:T(2,128)(2,1)S(1)}, u32[]{:S(2)}, u32[]{:S(2)}) collective-permute-start(bf16[2,7168]{1,0:T(2,128)(2,1)S(1)} %project.1), channel_id=1, source_target_pairs={{0,64},{4,68},{8,72},{12,76},{16,80},{20,84},{24,88},{28,92},{32,9... | collective-permute-start | bytes 86024 | tf_op jit(solution)/shard_map/ppermute | solution.py:23
  60.9 5.2 %collective-permute-start.8 = (bf16[2,7168]{1,0:T(2,128)(2,1)S(1)}, bf16[2,7168]{1,0:T(2,128)(2,1)S(1)}, u32[]{:S(2)}, u32[]{:S(2)}) collective-permute-start(bf16[2,7168]{1,0:T(2,128)(2,1)S(1)} %add_convert_fusion.2), channel_id=1, source_target_pairs={{0,48},{4,52},{8,56},{12,60},{16,32},{20,36},{24,40},{28,44},{32,1... | collective-permute-start | bytes 86024 | tf_op jit(solution)/shard_map/ppermute | solution.py:23
  61.5 5.4 %collective-permute-start.7 = (bf16[2,7168]{1,0:T(2,128)(2,1)S(1)}, bf16[2,7168]{1,0:T(2,128)(2,1)S(1)}, u32[]{:S(2)}, u32[]{:S(2)}) collective-permute-start(bf16[2,7168]{1,0:T(2,128)(2,1)S(1)} %add_convert_fusion.2), channel_id=1, source_target_pairs={{0,32},{4,36},{8,40},{12,44},{16,48},{20,52},{24,56},{28,60},{32,0... | collective-permute-start | bytes 86024 | tf_op jit(solution)/shard_map/ppermute | solution.py:23
  63.7 3.9 %collective-permute-start.6 = (bf16[2,7168]{1,0:T(2,128)(2,1)S(1)}, bf16[2,7168]{1,0:T(2,128)(2,1)S(1)}, u32[]{:S(2)}, u32[]{:S(2)}) collective-permute-start(bf16[2,7168]{1,0:T(2,128)(2,1)S(1)} %add_convert_fusion.2), channel_id=1, source_target_pairs={{0,16},{4,20},{8,24},{12,28},{16,0},{20,4},{24,8},{28,12},{32,48},... | collective-permute-start | bytes 86024 | tf_op jit(solution)/shard_map/ppermute | solution.py:23
  67.6 6.6 %collective-permute-start.11 = (bf16[2,7168]{1,0:T(2,128)(2,1)S(1)}, bf16[2,7168]{1,0:T(2,128)(2,1)S(1)}, u32[]{:S(2)}, u32[]{:S(2)}) collective-permute-start(bf16[2,7168]{1,0:T(2,128)(2,1)S(1)} %add_convert_fusion.1), channel_id=1, source_target_pairs={{0,12},{4,8},{8,4},{12,0},{16,28},{20,24},{24,20},{28,16},{32,44},... | collective-permute-start | bytes 86024 | tf_op jit(solution)/shard_map/ppermute | solution.py:23
  68.6 7.8 %collective-permute-start.10 = (bf16[2,7168]{1,0:T(2,128)(2,1)S(1)}, bf16[2,7168]{1,0:T(2,128)(2,1)S(1)}, u32[]{:S(2)}, u32[]{:S(2)}) collective-permute-start(bf16[2,7168]{1,0:T(2,128)(2,1)S(1)} %add_convert_fusion.1), channel_id=1, source_target_pairs={{0,8},{4,12},{8,0},{12,4},{16,24},{20,28},{24,16},{28,20},{32,40},... | collective-permute-start | bytes 86024 | tf_op jit(solution)/shard_map/ppermute | solution.py:23
  71.8 5.1 %collective-permute-start.9 = (bf16[2,7168]{1,0:T(2,128)(2,1)S(1)}, bf16[2,7168]{1,0:T(2,128)(2,1)S(1)}, u32[]{:S(2)}, u32[]{:S(2)}) collective-permute-start(bf16[2,7168]{1,0:T(2,128)(2,1)S(1)} %add_convert_fusion.1), channel_id=1, source_target_pairs={{0,4},{4,0},{8,12},{12,8},{16,20},{20,16},{24,28},{28,24},{32,36},... | collective-permute-start | bytes 86024 | tf_op jit(solution)/shard_map/ppermute | solution.py:23

commit v11 on v10

--- a/solution.py
+++ b/solution.py
@@ -17,6 +17,10 @@
 
 def xor_pairs(count, mask):
     return [(i, i ^ mask) for i in range(count)]
+
+
+def sum_of_two(x, count, mask):
+    return x.astype(F32) + lax.ppermute(x, CTX, xor_pairs(count, mask)).astype(F32)
 
 
 def sum_of_four(x, count, low):
@@ -239,7 +243,9 @@
         compiler_params=params,
         name="project",
     )(state.reshape(count * rows, state_size), w_uv, w_first, stay(w_out))
-    for low in (4, 2, 0):
+    for mask in (1, 3):
+        term = sum_of_two(term, count, mask).astype(BF16)
+    for low in (4, 2):
         term = sum_of_four(term, count, low).astype(BF16)
     return term
 

time: 77.9 us -> 79.5 us (1.021)
  waiting for transfers between devices: 12.3 us -> 19.6 us
  starting transfers between devices: 23.7 us -> 18.1 us
    ppermute x0 -> x2, waiting for transfers between devices: none -> 9.96 us  [sum_of_two(): lax.ppermute(x, CTX, xor_pairs(count, mask)).astype(F32)]
    ppermute x9 -> x6, starting transfers between devices: 14.9 us -> 8.36 us  [sum_of_four(): lax.ppermute(x, CTX, xor_pairs(count, k << low))]
    ppermute x9 -> x6, waiting for transfers between devices: 8.46 us -> 5.78 us  [sum_of_four(): lax.ppermute(x, CTX, xor_pairs(count, k << low))]
    ppermute x0 -> x2, starting transfers between devices: none -> 0.97 us  [sum_of_two(): lax.ppermute(x, CTX, xor_pairs(count, mask)).astype(F32)]
  transfers between devices with their start and end apart: 12 -> 11, of which waited for: 9 -> 9; matrix products, arithmetic and copies ran while one was open for 0% -> 0% of each run, Pallas kernels for 2% -> 2%
where the time goes in v11:
time: 79.5 us; the launch traced here: 79.2 us
  blocking collectives  34.2 us (43%)
  waiting for transfers between devices  19.6 us (25%)
  starting transfers between devices  18.1 us (23%)
  Pallas kernels  5.85 us (7%)
  other arithmetic  0.91 us (1%)
    all_to_all x1, blocking collectives, local(): lax.all_to_all(state.reshape(count, rows, state_size), CTX, split_axis=0,...  20.1 us
    all_to_all x1, blocking collectives, local(): lax.all_to_all(jnp.broadcast_to(column[None], (count // near, near, rows,...  14.2 us
    ppermute x2, waiting for transfers between devices, sum_of_two(): lax.ppermute(x, CTX, xor_pairs(count, mask)).astype(F32)  9.96 us
    ppermute x3, starting transfers between devices, local(): lax.ppermute(message, CTX, xor_pairs(count, k))  8.75 us
    ppermute x6, starting transfers between devices, sum_of_four(): lax.ppermute(x, CTX, xor_pairs(count, k << low))  8.36 us
    ppermute x6, waiting for transfers between devices, sum_of_four(): lax.ppermute(x, CTX, xor_pairs(count, k << low))  5.78 us
    ppermute x3, waiting for transfers between devices, local(): lax.ppermute(message, CTX, xor_pairs(count, k))  3.83 us
    pallas_call x1, Pallas kernels, local(): pl.pallas_call(functools.partial(project_kernel, rows, heads, latent), ou...  2.07 us
  transfers between devices with their start and end apart: 11, of which 9 were waited for; matrix products, arithmetic and copies ran while one was open for 0% of the time, Pallas kernels for 2%

profile of v11, /device:TPU:2, one launch (start us, length us, event | category | flops | bytes accessed | tf_op | source)
XLA Modules:
  0.0 79.2 jit_solution(10028751413845819590)
XLA Ops:
  0.0 0.8 message.1
  0.8 3.4 %collective-permute-start.2 = (bf16[2,1152]{1,0:T(2,128)(2,1)S(1)}, bf16[2,1152]{1,0:T(2,128)(2,1)S(1)}, u32[]{:S(2)}, u32[]{:S(2)}) collective-permute-start(bf16[2,1152]{1,0:T(2,128)(2,1)S(1)} %message.1), channel_id=1, source_target_pairs={{0,4},{4,0},{8,12},{12,8},{16,20},{20,16},{24,28},{28,24},{32,36},... | collective-permute-start | bytes 13832 | tf_op jit(solution)/shard_map/ppermute | solution.py:190
  4.2 5.4 %collective-permute-start.1 = (bf16[2,1152]{1,0:T(2,128)(2,1)S(1)}, bf16[2,1152]{1,0:T(2,128)(2,1)S(1)}, u32[]{:S(2)}, u32[]{:S(2)}) collective-permute-start(bf16[2,1152]{1,0:T(2,128)(2,1)S(1)} %message.1), channel_id=1, source_target_pairs={{0,8},{4,12},{8,0},{12,4},{16,24},{20,28},{24,16},{28,20},{32,40},... | collective-permute-start | bytes 13832 | tf_op jit(solution)/shard_map/ppermute | solution.py:190
  9.6 0.0 collective-permute-start
  9.6 1.9 %fetch.1 = (f32[2,512]{1,0:T(2,128)S(1)}, bf16[512,576]{1,0:T(8,128)(2,1)S(1)}, bf16[2,512,128]{2,1,0:T(8,128)(2,1)S(1)}, bf16[128,7168]{1,0:T(8,128)(2,1)S(1)}) custom-call(s32[1]{0:T(128)} %bitcast.here_ref, s32[2]{0:T(128)} %lengths_hbm.1, s32[2,256]{1,0:T(2,128)} %table_hbm.1, bf16[512,576]{1,0:T(8,128)(2,1)} %bitcast.2, bf16[2,512,128]{2,1,0:T(8,128)(2,1)} %w_uv_hbm.1, ...), custom_call_target="tpu_custom_call" | custom-call | bytes 5242880 | tf_op jit(solution)/shard_map/fetch/pallas_call | solution.py:192
  11.4 0.0 collective-permute-done.2
  11.4 0.2 collective-permute-done.1
  11.7 3.6 %collective-permute-done = bf16[2,1152]{1,0:T(2,128)(2,1)S(1)} collective-permute-done((bf16[2,1152]{1,0:T(2,128)(2,1)S(1)}, bf16[2,1152]{1,0:T(2,128)(2,1)S(1)}, u32[]{:S(2)}, u32[]{:S(2)}) %collective-permute-start) | collective-permute-done | bytes 4640 | tf_op jit(solution)/shard_map/ppermute | solution.py:190
  15.3 0.1 broadcast_select_fusion.1
  15.4 0.2 broadcast_in_dim.58
  15.5 14.2 %all_to_all.10 = bf16[16,4,2,1152]{3,2,1,0:T(2,128)(2,1)S(1)} all-to-all(bf16[16,4,2,1152]{3,2,1,0:T(2,128)(2,1)S(1)} %broadcast_in_dim.58), channel_id=1, replica_groups={{0,16,32,48,64,80,96,112,128,144,160,176,192,208,224,240},{4,20,36,52,6..., dimensions={0} | all-to-all | bytes 589824 | tf_op jit(solution)/shard_map/all_to_all | solution.py:218
  29.7 0.1 reshape.35.q_ref
  29.8 1.1 %attend.1 = bf16[128,1152]{1,0:T(8,128)(2,1)S(1)} custom-call(bf16[128,1152]{1,0:T(8,128)(2,1)S(1)} %reshape.35.q_ref, bf16[512,576]{1,0:T(8,128)(2,1)S(1)} %get-tuple-element.19.keys_ref, f32[2,512]{1,0:T(2,128)S(1)} %get-tuple-element.20.live_ref), custom_call_target="tpu_custom_call" | custom-call | tf_op jit(solution)/shard_map/attend/pallas_call | solution.py:224
  31.0 0.1 reshape.36
  31.1 20.1 %all_to_all.11 = bf16[64,2,1152]{2,1,0:T(2,128)(2,1)S(1)} all-to-all(bf16[64,2,1152]{2,1,0:T(2,128)(2,1)S(1)} %reshape.36), channel_id=1, replica_groups=mesh['ctx'=64,'grp'=4] {'ctx'}, dimensions={0} | all-to-all | bytes 589824 | tf_op jit(solution)/shard_map/all_to_all | solution.py:233
  51.2 0.1 reshape.37.state_ref
  51.3 2.1 %project.1 = bf16[2,7168]{1,0:T(2,128)(2,1)S(1)} custom-call(bf16[128,1152]{1,0:T(8,128)(2,1)S(1)} %reshape.37.state_ref, bf16[2,512,128]{2,1,0:T(8,128)(2,1)S(1)} %get-tuple-element.21.w_uv_ref, bf16[128,7168]{1,0:T(8,128)(2,1)S(1)} %get-tuple-element.22.first_ref, bf16[256,7168]{1,0:T(8,128)(2,1)} %w_out_hbm.3), custom_call_target="tpu_custom_call" | custom-call | tf_op jit(solution)/shard_map/project/pallas_call | solution.py:237
  53.4 0.6 collective-permute-start.3
  53.9 4.3 %collective-permute-done.3 = bf16[2,7168]{1,0:T(2,128)(2,1)S(1)} collective-permute-done((bf16[2,7168]{1,0:T(2,128)(2,1)S(1)}, bf16[2,7168]{1,0:T(2,128)(2,1)S(1)}, u32[]{:S(2)}, u32[]{:S(2)}) %collective-permute-start.3) | collective-permute-done | bytes 28704 | tf_op jit(solution)/shard_map/ppermute | solution.py:23
  58.2 0.4 collective-permute-start.4
  58.7 5.7 %collective-permute-done.4 = bf16[2,7168]{1,0:T(2,128)(2,1)S(1)} collective-permute-done((bf16[2,7168]{1,0:T(2,128)(2,1)S(1)}, bf16[2,7168]{1,0:T(2,128)(2,1)S(1)}, u32[]{:S(2)}, u32[]{:S(2)}) %collective-permute-start.4) | collective-permute-done | bytes 28704 | tf_op jit(solution)/shard_map/ppermute | solution.py:23
  64.4 0.2 collective-permute-start.7
  64.5 3.5 %collective-permute-start.6 = (bf16[2,7168]{1,0:T(2,128)(2,1)S(1)}, bf16[2,7168]{1,0:T(2,128)(2,1)S(1)}, u32[]{:S(2)}, u32[]{:S(2)}) collective-permute-start(bf16[2,7168]{1,0:T(2,128)(2,1)S(1)} %add_convert_fusion.2), channel_id=1, source_target_pairs={{0,128},{4,132},{8,136},{12,140},{16,144},{20,148},{24,152},{28,15... | collective-permute-start | bytes 86024 | tf_op jit(solution)/shard_map/ppermute | solution.py:27
  68.0 0.5 collective-permute-start.5
  68.5 0.0 collective-permute-done.7
  68.5 1.4 %collective-permute-done.6 = bf16[2,7168]{1,0:T(2,128)(2,1)S(1)} collective-permute-done((bf16[2,7168]{1,0:T(2,128)(2,1)S(1)}, bf16[2,7168]{1,0:T(2,128)(2,1)S(1)}, u32[]{:S(2)}, u32[]{:S(2)}) %collective-permute-start.6) | collective-permute-done | bytes 28704 | tf_op jit(solution)/shard_map/ppermute | solution.py:27
  69.9 2.0 %collective-permute-done.5 = bf16[2,7168]{1,0:T(2,128)(2,1)S(1)} collective-permute-done((bf16[2,7168]{1,0:T(2,128)(2,1)S(1)}, bf16[2,7168]{1,0:T(2,128)(2,1)S(1)}, u32[]{:S(2)}, u32[]{:S(2)}) %collective-permute-start.5) | collective-permute-done | bytes 28704 | tf_op jit(solution)/shard_map/ppermute | solution.py:27
  71.9 0.1 add_convert_fusion.1
  72.0 0.6 collective-permute-start.10
  72.5 2.2 %collective-permute-start.9 = (bf16[2,7168]{1,0:T(2,128)(2,1)S(1)}, bf16[2,7168]{1,0:T(2,128)(2,1)S(1)}, u32[]{:S(2)}, u32[]{:S(2)}) collective-permute-start(bf16[2,7168]{1,0:T(2,128)(2,1)S(1)} %add_convert_fusion.1), channel_id=1, source_target_pairs={{0,32},{4,36},{8,40},{12,44},{16,48},{20,52},{24,56},{28,60},{32,0... | collective-permute-start | bytes 86024 | tf_op jit(solution)/shard_map/ppermute | solution.py:27
  74.7 1.4 %collective-permute-start.8 = (bf16[2,7168]{1,0:T(2,128)(2,1)S(1)}, bf16[2,7168]{1,0:T(2,128)(2,1)S(1)}, u32[]{:S(2)}, u32[]{:S(2)}) collective-permute-start(bf16[2,7168]{1,0:T(2,128)(2,1)S(1)} %add_convert_fusion.1), channel_id=1, source_target_pairs={{0,16},{4,20},{8,24},{12,28},{16,0},{20,4},{24,8},{28,12},{32,48},... | collective-permute-start | bytes 86024 | tf_op jit(solution)/shard_map/ppermute | solution.py:27
  76.1 1.0 %collective-permute-done.10 = bf16[2,7168]{1,0:T(2,128)(2,1)S(1)} collective-permute-done((bf16[2,7168]{1,0:T(2,128)(2,1)S(1)}, bf16[2,7168]{1,0:T(2,128)(2,1)S(1)}, u32[]{:S(2)}, u32[]{:S(2)}) %collective-permute-start.10) | collective-permute-done | bytes 28704 | tf_op jit(solution)/shard_map/ppermute | solution.py:27
  77.1 0.8 collective-permute-done.9
  77.9 0.7 collective-permute-done.8
  78.6 0.7 add_convert_fusion
  (4 shorter events, 0.1 us)
Async XLA Ops:
  0.8 10.6 %collective-permute-start.2 = (bf16[2,1152]{1,0:T(2,128)(2,1)S(1)}, bf16[2,1152]{1,0:T(2,128)(2,1)S(1)}, u32[]{:S(2)}, u32[]{:S(2)}) collective-permute-start(bf16[2,1152]{1,0:T(2,128)(2,1)S(1)} %message.1), channel_id=1, source_target_pairs={{0,4},{4,0},{8,12},{12,8},{16,20},{20,16},{24,28},{28,24},{32,36},... | collective-permute-start | bytes 13832 | tf_op jit(solution)/shard_map/ppermute | solution.py:190
  4.2 7.5 %collective-permute-start.1 = (bf16[2,1152]{1,0:T(2,128)(2,1)S(1)}, bf16[2,1152]{1,0:T(2,128)(2,1)S(1)}, u32[]{:S(2)}, u32[]{:S(2)}) collective-permute-start(bf16[2,1152]{1,0:T(2,128)(2,1)S(1)} %message.1), channel_id=1, source_target_pairs={{0,8},{4,12},{8,0},{12,4},{16,24},{20,28},{24,16},{28,20},{32,40},... | collective-permute-start | bytes 13832 | tf_op jit(solution)/shard_map/ppermute | solution.py:190
  9.6 5.7 %collective-permute-start = (bf16[2,1152]{1,0:T(2,128)(2,1)S(1)}, bf16[2,1152]{1,0:T(2,128)(2,1)S(1)}, u32[]{:S(2)}, u32[]{:S(2)}) collective-permute-start(bf16[2,1152]{1,0:T(2,128)(2,1)S(1)} %message.1), channel_id=1, source_target_pairs={{0,12},{4,8},{8,4},{12,0},{16,28},{20,24},{24,20},{28,16},{32,44},... | collective-permute-start | bytes 13832 | tf_op jit(solution)/shard_map/ppermute | solution.py:190
  53.4 4.9 %collective-permute-start.3 = (bf16[2,7168]{1,0:T(2,128)(2,1)S(1)}, bf16[2,7168]{1,0:T(2,128)(2,1)S(1)}, u32[]{:S(2)}, u32[]{:S(2)}) collective-permute-start(bf16[2,7168]{1,0:T(2,128)(2,1)S(1)} %project.1), channel_id=1, source_target_pairs={{0,4},{4,0},{8,12},{12,8},{16,20},{20,16},{24,28},{28,24},{32,36},... | collective-permute-start | bytes 86024 | tf_op jit(solution)/shard_map/ppermute | solution.py:23
  58.2 6.1 %collective-permute-start.4 = (bf16[2,7168]{1,0:T(2,128)(2,1)S(1)}, bf16[2,7168]{1,0:T(2,128)(2,1)S(1)}, u32[]{:S(2)}, u32[]{:S(2)}) collective-permute-start(bf16[2,7168]{1,0:T(2,128)(2,1)S(1)} %add_convert_fusion.3), channel_id=1, source_target_pairs={{0,12},{4,8},{8,4},{12,0},{16,28},{20,24},{24,20},{28,16},{32,44},... | collective-permute-start | bytes 86024 | tf_op jit(solution)/shard_map/ppermute | solution.py:23
  64.4 4.2 %collective-permute-start.7 = (bf16[2,7168]{1,0:T(2,128)(2,1)S(1)}, bf16[2,7168]{1,0:T(2,128)(2,1)S(1)}, u32[]{:S(2)}, u32[]{:S(2)}) collective-permute-start(bf16[2,7168]{1,0:T(2,128)(2,1)S(1)} %add_convert_fusion.2), channel_id=1, source_target_pairs={{0,192},{4,196},{8,200},{12,204},{16,208},{20,212},{24,216},{28,22... | collective-permute-start | bytes 86024 | tf_op jit(solution)/shard_map/ppermute | solution.py:27
  64.5 5.4 %collective-permute-start.6 = (bf16[2,7168]{1,0:T(2,128)(2,1)S(1)}, bf16[2,7168]{1,0:T(2,128)(2,1)S(1)}, u32[]{:S(2)}, u32[]{:S(2)}) collective-permute-start(bf16[2,7168]{1,0:T(2,128)(2,1)S(1)} %add_convert_fusion.2), channel_id=1, source_target_pairs={{0,128},{4,132},{8,136},{12,140},{16,144},{20,148},{24,152},{28,15... | collective-permute-start | bytes 86024 | tf_op jit(solution)/shard_map/ppermute | solution.py:27
  68.0 3.9 %collective-permute-start.5 = (bf16[2,7168]{1,0:T(2,128)(2,1)S(1)}, bf16[2,7168]{1,0:T(2,128)(2,1)S(1)}, u32[]{:S(2)}, u32[]{:S(2)}) collective-permute-start(bf16[2,7168]{1,0:T(2,128)(2,1)S(1)} %add_convert_fusion.2), channel_id=1, source_target_pairs={{0,64},{4,68},{8,72},{12,76},{16,80},{20,84},{24,88},{28,92},{32,9... | collective-permute-start | bytes 86024 | tf_op jit(solution)/shard_map/ppermute | solution.py:27
  72.0 5.2 %collective-permute-start.10 = (bf16[2,7168]{1,0:T(2,128)(2,1)S(1)}, bf16[2,7168]{1,0:T(2,128)(2,1)S(1)}, u32[]{:S(2)}, u32[]{:S(2)}) collective-permute-start(bf16[2,7168]{1,0:T(2,128)(2,1)S(1)} %add_convert_fusion.1), channel_id=1, source_target_pairs={{0,48},{4,52},{8,56},{12,60},{16,32},{20,36},{24,40},{28,44},{32,1... | collective-permute-start | bytes 86024 | tf_op jit(solution)/shard_map/ppermute | solution.py:27
  72.5 5.4 %collective-permute-start.9 = (bf16[2,7168]{1,0:T(2,128)(2,1)S(1)}, bf16[2,7168]{1,0:T(2,128)(2,1)S(1)}, u32[]{:S(2)}, u32[]{:S(2)}) collective-permute-start(bf16[2,7168]{1,0:T(2,128)(2,1)S(1)} %add_convert_fusion.1), channel_id=1, source_target_pairs={{0,32},{4,36},{8,40},{12,44},{16,48},{20,52},{24,56},{28,60},{32,0... | collective-permute-start | bytes 86024 | tf_op jit(solution)/shard_map/ppermute | solution.py:27
  74.7 3.9 %collective-permute-start.8 = (bf16[2,7168]{1,0:T(2,128)(2,1)S(1)}, bf16[2,7168]{1,0:T(2,128)(2,1)S(1)}, u32[]{:S(2)}, u32[]{:S(2)}) collective-permute-start(bf16[2,7168]{1,0:T(2,128)(2,1)S(1)} %add_convert_fusion.1), channel_id=1, source_target_pairs={{0,16},{4,20},{8,24},{12,28},{16,0},{20,4},{24,8},{28,12},{32,48},... | collective-permute-start | bytes 86024 | tf_op jit(solution)/shard_map/ppermute | solution.py:27

commit v12 on v10

--- a/solution.py
+++ b/solution.py
@@ -20,7 +20,7 @@
 
 
 def sum_of_four(x, count, low):
-    a, b, c = (lax.ppermute(x, CTX, xor_pairs(count, k << low)) for k in (1, 2, 3))
+    a, c, b = (lax.ppermute(x, CTX, xor_pairs(count, k << low)) for k in (1, 3, 2))
     return (x.astype(F32) + a.astype(F32)) + (b.astype(F32) + c.astype(F32))
 
 
@@ -183,7 +183,7 @@
     )(stay(q_latent), stay(q_rope))
 
     near = 4
-    others = [lax.ppermute(message, CTX, xor_pairs(count, k)) for k in range(1, near)]
+    others = {k: lax.ppermute(message, CTX, xor_pairs(count, k)) for k in (1, 3, 2)}
     split = w_out.shape[0] // 2
     live, keys, w_uv, w_first = pl.pallas_call(
         functools.partial(fetch_kernel, page_len),
@@ -208,7 +208,7 @@
     away = lax.broadcasted_iota(jnp.int32, (near, 1, 1), 0) ^ (here % near)
     column = jnp.broadcast_to(message[None], (near, rows, size))
     for k in range(1, near):
-        column = jnp.where(away == k, others[k - 1][None], column)
+        column = jnp.where(away == k, others[k][None], column)
     column, live, keys, w_uv, w_first = lax.optimization_barrier((column, live, keys, w_uv, w_first))
     planes = [[i * near + k for i in range(count // near)] for k in range(near)]
     query = lax.all_to_all(

time: 77.9 us -> 77.9 us (level)
  no operation moved by 1% of the time
where the time goes in v12:
time: 77.9 us; the launch traced here: 77.6 us
  blocking collectives  34.2 us (44%)
  starting transfers between devices  23.7 us (30%)
  waiting for transfers between devices  12.3 us (16%)
  Pallas kernels  5.85 us (8%)
  other arithmetic  0.91 us (1%)
    all_to_all x1, blocking collectives, local(): lax.all_to_all(state.reshape(count, rows, state_size), CTX, split_axis=0,...  20.1 us
    ppermute x9, starting transfers between devices, sum_of_four(): lax.ppermute(x, CTX, xor_pairs(count, k << low))  14.9 us
    all_to_all x1, blocking collectives, local(): lax.all_to_all(jnp.broadcast_to(column[None], (count // near, near, rows,...  14.2 us
    ppermute x3, starting transfers between devices, local(): lax.ppermute(message, CTX, xor_pairs(count, k))  8.75 us
    ppermute x9, waiting for transfers between devices, sum_of_four(): lax.ppermute(x, CTX, xor_pairs(count, k << low))  8.46 us
    ppermute x3, waiting for transfers between devices, local(): lax.ppermute(message, CTX, xor_pairs(count, k))  3.83 us
    pallas_call x1, Pallas kernels, local(): pl.pallas_call(functools.partial(project_kernel, rows, heads, latent), ou...  2.07 us
    pallas_call x1, Pallas kernels, local(): pl.pallas_call(functools.partial(fetch_kernel, page_len), out_shape=(pltp...  1.85 us
  transfers between devices with their start and end apart: 12, of which 9 were waited for; matrix products, arithmetic and copies ran while one was open for 0% of the time, Pallas kernels for 2%

profile of v12, /device:TPU:2, one launch (start us, length us, event | category | flops | bytes accessed | tf_op | source)
XLA Modules:
  0.0 77.6 jit_solution(16209297149909705660)
XLA Ops:
  0.0 0.8 %message.1 = bf16[2,1152]{1,0:T(2,128)(2,1)S(1)} custom-call(bf16[2,2,512]{2,1,0:T(2,128)(2,1)} %q_latent_hbm.1, bf16[2,2,64]{2,1,0:T(2,128)(2,1)} %q_rope_hbm.1), custom_call_target="tpu_custom_call" | custom-call | tf_op jit(solution)/shard_map/message/pallas_call | solution.py:175
  0.8 3.4 %collective-permute-start.2 = (bf16[2,1152]{1,0:T(2,128)(2,1)S(1)}, bf16[2,1152]{1,0:T(2,128)(2,1)S(1)}, u32[]{:S(2)}, u32[]{:S(2)}) collective-permute-start(bf16[2,1152]{1,0:T(2,128)(2,1)S(1)} %message.1), channel_id=1, source_target_pairs={{0,4},{4,0},{8,12},{12,8},{16,20},{20,16},{24,28},{28,24},{32,36},... | collective-permute-start | bytes 13832 | tf_op jit(solution)/shard_map/ppermute | solution.py:186
  4.2 5.4 %collective-permute-start.1 = (bf16[2,1152]{1,0:T(2,128)(2,1)S(1)}, bf16[2,1152]{1,0:T(2,128)(2,1)S(1)}, u32[]{:S(2)}, u32[]{:S(2)}) collective-permute-start(bf16[2,1152]{1,0:T(2,128)(2,1)S(1)} %message.1), channel_id=1, source_target_pairs={{0,8},{4,12},{8,0},{12,4},{16,24},{20,28},{24,16},{28,20},{32,40},... | collective-permute-start | bytes 13832 | tf_op jit(solution)/shard_map/ppermute | solution.py:186
  9.6 0.0 collective-permute-start
  9.6 1.9 %fetch.1 = (f32[2,512]{1,0:T(2,128)S(1)}, bf16[512,576]{1,0:T(8,128)(2,1)S(1)}, bf16[2,512,128]{2,1,0:T(8,128)(2,1)S(1)}, bf16[128,7168]{1,0:T(8,128)(2,1)S(1)}) custom-call(s32[1]{0:T(128)} %bitcast.here_ref, s32[2]{0:T(128)} %lengths_hbm.1, s32[2,256]{1,0:T(2,128)} %table_hbm.1, bf16[512,576]{1,0:T(8,128)(2,1)} %bitcast.2, bf16[2,512,128]{2,1,0:T(8,128)(2,1)} %w_uv_hbm.1, ...), custom_call_target="tpu_custom_call" | custom-call | bytes 5242880 | tf_op jit(solution)/shard_map/fetch/pallas_call | solution.py:188
  11.4 0.0 collective-permute-done.2
  11.4 0.2 collective-permute-done.1
  11.7 3.6 %collective-permute-done = bf16[2,1152]{1,0:T(2,128)(2,1)S(1)} collective-permute-done((bf16[2,1152]{1,0:T(2,128)(2,1)S(1)}, bf16[2,1152]{1,0:T(2,128)(2,1)S(1)}, u32[]{:S(2)}, u32[]{:S(2)}) %collective-permute-start) | collective-permute-done | bytes 4640 | tf_op jit(solution)/shard_map/ppermute | solution.py:186
  15.3 0.1 broadcast_select_fusion.1
  15.4 0.2 broadcast_in_dim.58
  15.5 14.2 %all_to_all.10 = bf16[16,4,2,1152]{3,2,1,0:T(2,128)(2,1)S(1)} all-to-all(bf16[16,4,2,1152]{3,2,1,0:T(2,128)(2,1)S(1)} %broadcast_in_dim.58), channel_id=1, replica_groups={{0,16,32,48,64,80,96,112,128,144,160,176,192,208,224,240},{4,20,36,52,6..., dimensions={0} | all-to-all | bytes 589824 | tf_op jit(solution)/shard_map/all_to_all | solution.py:214
  29.7 0.1 reshape.35.q_ref
  29.8 1.1 %attend.1 = bf16[128,1152]{1,0:T(8,128)(2,1)S(1)} custom-call(bf16[128,1152]{1,0:T(8,128)(2,1)S(1)} %reshape.35.q_ref, bf16[512,576]{1,0:T(8,128)(2,1)S(1)} %get-tuple-element.19.keys_ref, f32[2,512]{1,0:T(2,128)S(1)} %get-tuple-element.20.live_ref), custom_call_target="tpu_custom_call" | custom-call | tf_op jit(solution)/shard_map/attend/pallas_call | solution.py:220
  31.0 0.1 reshape.36
  31.1 20.1 %all_to_all.11 = bf16[64,2,1152]{2,1,0:T(2,128)(2,1)S(1)} all-to-all(bf16[64,2,1152]{2,1,0:T(2,128)(2,1)S(1)} %reshape.36), channel_id=1, replica_groups=mesh['ctx'=64,'grp'=4] {'ctx'}, dimensions={0} | all-to-all | bytes 589824 | tf_op jit(solution)/shard_map/all_to_all | solution.py:229
  51.2 0.1 reshape.37.state_ref
  51.3 2.1 %project.1 = bf16[2,7168]{1,0:T(2,128)(2,1)S(1)} custom-call(bf16[128,1152]{1,0:T(8,128)(2,1)S(1)} %reshape.37.state_ref, bf16[2,512,128]{2,1,0:T(8,128)(2,1)S(1)} %get-tuple-element.21.w_uv_ref, bf16[128,7168]{1,0:T(8,128)(2,1)S(1)} %get-tuple-element.22.first_ref, bf16[256,7168]{1,0:T(8,128)(2,1)} %w_out_hbm.3), custom_call_target="tpu_custom_call" | custom-call | tf_op jit(solution)/shard_map/project/pallas_call | solution.py:233
  53.4 0.1 collective-permute-start.5
  53.5 3.5 %collective-permute-start.4 = (bf16[2,7168]{1,0:T(2,128)(2,1)S(1)}, bf16[2,7168]{1,0:T(2,128)(2,1)S(1)}, u32[]{:S(2)}, u32[]{:S(2)}) collective-permute-start(bf16[2,7168]{1,0:T(2,128)(2,1)S(1)} %project.1), channel_id=1, source_target_pairs={{0,128},{4,132},{8,136},{12,140},{16,144},{20,148},{24,152},{28,15... | collective-permute-start | bytes 86024 | tf_op jit(solution)/shard_map/ppermute | solution.py:23
  57.0 0.5 collective-permute-start.3
  57.5 0.0 collective-permute-done.5
  57.5 1.4 %collective-permute-done.4 = bf16[2,7168]{1,0:T(2,128)(2,1)S(1)} collective-permute-done((bf16[2,7168]{1,0:T(2,128)(2,1)S(1)}, bf16[2,7168]{1,0:T(2,128)(2,1)S(1)}, u32[]{:S(2)}, u32[]{:S(2)}) %collective-permute-start.4) | collective-permute-done | bytes 28704 | tf_op jit(solution)/shard_map/ppermute | solution.py:23
  58.9 1.9 %collective-permute-done.3 = bf16[2,7168]{1,0:T(2,128)(2,1)S(1)} collective-permute-done((bf16[2,7168]{1,0:T(2,128)(2,1)S(1)}, bf16[2,7168]{1,0:T(2,128)(2,1)S(1)}, u32[]{:S(2)}, u32[]{:S(2)}) %collective-permute-start.3) | collective-permute-done | bytes 28704 | tf_op jit(solution)/shard_map/ppermute | solution.py:23
  60.9 0.1 add_convert_fusion.2
  60.9 0.6 collective-permute-start.8
  61.5 2.1 %collective-permute-start.7 = (bf16[2,7168]{1,0:T(2,128)(2,1)S(1)}, bf16[2,7168]{1,0:T(2,128)(2,1)S(1)}, u32[]{:S(2)}, u32[]{:S(2)}) collective-permute-start(bf16[2,7168]{1,0:T(2,128)(2,1)S(1)} %add_convert_fusion.2), channel_id=1, source_target_pairs={{0,32},{4,36},{8,40},{12,44},{16,48},{20,52},{24,56},{28,60},{32,0... | collective-permute-start | bytes 86024 | tf_op jit(solution)/shard_map/ppermute | solution.py:23
  63.7 1.4 %collective-permute-start.6 = (bf16[2,7168]{1,0:T(2,128)(2,1)S(1)}, bf16[2,7168]{1,0:T(2,128)(2,1)S(1)}, u32[]{:S(2)}, u32[]{:S(2)}) collective-permute-start(bf16[2,7168]{1,0:T(2,128)(2,1)S(1)} %add_convert_fusion.2), channel_id=1, source_target_pairs={{0,16},{4,20},{8,24},{12,28},{16,0},{20,4},{24,8},{28,12},{32,48},... | collective-permute-start | bytes 86024 | tf_op jit(solution)/shard_map/ppermute | solution.py:23
  65.1 1.0 %collective-permute-done.8 = bf16[2,7168]{1,0:T(2,128)(2,1)S(1)} collective-permute-done((bf16[2,7168]{1,0:T(2,128)(2,1)S(1)}, bf16[2,7168]{1,0:T(2,128)(2,1)S(1)}, u32[]{:S(2)}, u32[]{:S(2)}) %collective-permute-start.8) | collective-permute-done | bytes 28704 | tf_op jit(solution)/shard_map/ppermute | solution.py:23
  66.1 0.8 %collective-permute-done.7 = bf16[2,7168]{1,0:T(2,128)(2,1)S(1)} collective-permute-done((bf16[2,7168]{1,0:T(2,128)(2,1)S(1)}, bf16[2,7168]{1,0:T(2,128)(2,1)S(1)}, u32[]{:S(2)}, u32[]{:S(2)}) %collective-permute-start.7) | collective-permute-done | bytes 28704 | tf_op jit(solution)/shard_map/ppermute | solution.py:23
  66.9 0.6 collective-permute-done.6
  67.5 0.1 add_convert_fusion.1
  67.6 1.0 %collective-permute-start.11 = (bf16[2,7168]{1,0:T(2,128)(2,1)S(1)}, bf16[2,7168]{1,0:T(2,128)(2,1)S(1)}, u32[]{:S(2)}, u32[]{:S(2)}) collective-permute-start(bf16[2,7168]{1,0:T(2,128)(2,1)S(1)} %add_convert_fusion.1), channel_id=1, source_target_pairs={{0,12},{4,8},{8,4},{12,0},{16,28},{20,24},{24,20},{28,16},{32,44},... | collective-permute-start | bytes 86024 | tf_op jit(solution)/shard_map/ppermute | solution.py:23
  68.6 3.2 %collective-permute-start.10 = (bf16[2,7168]{1,0:T(2,128)(2,1)S(1)}, bf16[2,7168]{1,0:T(2,128)(2,1)S(1)}, u32[]{:S(2)}, u32[]{:S(2)}) collective-permute-start(bf16[2,7168]{1,0:T(2,128)(2,1)S(1)} %add_convert_fusion.1), channel_id=1, source_target_pairs={{0,8},{4,12},{8,0},{12,4},{16,24},{20,28},{24,16},{28,20},{32,40},... | collective-permute-start | bytes 86024 | tf_op jit(solution)/shard_map/ppermute | solution.py:23
  71.8 2.4 %collective-permute-start.9 = (bf16[2,7168]{1,0:T(2,128)(2,1)S(1)}, bf16[2,7168]{1,0:T(2,128)(2,1)S(1)}, u32[]{:S(2)}, u32[]{:S(2)}) collective-permute-start(bf16[2,7168]{1,0:T(2,128)(2,1)S(1)} %add_convert_fusion.1), channel_id=1, source_target_pairs={{0,4},{4,0},{8,12},{12,8},{16,20},{20,16},{24,28},{28,24},{32,36},... | collective-permute-start | bytes 86024 | tf_op jit(solution)/shard_map/ppermute | solution.py:23
  74.2 0.0 collective-permute-done.11
  74.2 2.2 %collective-permute-done.10 = bf16[2,7168]{1,0:T(2,128)(2,1)S(1)} collective-permute-done((bf16[2,7168]{1,0:T(2,128)(2,1)S(1)}, bf16[2,7168]{1,0:T(2,128)(2,1)S(1)}, u32[]{:S(2)}, u32[]{:S(2)}) %collective-permute-start.10) | collective-permute-done | bytes 28704 | tf_op jit(solution)/shard_map/ppermute | solution.py:23
  76.4 0.5 collective-permute-done.9
  76.9 0.7 add_convert_fusion
  (2 shorter events, 0.0 us)
Async XLA Ops:
  0.8 10.6 %collective-permute-start.2 = (bf16[2,1152]{1,0:T(2,128)(2,1)S(1)}, bf16[2,1152]{1,0:T(2,128)(2,1)S(1)}, u32[]{:S(2)}, u32[]{:S(2)}) collective-permute-start(bf16[2,1152]{1,0:T(2,128)(2,1)S(1)} %message.1), channel_id=1, source_target_pairs={{0,4},{4,0},{8,12},{12,8},{16,20},{20,16},{24,28},{28,24},{32,36},... | collective-permute-start | bytes 13832 | tf_op jit(solution)/shard_map/ppermute | solution.py:186
  4.2 7.5 %collective-permute-start.1 = (bf16[2,1152]{1,0:T(2,128)(2,1)S(1)}, bf16[2,1152]{1,0:T(2,128)(2,1)S(1)}, u32[]{:S(2)}, u32[]{:S(2)}) collective-permute-start(bf16[2,1152]{1,0:T(2,128)(2,1)S(1)} %message.1), channel_id=1, source_target_pairs={{0,8},{4,12},{8,0},{12,4},{16,24},{20,28},{24,16},{28,20},{32,40},... | collective-permute-start | bytes 13832 | tf_op jit(solution)/shard_map/ppermute | solution.py:186
  9.6 5.7 %collective-permute-start = (bf16[2,1152]{1,0:T(2,128)(2,1)S(1)}, bf16[2,1152]{1,0:T(2,128)(2,1)S(1)}, u32[]{:S(2)}, u32[]{:S(2)}) collective-permute-start(bf16[2,1152]{1,0:T(2,128)(2,1)S(1)} %message.1), channel_id=1, source_target_pairs={{0,12},{4,8},{8,4},{12,0},{16,28},{20,24},{24,20},{28,16},{32,44},... | collective-permute-start | bytes 13832 | tf_op jit(solution)/shard_map/ppermute | solution.py:186
  53.4 4.2 %collective-permute-start.5 = (bf16[2,7168]{1,0:T(2,128)(2,1)S(1)}, bf16[2,7168]{1,0:T(2,128)(2,1)S(1)}, u32[]{:S(2)}, u32[]{:S(2)}) collective-permute-start(bf16[2,7168]{1,0:T(2,128)(2,1)S(1)} %project.1), channel_id=1, source_target_pairs={{0,192},{4,196},{8,200},{12,204},{16,208},{20,212},{24,216},{28,22... | collective-permute-start | bytes 86024 | tf_op jit(solution)/shard_map/ppermute | solution.py:23
  53.5 5.4 %collective-permute-start.4 = (bf16[2,7168]{1,0:T(2,128)(2,1)S(1)}, bf16[2,7168]{1,0:T(2,128)(2,1)S(1)}, u32[]{:S(2)}, u32[]{:S(2)}) collective-permute-start(bf16[2,7168]{1,0:T(2,128)(2,1)S(1)} %project.1), channel_id=1, source_target_pairs={{0,128},{4,132},{8,136},{12,140},{16,144},{20,148},{24,152},{28,15... | collective-permute-start | bytes 86024 | tf_op jit(solution)/shard_map/ppermute | solution.py:23
  57.0 3.9 %collective-permute-start.3 = (bf16[2,7168]{1,0:T(2,128)(2,1)S(1)}, bf16[2,7168]{1,0:T(2,128)(2,1)S(1)}, u32[]{:S(2)}, u32[]{:S(2)}) collective-permute-start(bf16[2,7168]{1,0:T(2,128)(2,1)S(1)} %project.1), channel_id=1, source_target_pairs={{0,64},{4,68},{8,72},{12,76},{16,80},{20,84},{24,88},{28,92},{32,9... | collective-permute-start | bytes 86024 | tf_op jit(solution)/shard_map/ppermute | solution.py:23
  60.9 5.2 %collective-permute-start.8 = (bf16[2,7168]{1,0:T(2,128)(2,1)S(1)}, bf16[2,7168]{1,0:T(2,128)(2,1)S(1)}, u32[]{:S(2)}, u32[]{:S(2)}) collective-permute-start(bf16[2,7168]{1,0:T(2,128)(2,1)S(1)} %add_convert_fusion.2), channel_id=1, source_target_pairs={{0,48},{4,52},{8,56},{12,60},{16,32},{20,36},{24,40},{28,44},{32,1... | collective-permute-start | bytes 86024 | tf_op jit(solution)/shard_map/ppermute | solution.py:23
  61.5 5.4 %collective-permute-start.7 = (bf16[2,7168]{1,0:T(2,128)(2,1)S(1)}, bf16[2,7168]{1,0:T(2,128)(2,1)S(1)}, u32[]{:S(2)}, u32[]{:S(2)}) collective-permute-start(bf16[2,7168]{1,0:T(2,128)(2,1)S(1)} %add_convert_fusion.2), channel_id=1, source_target_pairs={{0,32},{4,36},{8,40},{12,44},{16,48},{20,52},{24,56},{28,60},{32,0... | collective-permute-start | bytes 86024 | tf_op jit(solution)/shard_map/ppermute | solution.py:23
  63.7 3.9 %collective-permute-start.6 = (bf16[2,7168]{1,0:T(2,128)(2,1)S(1)}, bf16[2,7168]{1,0:T(2,128)(2,1)S(1)}, u32[]{:S(2)}, u32[]{:S(2)}) collective-permute-start(bf16[2,7168]{1,0:T(2,128)(2,1)S(1)} %add_convert_fusion.2), channel_id=1, source_target_pairs={{0,16},{4,20},{8,24},{12,28},{16,0},{20,4},{24,8},{28,12},{32,48},... | collective-permute-start | bytes 86024 | tf_op jit(solution)/shard_map/ppermute | solution.py:23
  67.6 6.6 %collective-permute-start.11 = (bf16[2,7168]{1,0:T(2,128)(2,1)S(1)}, bf16[2,7168]{1,0:T(2,128)(2,1)S(1)}, u32[]{:S(2)}, u32[]{:S(2)}) collective-permute-start(bf16[2,7168]{1,0:T(2,128)(2,1)S(1)} %add_convert_fusion.1), channel_id=1, source_target_pairs={{0,12},{4,8},{8,4},{12,0},{16,28},{20,24},{24,20},{28,16},{32,44},... | collective-permute-start | bytes 86024 | tf_op jit(solution)/shard_map/ppermute | solution.py:23
  68.6 7.8 %collective-permute-start.10 = (bf16[2,7168]{1,0:T(2,128)(2,1)S(1)}, bf16[2,7168]{1,0:T(2,128)(2,1)S(1)}, u32[]{:S(2)}, u32[]{:S(2)}) collective-permute-start(bf16[2,7168]{1,0:T(2,128)(2,1)S(1)} %add_convert_fusion.1), channel_id=1, source_target_pairs={{0,8},{4,12},{8,0},{12,4},{16,24},{20,28},{24,16},{28,20},{32,40},... | collective-permute-start | bytes 86024 | tf_op jit(solution)/shard_map/ppermute | solution.py:23
  71.8 5.1 %collective-permute-start.9 = (bf16[2,7168]{1,0:T(2,128)(2,1)S(1)}, bf16[2,7168]{1,0:T(2,128)(2,1)S(1)}, u32[]{:S(2)}, u32[]{:S(2)}) collective-permute-start(bf16[2,7168]{1,0:T(2,128)(2,1)S(1)} %add_convert_fusion.1), channel_id=1, source_target_pairs={{0,4},{4,0},{8,12},{12,8},{16,20},{20,16},{24,28},{28,24},{32,36},... | collective-permute-start | bytes 86024 | tf_op jit(solution)/shard_map/ppermute | solution.py:23

commit v13 on v12

--- a/solution.py
+++ b/solution.py
@@ -21,7 +21,7 @@
 
 def sum_of_four(x, count, low):
     a, c, b = (lax.ppermute(x, CTX, xor_pairs(count, k << low)) for k in (1, 3, 2))
-    return (x.astype(F32) + a.astype(F32)) + (b.astype(F32) + c.astype(F32))
+    return (x.astype(F32) + a.astype(F32)) + (c.astype(F32) + b.astype(F32))
 
 
 def message_kernel(q_latent_hbm, q_rope_hbm, message_ref, q_latent_ref, q_rope_ref, sems):
@@ -207,7 +207,7 @@
     )
     away = lax.broadcasted_iota(jnp.int32, (near, 1, 1), 0) ^ (here % near)
     column = jnp.broadcast_to(message[None], (near, rows, size))
-    for k in range(1, near):
+    for k in (2, 1, 3):
         column = jnp.where(away == k, others[k][None], column)
     column, live, keys, w_uv, w_first = lax.optimization_barrier((column, live, keys, w_uv, w_first))
     planes = [[i * near + k for i in range(count // near)] for k in range(near)]

time: 77.9 us -> 77.3 us (level)
  no operation moved by 1% of the time
where the time goes in v13:
time: 77.3 us; the launch traced here: 77.1 us
  blocking collectives  34 us (44%)
  starting transfers between devices  23.7 us (31%)
  waiting for transfers between devices  12.1 us (16%)
  Pallas kernels  5.85 us (8%)
  other arithmetic  0.91 us (1%)
    all_to_all x1, blocking collectives, local(): lax.all_to_all(state.reshape(count, rows, state_size), CTX, split_axis=0,...  19.8 us
    ppermute x9, starting transfers between devices, sum_of_four(): lax.ppermute(x, CTX, xor_pairs(count, k << low))  14.9 us
    all_to_all x1, blocking collectives, local(): lax.all_to_all(jnp.broadcast_to(column[None], (count // near, near, rows,...  14.2 us
    ppermute x3, starting transfers between devices, local(): lax.ppermute(message, CTX, xor_pairs(count, k))  8.75 us
    ppermute x9, waiting for transfers between devices, sum_of_four(): lax.ppermute(x, CTX, xor_pairs(count, k << low))  8.27 us
    ppermute x3, waiting for transfers between devices, local(): lax.ppermute(message, CTX, xor_pairs(count, k))  3.83 us
    pallas_call x1, Pallas kernels, local(): pl.pallas_call(functools.partial(project_kernel, rows, heads, latent), ou...  2.07 us
    pallas_call x1, Pallas kernels, local(): pl.pallas_call(functools.partial(fetch_kernel, page_len), out_shape=(pltp...  1.85 us
  transfers between devices with their start and end apart: 12, of which 9 were waited for; matrix products, arithmetic and copies ran while one was open for 0% of the time, Pallas kernels for 2%

profile of v13, /device:TPU:2, one launch (start us, length us, event | category | flops | bytes accessed | tf_op | source)
XLA Modules:
  0.0 77.1 jit_solution(15352370184329492701)
XLA Ops:
  0.0 0.8 %message.1 = bf16[2,1152]{1,0:T(2,128)(2,1)S(1)} custom-call(bf16[2,2,512]{2,1,0:T(2,128)(2,1)} %q_latent_hbm.1, bf16[2,2,64]{2,1,0:T(2,128)(2,1)} %q_rope_hbm.1), custom_call_target="tpu_custom_call" | custom-call | tf_op jit(solution)/shard_map/message/pallas_call | solution.py:175
  0.8 7.3 %collective-permute-start.2 = (bf16[2,1152]{1,0:T(2,128)(2,1)S(1)}, bf16[2,1152]{1,0:T(2,128)(2,1)S(1)}, u32[]{:S(2)}, u32[]{:S(2)}) collective-permute-start(bf16[2,1152]{1,0:T(2,128)(2,1)S(1)} %message.1), channel_id=1, source_target_pairs={{0,8},{4,12},{8,0},{12,4},{16,24},{20,28},{24,16},{28,20},{32,40},... | collective-permute-start | bytes 13832 | tf_op jit(solution)/shard_map/ppermute | solution.py:186
  8.1 1.5 %collective-permute-start.1 = (bf16[2,1152]{1,0:T(2,128)(2,1)S(1)}, bf16[2,1152]{1,0:T(2,128)(2,1)S(1)}, u32[]{:S(2)}, u32[]{:S(2)}) collective-permute-start(bf16[2,1152]{1,0:T(2,128)(2,1)S(1)} %message.1), channel_id=1, source_target_pairs={{0,4},{4,0},{8,12},{12,8},{16,20},{20,16},{24,28},{28,24},{32,36},... | collective-permute-start | bytes 13832 | tf_op jit(solution)/shard_map/ppermute | solution.py:186
  9.6 0.0 collective-permute-start
  9.6 1.9 %fetch.1 = (f32[2,512]{1,0:T(2,128)S(1)}, bf16[512,576]{1,0:T(8,128)(2,1)S(1)}, bf16[2,512,128]{2,1,0:T(8,128)(2,1)S(1)}, bf16[128,7168]{1,0:T(8,128)(2,1)S(1)}) custom-call(s32[1]{0:T(128)} %bitcast.here_ref, s32[2]{0:T(128)} %lengths_hbm.1, s32[2,256]{1,0:T(2,128)} %table_hbm.1, bf16[512,576]{1,0:T(8,128)(2,1)} %bitcast.2, bf16[2,512,128]{2,1,0:T(8,128)(2,1)} %w_uv_hbm.1, ...), custom_call_target="tpu_custom_call" | custom-call | bytes 5242880 | tf_op jit(solution)/shard_map/fetch/pallas_call | solution.py:188
  11.4 0.0 collective-permute-done.2
  11.4 1.1 %collective-permute-done.1 = bf16[2,1152]{1,0:T(2,128)(2,1)S(1)} collective-permute-done((bf16[2,1152]{1,0:T(2,128)(2,1)S(1)}, bf16[2,1152]{1,0:T(2,128)(2,1)S(1)}, u32[]{:S(2)}, u32[]{:S(2)}) %collective-permute-start.1) | collective-permute-done | bytes 4640 | tf_op jit(solution)/shard_map/ppermute | solution.py:186
  12.6 2.7 %collective-permute-done = bf16[2,1152]{1,0:T(2,128)(2,1)S(1)} collective-permute-done((bf16[2,1152]{1,0:T(2,128)(2,1)S(1)}, bf16[2,1152]{1,0:T(2,128)(2,1)S(1)}, u32[]{:S(2)}, u32[]{:S(2)}) %collective-permute-start) | collective-permute-done | bytes 4640 | tf_op jit(solution)/shard_map/ppermute | solution.py:186
  15.3 0.1 broadcast_select_fusion.1
  15.4 0.2 broadcast_in_dim.58
  15.5 14.2 %all_to_all.10 = bf16[16,4,2,1152]{3,2,1,0:T(2,128)(2,1)S(1)} all-to-all(bf16[16,4,2,1152]{3,2,1,0:T(2,128)(2,1)S(1)} %broadcast_in_dim.58), channel_id=1, replica_groups={{0,16,32,48,64,80,96,112,128,144,160,176,192,208,224,240},{4,20,36,52,6..., dimensions={0} | all-to-all | bytes 589824 | tf_op jit(solution)/shard_map/all_to_all | solution.py:214
  29.7 0.1 reshape.35.q_ref
  29.8 1.1 %attend.1 = bf16[128,1152]{1,0:T(8,128)(2,1)S(1)} custom-call(bf16[128,1152]{1,0:T(8,128)(2,1)S(1)} %reshape.35.q_ref, bf16[512,576]{1,0:T(8,128)(2,1)S(1)} %get-tuple-element.19.keys_ref, f32[2,512]{1,0:T(2,128)S(1)} %get-tuple-element.20.live_ref), custom_call_target="tpu_custom_call" | custom-call | tf_op jit(solution)/shard_map/attend/pallas_call | solution.py:220
  31.0 0.1 reshape.36
  31.1 19.8 %all_to_all.11 = bf16[64,2,1152]{2,1,0:T(2,128)(2,1)S(1)} all-to-all(bf16[64,2,1152]{2,1,0:T(2,128)(2,1)S(1)} %reshape.36), channel_id=1, replica_groups=mesh['ctx'=64,'grp'=4] {'ctx'}, dimensions={0} | all-to-all | bytes 589824 | tf_op jit(solution)/shard_map/all_to_all | solution.py:229
  50.9 0.1 reshape.37.state_ref
  51.0 2.1 %project.1 = bf16[2,7168]{1,0:T(2,128)(2,1)S(1)} custom-call(bf16[128,1152]{1,0:T(8,128)(2,1)S(1)} %reshape.37.state_ref, bf16[2,512,128]{2,1,0:T(8,128)(2,1)S(1)} %get-tuple-element.21.w_uv_ref, bf16[128,7168]{1,0:T(8,128)(2,1)S(1)} %get-tuple-element.22.first_ref, bf16[256,7168]{1,0:T(8,128)(2,1)} %w_out_hbm.3), custom_call_target="tpu_custom_call" | custom-call | tf_op jit(solution)/shard_map/project/pallas_call | solution.py:233
  53.1 1.3 %collective-permute-start.5 = (bf16[2,7168]{1,0:T(2,128)(2,1)S(1)}, bf16[2,7168]{1,0:T(2,128)(2,1)S(1)}, u32[]{:S(2)}, u32[]{:S(2)}) collective-permute-start(bf16[2,7168]{1,0:T(2,128)(2,1)S(1)} %project.1), channel_id=1, source_target_pairs={{0,128},{4,132},{8,136},{12,140},{16,144},{20,148},{24,152},{28,15... | collective-permute-start | bytes 86024 | tf_op jit(solution)/shard_map/ppermute | solution.py:23
  54.4 1.7 %collective-permute-start.4 = (bf16[2,7168]{1,0:T(2,128)(2,1)S(1)}, bf16[2,7168]{1,0:T(2,128)(2,1)S(1)}, u32[]{:S(2)}, u32[]{:S(2)}) collective-permute-start(bf16[2,7168]{1,0:T(2,128)(2,1)S(1)} %project.1), channel_id=1, source_target_pairs={{0,192},{4,196},{8,200},{12,204},{16,208},{20,212},{24,216},{28,22... | collective-permute-start | bytes 86024 | tf_op jit(solution)/shard_map/ppermute | solution.py:23
  56.1 1.8 %collective-permute-start.3 = (bf16[2,7168]{1,0:T(2,128)(2,1)S(1)}, bf16[2,7168]{1,0:T(2,128)(2,1)S(1)}, u32[]{:S(2)}, u32[]{:S(2)}) collective-permute-start(bf16[2,7168]{1,0:T(2,128)(2,1)S(1)} %project.1), channel_id=1, source_target_pairs={{0,64},{4,68},{8,72},{12,76},{16,80},{20,84},{24,88},{28,92},{32,9... | collective-permute-start | bytes 86024 | tf_op jit(solution)/shard_map/ppermute | solution.py:23
  57.9 0.7 collective-permute-done.5
  58.6 0.0 collective-permute-done.4
  58.6 1.4 %collective-permute-done.3 = bf16[2,7168]{1,0:T(2,128)(2,1)S(1)} collective-permute-done((bf16[2,7168]{1,0:T(2,128)(2,1)S(1)}, bf16[2,7168]{1,0:T(2,128)(2,1)S(1)}, u32[]{:S(2)}, u32[]{:S(2)}) %collective-permute-start.3) | collective-permute-done | bytes 28704 | tf_op jit(solution)/shard_map/ppermute | solution.py:23
  60.0 0.1 add_convert_fusion.2
  60.0 0.6 collective-permute-start.8
  60.6 2.8 %collective-permute-start.7 = (bf16[2,7168]{1,0:T(2,128)(2,1)S(1)}, bf16[2,7168]{1,0:T(2,128)(2,1)S(1)}, u32[]{:S(2)}, u32[]{:S(2)}) collective-permute-start(bf16[2,7168]{1,0:T(2,128)(2,1)S(1)} %add_convert_fusion.2), channel_id=1, source_target_pairs={{0,48},{4,52},{8,56},{12,60},{16,32},{20,36},{24,40},{28,44},{32,1... | collective-permute-start | bytes 86024 | tf_op jit(solution)/shard_map/ppermute | solution.py:23
  63.4 0.2 collective-permute-start.6
  63.6 1.9 %collective-permute-done.8 = bf16[2,7168]{1,0:T(2,128)(2,1)S(1)} collective-permute-done((bf16[2,7168]{1,0:T(2,128)(2,1)S(1)}, bf16[2,7168]{1,0:T(2,128)(2,1)S(1)}, u32[]{:S(2)}, u32[]{:S(2)}) %collective-permute-start.8) | collective-permute-done | bytes 28704 | tf_op jit(solution)/shard_map/ppermute | solution.py:23
  65.5 0.3 collective-permute-done.7
  65.8 1.5 %collective-permute-done.6 = bf16[2,7168]{1,0:T(2,128)(2,1)S(1)} collective-permute-done((bf16[2,7168]{1,0:T(2,128)(2,1)S(1)}, bf16[2,7168]{1,0:T(2,128)(2,1)S(1)}, u32[]{:S(2)}, u32[]{:S(2)}) %collective-permute-start.6) | collective-permute-done | bytes 28704 | tf_op jit(solution)/shard_map/ppermute | solution.py:23
  67.3 0.1 add_convert_fusion.1
  67.3 0.1 collective-permute-start.11
  67.4 4.2 %collective-permute-start.10 = (bf16[2,7168]{1,0:T(2,128)(2,1)S(1)}, bf16[2,7168]{1,0:T(2,128)(2,1)S(1)}, u32[]{:S(2)}, u32[]{:S(2)}) collective-permute-start(bf16[2,7168]{1,0:T(2,128)(2,1)S(1)} %add_convert_fusion.1), channel_id=1, source_target_pairs={{0,12},{4,8},{8,4},{12,0},{16,28},{20,24},{24,20},{28,16},{32,44},... | collective-permute-start | bytes 86024 | tf_op jit(solution)/shard_map/ppermute | solution.py:23
  71.7 2.3 %collective-permute-start.9 = (bf16[2,7168]{1,0:T(2,128)(2,1)S(1)}, bf16[2,7168]{1,0:T(2,128)(2,1)S(1)}, u32[]{:S(2)}, u32[]{:S(2)}) collective-permute-start(bf16[2,7168]{1,0:T(2,128)(2,1)S(1)} %add_convert_fusion.1), channel_id=1, source_target_pairs={{0,4},{4,0},{8,12},{12,8},{16,20},{20,16},{24,28},{28,24},{32,36},... | collective-permute-start | bytes 86024 | tf_op jit(solution)/shard_map/ppermute | solution.py:23
  73.9 1.4 %collective-permute-done.11 = bf16[2,7168]{1,0:T(2,128)(2,1)S(1)} collective-permute-done((bf16[2,7168]{1,0:T(2,128)(2,1)S(1)}, bf16[2,7168]{1,0:T(2,128)(2,1)S(1)}, u32[]{:S(2)}, u32[]{:S(2)}) %collective-permute-start.11) | collective-permute-done | bytes 28704 | tf_op jit(solution)/shard_map/ppermute | solution.py:23
  75.3 0.0 collective-permute-done.10
  75.3 1.1 %collective-permute-done.9 = bf16[2,7168]{1,0:T(2,128)(2,1)S(1)} collective-permute-done((bf16[2,7168]{1,0:T(2,128)(2,1)S(1)}, bf16[2,7168]{1,0:T(2,128)(2,1)S(1)}, u32[]{:S(2)}, u32[]{:S(2)}) %collective-permute-start.9) | collective-permute-done | bytes 28704 | tf_op jit(solution)/shard_map/ppermute | solution.py:23
  76.4 0.7 add_convert_fusion
  (2 shorter events, 0.0 us)
Async XLA Ops:
  0.8 10.6 %collective-permute-start.2 = (bf16[2,1152]{1,0:T(2,128)(2,1)S(1)}, bf16[2,1152]{1,0:T(2,128)(2,1)S(1)}, u32[]{:S(2)}, u32[]{:S(2)}) collective-permute-start(bf16[2,1152]{1,0:T(2,128)(2,1)S(1)} %message.1), channel_id=1, source_target_pairs={{0,8},{4,12},{8,0},{12,4},{16,24},{20,28},{24,16},{28,20},{32,40},... | collective-permute-start | bytes 13832 | tf_op jit(solution)/shard_map/ppermute | solution.py:186
  8.1 4.5 %collective-permute-start.1 = (bf16[2,1152]{1,0:T(2,128)(2,1)S(1)}, bf16[2,1152]{1,0:T(2,128)(2,1)S(1)}, u32[]{:S(2)}, u32[]{:S(2)}) collective-permute-start(bf16[2,1152]{1,0:T(2,128)(2,1)S(1)} %message.1), channel_id=1, source_target_pairs={{0,4},{4,0},{8,12},{12,8},{16,20},{20,16},{24,28},{28,24},{32,36},... | collective-permute-start | bytes 13832 | tf_op jit(solution)/shard_map/ppermute | solution.py:186
  9.6 5.7 %collective-permute-start = (bf16[2,1152]{1,0:T(2,128)(2,1)S(1)}, bf16[2,1152]{1,0:T(2,128)(2,1)S(1)}, u32[]{:S(2)}, u32[]{:S(2)}) collective-permute-start(bf16[2,1152]{1,0:T(2,128)(2,1)S(1)} %message.1), channel_id=1, source_target_pairs={{0,12},{4,8},{8,4},{12,0},{16,28},{20,24},{24,20},{28,16},{32,44},... | collective-permute-start | bytes 13832 | tf_op jit(solution)/shard_map/ppermute | solution.py:186
  53.1 5.5 %collective-permute-start.5 = (bf16[2,7168]{1,0:T(2,128)(2,1)S(1)}, bf16[2,7168]{1,0:T(2,128)(2,1)S(1)}, u32[]{:S(2)}, u32[]{:S(2)}) collective-permute-start(bf16[2,7168]{1,0:T(2,128)(2,1)S(1)} %project.1), channel_id=1, source_target_pairs={{0,128},{4,132},{8,136},{12,140},{16,144},{20,148},{24,152},{28,15... | collective-permute-start | bytes 86024 | tf_op jit(solution)/shard_map/ppermute | solution.py:23
  54.4 4.2 %collective-permute-start.4 = (bf16[2,7168]{1,0:T(2,128)(2,1)S(1)}, bf16[2,7168]{1,0:T(2,128)(2,1)S(1)}, u32[]{:S(2)}, u32[]{:S(2)}) collective-permute-start(bf16[2,7168]{1,0:T(2,128)(2,1)S(1)} %project.1), channel_id=1, source_target_pairs={{0,192},{4,196},{8,200},{12,204},{16,208},{20,212},{24,216},{28,22... | collective-permute-start | bytes 86024 | tf_op jit(solution)/shard_map/ppermute | solution.py:23
  56.1 3.9 %collective-permute-start.3 = (bf16[2,7168]{1,0:T(2,128)(2,1)S(1)}, bf16[2,7168]{1,0:T(2,128)(2,1)S(1)}, u32[]{:S(2)}, u32[]{:S(2)}) collective-permute-start(bf16[2,7168]{1,0:T(2,128)(2,1)S(1)} %project.1), channel_id=1, source_target_pairs={{0,64},{4,68},{8,72},{12,76},{16,80},{20,84},{24,88},{28,92},{32,9... | collective-permute-start | bytes 86024 | tf_op jit(solution)/shard_map/ppermute | solution.py:23
  60.0 5.5 %collective-permute-start.8 = (bf16[2,7168]{1,0:T(2,128)(2,1)S(1)}, bf16[2,7168]{1,0:T(2,128)(2,1)S(1)}, u32[]{:S(2)}, u32[]{:S(2)}) collective-permute-start(bf16[2,7168]{1,0:T(2,128)(2,1)S(1)} %add_convert_fusion.2), channel_id=1, source_target_pairs={{0,32},{4,36},{8,40},{12,44},{16,48},{20,52},{24,56},{28,60},{32,0... | collective-permute-start | bytes 86024 | tf_op jit(solution)/shard_map/ppermute | solution.py:23
  60.6 5.2 %collective-permute-start.7 = (bf16[2,7168]{1,0:T(2,128)(2,1)S(1)}, bf16[2,7168]{1,0:T(2,128)(2,1)S(1)}, u32[]{:S(2)}, u32[]{:S(2)}) collective-permute-start(bf16[2,7168]{1,0:T(2,128)(2,1)S(1)} %add_convert_fusion.2), channel_id=1, source_target_pairs={{0,48},{4,52},{8,56},{12,60},{16,32},{20,36},{24,40},{28,44},{32,1... | collective-permute-start | bytes 86024 | tf_op jit(solution)/shard_map/ppermute | solution.py:23
  63.4 3.9 %collective-permute-start.6 = (bf16[2,7168]{1,0:T(2,128)(2,1)S(1)}, bf16[2,7168]{1,0:T(2,128)(2,1)S(1)}, u32[]{:S(2)}, u32[]{:S(2)}) collective-permute-start(bf16[2,7168]{1,0:T(2,128)(2,1)S(1)} %add_convert_fusion.2), channel_id=1, source_target_pairs={{0,16},{4,20},{8,24},{12,28},{16,0},{20,4},{24,8},{28,12},{32,48},... | collective-permute-start | bytes 86024 | tf_op jit(solution)/shard_map/ppermute | solution.py:23
  67.3 7.9 %collective-permute-start.11 = (bf16[2,7168]{1,0:T(2,128)(2,1)S(1)}, bf16[2,7168]{1,0:T(2,128)(2,1)S(1)}, u32[]{:S(2)}, u32[]{:S(2)}) collective-permute-start(bf16[2,7168]{1,0:T(2,128)(2,1)S(1)} %add_convert_fusion.1), channel_id=1, source_target_pairs={{0,8},{4,12},{8,0},{12,4},{16,24},{20,28},{24,16},{28,20},{32,40},... | collective-permute-start | bytes 86024 | tf_op jit(solution)/shard_map/ppermute | solution.py:23
  67.4 7.8 %collective-permute-start.10 = (bf16[2,7168]{1,0:T(2,128)(2,1)S(1)}, bf16[2,7168]{1,0:T(2,128)(2,1)S(1)}, u32[]{:S(2)}, u32[]{:S(2)}) collective-permute-start(bf16[2,7168]{1,0:T(2,128)(2,1)S(1)} %add_convert_fusion.1), channel_id=1, source_target_pairs={{0,12},{4,8},{8,4},{12,0},{16,28},{20,24},{24,20},{28,16},{32,44},... | collective-permute-start | bytes 86024 | tf_op jit(solution)/shard_map/ppermute | solution.py:23
  71.7 4.8 %collective-permute-start.9 = (bf16[2,7168]{1,0:T(2,128)(2,1)S(1)}, bf16[2,7168]{1,0:T(2,128)(2,1)S(1)}, u32[]{:S(2)}, u32[]{:S(2)}) collective-permute-start(bf16[2,7168]{1,0:T(2,128)(2,1)S(1)} %add_convert_fusion.1), channel_id=1, source_target_pairs={{0,4},{4,0},{8,12},{12,8},{16,20},{20,16},{24,28},{28,24},{32,36},... | collective-permute-start | bytes 86024 | tf_op jit(solution)/shard_map/ppermute | solution.py:23

commit v14 on v13

--- a/solution.py
+++ b/solution.py
@@ -151,9 +151,13 @@
         axis=0,
     ).astype(BF16)
     term = jnp.dot(flat[:, :split], first_ref[...], preferred_element_type=F32)
-    for copy in copies:
+    for k, copy in enumerate(copies):
         copy.wait()
-    term += jnp.dot(flat[:, split:], second_ref[...], preferred_element_type=F32)
+        term += jnp.dot(
+            flat[:, split + k * step : split + (k + 1) * step],
+            second_ref[k * step : (k + 1) * step],
+            preferred_element_type=F32,
+        )
     term_ref[...] = term.astype(term_ref.dtype)
 
 
@@ -229,7 +233,7 @@
     state = lax.all_to_all(
         state.reshape(count, rows, state_size), CTX, split_axis=0, concat_axis=0, tiled=True
     )
-    parts = 4
+    parts = 2
     term = pl.pallas_call(
         functools.partial(project_kernel, rows, heads, latent),
         out_shape=jax.ShapeDtypeStruct((rows, w_out.shape[1]), BF16),

time: 77.3 us -> 77.2 us (level)
  no operation moved by 1% of the time
where the time goes in v14:
time: 77.2 us; the launch traced here: 76.9 us
  blocking collectives  34 us (44%)
  starting transfers between devices  23.7 us (31%)
  waiting for transfers between devices  12.1 us (16%)
  Pallas kernels  5.69 us (7%)
  other arithmetic  0.91 us (1%)
    all_to_all x1, blocking collectives, local(): lax.all_to_all(state.reshape(count, rows, state_size), CTX, split_axis=0,...  19.8 us
    ppermute x9, starting transfers between devices, sum_of_four(): lax.ppermute(x, CTX, xor_pairs(count, k << low))  14.9 us
    all_to_all x1, blocking collectives, local(): lax.all_to_all(jnp.broadcast_to(column[None], (count // near, near, rows,...  14.2 us
    ppermute x3, starting transfers between devices, local(): lax.ppermute(message, CTX, xor_pairs(count, k))  8.75 us
    ppermute x9, waiting for transfers between devices, sum_of_four(): lax.ppermute(x, CTX, xor_pairs(count, k << low))  8.27 us
    ppermute x3, waiting for transfers between devices, local(): lax.ppermute(message, CTX, xor_pairs(count, k))  3.83 us
    pallas_call x1, Pallas kernels, local(): pl.pallas_call(functools.partial(project_kernel, rows, heads, latent), ou...  1.91 us
    pallas_call x1, Pallas kernels, local(): pl.pallas_call(functools.partial(fetch_kernel, page_len), out_shape=(pltp...  1.85 us
  transfers between devices with their start and end apart: 12, of which 9 were waited for; matrix products, arithmetic and copies ran while one was open for 0% of the time, Pallas kernels for 2%

profile of v14, /device:TPU:2, one launch (start us, length us, event | category | flops | bytes accessed | tf_op | source)
XLA Modules:
  0.0 76.9 jit_solution(5248656577222174559)
XLA Ops:
  0.0 0.8 %message.1 = bf16[2,1152]{1,0:T(2,128)(2,1)S(1)} custom-call(bf16[2,2,512]{2,1,0:T(2,128)(2,1)} %q_latent_hbm.1, bf16[2,2,64]{2,1,0:T(2,128)(2,1)} %q_rope_hbm.1), custom_call_target="tpu_custom_call" | custom-call | tf_op jit(solution)/shard_map/message/pallas_call | solution.py:179
  0.8 7.3 %collective-permute-start.2 = (bf16[2,1152]{1,0:T(2,128)(2,1)S(1)}, bf16[2,1152]{1,0:T(2,128)(2,1)S(1)}, u32[]{:S(2)}, u32[]{:S(2)}) collective-permute-start(bf16[2,1152]{1,0:T(2,128)(2,1)S(1)} %message.1), channel_id=1, source_target_pairs={{0,8},{4,12},{8,0},{12,4},{16,24},{20,28},{24,16},{28,20},{32,40},... | collective-permute-start | bytes 13832 | tf_op jit(solution)/shard_map/ppermute | solution.py:190
  8.1 1.5 %collective-permute-start.1 = (bf16[2,1152]{1,0:T(2,128)(2,1)S(1)}, bf16[2,1152]{1,0:T(2,128)(2,1)S(1)}, u32[]{:S(2)}, u32[]{:S(2)}) collective-permute-start(bf16[2,1152]{1,0:T(2,128)(2,1)S(1)} %message.1), channel_id=1, source_target_pairs={{0,4},{4,0},{8,12},{12,8},{16,20},{20,16},{24,28},{28,24},{32,36},... | collective-permute-start | bytes 13832 | tf_op jit(solution)/shard_map/ppermute | solution.py:190
  9.6 0.0 collective-permute-start
  9.6 1.9 %fetch.1 = (f32[2,512]{1,0:T(2,128)S(1)}, bf16[512,576]{1,0:T(8,128)(2,1)S(1)}, bf16[2,512,128]{2,1,0:T(8,128)(2,1)S(1)}, bf16[128,7168]{1,0:T(8,128)(2,1)S(1)}) custom-call(s32[1]{0:T(128)} %bitcast.here_ref, s32[2]{0:T(128)} %lengths_hbm.1, s32[2,256]{1,0:T(2,128)} %table_hbm.1, bf16[512,576]{1,0:T(8,128)(2,1)} %bitcast.2, bf16[2,512,128]{2,1,0:T(8,128)(2,1)} %w_uv_hbm.1, ...), custom_call_target="tpu_custom_call" | custom-call | bytes 5242880 | tf_op jit(solution)/shard_map/fetch/pallas_call | solution.py:192
  11.4 0.0 collective-permute-done.2
  11.4 1.1 %collective-permute-done.1 = bf16[2,1152]{1,0:T(2,128)(2,1)S(1)} collective-permute-done((bf16[2,1152]{1,0:T(2,128)(2,1)S(1)}, bf16[2,1152]{1,0:T(2,128)(2,1)S(1)}, u32[]{:S(2)}, u32[]{:S(2)}) %collective-permute-start.1) | collective-permute-done | bytes 4640 | tf_op jit(solution)/shard_map/ppermute | solution.py:190
  12.6 2.7 %collective-permute-done = bf16[2,1152]{1,0:T(2,128)(2,1)S(1)} collective-permute-done((bf16[2,1152]{1,0:T(2,128)(2,1)S(1)}, bf16[2,1152]{1,0:T(2,128)(2,1)S(1)}, u32[]{:S(2)}, u32[]{:S(2)}) %collective-permute-start) | collective-permute-done | bytes 4640 | tf_op jit(solution)/shard_map/ppermute | solution.py:190
  15.3 0.1 broadcast_select_fusion.1
  15.4 0.2 broadcast_in_dim.58
  15.5 14.2 %all_to_all.10 = bf16[16,4,2,1152]{3,2,1,0:T(2,128)(2,1)S(1)} all-to-all(bf16[16,4,2,1152]{3,2,1,0:T(2,128)(2,1)S(1)} %broadcast_in_dim.58), channel_id=1, replica_groups={{0,16,32,48,64,80,96,112,128,144,160,176,192,208,224,240},{4,20,36,52,6..., dimensions={0} | all-to-all | bytes 589824 | tf_op jit(solution)/shard_map/all_to_all | solution.py:218
  29.7 0.1 reshape.35.q_ref
  29.8 1.1 %attend.1 = bf16[128,1152]{1,0:T(8,128)(2,1)S(1)} custom-call(bf16[128,1152]{1,0:T(8,128)(2,1)S(1)} %reshape.35.q_ref, bf16[512,576]{1,0:T(8,128)(2,1)S(1)} %get-tuple-element.19.keys_ref, f32[2,512]{1,0:T(2,128)S(1)} %get-tuple-element.20.live_ref), custom_call_target="tpu_custom_call" | custom-call | tf_op jit(solution)/shard_map/attend/pallas_call | solution.py:224
  31.0 0.1 reshape.36
  31.1 19.8 %all_to_all.11 = bf16[64,2,1152]{2,1,0:T(2,128)(2,1)S(1)} all-to-all(bf16[64,2,1152]{2,1,0:T(2,128)(2,1)S(1)} %reshape.36), channel_id=1, replica_groups=mesh['ctx'=64,'grp'=4] {'ctx'}, dimensions={0} | all-to-all | bytes 589824 | tf_op jit(solution)/shard_map/all_to_all | solution.py:233
  50.9 0.1 reshape.37.state_ref
  51.0 1.9 %project.1 = bf16[2,7168]{1,0:T(2,128)(2,1)S(1)} custom-call(bf16[128,1152]{1,0:T(8,128)(2,1)S(1)} %reshape.37.state_ref, bf16[2,512,128]{2,1,0:T(8,128)(2,1)S(1)} %get-tuple-element.21.w_uv_ref, bf16[128,7168]{1,0:T(8,128)(2,1)S(1)} %get-tuple-element.22.first_ref, bf16[256,7168]{1,0:T(8,128)(2,1)} %w_out_hbm.3), custom_call_target="tpu_custom_call" | custom-call | tf_op jit(solution)/shard_map/project/pallas_call | solution.py:237
  52.9 1.3 %collective-permute-start.5 = (bf16[2,7168]{1,0:T(2,128)(2,1)S(1)}, bf16[2,7168]{1,0:T(2,128)(2,1)S(1)}, u32[]{:S(2)}, u32[]{:S(2)}) collective-permute-start(bf16[2,7168]{1,0:T(2,128)(2,1)S(1)} %project.1), channel_id=1, source_target_pairs={{0,128},{4,132},{8,136},{12,140},{16,144},{20,148},{24,152},{28,15... | collective-permute-start | bytes 86024 | tf_op jit(solution)/shard_map/ppermute | solution.py:23
  54.2 1.7 %collective-permute-start.4 = (bf16[2,7168]{1,0:T(2,128)(2,1)S(1)}, bf16[2,7168]{1,0:T(2,128)(2,1)S(1)}, u32[]{:S(2)}, u32[]{:S(2)}) collective-permute-start(bf16[2,7168]{1,0:T(2,128)(2,1)S(1)} %project.1), channel_id=1, source_target_pairs={{0,192},{4,196},{8,200},{12,204},{16,208},{20,212},{24,216},{28,22... | collective-permute-start | bytes 86024 | tf_op jit(solution)/shard_map/ppermute | solution.py:23
  55.9 1.8 %collective-permute-start.3 = (bf16[2,7168]{1,0:T(2,128)(2,1)S(1)}, bf16[2,7168]{1,0:T(2,128)(2,1)S(1)}, u32[]{:S(2)}, u32[]{:S(2)}) collective-permute-start(bf16[2,7168]{1,0:T(2,128)(2,1)S(1)} %project.1), channel_id=1, source_target_pairs={{0,64},{4,68},{8,72},{12,76},{16,80},{20,84},{24,88},{28,92},{32,9... | collective-permute-start | bytes 86024 | tf_op jit(solution)/shard_map/ppermute | solution.py:23
  57.7 0.7 collective-permute-done.5
  58.4 0.0 collective-permute-done.4
  58.4 1.4 %collective-permute-done.3 = bf16[2,7168]{1,0:T(2,128)(2,1)S(1)} collective-permute-done((bf16[2,7168]{1,0:T(2,128)(2,1)S(1)}, bf16[2,7168]{1,0:T(2,128)(2,1)S(1)}, u32[]{:S(2)}, u32[]{:S(2)}) %collective-permute-start.3) | collective-permute-done | bytes 28704 | tf_op jit(solution)/shard_map/ppermute | solution.py:23
  59.8 0.1 add_convert_fusion.2
  59.9 0.6 collective-permute-start.8
  60.5 2.8 %collective-permute-start.7 = (bf16[2,7168]{1,0:T(2,128)(2,1)S(1)}, bf16[2,7168]{1,0:T(2,128)(2,1)S(1)}, u32[]{:S(2)}, u32[]{:S(2)}) collective-permute-start(bf16[2,7168]{1,0:T(2,128)(2,1)S(1)} %add_convert_fusion.2), channel_id=1, source_target_pairs={{0,48},{4,52},{8,56},{12,60},{16,32},{20,36},{24,40},{28,44},{32,1... | collective-permute-start | bytes 86024 | tf_op jit(solution)/shard_map/ppermute | solution.py:23
  63.2 0.2 collective-permute-start.6
  63.5 1.9 %collective-permute-done.8 = bf16[2,7168]{1,0:T(2,128)(2,1)S(1)} collective-permute-done((bf16[2,7168]{1,0:T(2,128)(2,1)S(1)}, bf16[2,7168]{1,0:T(2,128)(2,1)S(1)}, u32[]{:S(2)}, u32[]{:S(2)}) %collective-permute-start.8) | collective-permute-done | bytes 28704 | tf_op jit(solution)/shard_map/ppermute | solution.py:23
  65.3 0.3 collective-permute-done.7
  65.6 1.5 %collective-permute-done.6 = bf16[2,7168]{1,0:T(2,128)(2,1)S(1)} collective-permute-done((bf16[2,7168]{1,0:T(2,128)(2,1)S(1)}, bf16[2,7168]{1,0:T(2,128)(2,1)S(1)}, u32[]{:S(2)}, u32[]{:S(2)}) %collective-permute-start.6) | collective-permute-done | bytes 28704 | tf_op jit(solution)/shard_map/ppermute | solution.py:23
  67.1 0.1 add_convert_fusion.1
  67.2 0.1 collective-permute-start.11
  67.3 4.2 %collective-permute-start.10 = (bf16[2,7168]{1,0:T(2,128)(2,1)S(1)}, bf16[2,7168]{1,0:T(2,128)(2,1)S(1)}, u32[]{:S(2)}, u32[]{:S(2)}) collective-permute-start(bf16[2,7168]{1,0:T(2,128)(2,1)S(1)} %add_convert_fusion.1), channel_id=1, source_target_pairs={{0,12},{4,8},{8,4},{12,0},{16,28},{20,24},{24,20},{28,16},{32,44},... | collective-permute-start | bytes 86024 | tf_op jit(solution)/shard_map/ppermute | solution.py:23
  71.5 2.3 %collective-permute-start.9 = (bf16[2,7168]{1,0:T(2,128)(2,1)S(1)}, bf16[2,7168]{1,0:T(2,128)(2,1)S(1)}, u32[]{:S(2)}, u32[]{:S(2)}) collective-permute-start(bf16[2,7168]{1,0:T(2,128)(2,1)S(1)} %add_convert_fusion.1), channel_id=1, source_target_pairs={{0,4},{4,0},{8,12},{12,8},{16,20},{20,16},{24,28},{28,24},{32,36},... | collective-permute-start | bytes 86024 | tf_op jit(solution)/shard_map/ppermute | solution.py:23
  73.8 1.4 %collective-permute-done.11 = bf16[2,7168]{1,0:T(2,128)(2,1)S(1)} collective-permute-done((bf16[2,7168]{1,0:T(2,128)(2,1)S(1)}, bf16[2,7168]{1,0:T(2,128)(2,1)S(1)}, u32[]{:S(2)}, u32[]{:S(2)}) %collective-permute-start.11) | collective-permute-done | bytes 28704 | tf_op jit(solution)/shard_map/ppermute | solution.py:23
  75.1 0.0 collective-permute-done.10
  75.1 1.1 %collective-permute-done.9 = bf16[2,7168]{1,0:T(2,128)(2,1)S(1)} collective-permute-done((bf16[2,7168]{1,0:T(2,128)(2,1)S(1)}, bf16[2,7168]{1,0:T(2,128)(2,1)S(1)}, u32[]{:S(2)}, u32[]{:S(2)}) %collective-permute-start.9) | collective-permute-done | bytes 28704 | tf_op jit(solution)/shard_map/ppermute | solution.py:23
  76.3 0.7 add_convert_fusion
  (2 shorter events, 0.0 us)
Async XLA Ops:
  0.8 10.6 %collective-permute-start.2 = (bf16[2,1152]{1,0:T(2,128)(2,1)S(1)}, bf16[2,1152]{1,0:T(2,128)(2,1)S(1)}, u32[]{:S(2)}, u32[]{:S(2)}) collective-permute-start(bf16[2,1152]{1,0:T(2,128)(2,1)S(1)} %message.1), channel_id=1, source_target_pairs={{0,8},{4,12},{8,0},{12,4},{16,24},{20,28},{24,16},{28,20},{32,40},... | collective-permute-start | bytes 13832 | tf_op jit(solution)/shard_map/ppermute | solution.py:190
  8.1 4.5 %collective-permute-start.1 = (bf16[2,1152]{1,0:T(2,128)(2,1)S(1)}, bf16[2,1152]{1,0:T(2,128)(2,1)S(1)}, u32[]{:S(2)}, u32[]{:S(2)}) collective-permute-start(bf16[2,1152]{1,0:T(2,128)(2,1)S(1)} %message.1), channel_id=1, source_target_pairs={{0,4},{4,0},{8,12},{12,8},{16,20},{20,16},{24,28},{28,24},{32,36},... | collective-permute-start | bytes 13832 | tf_op jit(solution)/shard_map/ppermute | solution.py:190
  9.6 5.7 %collective-permute-start = (bf16[2,1152]{1,0:T(2,128)(2,1)S(1)}, bf16[2,1152]{1,0:T(2,128)(2,1)S(1)}, u32[]{:S(2)}, u32[]{:S(2)}) collective-permute-start(bf16[2,1152]{1,0:T(2,128)(2,1)S(1)} %message.1), channel_id=1, source_target_pairs={{0,12},{4,8},{8,4},{12,0},{16,28},{20,24},{24,20},{28,16},{32,44},... | collective-permute-start | bytes 13832 | tf_op jit(solution)/shard_map/ppermute | solution.py:190
  52.9 5.5 %collective-permute-start.5 = (bf16[2,7168]{1,0:T(2,128)(2,1)S(1)}, bf16[2,7168]{1,0:T(2,128)(2,1)S(1)}, u32[]{:S(2)}, u32[]{:S(2)}) collective-permute-start(bf16[2,7168]{1,0:T(2,128)(2,1)S(1)} %project.1), channel_id=1, source_target_pairs={{0,128},{4,132},{8,136},{12,140},{16,144},{20,148},{24,152},{28,15... | collective-permute-start | bytes 86024 | tf_op jit(solution)/shard_map/ppermute | solution.py:23
  54.2 4.2 %collective-permute-start.4 = (bf16[2,7168]{1,0:T(2,128)(2,1)S(1)}, bf16[2,7168]{1,0:T(2,128)(2,1)S(1)}, u32[]{:S(2)}, u32[]{:S(2)}) collective-permute-start(bf16[2,7168]{1,0:T(2,128)(2,1)S(1)} %project.1), channel_id=1, source_target_pairs={{0,192},{4,196},{8,200},{12,204},{16,208},{20,212},{24,216},{28,22... | collective-permute-start | bytes 86024 | tf_op jit(solution)/shard_map/ppermute | solution.py:23
  55.9 3.9 %collective-permute-start.3 = (bf16[2,7168]{1,0:T(2,128)(2,1)S(1)}, bf16[2,7168]{1,0:T(2,128)(2,1)S(1)}, u32[]{:S(2)}, u32[]{:S(2)}) collective-permute-start(bf16[2,7168]{1,0:T(2,128)(2,1)S(1)} %project.1), channel_id=1, source_target_pairs={{0,64},{4,68},{8,72},{12,76},{16,80},{20,84},{24,88},{28,92},{32,9... | collective-permute-start | bytes 86024 | tf_op jit(solution)/shard_map/ppermute | solution.py:23
  59.9 5.5 %collective-permute-start.8 = (bf16[2,7168]{1,0:T(2,128)(2,1)S(1)}, bf16[2,7168]{1,0:T(2,128)(2,1)S(1)}, u32[]{:S(2)}, u32[]{:S(2)}) collective-permute-start(bf16[2,7168]{1,0:T(2,128)(2,1)S(1)} %add_convert_fusion.2), channel_id=1, source_target_pairs={{0,32},{4,36},{8,40},{12,44},{16,48},{20,52},{24,56},{28,60},{32,0... | collective-permute-start | bytes 86024 | tf_op jit(solution)/shard_map/ppermute | solution.py:23
  60.5 5.2 %collective-permute-start.7 = (bf16[2,7168]{1,0:T(2,128)(2,1)S(1)}, bf16[2,7168]{1,0:T(2,128)(2,1)S(1)}, u32[]{:S(2)}, u32[]{:S(2)}) collective-permute-start(bf16[2,7168]{1,0:T(2,128)(2,1)S(1)} %add_convert_fusion.2), channel_id=1, source_target_pairs={{0,48},{4,52},{8,56},{12,60},{16,32},{20,36},{24,40},{28,44},{32,1... | collective-permute-start | bytes 86024 | tf_op jit(solution)/shard_map/ppermute | solution.py:23
  63.2 3.9 %collective-permute-start.6 = (bf16[2,7168]{1,0:T(2,128)(2,1)S(1)}, bf16[2,7168]{1,0:T(2,128)(2,1)S(1)}, u32[]{:S(2)}, u32[]{:S(2)}) collective-permute-start(bf16[2,7168]{1,0:T(2,128)(2,1)S(1)} %add_convert_fusion.2), channel_id=1, source_target_pairs={{0,16},{4,20},{8,24},{12,28},{16,0},{20,4},{24,8},{28,12},{32,48},... | collective-permute-start | bytes 86024 | tf_op jit(solution)/shard_map/ppermute | solution.py:23
  67.2 7.9 %collective-permute-start.11 = (bf16[2,7168]{1,0:T(2,128)(2,1)S(1)}, bf16[2,7168]{1,0:T(2,128)(2,1)S(1)}, u32[]{:S(2)}, u32[]{:S(2)}) collective-permute-start(bf16[2,7168]{1,0:T(2,128)(2,1)S(1)} %add_convert_fusion.1), channel_id=1, source_target_pairs={{0,8},{4,12},{8,0},{12,4},{16,24},{20,28},{24,16},{28,20},{32,40},... | collective-permute-start | bytes 86024 | tf_op jit(solution)/shard_map/ppermute | solution.py:23
  67.3 7.8 %collective-permute-start.10 = (bf16[2,7168]{1,0:T(2,128)(2,1)S(1)}, bf16[2,7168]{1,0:T(2,128)(2,1)S(1)}, u32[]{:S(2)}, u32[]{:S(2)}) collective-permute-start(bf16[2,7168]{1,0:T(2,128)(2,1)S(1)} %add_convert_fusion.1), channel_id=1, source_target_pairs={{0,12},{4,8},{8,4},{12,0},{16,28},{20,24},{24,20},{28,16},{32,44},... | collective-permute-start | bytes 86024 | tf_op jit(solution)/shard_map/ppermute | solution.py:23
  71.5 4.8 %collective-permute-start.9 = (bf16[2,7168]{1,0:T(2,128)(2,1)S(1)}, bf16[2,7168]{1,0:T(2,128)(2,1)S(1)}, u32[]{:S(2)}, u32[]{:S(2)}) collective-permute-start(bf16[2,7168]{1,0:T(2,128)(2,1)S(1)} %add_convert_fusion.1), channel_id=1, source_target_pairs={{0,4},{4,0},{8,12},{12,8},{16,20},{20,16},{24,28},{28,24},{32,36},... | collective-permute-start | bytes 86024 | tf_op jit(solution)/shard_map/ppermute | solution.py:23

commit v15 on v8

--- a/solution.py
+++ b/solution.py
@@ -20,8 +20,8 @@
 
 
 def sum_of_four(x, count, low):
-    a, b, c = (lax.ppermute(x, CTX, xor_pairs(count, k << low)) for k in (1, 2, 3))
-    return (x.astype(F32) + a.astype(F32)) + (b.astype(F32) + c.astype(F32))
+    a, c, b = (lax.ppermute(x, CTX, xor_pairs(count, k << low)) for k in (1, 3, 2))
+    return (x.astype(F32) + a.astype(F32)) + (c.astype(F32) + b.astype(F32))
 
 
 def message_kernel(q_latent_hbm, q_rope_hbm, message_ref, q_latent_ref, q_rope_ref, sems):
@@ -52,7 +52,7 @@
 ):
     pairs = [
         (lengths_hbm, lengths_ref), (table_hbm, table_ref), (cache_hbm, keys_ref), (w_uv_hbm, w_uv_ref),
-        (w_out_hbm.at[:, : w_out_ref.shape[1]], w_out_ref),
+        (w_out_hbm, w_out_ref),
     ]
     copies = [pltpu.make_async_copy(a, b, sems.at[k]) for k, (a, b) in enumerate(pairs)]
     for copy in copies:
@@ -78,7 +78,9 @@
 
 
 def attend_kernel(rows, heads, latent, rope, q_ref, keys_ref, live_ref, state_ref):
-    count = q_ref.shape[0]
+    size = q_ref.shape[2]
+    count = q_ref.shape[0] * rows
+    queries = q_ref[...].reshape(count, size)
     tokens = keys_ref.shape[0]
     row = lax.broadcasted_iota(jnp.int32, (count, 1), 0) % rows
     live = jnp.broadcast_to(live_ref[0:1, :], (count, tokens))
@@ -86,11 +88,12 @@
         live = jnp.where(row == r, live_ref[r : r + 1, :], live)
     live = live > 0.5
     side = heads * latent
-    lane = lax.broadcasted_iota(jnp.int32, (count, state_ref.shape[1] - side), 1)
+    lane = lax.broadcasted_iota(jnp.int32, (count, LANES), 1)
     stats = jnp.zeros(lane.shape, F32)
+    states = []
     for h in range(heads):
         query = jnp.concatenate(
-            [q_ref[:, h * latent : (h + 1) * latent], q_ref[:, side + h * rope : side + (h + 1) * rope]], axis=1
+            [queries[:, h * latent : (h + 1) * latent], queries[:, side + h * rope : side + (h + 1) * rope]], axis=1
         )
         scores = lax.dot_general(
             query, keys_ref[...], (((1,), (1,)), ((), ())), preferred_element_type=F32
@@ -100,25 +103,24 @@
         weights = jnp.where(live, jnp.exp(scores - shift), 0.0).astype(BF16)
         total = jnp.sum(weights.astype(F32), axis=1, keepdims=True)
         outs = jnp.dot(weights, keys_ref[:, :latent], preferred_element_type=F32)
-        state_ref[:, h * latent : (h + 1) * latent] = outs.astype(BF16)
+        states.append(outs.astype(BF16))
         high = total.astype(BF16).astype(F32)
         for k, value in enumerate((shift, high, total - high)):
             stats = jnp.where(lane == 3 * h + k, value, stats)
-    state_ref[:, side:] = stats.astype(BF16)
-
-
-def project_kernel(rows, heads, latent, state_ref, w_uv_ref, first_ref, w_out_hbm, term_ref, second_ref, sem):
-    split = first_ref.shape[1]
-    copy = pltpu.make_async_copy(w_out_hbm.at[:, split:], second_ref, sem)
-    copy.start()
-    count = state_ref.shape[0]
+    states.append(stats.astype(BF16))
+    state_ref[...] = jnp.concatenate(states, axis=1).reshape(state_ref.shape)
+
+
+def project_kernel(rows, heads, latent, messages_ref, w_uv_ref, w_out_ref, term_ref):
+    count = messages_ref.shape[0] * rows
+    states = messages_ref[...].reshape(count, messages_ref.shape[2])
     mixed = rows * heads
     side = heads * latent
     lane = lax.broadcasted_iota(jnp.int32, (count, LANES), 1)
     row = lax.broadcasted_iota(jnp.int32, (count, LANES), 0) % rows
     column = lane % mixed
     own = (column // heads == row) & (lane < 2 * mixed)
-    stats = state_ref[:, side:].astype(F32)
+    stats = states[:, side:].astype(F32)
     shift = jnp.full((count, LANES), 2 * NEG, F32)
     for h in range(heads):
         shift = jnp.where(own & (column % heads == h), stats[:, 3 * h : 3 * h + 1], shift)
@@ -127,7 +129,7 @@
     high = factor.astype(BF16).astype(F32)
     factor = jnp.where(lane < mixed, high, factor - high).astype(BF16)
     merged = lax.dot_general(
-        factor, state_ref[...], (((0,), (0,)), ((), ())), preferred_element_type=F32
+        factor, states, (((0,), (0,)), ((), ())), preferred_element_type=F32
     )
     merged = merged[:mixed] + merged[mixed : 2 * mixed]
     parts = []
@@ -142,9 +144,7 @@
         ],
         axis=0,
     ).astype(BF16)
-    term_ref[:, :split] = jnp.dot(flat, first_ref[...], preferred_element_type=F32).astype(term_ref.dtype)
-    copy.wait()
-    term_ref[:, split:] = jnp.dot(flat, second_ref[...], preferred_element_type=F32).astype(term_ref.dtype)
+    term_ref[...] = jnp.dot(flat, w_out_ref[...], preferred_element_type=F32).astype(term_ref.dtype)
 
 
 def local(q_latent, q_rope, latent_cache, page_table, lengths, w_uv, w_out):
@@ -173,15 +173,14 @@
     )(stay(q_latent), stay(q_rope))
 
     near = 4
-    others = [lax.ppermute(message, CTX, xor_pairs(count, k)) for k in range(1, near)]
-    split = w_out.shape[1] // 2 // LANES * LANES
-    live, keys, w_uv, w_first = pl.pallas_call(
+    others = {k: lax.ppermute(message, CTX, xor_pairs(count, k)) for k in (1, 3, 2)}
+    live, keys, w_uv, w_out_near = pl.pallas_call(
         functools.partial(fetch_kernel, page_len),
         out_shape=(
             pltpu.VMEM((rows, tokens), F32),
             pltpu.VMEM((tokens, width), BF16),
             pltpu.VMEM(w_uv.shape, BF16),
-            pltpu.VMEM((w_out.shape[0], split), BF16),
+            pltpu.VMEM(w_out.shape, BF16),
         ),
         in_specs=[smem, hbm, hbm, hbm, hbm, hbm],
         out_specs=(vmem, vmem, vmem, vmem),
@@ -197,9 +196,9 @@
     )
     away = lax.broadcasted_iota(jnp.int32, (near, 1, 1), 0) ^ (here % near)
     column = jnp.broadcast_to(message[None], (near, rows, size))
-    for k in range(1, near):
-        column = jnp.where(away == k, others[k - 1][None], column)
-    column, live, keys, w_uv, w_first = lax.optimization_barrier((column, live, keys, w_uv, w_first))
+    for k in (2, 1, 3):
+        column = jnp.where(away == k, others[k][None], column)
+    column, live, keys, w_uv, w_out_near = lax.optimization_barrier((column, live, keys, w_uv, w_out_near))
     planes = [[i * near + k for i in range(count // near)] for k in range(near)]
     query = lax.all_to_all(
         jnp.broadcast_to(column[None], (count // near, near, rows, size)),
@@ -209,25 +208,22 @@
     state_size = heads * latent + LANES
     state = pl.pallas_call(
         functools.partial(attend_kernel, rows, heads, latent, rope),
-        out_shape=jax.ShapeDtypeStruct((count * rows, state_size), BF16),
+        out_shape=jax.ShapeDtypeStruct((count, rows, state_size), BF16),
         in_specs=[vmem, vmem, vmem],
         out_specs=vmem,
         compiler_params=params,
         name="attend",
-    )(query.reshape(count * rows, size), keys, live)
-
-    state = lax.all_to_all(
-        state.reshape(count, rows, state_size), CTX, split_axis=0, concat_axis=0, tiled=True
-    )
+    )(query.reshape(count, rows, size), keys, live)
+
+    state = lax.all_to_all(state, CTX, split_axis=0, concat_axis=0, tiled=True)
     term = pl.pallas_call(
         functools.partial(project_kernel, rows, heads, latent),
         out_shape=jax.ShapeDtypeStruct((rows, w_out.shape[1]), BF16),
-        in_specs=[vmem, vmem, vmem, hbm],
+        in_specs=[vmem, vmem, vmem],
         out_specs=vmem,
-        scratch_shapes=[pltpu.VMEM((w_out.shape[0], w_out.shape[1] - split), BF16), dma],
         compiler_params=params,
         name="project",
-    )(state.reshape(count * rows, state_size), w_uv, w_first, stay(w_out))
+    )(state, w_uv, w_out_near)
     for low in (4, 2, 0):
         term = sum_of_four(term, count, low).astype(BF16)
     return term

time: 78.2 us -> 76.7 us (0.981)
    pallas_call x1, Pallas kernels: 2.37 us -> 1.26 us  [local(): pl.pallas_call(functools.partial(project_kernel, rows, heads, latent), ou...]
  transfers between devices with their start and end apart: 12 -> 12, of which waited for: 9 -> 9; matrix products, arithmetic and copies ran while one was open for 0% -> 0% of each run, Pallas kernels for 2% -> 3%
where the time goes in v15:
time: 76.7 us; the launch traced here: 76.5 us
  blocking collectives  34.2 us (45%)
  starting transfers between devices  23.7 us (31%)
  waiting for transfers between devices  11.9 us (16%)
  Pallas kernels  5.6 us (7%)
  other arithmetic  0.91 us (1%)
    all_to_all x1, blocking collectives, local(): state = lax.all_to_all(state, CTX, split_axis=0, concat_axis=0, tiled=True)  20 us
    ppermute x9, starting transfers between devices, sum_of_four(): lax.ppermute(x, CTX, xor_pairs(count, k << low))  14.9 us
    all_to_all x1, blocking collectives, local(): lax.all_to_all(jnp.broadcast_to(column[None], (count // near, near, rows,...  14.2 us
    ppermute x3, starting transfers between devices, local(): lax.ppermute(message, CTX, xor_pairs(count, k))  8.75 us
    ppermute x9, waiting for transfers between devices, sum_of_four(): lax.ppermute(x, CTX, xor_pairs(count, k << low))  8.58 us
    ppermute x3, waiting for transfers between devices, local(): lax.ppermute(message, CTX, xor_pairs(count, k))  3.29 us
    pallas_call x1, Pallas kernels, local(): pl.pallas_call(functools.partial(fetch_kernel, page_len), out_shape=(pltp...  2.39 us
  transfers between devices with their start and end apart: 12, of which 9 were waited for; matrix products, arithmetic and copies ran while one was open for 0% of the time, Pallas kernels for 3%

profile of v15, /device:TPU:2, one launch (start us, length us, event | category | flops | bytes accessed | tf_op | source)
XLA Modules:
  0.0 76.5 jit_solution(10079914408491458182)
XLA Ops:
  0.0 0.8 %message.1 = bf16[2,1152]{1,0:T(2,128)(2,1)S(1)} custom-call(bf16[2,2,512]{2,1,0:T(2,128)(2,1)} %q_latent_hbm.1, bf16[2,2,64]{2,1,0:T(2,128)(2,1)} %q_rope_hbm.1), custom_call_target="tpu_custom_call" | custom-call | tf_op jit(solution)/shard_map/message/pallas_call | solution.py:165
  0.8 7.3 %collective-permute-start.2 = (bf16[2,1152]{1,0:T(2,128)(2,1)S(1)}, bf16[2,1152]{1,0:T(2,128)(2,1)S(1)}, u32[]{:S(2)}, u32[]{:S(2)}) collective-permute-start(bf16[2,1152]{1,0:T(2,128)(2,1)S(1)} %message.1), channel_id=1, source_target_pairs={{0,8},{4,12},{8,0},{12,4},{16,24},{20,28},{24,16},{28,20},{32,40},... | collective-permute-start | bytes 13832 | tf_op jit(solution)/shard_map/ppermute | solution.py:176
  8.1 1.5 %collective-permute-start.1 = (bf16[2,1152]{1,0:T(2,128)(2,1)S(1)}, bf16[2,1152]{1,0:T(2,128)(2,1)S(1)}, u32[]{:S(2)}, u32[]{:S(2)}) collective-permute-start(bf16[2,1152]{1,0:T(2,128)(2,1)S(1)} %message.1), channel_id=1, source_target_pairs={{0,4},{4,0},{8,12},{12,8},{16,20},{20,16},{24,28},{28,24},{32,36},... | collective-permute-start | bytes 13832 | tf_op jit(solution)/shard_map/ppermute | solution.py:176
  9.6 0.0 collective-permute-start
  9.6 2.4 %fetch.1 = (f32[2,512]{1,0:T(2,128)S(1)}, bf16[512,576]{1,0:T(8,128)(2,1)S(1)}, bf16[2,512,128]{2,1,0:T(8,128)(2,1)S(1)}, bf16[256,7168]{1,0:T(8,128)(2,1)S(1)}) custom-call(s32[1]{0:T(128)} %bitcast.here_ref, s32[2]{0:T(128)} %lengths_hbm.1, s32[2,256]{1,0:T(2,128)} %table_hbm.1, bf16[512,576]{1,0:T(8,128)(2,1)} %bitcast.4, bf16[2,512,128]{2,1,0:T(8,128)(2,1)} %w_uv_hbm.1, ...), custom_call_target="tpu_custom_call" | custom-call | bytes 5242880 | tf_op jit(solution)/shard_map/fetch/pallas_call | solution.py:177
  12.0 0.0 collective-permute-done.2
  12.0 0.6 collective-permute-done.1
  12.6 2.7 %collective-permute-done = bf16[2,1152]{1,0:T(2,128)(2,1)S(1)} collective-permute-done((bf16[2,1152]{1,0:T(2,128)(2,1)S(1)}, bf16[2,1152]{1,0:T(2,128)(2,1)S(1)}, u32[]{:S(2)}, u32[]{:S(2)}) %collective-permute-start) | collective-permute-done | bytes 4640 | tf_op jit(solution)/shard_map/ppermute | solution.py:176
  15.3 0.1 broadcast_select_fusion.1
  15.4 0.2 broadcast_in_dim.58
  15.5 14.2 %all_to_all.10 = bf16[16,4,2,1152]{3,2,1,0:T(2,128)(2,1)S(1)} all-to-all(bf16[16,4,2,1152]{3,2,1,0:T(2,128)(2,1)S(1)} %broadcast_in_dim.58), channel_id=1, replica_groups={{0,16,32,48,64,80,96,112,128,144,160,176,192,208,224,240},{4,20,36,52,6..., dimensions={0} | all-to-all | bytes 589824 | tf_op jit(solution)/shard_map/all_to_all | solution.py:203
  29.7 1.2 %attend.1 = bf16[64,2,1152]{2,1,0:T(2,128)(2,1)S(1)} custom-call(bf16[64,2,1152]{2,1,0:T(2,128)(2,1)S(1)} %bitcast.3, bf16[512,576]{1,0:T(8,128)(2,1)S(1)} %get-tuple-element.19.keys_ref, f32[2,512]{1,0:T(2,128)S(1)} %get-tuple-element.20.live_ref), custom_call_target="tpu_custom_call" | custom-call | tf_op jit(solution)/shard_map/attend/pallas_call | solution.py:209
  30.9 20.0 %all_to_all.11.messages_ref = bf16[64,2,1152]{2,1,0:T(2,128)(2,1)S(1)} all-to-all(bf16[64,2,1152]{2,1,0:T(2,128)(2,1)S(1)} %attend.1), channel_id=1, replica_groups=mesh['ctx'=64,'grp'=4] {'ctx'}, dimensions={0} | all-to-all | bytes 589824 | tf_op jit(solution)/shard_map/all_to_all | solution.py:218
  50.9 1.3 %project.1 = bf16[2,7168]{1,0:T(2,128)(2,1)S(1)} custom-call(bf16[64,2,1152]{2,1,0:T(2,128)(2,1)S(1)} %all_to_all.11.messages_ref, bf16[2,512,128]{2,1,0:T(8,128)(2,1)S(1)} %get-tuple-element.21.w_uv_ref, bf16[256,7168]{1,0:T(8,128)(2,1)S(1)} %get-tuple-element.22.w_out_ref), custom_call_target="tpu_custom_call" | custom-call | tf_op jit(solution)/shard_map/project/pallas_call | solution.py:219
  52.2 1.3 %collective-permute-start.5 = (bf16[2,7168]{1,0:T(2,128)(2,1)S(1)}, bf16[2,7168]{1,0:T(2,128)(2,1)S(1)}, u32[]{:S(2)}, u32[]{:S(2)}) collective-permute-start(bf16[2,7168]{1,0:T(2,128)(2,1)S(1)} %project.1), channel_id=1, source_target_pairs={{0,128},{4,132},{8,136},{12,140},{16,144},{20,148},{24,152},{28,15... | collective-permute-start | bytes 86024 | tf_op jit(solution)/shard_map/ppermute | solution.py:23
  53.5 1.7 %collective-permute-start.4 = (bf16[2,7168]{1,0:T(2,128)(2,1)S(1)}, bf16[2,7168]{1,0:T(2,128)(2,1)S(1)}, u32[]{:S(2)}, u32[]{:S(2)}) collective-permute-start(bf16[2,7168]{1,0:T(2,128)(2,1)S(1)} %project.1), channel_id=1, source_target_pairs={{0,192},{4,196},{8,200},{12,204},{16,208},{20,212},{24,216},{28,22... | collective-permute-start | bytes 86024 | tf_op jit(solution)/shard_map/ppermute | solution.py:23
  55.2 1.7 %collective-permute-start.3 = (bf16[2,7168]{1,0:T(2,128)(2,1)S(1)}, bf16[2,7168]{1,0:T(2,128)(2,1)S(1)}, u32[]{:S(2)}, u32[]{:S(2)}) collective-permute-start(bf16[2,7168]{1,0:T(2,128)(2,1)S(1)} %project.1), channel_id=1, source_target_pairs={{0,64},{4,68},{8,72},{12,76},{16,80},{20,84},{24,88},{28,92},{32,9... | collective-permute-start | bytes 86024 | tf_op jit(solution)/shard_map/ppermute | solution.py:23
  56.9 0.7 collective-permute-done.5
  57.6 0.0 collective-permute-done.4
  57.7 1.4 %collective-permute-done.3 = bf16[2,7168]{1,0:T(2,128)(2,1)S(1)} collective-permute-done((bf16[2,7168]{1,0:T(2,128)(2,1)S(1)}, bf16[2,7168]{1,0:T(2,128)(2,1)S(1)}, u32[]{:S(2)}, u32[]{:S(2)}) %collective-permute-start.3) | collective-permute-done | bytes 28704 | tf_op jit(solution)/shard_map/ppermute | solution.py:23
  59.1 0.1 add_convert_fusion.2
  59.1 0.7 collective-permute-start.8
  59.8 2.7 %collective-permute-start.7 = (bf16[2,7168]{1,0:T(2,128)(2,1)S(1)}, bf16[2,7168]{1,0:T(2,128)(2,1)S(1)}, u32[]{:S(2)}, u32[]{:S(2)}) collective-permute-start(bf16[2,7168]{1,0:T(2,128)(2,1)S(1)} %add_convert_fusion.2), channel_id=1, source_target_pairs={{0,48},{4,52},{8,56},{12,60},{16,32},{20,36},{24,40},{28,44},{32,1... | collective-permute-start | bytes 86024 | tf_op jit(solution)/shard_map/ppermute | solution.py:23
  62.5 0.2 collective-permute-start.6
  62.7 1.9 %collective-permute-done.8 = bf16[2,7168]{1,0:T(2,128)(2,1)S(1)} collective-permute-done((bf16[2,7168]{1,0:T(2,128)(2,1)S(1)}, bf16[2,7168]{1,0:T(2,128)(2,1)S(1)}, u32[]{:S(2)}, u32[]{:S(2)}) %collective-permute-start.8) | collective-permute-done | bytes 28704 | tf_op jit(solution)/shard_map/ppermute | solution.py:23
  64.6 0.3 collective-permute-done.7
  64.9 1.5 %collective-permute-done.6 = bf16[2,7168]{1,0:T(2,128)(2,1)S(1)} collective-permute-done((bf16[2,7168]{1,0:T(2,128)(2,1)S(1)}, bf16[2,7168]{1,0:T(2,128)(2,1)S(1)}, u32[]{:S(2)}, u32[]{:S(2)}) %collective-permute-start.6) | collective-permute-done | bytes 28704 | tf_op jit(solution)/shard_map/ppermute | solution.py:23
  66.4 0.1 add_convert_fusion.1
  66.4 0.1 collective-permute-start.11
  66.5 4.5 %collective-permute-start.10 = (bf16[2,7168]{1,0:T(2,128)(2,1)S(1)}, bf16[2,7168]{1,0:T(2,128)(2,1)S(1)}, u32[]{:S(2)}, u32[]{:S(2)}) collective-permute-start(bf16[2,7168]{1,0:T(2,128)(2,1)S(1)} %add_convert_fusion.1), channel_id=1, source_target_pairs={{0,12},{4,8},{8,4},{12,0},{16,28},{20,24},{24,20},{28,16},{32,44},... | collective-permute-start | bytes 86024 | tf_op jit(solution)/shard_map/ppermute | solution.py:23
  71.0 2.0 %collective-permute-start.9 = (bf16[2,7168]{1,0:T(2,128)(2,1)S(1)}, bf16[2,7168]{1,0:T(2,128)(2,1)S(1)}, u32[]{:S(2)}, u32[]{:S(2)}) collective-permute-start(bf16[2,7168]{1,0:T(2,128)(2,1)S(1)} %add_convert_fusion.1), channel_id=1, source_target_pairs={{0,4},{4,0},{8,12},{12,8},{16,20},{20,16},{24,28},{28,24},{32,36},... | collective-permute-start | bytes 86024 | tf_op jit(solution)/shard_map/ppermute | solution.py:23
  73.0 1.3 %collective-permute-done.11 = bf16[2,7168]{1,0:T(2,128)(2,1)S(1)} collective-permute-done((bf16[2,7168]{1,0:T(2,128)(2,1)S(1)}, bf16[2,7168]{1,0:T(2,128)(2,1)S(1)}, u32[]{:S(2)}, u32[]{:S(2)}) %collective-permute-start.11) | collective-permute-done | bytes 28704 | tf_op jit(solution)/shard_map/ppermute | solution.py:23
  74.3 0.0 collective-permute-done.10
  74.3 1.5 %collective-permute-done.9 = bf16[2,7168]{1,0:T(2,128)(2,1)S(1)} collective-permute-done((bf16[2,7168]{1,0:T(2,128)(2,1)S(1)}, bf16[2,7168]{1,0:T(2,128)(2,1)S(1)}, u32[]{:S(2)}, u32[]{:S(2)}) %collective-permute-start.9) | collective-permute-done | bytes 28704 | tf_op jit(solution)/shard_map/ppermute | solution.py:23
  75.8 0.7 add_convert_fusion
  (2 shorter events, 0.0 us)
Async XLA Ops:
  0.8 11.2 %collective-permute-start.2 = (bf16[2,1152]{1,0:T(2,128)(2,1)S(1)}, bf16[2,1152]{1,0:T(2,128)(2,1)S(1)}, u32[]{:S(2)}, u32[]{:S(2)}) collective-permute-start(bf16[2,1152]{1,0:T(2,128)(2,1)S(1)} %message.1), channel_id=1, source_target_pairs={{0,8},{4,12},{8,0},{12,4},{16,24},{20,28},{24,16},{28,20},{32,40},... | collective-permute-start | bytes 13832 | tf_op jit(solution)/shard_map/ppermute | solution.py:176
  8.1 4.5 %collective-permute-start.1 = (bf16[2,1152]{1,0:T(2,128)(2,1)S(1)}, bf16[2,1152]{1,0:T(2,128)(2,1)S(1)}, u32[]{:S(2)}, u32[]{:S(2)}) collective-permute-start(bf16[2,1152]{1,0:T(2,128)(2,1)S(1)} %message.1), channel_id=1, source_target_pairs={{0,4},{4,0},{8,12},{12,8},{16,20},{20,16},{24,28},{28,24},{32,36},... | collective-permute-start | bytes 13832 | tf_op jit(solution)/shard_map/ppermute | solution.py:176
  9.6 5.7 %collective-permute-start = (bf16[2,1152]{1,0:T(2,128)(2,1)S(1)}, bf16[2,1152]{1,0:T(2,128)(2,1)S(1)}, u32[]{:S(2)}, u32[]{:S(2)}) collective-permute-start(bf16[2,1152]{1,0:T(2,128)(2,1)S(1)} %message.1), channel_id=1, source_target_pairs={{0,12},{4,8},{8,4},{12,0},{16,28},{20,24},{24,20},{28,16},{32,44},... | collective-permute-start | bytes 13832 | tf_op jit(solution)/shard_map/ppermute | solution.py:176
  52.2 5.5 %collective-permute-start.5 = (bf16[2,7168]{1,0:T(2,128)(2,1)S(1)}, bf16[2,7168]{1,0:T(2,128)(2,1)S(1)}, u32[]{:S(2)}, u32[]{:S(2)}) collective-permute-start(bf16[2,7168]{1,0:T(2,128)(2,1)S(1)} %project.1), channel_id=1, source_target_pairs={{0,128},{4,132},{8,136},{12,140},{16,144},{20,148},{24,152},{28,15... | collective-permute-start | bytes 86024 | tf_op jit(solution)/shard_map/ppermute | solution.py:23
  53.5 4.2 %collective-permute-start.4 = (bf16[2,7168]{1,0:T(2,128)(2,1)S(1)}, bf16[2,7168]{1,0:T(2,128)(2,1)S(1)}, u32[]{:S(2)}, u32[]{:S(2)}) collective-permute-start(bf16[2,7168]{1,0:T(2,128)(2,1)S(1)} %project.1), channel_id=1, source_target_pairs={{0,192},{4,196},{8,200},{12,204},{16,208},{20,212},{24,216},{28,22... | collective-permute-start | bytes 86024 | tf_op jit(solution)/shard_map/ppermute | solution.py:23
  55.2 3.9 %collective-permute-start.3 = (bf16[2,7168]{1,0:T(2,128)(2,1)S(1)}, bf16[2,7168]{1,0:T(2,128)(2,1)S(1)}, u32[]{:S(2)}, u32[]{:S(2)}) collective-permute-start(bf16[2,7168]{1,0:T(2,128)(2,1)S(1)} %project.1), channel_id=1, source_target_pairs={{0,64},{4,68},{8,72},{12,76},{16,80},{20,84},{24,88},{28,92},{32,9... | collective-permute-start | bytes 86024 | tf_op jit(solution)/shard_map/ppermute | solution.py:23
  59.1 5.5 %collective-permute-start.8 = (bf16[2,7168]{1,0:T(2,128)(2,1)S(1)}, bf16[2,7168]{1,0:T(2,128)(2,1)S(1)}, u32[]{:S(2)}, u32[]{:S(2)}) collective-permute-start(bf16[2,7168]{1,0:T(2,128)(2,1)S(1)} %add_convert_fusion.2), channel_id=1, source_target_pairs={{0,32},{4,36},{8,40},{12,44},{16,48},{20,52},{24,56},{28,60},{32,0... | collective-permute-start | bytes 86024 | tf_op jit(solution)/shard_map/ppermute | solution.py:23
  59.8 5.1 %collective-permute-start.7 = (bf16[2,7168]{1,0:T(2,128)(2,1)S(1)}, bf16[2,7168]{1,0:T(2,128)(2,1)S(1)}, u32[]{:S(2)}, u32[]{:S(2)}) collective-permute-start(bf16[2,7168]{1,0:T(2,128)(2,1)S(1)} %add_convert_fusion.2), channel_id=1, source_target_pairs={{0,48},{4,52},{8,56},{12,60},{16,32},{20,36},{24,40},{28,44},{32,1... | collective-permute-start | bytes 86024 | tf_op jit(solution)/shard_map/ppermute | solution.py:23
  62.5 3.9 %collective-permute-start.6 = (bf16[2,7168]{1,0:T(2,128)(2,1)S(1)}, bf16[2,7168]{1,0:T(2,128)(2,1)S(1)}, u32[]{:S(2)}, u32[]{:S(2)}) collective-permute-start(bf16[2,7168]{1,0:T(2,128)(2,1)S(1)} %add_convert_fusion.2), channel_id=1, source_target_pairs={{0,16},{4,20},{8,24},{12,28},{16,0},{20,4},{24,8},{28,12},{32,48},... | collective-permute-start | bytes 86024 | tf_op jit(solution)/shard_map/ppermute | solution.py:23
  66.4 7.9 %collective-permute-start.11 = (bf16[2,7168]{1,0:T(2,128)(2,1)S(1)}, bf16[2,7168]{1,0:T(2,128)(2,1)S(1)}, u32[]{:S(2)}, u32[]{:S(2)}) collective-permute-start(bf16[2,7168]{1,0:T(2,128)(2,1)S(1)} %add_convert_fusion.1), channel_id=1, source_target_pairs={{0,8},{4,12},{8,0},{12,4},{16,24},{20,28},{24,16},{28,20},{32,40},... | collective-permute-start | bytes 86024 | tf_op jit(solution)/shard_map/ppermute | solution.py:23
  66.5 7.8 %collective-permute-start.10 = (bf16[2,7168]{1,0:T(2,128)(2,1)S(1)}, bf16[2,7168]{1,0:T(2,128)(2,1)S(1)}, u32[]{:S(2)}, u32[]{:S(2)}) collective-permute-start(bf16[2,7168]{1,0:T(2,128)(2,1)S(1)} %add_convert_fusion.1), channel_id=1, source_target_pairs={{0,12},{4,8},{8,4},{12,0},{16,28},{20,24},{24,20},{28,16},{32,44},... | collective-permute-start | bytes 86024 | tf_op jit(solution)/shard_map/ppermute | solution.py:23
  71.0 4.8 %collective-permute-start.9 = (bf16[2,7168]{1,0:T(2,128)(2,1)S(1)}, bf16[2,7168]{1,0:T(2,128)(2,1)S(1)}, u32[]{:S(2)}, u32[]{:S(2)}) collective-permute-start(bf16[2,7168]{1,0:T(2,128)(2,1)S(1)} %add_convert_fusion.1), channel_id=1, source_target_pairs={{0,4},{4,0},{8,12},{12,8},{16,20},{20,16},{24,28},{28,24},{32,36},... | collective-permute-start | bytes 86024 | tf_op jit(solution)/shard_map/ppermute | solution.py:23

commit v16 on v15

--- a/solution.py
+++ b/solution.py
@@ -21,7 +21,7 @@
 
 def sum_of_four(x, count, low):
     a, c, b = (lax.ppermute(x, CTX, xor_pairs(count, k << low)) for k in (1, 3, 2))
-    return (x.astype(F32) + a.astype(F32)) + (c.astype(F32) + b.astype(F32))
+    return (x.astype(F32) + c.astype(F32)) + (a.astype(F32) + b.astype(F32))
 
 
 def message_kernel(q_latent_hbm, q_rope_hbm, message_ref, q_latent_ref, q_rope_ref, sems):

time: 76.7 us -> 76.9 us (level)
  no operation moved by 1% of the time
where the time goes in v16:
time: 76.9 us; the launch traced here: 76.3 us
  blocking collectives  34.2 us (44%)
  starting transfers between devices  23.7 us (31%)
  waiting for transfers between devices  11.7 us (15%)
  Pallas kernels  5.6 us (7%)
  other arithmetic  0.91 us (1%)
    all_to_all x1, blocking collectives, local(): state = lax.all_to_all(state, CTX, split_axis=0, concat_axis=0, tiled=True)  20 us
    ppermute x9, starting transfers between devices, sum_of_four(): lax.ppermute(x, CTX, xor_pairs(count, k << low))  14.9 us
    all_to_all x1, blocking collectives, local(): lax.all_to_all(jnp.broadcast_to(column[None], (count // near, near, rows,...  14.2 us
    ppermute x3, starting transfers between devices, local(): lax.ppermute(message, CTX, xor_pairs(count, k))  8.75 us
    ppermute x9, waiting for transfers between devices, sum_of_four(): lax.ppermute(x, CTX, xor_pairs(count, k << low))  8.41 us
    ppermute x3, waiting for transfers between devices, local(): lax.ppermute(message, CTX, xor_pairs(count, k))  3.29 us
    pallas_call x1, Pallas kernels, local(): pl.pallas_call(functools.partial(fetch_kernel, page_len), out_shape=(pltp...  2.39 us
  transfers between devices with their start and end apart: 12, of which 9 were waited for; matrix products, arithmetic and copies ran while one was open for 0% of the time, Pallas kernels for 3%

profile of v16, /device:TPU:2, one launch (start us, length us, event | category | flops | bytes accessed | tf_op | source)
XLA Modules:
  0.0 76.3 jit_solution(15248220248336904791)
XLA Ops:
  0.0 0.8 %message.1 = bf16[2,1152]{1,0:T(2,128)(2,1)S(1)} custom-call(bf16[2,2,512]{2,1,0:T(2,128)(2,1)} %q_latent_hbm.1, bf16[2,2,64]{2,1,0:T(2,128)(2,1)} %q_rope_hbm.1), custom_call_target="tpu_custom_call" | custom-call | tf_op jit(solution)/shard_map/message/pallas_call | solution.py:165
  0.8 7.3 %collective-permute-start.2 = (bf16[2,1152]{1,0:T(2,128)(2,1)S(1)}, bf16[2,1152]{1,0:T(2,128)(2,1)S(1)}, u32[]{:S(2)}, u32[]{:S(2)}) collective-permute-start(bf16[2,1152]{1,0:T(2,128)(2,1)S(1)} %message.1), channel_id=1, source_target_pairs={{0,8},{4,12},{8,0},{12,4},{16,24},{20,28},{24,16},{28,20},{32,40},... | collective-permute-start | bytes 13832 | tf_op jit(solution)/shard_map/ppermute | solution.py:176
  8.1 1.5 %collective-permute-start.1 = (bf16[2,1152]{1,0:T(2,128)(2,1)S(1)}, bf16[2,1152]{1,0:T(2,128)(2,1)S(1)}, u32[]{:S(2)}, u32[]{:S(2)}) collective-permute-start(bf16[2,1152]{1,0:T(2,128)(2,1)S(1)} %message.1), channel_id=1, source_target_pairs={{0,4},{4,0},{8,12},{12,8},{16,20},{20,16},{24,28},{28,24},{32,36},... | collective-permute-start | bytes 13832 | tf_op jit(solution)/shard_map/ppermute | solution.py:176
  9.6 0.0 collective-permute-start
  9.6 2.4 %fetch.1 = (f32[2,512]{1,0:T(2,128)S(1)}, bf16[512,576]{1,0:T(8,128)(2,1)S(1)}, bf16[2,512,128]{2,1,0:T(8,128)(2,1)S(1)}, bf16[256,7168]{1,0:T(8,128)(2,1)S(1)}) custom-call(s32[1]{0:T(128)} %bitcast.here_ref, s32[2]{0:T(128)} %lengths_hbm.1, s32[2,256]{1,0:T(2,128)} %table_hbm.1, bf16[512,576]{1,0:T(8,128)(2,1)} %bitcast.4, bf16[2,512,128]{2,1,0:T(8,128)(2,1)} %w_uv_hbm.1, ...), custom_call_target="tpu_custom_call" | custom-call | bytes 5242880 | tf_op jit(solution)/shard_map/fetch/pallas_call | solution.py:177
  12.0 0.0 collective-permute-done.2
  12.0 0.6 collective-permute-done.1
  12.6 2.7 %collective-permute-done = bf16[2,1152]{1,0:T(2,128)(2,1)S(1)} collective-permute-done((bf16[2,1152]{1,0:T(2,128)(2,1)S(1)}, bf16[2,1152]{1,0:T(2,128)(2,1)S(1)}, u32[]{:S(2)}, u32[]{:S(2)}) %collective-permute-start) | collective-permute-done | bytes 4640 | tf_op jit(solution)/shard_map/ppermute | solution.py:176
  15.3 0.1 broadcast_select_fusion.1
  15.4 0.2 broadcast_in_dim.58
  15.5 14.2 %all_to_all.10 = bf16[16,4,2,1152]{3,2,1,0:T(2,128)(2,1)S(1)} all-to-all(bf16[16,4,2,1152]{3,2,1,0:T(2,128)(2,1)S(1)} %broadcast_in_dim.58), channel_id=1, replica_groups={{0,16,32,48,64,80,96,112,128,144,160,176,192,208,224,240},{4,20,36,52,6..., dimensions={0} | all-to-all | bytes 589824 | tf_op jit(solution)/shard_map/all_to_all | solution.py:203
  29.7 1.2 %attend.1 = bf16[64,2,1152]{2,1,0:T(2,128)(2,1)S(1)} custom-call(bf16[64,2,1152]{2,1,0:T(2,128)(2,1)S(1)} %bitcast.3, bf16[512,576]{1,0:T(8,128)(2,1)S(1)} %get-tuple-element.19.keys_ref, f32[2,512]{1,0:T(2,128)S(1)} %get-tuple-element.20.live_ref), custom_call_target="tpu_custom_call" | custom-call | tf_op jit(solution)/shard_map/attend/pallas_call | solution.py:209
  30.9 20.0 %all_to_all.11.messages_ref = bf16[64,2,1152]{2,1,0:T(2,128)(2,1)S(1)} all-to-all(bf16[64,2,1152]{2,1,0:T(2,128)(2,1)S(1)} %attend.1), channel_id=1, replica_groups=mesh['ctx'=64,'grp'=4] {'ctx'}, dimensions={0} | all-to-all | bytes 589824 | tf_op jit(solution)/shard_map/all_to_all | solution.py:218
  50.9 1.3 %project.1 = bf16[2,7168]{1,0:T(2,128)(2,1)S(1)} custom-call(bf16[64,2,1152]{2,1,0:T(2,128)(2,1)S(1)} %all_to_all.11.messages_ref, bf16[2,512,128]{2,1,0:T(8,128)(2,1)S(1)} %get-tuple-element.21.w_uv_ref, bf16[256,7168]{1,0:T(8,128)(2,1)S(1)} %get-tuple-element.22.w_out_ref), custom_call_target="tpu_custom_call" | custom-call | tf_op jit(solution)/shard_map/project/pallas_call | solution.py:219
  52.2 1.3 %collective-permute-start.5 = (bf16[2,7168]{1,0:T(2,128)(2,1)S(1)}, bf16[2,7168]{1,0:T(2,128)(2,1)S(1)}, u32[]{:S(2)}, u32[]{:S(2)}) collective-permute-start(bf16[2,7168]{1,0:T(2,128)(2,1)S(1)} %project.1), channel_id=1, source_target_pairs={{0,128},{4,132},{8,136},{12,140},{16,144},{20,148},{24,152},{28,15... | collective-permute-start | bytes 86024 | tf_op jit(solution)/shard_map/ppermute | solution.py:23
  53.5 0.9 %collective-permute-start.4 = (bf16[2,7168]{1,0:T(2,128)(2,1)S(1)}, bf16[2,7168]{1,0:T(2,128)(2,1)S(1)}, u32[]{:S(2)}, u32[]{:S(2)}) collective-permute-start(bf16[2,7168]{1,0:T(2,128)(2,1)S(1)} %project.1), channel_id=1, source_target_pairs={{0,64},{4,68},{8,72},{12,76},{16,80},{20,84},{24,88},{28,92},{32,9... | collective-permute-start | bytes 86024 | tf_op jit(solution)/shard_map/ppermute | solution.py:23
  54.3 2.0 %collective-permute-start.3 = (bf16[2,7168]{1,0:T(2,128)(2,1)S(1)}, bf16[2,7168]{1,0:T(2,128)(2,1)S(1)}, u32[]{:S(2)}, u32[]{:S(2)}) collective-permute-start(bf16[2,7168]{1,0:T(2,128)(2,1)S(1)} %project.1), channel_id=1, source_target_pairs={{0,192},{4,196},{8,200},{12,204},{16,208},{20,212},{24,216},{28,22... | collective-permute-start | bytes 86024 | tf_op jit(solution)/shard_map/ppermute | solution.py:23
  56.3 1.3 %collective-permute-done.5 = bf16[2,7168]{1,0:T(2,128)(2,1)S(1)} collective-permute-done((bf16[2,7168]{1,0:T(2,128)(2,1)S(1)}, bf16[2,7168]{1,0:T(2,128)(2,1)S(1)}, u32[]{:S(2)}, u32[]{:S(2)}) %collective-permute-start.5) | collective-permute-done | bytes 28704 | tf_op jit(solution)/shard_map/ppermute | solution.py:23
  57.6 0.0 collective-permute-done.4
  57.6 0.6 collective-permute-done.3
  58.2 0.1 add_convert_fusion.2
  58.3 1.8 %collective-permute-start.8 = (bf16[2,7168]{1,0:T(2,128)(2,1)S(1)}, bf16[2,7168]{1,0:T(2,128)(2,1)S(1)}, u32[]{:S(2)}, u32[]{:S(2)}) collective-permute-start(bf16[2,7168]{1,0:T(2,128)(2,1)S(1)} %add_convert_fusion.2), channel_id=1, source_target_pairs={{0,32},{4,36},{8,40},{12,44},{16,48},{20,52},{24,56},{28,60},{32,0... | collective-permute-start | bytes 86024 | tf_op jit(solution)/shard_map/ppermute | solution.py:23
  60.1 0.7 collective-permute-start.7
  60.8 1.7 %collective-permute-start.6 = (bf16[2,7168]{1,0:T(2,128)(2,1)S(1)}, bf16[2,7168]{1,0:T(2,128)(2,1)S(1)}, u32[]{:S(2)}, u32[]{:S(2)}) collective-permute-start(bf16[2,7168]{1,0:T(2,128)(2,1)S(1)} %add_convert_fusion.2), channel_id=1, source_target_pairs={{0,48},{4,52},{8,56},{12,60},{16,32},{20,36},{24,40},{28,44},{32,1... | collective-permute-start | bytes 86024 | tf_op jit(solution)/shard_map/ppermute | solution.py:23
  62.5 1.3 %collective-permute-done.8 = bf16[2,7168]{1,0:T(2,128)(2,1)S(1)} collective-permute-done((bf16[2,7168]{1,0:T(2,128)(2,1)S(1)}, bf16[2,7168]{1,0:T(2,128)(2,1)S(1)}, u32[]{:S(2)}, u32[]{:S(2)}) %collective-permute-start.8) | collective-permute-done | bytes 28704 | tf_op jit(solution)/shard_map/ppermute | solution.py:23
  63.7 0.2 collective-permute-done.7
  64.0 1.9 %collective-permute-done.6 = bf16[2,7168]{1,0:T(2,128)(2,1)S(1)} collective-permute-done((bf16[2,7168]{1,0:T(2,128)(2,1)S(1)}, bf16[2,7168]{1,0:T(2,128)(2,1)S(1)}, u32[]{:S(2)}, u32[]{:S(2)}) %collective-permute-start.6) | collective-permute-done | bytes 28704 | tf_op jit(solution)/shard_map/ppermute | solution.py:23
  65.8 0.1 add_convert_fusion.1
  65.9 1.5 %collective-permute-start.11 = (bf16[2,7168]{1,0:T(2,128)(2,1)S(1)}, bf16[2,7168]{1,0:T(2,128)(2,1)S(1)}, u32[]{:S(2)}, u32[]{:S(2)}) collective-permute-start(bf16[2,7168]{1,0:T(2,128)(2,1)S(1)} %add_convert_fusion.1), channel_id=1, source_target_pairs={{0,8},{4,12},{8,0},{12,4},{16,24},{20,28},{24,16},{28,20},{32,40},... | collective-permute-start | bytes 86024 | tf_op jit(solution)/shard_map/ppermute | solution.py:23
  67.4 2.2 %collective-permute-start.10 = (bf16[2,7168]{1,0:T(2,128)(2,1)S(1)}, bf16[2,7168]{1,0:T(2,128)(2,1)S(1)}, u32[]{:S(2)}, u32[]{:S(2)}) collective-permute-start(bf16[2,7168]{1,0:T(2,128)(2,1)S(1)} %add_convert_fusion.1), channel_id=1, source_target_pairs={{0,4},{4,0},{8,12},{12,8},{16,20},{20,16},{24,28},{28,24},{32,36},... | collective-permute-start | bytes 86024 | tf_op jit(solution)/shard_map/ppermute | solution.py:23
  69.6 2.9 %collective-permute-start.9 = (bf16[2,7168]{1,0:T(2,128)(2,1)S(1)}, bf16[2,7168]{1,0:T(2,128)(2,1)S(1)}, u32[]{:S(2)}, u32[]{:S(2)}) collective-permute-start(bf16[2,7168]{1,0:T(2,128)(2,1)S(1)} %add_convert_fusion.1), channel_id=1, source_target_pairs={{0,12},{4,8},{8,4},{12,0},{16,28},{20,24},{24,20},{28,16},{32,44},... | collective-permute-start | bytes 86024 | tf_op jit(solution)/shard_map/ppermute | solution.py:23
  72.5 1.3 %collective-permute-done.11 = bf16[2,7168]{1,0:T(2,128)(2,1)S(1)} collective-permute-done((bf16[2,7168]{1,0:T(2,128)(2,1)S(1)}, bf16[2,7168]{1,0:T(2,128)(2,1)S(1)}, u32[]{:S(2)}, u32[]{:S(2)}) %collective-permute-start.11) | collective-permute-done | bytes 28704 | tf_op jit(solution)/shard_map/ppermute | solution.py:23
  73.8 0.0 collective-permute-done.10
  73.8 1.9 %collective-permute-done.9 = bf16[2,7168]{1,0:T(2,128)(2,1)S(1)} collective-permute-done((bf16[2,7168]{1,0:T(2,128)(2,1)S(1)}, bf16[2,7168]{1,0:T(2,128)(2,1)S(1)}, u32[]{:S(2)}, u32[]{:S(2)}) %collective-permute-start.9) | collective-permute-done | bytes 28704 | tf_op jit(solution)/shard_map/ppermute | solution.py:23
  75.6 0.7 add_convert_fusion
  (2 shorter events, 0.0 us)
Async XLA Ops:
  0.8 11.2 %collective-permute-start.2 = (bf16[2,1152]{1,0:T(2,128)(2,1)S(1)}, bf16[2,1152]{1,0:T(2,128)(2,1)S(1)}, u32[]{:S(2)}, u32[]{:S(2)}) collective-permute-start(bf16[2,1152]{1,0:T(2,128)(2,1)S(1)} %message.1), channel_id=1, source_target_pairs={{0,8},{4,12},{8,0},{12,4},{16,24},{20,28},{24,16},{28,20},{32,40},... | collective-permute-start | bytes 13832 | tf_op jit(solution)/shard_map/ppermute | solution.py:176
  8.1 4.5 %collective-permute-start.1 = (bf16[2,1152]{1,0:T(2,128)(2,1)S(1)}, bf16[2,1152]{1,0:T(2,128)(2,1)S(1)}, u32[]{:S(2)}, u32[]{:S(2)}) collective-permute-start(bf16[2,1152]{1,0:T(2,128)(2,1)S(1)} %message.1), channel_id=1, source_target_pairs={{0,4},{4,0},{8,12},{12,8},{16,20},{20,16},{24,28},{28,24},{32,36},... | collective-permute-start | bytes 13832 | tf_op jit(solution)/shard_map/ppermute | solution.py:176
  9.6 5.7 %collective-permute-start = (bf16[2,1152]{1,0:T(2,128)(2,1)S(1)}, bf16[2,1152]{1,0:T(2,128)(2,1)S(1)}, u32[]{:S(2)}, u32[]{:S(2)}) collective-permute-start(bf16[2,1152]{1,0:T(2,128)(2,1)S(1)} %message.1), channel_id=1, source_target_pairs={{0,12},{4,8},{8,4},{12,0},{16,28},{20,24},{24,20},{28,16},{32,44},... | collective-permute-start | bytes 13832 | tf_op jit(solution)/shard_map/ppermute | solution.py:176
  52.2 5.4 %collective-permute-start.5 = (bf16[2,7168]{1,0:T(2,128)(2,1)S(1)}, bf16[2,7168]{1,0:T(2,128)(2,1)S(1)}, u32[]{:S(2)}, u32[]{:S(2)}) collective-permute-start(bf16[2,7168]{1,0:T(2,128)(2,1)S(1)} %project.1), channel_id=1, source_target_pairs={{0,128},{4,132},{8,136},{12,140},{16,144},{20,148},{24,152},{28,15... | collective-permute-start | bytes 86024 | tf_op jit(solution)/shard_map/ppermute | solution.py:23
  53.5 4.1 %collective-permute-start.4 = (bf16[2,7168]{1,0:T(2,128)(2,1)S(1)}, bf16[2,7168]{1,0:T(2,128)(2,1)S(1)}, u32[]{:S(2)}, u32[]{:S(2)}) collective-permute-start(bf16[2,7168]{1,0:T(2,128)(2,1)S(1)} %project.1), channel_id=1, source_target_pairs={{0,64},{4,68},{8,72},{12,76},{16,80},{20,84},{24,88},{28,92},{32,9... | collective-permute-start | bytes 86024 | tf_op jit(solution)/shard_map/ppermute | solution.py:23
  54.3 3.9 %collective-permute-start.3 = (bf16[2,7168]{1,0:T(2,128)(2,1)S(1)}, bf16[2,7168]{1,0:T(2,128)(2,1)S(1)}, u32[]{:S(2)}, u32[]{:S(2)}) collective-permute-start(bf16[2,7168]{1,0:T(2,128)(2,1)S(1)} %project.1), channel_id=1, source_target_pairs={{0,192},{4,196},{8,200},{12,204},{16,208},{20,212},{24,216},{28,22... | collective-permute-start | bytes 86024 | tf_op jit(solution)/shard_map/ppermute | solution.py:23
  58.3 5.5 %collective-permute-start.8 = (bf16[2,7168]{1,0:T(2,128)(2,1)S(1)}, bf16[2,7168]{1,0:T(2,128)(2,1)S(1)}, u32[]{:S(2)}, u32[]{:S(2)}) collective-permute-start(bf16[2,7168]{1,0:T(2,128)(2,1)S(1)} %add_convert_fusion.2), channel_id=1, source_target_pairs={{0,32},{4,36},{8,40},{12,44},{16,48},{20,52},{24,56},{28,60},{32,0... | collective-permute-start | bytes 86024 | tf_op jit(solution)/shard_map/ppermute | solution.py:23
  60.1 3.9 %collective-permute-start.7 = (bf16[2,7168]{1,0:T(2,128)(2,1)S(1)}, bf16[2,7168]{1,0:T(2,128)(2,1)S(1)}, u32[]{:S(2)}, u32[]{:S(2)}) collective-permute-start(bf16[2,7168]{1,0:T(2,128)(2,1)S(1)} %add_convert_fusion.2), channel_id=1, source_target_pairs={{0,16},{4,20},{8,24},{12,28},{16,0},{20,4},{24,8},{28,12},{32,48},... | collective-permute-start | bytes 86024 | tf_op jit(solution)/shard_map/ppermute | solution.py:23
  60.8 5.1 %collective-permute-start.6 = (bf16[2,7168]{1,0:T(2,128)(2,1)S(1)}, bf16[2,7168]{1,0:T(2,128)(2,1)S(1)}, u32[]{:S(2)}, u32[]{:S(2)}) collective-permute-start(bf16[2,7168]{1,0:T(2,128)(2,1)S(1)} %add_convert_fusion.2), channel_id=1, source_target_pairs={{0,48},{4,52},{8,56},{12,60},{16,32},{20,36},{24,40},{28,44},{32,1... | collective-permute-start | bytes 86024 | tf_op jit(solution)/shard_map/ppermute | solution.py:23
  65.9 7.9 %collective-permute-start.11 = (bf16[2,7168]{1,0:T(2,128)(2,1)S(1)}, bf16[2,7168]{1,0:T(2,128)(2,1)S(1)}, u32[]{:S(2)}, u32[]{:S(2)}) collective-permute-start(bf16[2,7168]{1,0:T(2,128)(2,1)S(1)} %add_convert_fusion.1), channel_id=1, source_target_pairs={{0,8},{4,12},{8,0},{12,4},{16,24},{20,28},{24,16},{28,20},{32,40},... | collective-permute-start | bytes 86024 | tf_op jit(solution)/shard_map/ppermute | solution.py:23
  67.4 6.4 %collective-permute-start.10 = (bf16[2,7168]{1,0:T(2,128)(2,1)S(1)}, bf16[2,7168]{1,0:T(2,128)(2,1)S(1)}, u32[]{:S(2)}, u32[]{:S(2)}) collective-permute-start(bf16[2,7168]{1,0:T(2,128)(2,1)S(1)} %add_convert_fusion.1), channel_id=1, source_target_pairs={{0,4},{4,0},{8,12},{12,8},{16,20},{20,16},{24,28},{28,24},{32,36},... | collective-permute-start | bytes 86024 | tf_op jit(solution)/shard_map/ppermute | solution.py:23
  69.6 6.1 %collective-permute-start.9 = (bf16[2,7168]{1,0:T(2,128)(2,1)S(1)}, bf16[2,7168]{1,0:T(2,128)(2,1)S(1)}, u32[]{:S(2)}, u32[]{:S(2)}) collective-permute-start(bf16[2,7168]{1,0:T(2,128)(2,1)S(1)} %add_convert_fusion.1), channel_id=1, source_target_pairs={{0,12},{4,8},{8,4},{12,0},{16,28},{20,24},{24,20},{28,16},{32,44},... | collective-permute-start | bytes 86024 | tf_op jit(solution)/shard_map/ppermute | solution.py:23

commit v17 on v15

--- a/solution.py
+++ b/solution.py
@@ -196,7 +196,7 @@
     )
     away = lax.broadcasted_iota(jnp.int32, (near, 1, 1), 0) ^ (here % near)
     column = jnp.broadcast_to(message[None], (near, rows, size))
-    for k in (2, 1, 3):
+    for k in (2, 3, 1):
         column = jnp.where(away == k, others[k][None], column)
     column, live, keys, w_uv, w_out_near = lax.optimization_barrier((column, live, keys, w_uv, w_out_near))
     planes = [[i * near + k for i in range(count // near)] for k in range(near)]

time: 76.7 us -> 76.9 us (level)
  blocking collectives: 34.2 us -> 36.3 us
  waiting for transfers between devices: 11.9 us -> 10.1 us
    all_to_all x1, blocking collectives: 20 us -> 22.1 us  [local(): state = lax.all_to_all(state, CTX, split_axis=0, concat_axis=0, tiled=True)]
    ppermute x3, waiting for transfers between devices: 3.29 us -> 1.83 us  [local(): lax.ppermute(message, CTX, xor_pairs(count, k))]
  transfers between devices with their start and end apart: 12 -> 12, of which waited for: 9 -> 8; matrix products, arithmetic and copies ran while one was open for 0% -> 0% of each run, Pallas kernels for 3% -> 3%
where the time goes in v17:
time: 76.9 us; the launch traced here: 76.7 us
  blocking collectives  36.3 us (47%)
  starting transfers between devices  23.7 us (31%)
  waiting for transfers between devices  10.1 us (13%)
  Pallas kernels  5.59 us (7%)
  other arithmetic  0.91 us (1%)
    all_to_all x1, blocking collectives, local(): state = lax.all_to_all(state, CTX, split_axis=0, concat_axis=0, tiled=True)  22.1 us
    ppermute x9, starting transfers between devices, sum_of_four(): lax.ppermute(x, CTX, xor_pairs(count, k << low))  14.9 us
    all_to_all x1, blocking collectives, local(): lax.all_to_all(jnp.broadcast_to(column[None], (count // near, near, rows,...  14.2 us
    ppermute x3, starting transfers between devices, local(): lax.ppermute(message, CTX, xor_pairs(count, k))  8.75 us
    ppermute x9, waiting for transfers between devices, sum_of_four(): lax.ppermute(x, CTX, xor_pairs(count, k << low))  8.24 us
    pallas_call x1, Pallas kernels, local(): pl.pallas_call(functools.partial(fetch_kernel, page_len), out_shape=(pltp...  2.39 us
    ppermute x3, waiting for transfers between devices, local(): lax.ppermute(message, CTX, xor_pairs(count, k))  1.83 us
  transfers between devices with their start and end apart: 12, of which 8 were waited for; matrix products, arithmetic and copies ran while one was open for 0% of the time, Pallas kernels for 3%

profile of v17, /device:TPU:2, one launch (start us, length us, event | category | flops | bytes accessed | tf_op | source)
XLA Modules:
  0.0 76.7 jit_solution(4843159984317539847)
XLA Ops:
  0.0 0.8 %message.1 = bf16[2,1152]{1,0:T(2,128)(2,1)S(1)} custom-call(bf16[2,2,512]{2,1,0:T(2,128)(2,1)} %q_latent_hbm.1, bf16[2,2,64]{2,1,0:T(2,128)(2,1)} %q_rope_hbm.1), custom_call_target="tpu_custom_call" | custom-call | tf_op jit(solution)/shard_map/message/pallas_call | solution.py:165
  0.8 7.3 %collective-permute-start.2 = (bf16[2,1152]{1,0:T(2,128)(2,1)S(1)}, bf16[2,1152]{1,0:T(2,128)(2,1)S(1)}, u32[]{:S(2)}, u32[]{:S(2)}) collective-permute-start(bf16[2,1152]{1,0:T(2,128)(2,1)S(1)} %message.1), channel_id=1, source_target_pairs={{0,8},{4,12},{8,0},{12,4},{16,24},{20,28},{24,16},{28,20},{32,40},... | collective-permute-start | bytes 13832 | tf_op jit(solution)/shard_map/ppermute | solution.py:176
  8.1 0.0 collective-permute-start.1
  8.1 1.5 %collective-permute-start = (bf16[2,1152]{1,0:T(2,128)(2,1)S(1)}, bf16[2,1152]{1,0:T(2,128)(2,1)S(1)}, u32[]{:S(2)}, u32[]{:S(2)}) collective-permute-start(bf16[2,1152]{1,0:T(2,128)(2,1)S(1)} %message.1), channel_id=1, source_target_pairs={{0,4},{4,0},{8,12},{12,8},{16,20},{20,16},{24,28},{28,24},{32,36},... | collective-permute-start | bytes 13832 | tf_op jit(solution)/shard_map/ppermute | solution.py:176
  9.6 2.4 %fetch.1 = (f32[2,512]{1,0:T(2,128)S(1)}, bf16[512,576]{1,0:T(8,128)(2,1)S(1)}, bf16[2,512,128]{2,1,0:T(8,128)(2,1)S(1)}, bf16[256,7168]{1,0:T(8,128)(2,1)S(1)}) custom-call(s32[1]{0:T(128)} %bitcast.here_ref, s32[2]{0:T(128)} %lengths_hbm.1, s32[2,256]{1,0:T(2,128)} %table_hbm.1, bf16[512,576]{1,0:T(8,128)(2,1)} %bitcast.4, bf16[2,512,128]{2,1,0:T(8,128)(2,1)} %w_uv_hbm.1, ...), custom_call_target="tpu_custom_call" | custom-call | bytes 5242880 | tf_op jit(solution)/shard_map/fetch/pallas_call | solution.py:177
  12.0 0.0 collective-permute-done.2
  12.0 1.8 %collective-permute-done.1 = bf16[2,1152]{1,0:T(2,128)(2,1)S(1)} collective-permute-done((bf16[2,1152]{1,0:T(2,128)(2,1)S(1)}, bf16[2,1152]{1,0:T(2,128)(2,1)S(1)}, u32[]{:S(2)}, u32[]{:S(2)}) %collective-permute-start.1) | collective-permute-done | bytes 4640 | tf_op jit(solution)/shard_map/ppermute | solution.py:176
  13.8 0.0 collective-permute-done
  13.8 0.1 broadcast_select_fusion.1
  13.9 0.2 broadcast_in_dim.58
  14.1 14.2 %all_to_all.10 = bf16[16,4,2,1152]{3,2,1,0:T(2,128)(2,1)S(1)} all-to-all(bf16[16,4,2,1152]{3,2,1,0:T(2,128)(2,1)S(1)} %broadcast_in_dim.58), channel_id=1, replica_groups={{0,16,32,48,64,80,96,112,128,144,160,176,192,208,224,240},{4,20,36,52,6..., dimensions={0} | all-to-all | bytes 589824 | tf_op jit(solution)/shard_map/all_to_all | solution.py:203
  28.3 1.1 %attend.1 = bf16[64,2,1152]{2,1,0:T(2,128)(2,1)S(1)} custom-call(bf16[64,2,1152]{2,1,0:T(2,128)(2,1)S(1)} %bitcast.3, bf16[512,576]{1,0:T(8,128)(2,1)S(1)} %get-tuple-element.19.keys_ref, f32[2,512]{1,0:T(2,128)S(1)} %get-tuple-element.20.live_ref), custom_call_target="tpu_custom_call" | custom-call | tf_op jit(solution)/shard_map/attend/pallas_call | solution.py:209
  29.4 22.1 %all_to_all.11.messages_ref = bf16[64,2,1152]{2,1,0:T(2,128)(2,1)S(1)} all-to-all(bf16[64,2,1152]{2,1,0:T(2,128)(2,1)S(1)} %attend.1), channel_id=1, replica_groups=mesh['ctx'=64,'grp'=4] {'ctx'}, dimensions={0} | all-to-all | bytes 589824 | tf_op jit(solution)/shard_map/all_to_all | solution.py:218
  51.5 1.3 %project.1 = bf16[2,7168]{1,0:T(2,128)(2,1)S(1)} custom-call(bf16[64,2,1152]{2,1,0:T(2,128)(2,1)S(1)} %all_to_all.11.messages_ref, bf16[2,512,128]{2,1,0:T(8,128)(2,1)S(1)} %get-tuple-element.21.w_uv_ref, bf16[256,7168]{1,0:T(8,128)(2,1)S(1)} %get-tuple-element.22.w_out_ref), custom_call_target="tpu_custom_call" | custom-call | tf_op jit(solution)/shard_map/project/pallas_call | solution.py:219
  52.8 1.3 %collective-permute-start.5 = (bf16[2,7168]{1,0:T(2,128)(2,1)S(1)}, bf16[2,7168]{1,0:T(2,128)(2,1)S(1)}, u32[]{:S(2)}, u32[]{:S(2)}) collective-permute-start(bf16[2,7168]{1,0:T(2,128)(2,1)S(1)} %project.1), channel_id=1, source_target_pairs={{0,128},{4,132},{8,136},{12,140},{16,144},{20,148},{24,152},{28,15... | collective-permute-start | bytes 86024 | tf_op jit(solution)/shard_map/ppermute | solution.py:23
  54.1 1.7 %collective-permute-start.4 = (bf16[2,7168]{1,0:T(2,128)(2,1)S(1)}, bf16[2,7168]{1,0:T(2,128)(2,1)S(1)}, u32[]{:S(2)}, u32[]{:S(2)}) collective-permute-start(bf16[2,7168]{1,0:T(2,128)(2,1)S(1)} %project.1), channel_id=1, source_target_pairs={{0,192},{4,196},{8,200},{12,204},{16,208},{20,212},{24,216},{28,22... | collective-permute-start | bytes 86024 | tf_op jit(solution)/shard_map/ppermute | solution.py:23
  55.8 1.7 %collective-permute-start.3 = (bf16[2,7168]{1,0:T(2,128)(2,1)S(1)}, bf16[2,7168]{1,0:T(2,128)(2,1)S(1)}, u32[]{:S(2)}, u32[]{:S(2)}) collective-permute-start(bf16[2,7168]{1,0:T(2,128)(2,1)S(1)} %project.1), channel_id=1, source_target_pairs={{0,64},{4,68},{8,72},{12,76},{16,80},{20,84},{24,88},{28,92},{32,9... | collective-permute-start | bytes 86024 | tf_op jit(solution)/shard_map/ppermute | solution.py:23
  57.5 0.7 collective-permute-done.5
  58.2 0.0 collective-permute-done.4
  58.2 1.4 %collective-permute-done.3 = bf16[2,7168]{1,0:T(2,128)(2,1)S(1)} collective-permute-done((bf16[2,7168]{1,0:T(2,128)(2,1)S(1)}, bf16[2,7168]{1,0:T(2,128)(2,1)S(1)}, u32[]{:S(2)}, u32[]{:S(2)}) %collective-permute-start.3) | collective-permute-done | bytes 28704 | tf_op jit(solution)/shard_map/ppermute | solution.py:23
  59.6 0.1 add_convert_fusion.2
  59.7 0.6 collective-permute-start.8
  60.3 2.8 %collective-permute-start.7 = (bf16[2,7168]{1,0:T(2,128)(2,1)S(1)}, bf16[2,7168]{1,0:T(2,128)(2,1)S(1)}, u32[]{:S(2)}, u32[]{:S(2)}) collective-permute-start(bf16[2,7168]{1,0:T(2,128)(2,1)S(1)} %add_convert_fusion.2), channel_id=1, source_target_pairs={{0,48},{4,52},{8,56},{12,60},{16,32},{20,36},{24,40},{28,44},{32,1... | collective-permute-start | bytes 86024 | tf_op jit(solution)/shard_map/ppermute | solution.py:23
  63.1 0.2 collective-permute-start.6
  63.3 1.9 %collective-permute-done.8 = bf16[2,7168]{1,0:T(2,128)(2,1)S(1)} collective-permute-done((bf16[2,7168]{1,0:T(2,128)(2,1)S(1)}, bf16[2,7168]{1,0:T(2,128)(2,1)S(1)}, u32[]{:S(2)}, u32[]{:S(2)}) %collective-permute-start.8) | collective-permute-done | bytes 28704 | tf_op jit(solution)/shard_map/ppermute | solution.py:23
  65.2 0.3 collective-permute-done.7
  65.5 1.4 %collective-permute-done.6 = bf16[2,7168]{1,0:T(2,128)(2,1)S(1)} collective-permute-done((bf16[2,7168]{1,0:T(2,128)(2,1)S(1)}, bf16[2,7168]{1,0:T(2,128)(2,1)S(1)}, u32[]{:S(2)}, u32[]{:S(2)}) %collective-permute-start.6) | collective-permute-done | bytes 28704 | tf_op jit(solution)/shard_map/ppermute | solution.py:23
  66.9 0.1 add_convert_fusion.1
  67.0 0.3 collective-permute-start.11
  67.3 3.9 %collective-permute-start.10 = (bf16[2,7168]{1,0:T(2,128)(2,1)S(1)}, bf16[2,7168]{1,0:T(2,128)(2,1)S(1)}, u32[]{:S(2)}, u32[]{:S(2)}) collective-permute-start(bf16[2,7168]{1,0:T(2,128)(2,1)S(1)} %add_convert_fusion.1), channel_id=1, source_target_pairs={{0,12},{4,8},{8,4},{12,0},{16,28},{20,24},{24,20},{28,16},{32,44},... | collective-permute-start | bytes 86024 | tf_op jit(solution)/shard_map/ppermute | solution.py:23
  71.2 2.4 %collective-permute-start.9 = (bf16[2,7168]{1,0:T(2,128)(2,1)S(1)}, bf16[2,7168]{1,0:T(2,128)(2,1)S(1)}, u32[]{:S(2)}, u32[]{:S(2)}) collective-permute-start(bf16[2,7168]{1,0:T(2,128)(2,1)S(1)} %add_convert_fusion.1), channel_id=1, source_target_pairs={{0,4},{4,0},{8,12},{12,8},{16,20},{20,16},{24,28},{28,24},{32,36},... | collective-permute-start | bytes 86024 | tf_op jit(solution)/shard_map/ppermute | solution.py:23
  73.6 1.6 %collective-permute-done.11 = bf16[2,7168]{1,0:T(2,128)(2,1)S(1)} collective-permute-done((bf16[2,7168]{1,0:T(2,128)(2,1)S(1)}, bf16[2,7168]{1,0:T(2,128)(2,1)S(1)}, u32[]{:S(2)}, u32[]{:S(2)}) %collective-permute-start.11) | collective-permute-done | bytes 28704 | tf_op jit(solution)/shard_map/ppermute | solution.py:23
  75.2 0.0 collective-permute-done.10
  75.2 0.9 %collective-permute-done.9 = bf16[2,7168]{1,0:T(2,128)(2,1)S(1)} collective-permute-done((bf16[2,7168]{1,0:T(2,128)(2,1)S(1)}, bf16[2,7168]{1,0:T(2,128)(2,1)S(1)}, u32[]{:S(2)}, u32[]{:S(2)}) %collective-permute-start.9) | collective-permute-done | bytes 28704 | tf_op jit(solution)/shard_map/ppermute | solution.py:23
  76.1 0.7 add_convert_fusion
  (2 shorter events, 0.0 us)
Async XLA Ops:
  0.8 11.2 %collective-permute-start.2 = (bf16[2,1152]{1,0:T(2,128)(2,1)S(1)}, bf16[2,1152]{1,0:T(2,128)(2,1)S(1)}, u32[]{:S(2)}, u32[]{:S(2)}) collective-permute-start(bf16[2,1152]{1,0:T(2,128)(2,1)S(1)} %message.1), channel_id=1, source_target_pairs={{0,8},{4,12},{8,0},{12,4},{16,24},{20,28},{24,16},{28,20},{32,40},... | collective-permute-start | bytes 13832 | tf_op jit(solution)/shard_map/ppermute | solution.py:176
  8.1 5.7 %collective-permute-start.1 = (bf16[2,1152]{1,0:T(2,128)(2,1)S(1)}, bf16[2,1152]{1,0:T(2,128)(2,1)S(1)}, u32[]{:S(2)}, u32[]{:S(2)}) collective-permute-start(bf16[2,1152]{1,0:T(2,128)(2,1)S(1)} %message.1), channel_id=1, source_target_pairs={{0,12},{4,8},{8,4},{12,0},{16,28},{20,24},{24,20},{28,16},{32,44},... | collective-permute-start | bytes 13832 | tf_op jit(solution)/shard_map/ppermute | solution.py:176
  8.1 5.7 %collective-permute-start = (bf16[2,1152]{1,0:T(2,128)(2,1)S(1)}, bf16[2,1152]{1,0:T(2,128)(2,1)S(1)}, u32[]{:S(2)}, u32[]{:S(2)}) collective-permute-start(bf16[2,1152]{1,0:T(2,128)(2,1)S(1)} %message.1), channel_id=1, source_target_pairs={{0,4},{4,0},{8,12},{12,8},{16,20},{20,16},{24,28},{28,24},{32,36},... | collective-permute-start | bytes 13832 | tf_op jit(solution)/shard_map/ppermute | solution.py:176
  52.8 5.5 %collective-permute-start.5 = (bf16[2,7168]{1,0:T(2,128)(2,1)S(1)}, bf16[2,7168]{1,0:T(2,128)(2,1)S(1)}, u32[]{:S(2)}, u32[]{:S(2)}) collective-permute-start(bf16[2,7168]{1,0:T(2,128)(2,1)S(1)} %project.1), channel_id=1, source_target_pairs={{0,128},{4,132},{8,136},{12,140},{16,144},{20,148},{24,152},{28,15... | collective-permute-start | bytes 86024 | tf_op jit(solution)/shard_map/ppermute | solution.py:23
  54.1 4.2 %collective-permute-start.4 = (bf16[2,7168]{1,0:T(2,128)(2,1)S(1)}, bf16[2,7168]{1,0:T(2,128)(2,1)S(1)}, u32[]{:S(2)}, u32[]{:S(2)}) collective-permute-start(bf16[2,7168]{1,0:T(2,128)(2,1)S(1)} %project.1), channel_id=1, source_target_pairs={{0,192},{4,196},{8,200},{12,204},{16,208},{20,212},{24,216},{28,22... | collective-permute-start | bytes 86024 | tf_op jit(solution)/shard_map/ppermute | solution.py:23
  55.8 3.9 %collective-permute-start.3 = (bf16[2,7168]{1,0:T(2,128)(2,1)S(1)}, bf16[2,7168]{1,0:T(2,128)(2,1)S(1)}, u32[]{:S(2)}, u32[]{:S(2)}) collective-permute-start(bf16[2,7168]{1,0:T(2,128)(2,1)S(1)} %project.1), channel_id=1, source_target_pairs={{0,64},{4,68},{8,72},{12,76},{16,80},{20,84},{24,88},{28,92},{32,9... | collective-permute-start | bytes 86024 | tf_op jit(solution)/shard_map/ppermute | solution.py:23
  59.7 5.5 %collective-permute-start.8 = (bf16[2,7168]{1,0:T(2,128)(2,1)S(1)}, bf16[2,7168]{1,0:T(2,128)(2,1)S(1)}, u32[]{:S(2)}, u32[]{:S(2)}) collective-permute-start(bf16[2,7168]{1,0:T(2,128)(2,1)S(1)} %add_convert_fusion.2), channel_id=1, source_target_pairs={{0,32},{4,36},{8,40},{12,44},{16,48},{20,52},{24,56},{28,60},{32,0... | collective-permute-start | bytes 86024 | tf_op jit(solution)/shard_map/ppermute | solution.py:23
  60.3 5.2 %collective-permute-start.7 = (bf16[2,7168]{1,0:T(2,128)(2,1)S(1)}, bf16[2,7168]{1,0:T(2,128)(2,1)S(1)}, u32[]{:S(2)}, u32[]{:S(2)}) collective-permute-start(bf16[2,7168]{1,0:T(2,128)(2,1)S(1)} %add_convert_fusion.2), channel_id=1, source_target_pairs={{0,48},{4,52},{8,56},{12,60},{16,32},{20,36},{24,40},{28,44},{32,1... | collective-permute-start | bytes 86024 | tf_op jit(solution)/shard_map/ppermute | solution.py:23
  63.1 3.9 %collective-permute-start.6 = (bf16[2,7168]{1,0:T(2,128)(2,1)S(1)}, bf16[2,7168]{1,0:T(2,128)(2,1)S(1)}, u32[]{:S(2)}, u32[]{:S(2)}) collective-permute-start(bf16[2,7168]{1,0:T(2,128)(2,1)S(1)} %add_convert_fusion.2), channel_id=1, source_target_pairs={{0,16},{4,20},{8,24},{12,28},{16,0},{20,4},{24,8},{28,12},{32,48},... | collective-permute-start | bytes 86024 | tf_op jit(solution)/shard_map/ppermute | solution.py:23
  67.0 8.2 %collective-permute-start.11 = (bf16[2,7168]{1,0:T(2,128)(2,1)S(1)}, bf16[2,7168]{1,0:T(2,128)(2,1)S(1)}, u32[]{:S(2)}, u32[]{:S(2)}) collective-permute-start(bf16[2,7168]{1,0:T(2,128)(2,1)S(1)} %add_convert_fusion.1), channel_id=1, source_target_pairs={{0,8},{4,12},{8,0},{12,4},{16,24},{20,28},{24,16},{28,20},{32,40},... | collective-permute-start | bytes 86024 | tf_op jit(solution)/shard_map/ppermute | solution.py:23
  67.3 7.8 %collective-permute-start.10 = (bf16[2,7168]{1,0:T(2,128)(2,1)S(1)}, bf16[2,7168]{1,0:T(2,128)(2,1)S(1)}, u32[]{:S(2)}, u32[]{:S(2)}) collective-permute-start(bf16[2,7168]{1,0:T(2,128)(2,1)S(1)} %add_convert_fusion.1), channel_id=1, source_target_pairs={{0,12},{4,8},{8,4},{12,0},{16,28},{20,24},{24,20},{28,16},{32,44},... | collective-permute-start | bytes 86024 | tf_op jit(solution)/shard_map/ppermute | solution.py:23
  71.2 4.8 %collective-permute-start.9 = (bf16[2,7168]{1,0:T(2,128)(2,1)S(1)}, bf16[2,7168]{1,0:T(2,128)(2,1)S(1)}, u32[]{:S(2)}, u32[]{:S(2)}) collective-permute-start(bf16[2,7168]{1,0:T(2,128)(2,1)S(1)} %add_convert_fusion.1), channel_id=1, source_target_pairs={{0,4},{4,0},{8,12},{12,8},{16,20},{20,16},{24,28},{28,24},{32,36},... | collective-permute-start | bytes 86024 | tf_op jit(solution)/shard_map/ppermute | solution.py:23

commit v18 on v17

--- a/solution.py
+++ b/solution.py
@@ -75,6 +75,18 @@
         live_ref[r : r + 1, :] = jnp.max(jnp.where(alive, 1.0, 0.0), axis=0, keepdims=True)
     for copy in copies[2:]:
         copy.wait()
+
+
+def spread_kernel(here_ref, *refs):
+    *parts, out_ref = refs
+    near = len(parts)
+    values = [part[...].astype(F32) for part in parts]
+    for k in range(near):
+        away = lax.rem(here_ref[0], near) ^ k
+        value = values[0]
+        for j in range(1, near):
+            value = jnp.where(away == j, values[j], value)
+        out_ref[:, k] = jnp.broadcast_to(value[None], (out_ref.shape[0],) + value.shape).astype(BF16)
 
 
 def attend_kernel(rows, heads, latent, rope, q_ref, keys_ref, live_ref, state_ref):
@@ -194,15 +206,20 @@
         here.reshape(1), stay(lengths), stay(page_table), stay(latent_cache.reshape(tokens, width)),
         stay(w_uv), stay(w_out),
     )
-    away = lax.broadcasted_iota(jnp.int32, (near, 1, 1), 0) ^ (here % near)
-    column = jnp.broadcast_to(message[None], (near, rows, size))
-    for k in (2, 3, 1):
-        column = jnp.where(away == k, others[k][None], column)
-    column, live, keys, w_uv, w_out_near = lax.optimization_barrier((column, live, keys, w_uv, w_out_near))
+    ready = lax.optimization_barrier((message, *others.values(), live, keys, w_uv, w_out_near))
+    message, live, keys, w_uv, w_out_near = ready[0], *ready[near:]
+    others = dict(zip(others, ready[1:near]))
+    query = pl.pallas_call(
+        spread_kernel,
+        out_shape=jax.ShapeDtypeStruct((count // near, near, rows, size), BF16),
+        in_specs=[smem] + [vmem] * near,
+        out_specs=vmem,
+        compiler_params=params,
+        name="spread",
+    )(here.reshape(1), message, *[others[k] for k in range(1, near)])
     planes = [[i * near + k for i in range(count // near)] for k in range(near)]
     query = lax.all_to_all(
-        jnp.broadcast_to(column[None], (count // near, near, rows, size)),
-        CTX, split_axis=0, concat_axis=0, axis_index_groups=planes, tiled=True,
+        query, CTX, split_axis=0, concat_axis=0, axis_index_groups=planes, tiled=True
     )
 
     state_size = heads * latent + LANES

time: 76.9 us -> 76.7 us (level)
  no operation moved by 1% of the time
where the time goes in v18:
time: 76.7 us; the launch traced here: 76.5 us
  blocking collectives  36.2 us (47%)
  starting transfers between devices  23.7 us (31%)
  waiting for transfers between devices  10.1 us (13%)
  Pallas kernels  5.63 us (7%)
  other arithmetic  0.8 us (1%)
    all_to_all x1, blocking collectives, local(): state = lax.all_to_all(state, CTX, split_axis=0, concat_axis=0, tiled=True)  22.1 us
    ppermute x9, starting transfers between devices, sum_of_four(): lax.ppermute(x, CTX, xor_pairs(count, k << low))  14.9 us
    all_to_all x1, blocking collectives, local(): lax.all_to_all(query, CTX, split_axis=0, concat_axis=0, axis_index_groups...  14.2 us
    ppermute x3, starting transfers between devices, local(): lax.ppermute(message, CTX, xor_pairs(count, k))  8.75 us
    ppermute x9, waiting for transfers between devices, sum_of_four(): lax.ppermute(x, CTX, xor_pairs(count, k << low))  8.27 us
    pallas_call x1, Pallas kernels, local(): pl.pallas_call(functools.partial(fetch_kernel, page_len), out_shape=(pltp...  2.38 us
    ppermute x3, waiting for transfers between devices, local(): lax.ppermute(message, CTX, xor_pairs(count, k))  1.85 us
  transfers between devices with their start and end apart: 12, of which 8 were waited for; matrix products, arithmetic and copies ran while one was open for 0% of the time, Pallas kernels for 3%

profile of v18, /device:TPU:2, one launch (start us, length us, event | category | flops | bytes accessed | tf_op | source)
XLA Modules:
  0.0 76.5 jit_solution(4639940724360377088)
XLA Ops:
  0.0 0.8 %message.1.refs_0_ = bf16[2,1152]{1,0:T(2,128)(2,1)S(1)} custom-call(bf16[2,2,512]{2,1,0:T(2,128)(2,1)} %q_latent_hbm.1, bf16[2,2,64]{2,1,0:T(2,128)(2,1)} %q_rope_hbm.1), custom_call_target="tpu_custom_call" | custom-call | tf_op jit(solution)/shard_map/message/pallas_call | solution.py:177
  0.8 7.3 %collective-permute-start.2 = (bf16[2,1152]{1,0:T(2,128)(2,1)S(1)}, bf16[2,1152]{1,0:T(2,128)(2,1)S(1)}, u32[]{:S(2)}, u32[]{:S(2)}) collective-permute-start(bf16[2,1152]{1,0:T(2,128)(2,1)S(1)} %message.1.refs_0_), channel_id=1, source_target_pairs={{0,8},{4,12},{8,0},{12,4},{16,24},{20,28},{24,16},{28,20},{32,40},... | collective-permute-start | bytes 13832 | tf_op jit(solution)/shard_map/ppermute | solution.py:188
  8.1 0.0 collective-permute-start.1
  8.1 1.5 %collective-permute-start = (bf16[2,1152]{1,0:T(2,128)(2,1)S(1)}, bf16[2,1152]{1,0:T(2,128)(2,1)S(1)}, u32[]{:S(2)}, u32[]{:S(2)}) collective-permute-start(bf16[2,1152]{1,0:T(2,128)(2,1)S(1)} %message.1.refs_0_), channel_id=1, source_target_pairs={{0,4},{4,0},{8,12},{12,8},{16,20},{20,16},{24,28},{28,24},{32,36},... | collective-permute-start | bytes 13832 | tf_op jit(solution)/shard_map/ppermute | solution.py:188
  9.6 2.4 %fetch.1 = (f32[2,512]{1,0:T(2,128)S(1)}, bf16[512,576]{1,0:T(8,128)(2,1)S(1)}, bf16[2,512,128]{2,1,0:T(8,128)(2,1)S(1)}, bf16[256,7168]{1,0:T(8,128)(2,1)S(1)}) custom-call(s32[1]{0:T(128)} %bitcast.here_ref, s32[2]{0:T(128)} %lengths_hbm.1, s32[2,256]{1,0:T(2,128)} %table_hbm.1, bf16[512,576]{1,0:T(8,128)(2,1)} %bitcast.4, bf16[2,512,128]{2,1,0:T(8,128)(2,1)} %w_uv_hbm.1, ...), custom_call_target="tpu_custom_call" | custom-call | bytes 5242880 | tf_op jit(solution)/shard_map/fetch/pallas_call | solution.py:189
  11.9 0.0 collective-permute-done.2.refs_2_
  12.0 1.8 %collective-permute-done.1.refs_3_ = bf16[2,1152]{1,0:T(2,128)(2,1)S(1)} collective-permute-done((bf16[2,1152]{1,0:T(2,128)(2,1)S(1)}, bf16[2,1152]{1,0:T(2,128)(2,1)S(1)}, u32[]{:S(2)}, u32[]{:S(2)}) %collective-permute-start.1) | collective-permute-done | bytes 4640 | tf_op jit(solution)/shard_map/ppermute | solution.py:188
  13.8 0.0 collective-permute-done.refs_1_
  13.9 14.2 %all_to_all.10 = bf16[16,4,2,1152]{3,2,1,0:T(2,128)(2,1)S(1)} all-to-all(bf16[16,4,2,1152]{3,2,1,0:T(2,128)(2,1)S(1)} %spread.1), channel_id=1, replica_groups={{0,16,32,48,64,80,96,112,128,144,160,176,192,208,224,240},{4,20,36,52,6..., dimensions={0} | all-to-all | bytes 589824 | tf_op jit(solution)/shard_map/all_to_all | solution.py:221
  28.0 1.2 %attend.1 = bf16[64,2,1152]{2,1,0:T(2,128)(2,1)S(1)} custom-call(bf16[64,2,1152]{2,1,0:T(2,128)(2,1)S(1)} %bitcast.3, bf16[512,576]{1,0:T(8,128)(2,1)S(1)} %get-tuple-element.25.keys_ref, f32[2,512]{1,0:T(2,128)S(1)} %get-tuple-element.26.live_ref), custom_call_target="tpu_custom_call" | custom-call | tf_op jit(solution)/shard_map/attend/pallas_call | solution.py:226
  29.2 22.1 %all_to_all.11.messages_ref = bf16[64,2,1152]{2,1,0:T(2,128)(2,1)S(1)} all-to-all(bf16[64,2,1152]{2,1,0:T(2,128)(2,1)S(1)} %attend.1), channel_id=1, replica_groups=mesh['ctx'=64,'grp'=4] {'ctx'}, dimensions={0} | all-to-all | bytes 589824 | tf_op jit(solution)/shard_map/all_to_all | solution.py:235
  51.3 1.3 %project.1 = bf16[2,7168]{1,0:T(2,128)(2,1)S(1)} custom-call(bf16[64,2,1152]{2,1,0:T(2,128)(2,1)S(1)} %all_to_all.11.messages_ref, bf16[2,512,128]{2,1,0:T(8,128)(2,1)S(1)} %get-tuple-element.27.w_uv_ref, bf16[256,7168]{1,0:T(8,128)(2,1)S(1)} %get-tuple-element.28.w_out_ref), custom_call_target="tpu_custom_call" | custom-call | tf_op jit(solution)/shard_map/project/pallas_call | solution.py:236
  52.5 1.3 %collective-permute-start.5 = (bf16[2,7168]{1,0:T(2,128)(2,1)S(1)}, bf16[2,7168]{1,0:T(2,128)(2,1)S(1)}, u32[]{:S(2)}, u32[]{:S(2)}) collective-permute-start(bf16[2,7168]{1,0:T(2,128)(2,1)S(1)} %project.1), channel_id=1, source_target_pairs={{0,128},{4,132},{8,136},{12,140},{16,144},{20,148},{24,152},{28,15... | collective-permute-start | bytes 86024 | tf_op jit(solution)/shard_map/ppermute | solution.py:23
  53.8 1.7 %collective-permute-start.4 = (bf16[2,7168]{1,0:T(2,128)(2,1)S(1)}, bf16[2,7168]{1,0:T(2,128)(2,1)S(1)}, u32[]{:S(2)}, u32[]{:S(2)}) collective-permute-start(bf16[2,7168]{1,0:T(2,128)(2,1)S(1)} %project.1), channel_id=1, source_target_pairs={{0,192},{4,196},{8,200},{12,204},{16,208},{20,212},{24,216},{28,22... | collective-permute-start | bytes 86024 | tf_op jit(solution)/shard_map/ppermute | solution.py:23
  55.6 1.7 %collective-permute-start.3 = (bf16[2,7168]{1,0:T(2,128)(2,1)S(1)}, bf16[2,7168]{1,0:T(2,128)(2,1)S(1)}, u32[]{:S(2)}, u32[]{:S(2)}) collective-permute-start(bf16[2,7168]{1,0:T(2,128)(2,1)S(1)} %project.1), channel_id=1, source_target_pairs={{0,64},{4,68},{8,72},{12,76},{16,80},{20,84},{24,88},{28,92},{32,9... | collective-permute-start | bytes 86024 | tf_op jit(solution)/shard_map/ppermute | solution.py:23
  57.3 0.7 collective-permute-done.5
  58.0 0.0 collective-permute-done.4
  58.0 1.4 %collective-permute-done.3 = bf16[2,7168]{1,0:T(2,128)(2,1)S(1)} collective-permute-done((bf16[2,7168]{1,0:T(2,128)(2,1)S(1)}, bf16[2,7168]{1,0:T(2,128)(2,1)S(1)}, u32[]{:S(2)}, u32[]{:S(2)}) %collective-permute-start.3) | collective-permute-done | bytes 28704 | tf_op jit(solution)/shard_map/ppermute | solution.py:23
  59.4 0.1 add_convert_fusion.2
  59.5 0.7 collective-permute-start.8
  60.2 2.7 %collective-permute-start.7 = (bf16[2,7168]{1,0:T(2,128)(2,1)S(1)}, bf16[2,7168]{1,0:T(2,128)(2,1)S(1)}, u32[]{:S(2)}, u32[]{:S(2)}) collective-permute-start(bf16[2,7168]{1,0:T(2,128)(2,1)S(1)} %add_convert_fusion.2), channel_id=1, source_target_pairs={{0,48},{4,52},{8,56},{12,60},{16,32},{20,36},{24,40},{28,44},{32,1... | collective-permute-start | bytes 86024 | tf_op jit(solution)/shard_map/ppermute | solution.py:23
  62.8 0.3 collective-permute-start.6
  63.1 1.9 %collective-permute-done.8 = bf16[2,7168]{1,0:T(2,128)(2,1)S(1)} collective-permute-done((bf16[2,7168]{1,0:T(2,128)(2,1)S(1)}, bf16[2,7168]{1,0:T(2,128)(2,1)S(1)}, u32[]{:S(2)}, u32[]{:S(2)}) %collective-permute-start.8) | collective-permute-done | bytes 28704 | tf_op jit(solution)/shard_map/ppermute | solution.py:23
  65.0 0.3 collective-permute-done.7
  65.3 1.4 %collective-permute-done.6 = bf16[2,7168]{1,0:T(2,128)(2,1)S(1)} collective-permute-done((bf16[2,7168]{1,0:T(2,128)(2,1)S(1)}, bf16[2,7168]{1,0:T(2,128)(2,1)S(1)}, u32[]{:S(2)}, u32[]{:S(2)}) %collective-permute-start.6) | collective-permute-done | bytes 28704 | tf_op jit(solution)/shard_map/ppermute | solution.py:23
  66.7 0.1 add_convert_fusion.1
  66.8 0.3 collective-permute-start.11
  67.1 3.9 %collective-permute-start.10 = (bf16[2,7168]{1,0:T(2,128)(2,1)S(1)}, bf16[2,7168]{1,0:T(2,128)(2,1)S(1)}, u32[]{:S(2)}, u32[]{:S(2)}) collective-permute-start(bf16[2,7168]{1,0:T(2,128)(2,1)S(1)} %add_convert_fusion.1), channel_id=1, source_target_pairs={{0,12},{4,8},{8,4},{12,0},{16,28},{20,24},{24,20},{28,16},{32,44},... | collective-permute-start | bytes 86024 | tf_op jit(solution)/shard_map/ppermute | solution.py:23
  71.0 2.3 %collective-permute-start.9 = (bf16[2,7168]{1,0:T(2,128)(2,1)S(1)}, bf16[2,7168]{1,0:T(2,128)(2,1)S(1)}, u32[]{:S(2)}, u32[]{:S(2)}) collective-permute-start(bf16[2,7168]{1,0:T(2,128)(2,1)S(1)} %add_convert_fusion.1), channel_id=1, source_target_pairs={{0,4},{4,0},{8,12},{12,8},{16,20},{20,16},{24,28},{28,24},{32,36},... | collective-permute-start | bytes 86024 | tf_op jit(solution)/shard_map/ppermute | solution.py:23
  73.3 1.6 %collective-permute-done.11 = bf16[2,7168]{1,0:T(2,128)(2,1)S(1)} collective-permute-done((bf16[2,7168]{1,0:T(2,128)(2,1)S(1)}, bf16[2,7168]{1,0:T(2,128)(2,1)S(1)}, u32[]{:S(2)}, u32[]{:S(2)}) %collective-permute-start.11) | collective-permute-done | bytes 28704 | tf_op jit(solution)/shard_map/ppermute | solution.py:23
  74.9 0.0 collective-permute-done.10
  74.9 0.9 %collective-permute-done.9 = bf16[2,7168]{1,0:T(2,128)(2,1)S(1)} collective-permute-done((bf16[2,7168]{1,0:T(2,128)(2,1)S(1)}, bf16[2,7168]{1,0:T(2,128)(2,1)S(1)}, u32[]{:S(2)}, u32[]{:S(2)}) %collective-permute-start.9) | collective-permute-done | bytes 28704 | tf_op jit(solution)/shard_map/ppermute | solution.py:23
  75.8 0.7 add_convert_fusion
  (1 shorter events, 0.0 us)
Async XLA Ops:
  0.8 11.1 %collective-permute-start.2 = (bf16[2,1152]{1,0:T(2,128)(2,1)S(1)}, bf16[2,1152]{1,0:T(2,128)(2,1)S(1)}, u32[]{:S(2)}, u32[]{:S(2)}) collective-permute-start(bf16[2,1152]{1,0:T(2,128)(2,1)S(1)} %message.1.refs_0_), channel_id=1, source_target_pairs={{0,8},{4,12},{8,0},{12,4},{16,24},{20,28},{24,16},{28,20},{32,40},... | collective-permute-start | bytes 13832 | tf_op jit(solution)/shard_map/ppermute | solution.py:188
  8.1 5.7 %collective-permute-start.1 = (bf16[2,1152]{1,0:T(2,128)(2,1)S(1)}, bf16[2,1152]{1,0:T(2,128)(2,1)S(1)}, u32[]{:S(2)}, u32[]{:S(2)}) collective-permute-start(bf16[2,1152]{1,0:T(2,128)(2,1)S(1)} %message.1.refs_0_), channel_id=1, source_target_pairs={{0,12},{4,8},{8,4},{12,0},{16,28},{20,24},{24,20},{28,16},{32,44},... | collective-permute-start | bytes 13832 | tf_op jit(solution)/shard_map/ppermute | solution.py:188
  8.1 5.7 %collective-permute-start = (bf16[2,1152]{1,0:T(2,128)(2,1)S(1)}, bf16[2,1152]{1,0:T(2,128)(2,1)S(1)}, u32[]{:S(2)}, u32[]{:S(2)}) collective-permute-start(bf16[2,1152]{1,0:T(2,128)(2,1)S(1)} %message.1.refs_0_), channel_id=1, source_target_pairs={{0,4},{4,0},{8,12},{12,8},{16,20},{20,16},{24,28},{28,24},{32,36},... | collective-permute-start | bytes 13832 | tf_op jit(solution)/shard_map/ppermute | solution.py:188
  52.5 5.5 %collective-permute-start.5 = (bf16[2,7168]{1,0:T(2,128)(2,1)S(1)}, bf16[2,7168]{1,0:T(2,128)(2,1)S(1)}, u32[]{:S(2)}, u32[]{:S(2)}) collective-permute-start(bf16[2,7168]{1,0:T(2,128)(2,1)S(1)} %project.1), channel_id=1, source_target_pairs={{0,128},{4,132},{8,136},{12,140},{16,144},{20,148},{24,152},{28,15... | collective-permute-start | bytes 86024 | tf_op jit(solution)/shard_map/ppermute | solution.py:23
  53.8 4.2 %collective-permute-start.4 = (bf16[2,7168]{1,0:T(2,128)(2,1)S(1)}, bf16[2,7168]{1,0:T(2,128)(2,1)S(1)}, u32[]{:S(2)}, u32[]{:S(2)}) collective-permute-start(bf16[2,7168]{1,0:T(2,128)(2,1)S(1)} %project.1), channel_id=1, source_target_pairs={{0,192},{4,196},{8,200},{12,204},{16,208},{20,212},{24,216},{28,22... | collective-permute-start | bytes 86024 | tf_op jit(solution)/shard_map/ppermute | solution.py:23
  55.6 3.9 %collective-permute-start.3 = (bf16[2,7168]{1,0:T(2,128)(2,1)S(1)}, bf16[2,7168]{1,0:T(2,128)(2,1)S(1)}, u32[]{:S(2)}, u32[]{:S(2)}) collective-permute-start(bf16[2,7168]{1,0:T(2,128)(2,1)S(1)} %project.1), channel_id=1, source_target_pairs={{0,64},{4,68},{8,72},{12,76},{16,80},{20,84},{24,88},{28,92},{32,9... | collective-permute-start | bytes 86024 | tf_op jit(solution)/shard_map/ppermute | solution.py:23
  59.5 5.5 %collective-permute-start.8 = (bf16[2,7168]{1,0:T(2,128)(2,1)S(1)}, bf16[2,7168]{1,0:T(2,128)(2,1)S(1)}, u32[]{:S(2)}, u32[]{:S(2)}) collective-permute-start(bf16[2,7168]{1,0:T(2,128)(2,1)S(1)} %add_convert_fusion.2), channel_id=1, source_target_pairs={{0,32},{4,36},{8,40},{12,44},{16,48},{20,52},{24,56},{28,60},{32,0... | collective-permute-start | bytes 86024 | tf_op jit(solution)/shard_map/ppermute | solution.py:23
  60.2 5.1 %collective-permute-start.7 = (bf16[2,7168]{1,0:T(2,128)(2,1)S(1)}, bf16[2,7168]{1,0:T(2,128)(2,1)S(1)}, u32[]{:S(2)}, u32[]{:S(2)}) collective-permute-start(bf16[2,7168]{1,0:T(2,128)(2,1)S(1)} %add_convert_fusion.2), channel_id=1, source_target_pairs={{0,48},{4,52},{8,56},{12,60},{16,32},{20,36},{24,40},{28,44},{32,1... | collective-permute-start | bytes 86024 | tf_op jit(solution)/shard_map/ppermute | solution.py:23
  62.8 3.9 %collective-permute-start.6 = (bf16[2,7168]{1,0:T(2,128)(2,1)S(1)}, bf16[2,7168]{1,0:T(2,128)(2,1)S(1)}, u32[]{:S(2)}, u32[]{:S(2)}) collective-permute-start(bf16[2,7168]{1,0:T(2,128)(2,1)S(1)} %add_convert_fusion.2), channel_id=1, source_target_pairs={{0,16},{4,20},{8,24},{12,28},{16,0},{20,4},{24,8},{28,12},{32,48},... | collective-permute-start | bytes 86024 | tf_op jit(solution)/shard_map/ppermute | solution.py:23
  66.8 8.2 %collective-permute-start.11 = (bf16[2,7168]{1,0:T(2,128)(2,1)S(1)}, bf16[2,7168]{1,0:T(2,128)(2,1)S(1)}, u32[]{:S(2)}, u32[]{:S(2)}) collective-permute-start(bf16[2,7168]{1,0:T(2,128)(2,1)S(1)} %add_convert_fusion.1), channel_id=1, source_target_pairs={{0,8},{4,12},{8,0},{12,4},{16,24},{20,28},{24,16},{28,20},{32,40},... | collective-permute-start | bytes 86024 | tf_op jit(solution)/shard_map/ppermute | solution.py:23
  67.1 7.8 %collective-permute-start.10 = (bf16[2,7168]{1,0:T(2,128)(2,1)S(1)}, bf16[2,7168]{1,0:T(2,128)(2,1)S(1)}, u32[]{:S(2)}, u32[]{:S(2)}) collective-permute-start(bf16[2,7168]{1,0:T(2,128)(2,1)S(1)} %add_convert_fusion.1), channel_id=1, source_target_pairs={{0,12},{4,8},{8,4},{12,0},{16,28},{20,24},{24,20},{28,16},{32,44},... | collective-permute-start | bytes 86024 | tf_op jit(solution)/shard_map/ppermute | solution.py:23
  71.0 4.8 %collective-permute-start.9 = (bf16[2,7168]{1,0:T(2,128)(2,1)S(1)}, bf16[2,7168]{1,0:T(2,128)(2,1)S(1)}, u32[]{:S(2)}, u32[]{:S(2)}) collective-permute-start(bf16[2,7168]{1,0:T(2,128)(2,1)S(1)} %add_convert_fusion.1), channel_id=1, source_target_pairs={{0,4},{4,0},{8,12},{12,8},{16,20},{20,16},{24,28},{28,24},{32,36},... | collective-permute-start | bytes 86024 | tf_op jit(solution)/shard_map/ppermute | solution.py:23
